TPU v7x, 32 devices: a whole 2x2x4 slice. The times are simulated.
32 devices in a mesh: groups: 2 (over x), dp: 16 (over z, y, core).
Axes of the slice: x: 2, y: 2, z: 4, core: 2. Of those that a mesh axis runs over, the one named last changes fastest.
Arguments:
- context: bfloat16 [16384, 2048], P(('groups', 'dp')), parts along dimension 0, may hold values from -6 to 6
- residual: bfloat16 [16384, 4096], P(('groups', 'dp')), parts along dimension 0
- out_proj: bfloat16 [2048, 4096], P(None, 'dp'), may hold values from -0.125 to 0.125
- norm_gain: float32 [4096], replicated, may hold values from 0.5 to 1.5
- lengths: int32 [32], P(('groups', 'dp')), parts along dimension 0, may hold values from 64 to 512, as said below
- queries: bfloat16 [3584, 4096], P(('groups', 'dp')), parts along dimension 0
- pattern: int32 [32, 7], P(('groups', 'dp')), parts along dimension 0, may hold values from 0 to 1, as said below
Outputs:
- embedded: float32 [32, 4096], P(('groups', 'dp')), parts along dimension 0
- recalled: float32 [32, 4096], P(('groups', 'dp')), parts along dimension 0
- log_total: float32 [32], P(('groups', 'dp')), parts along dimension 0
There are 2 independent parts, one for each index of `groups`. A program takes and returns all parts, laid end to end along the dimension named above; an argument that names none is the same for every part. Nothing has to cross between parts.
Inputs may be any that keep to these rules, and one draw needn't show every extreme that they name: `lengths`: token slots of a passage from its length on are padding; some passage of every draw is full. `pattern`: entry 1 marks a query block as candidates of all passages of a passage block; every row holds one or two ones, and some row two.
All inputs are finite; a program needn't handle non-finite values.
Results may differ from a plain program's by a relative error of at most 0.007.
Values may be sent and summed in bfloat16 or wider, within the bound.
No kernel may reach another device: no remote copies, remote signals or barrier semaphores. Data moves between devices by JAX's collectives and lax.ppermute only.
A program may use at most 128 MiB of HBM per device.

v0:
```python
import math

import jax
import jax.numpy as jnp
from jax import lax
from jax.sharding import PartitionSpec as P

QB = 256


def per_device(context, residual, out_proj, norm_gain, lengths, queries, pattern):
    tok_rows = context.shape[0]
    features = residual.shape[1]
    passages_here = lengths.shape[0]
    seq_len = tok_rows // passages_here
    branch = jnp.dot(
        context,
        lax.all_gather(out_proj, "dp", axis=1, tiled=True),
        preferred_element_type=jnp.float32,
    )
    hidden_sum = residual.astype(jnp.float32) + branch
    normed = (
        hidden_sum
        * lax.rsqrt(jnp.mean(hidden_sum * hidden_sum, axis=-1, keepdims=True) + 1e-05)
        * norm_gain
    )
    shaped = normed.reshape(passages_here, seq_len, features)
    valid_mask = (jnp.arange(seq_len)[None, :] < lengths[:, None]).astype(jnp.float32)
    pooled = jnp.sum(shaped * valid_mask[:, :, None], axis=1) / lengths.astype(jnp.float32)[:, None]
    embedded = pooled * lax.rsqrt(jnp.mean(pooled * pooled, axis=-1, keepdims=True) + 1e-06)
    emb_half = embedded.astype(jnp.bfloat16)
    temper = 1.0 / (0.02 * math.sqrt(features))
    contract = (((1,), (1,)), ((), ()))
    gathered = lax.all_gather(queries, "dp", axis=0, tiled=True)
    scores = (
        lax.dot_general(emb_half, gathered, contract, preferred_element_type=jnp.float32) * temper
    )
    cand_mask = jnp.repeat(pattern, QB, axis=1) > 0
    peak_score = jnp.max(jnp.where(cand_mask, scores, -jnp.inf), axis=1)
    weights = jnp.where(cand_mask, jnp.exp(scores - peak_score[:, None]), 0.0)
    totals = jnp.sum(weights, axis=1)
    recalled = (
        jnp.dot(weights.astype(jnp.bfloat16), gathered, preferred_element_type=jnp.float32)
        / totals[:, None]
    )
    log_total = peak_score + jnp.log(totals)
    return (embedded, recalled, log_total)


def solution(mesh):
    in_specs = (
        P(("groups", "dp"), None),
        P(("groups", "dp"), None),
        P(None, "dp"),
        P(),
        P(("groups", "dp")),
        P(("groups", "dp"), None),
        P(("groups", "dp"), None),
    )
    out_specs = (P(("groups", "dp"), None), P(("groups", "dp"), None), P(("groups", "dp")))
    return jax.shard_map(
        per_device, mesh=mesh, in_specs=in_specs, out_specs=out_specs, check_vma=False
    )
```

profile of v0, /device:TPU:0, one launch (start us, length us, event | category | flops | bytes accessed | tf_op | source)
XLA Modules:
  0.0 286.5 jit_solution(8110786776017651474)
XLA Ops:
  7.2 0.0 copy-start
  7.2 0.0 all-gather.3.cloned.1.call-start
  7.2 0.7 all-gather.3.cloned.1.call-update
  7.9 0.0 all-gather.5.cloned.1.call-start
  8.0 0.7 all-gather.5.cloned.1.call-update
  9.3 0.7 compare_bitcast_fusion
  10.0 0.1 broadcast_in_dim.8
  10.1 0.0 copy-start.1
  10.1 133.2 %all-gather.3.cloned.1.call-done = bf16[2048,4096]{1,0:T(8,128)(2,1)} async-done(((bf16[2048,256]{1,0:T(8,128)(2,1)}), bf16[2048,4096]{1,0:T(8,128)(2,1)}) %all-gather.3.cloned.1.call-update) | async-done | bytes 16777232 | tf_op jit(solution)/shard_map/all_gather | solution.py:18
  143.2 0.0 copy-done
  143.2 13.3 %multiply_reduce_fusion.1 = (f32[512]{0:T(512)S(1)}, f32[512,4096]{1,0:T(8,128)S(1)}) fusion(bf16[512,2048]{1,0:T(8,128)(2,1)S(1)} %copy-done, bf16[2048,4096]{1,0:T(8,128)(2,1)} %all-gather.3.cloned.1.call-done, bf16[512,4096]{1,0:T(8,128)(2,1)} %param.8), kind=kOutput, calls=%fused_computation.1 | convolution fusion | flops 8598323200 | bytes 31459328 | tf_op jit(solution)/shard_map/dot_general | solution.py:16
  156.5 0.0 copy-done.1
  156.5 1.9 multiply_reduce_fusion
  158.5 0.6 multiply_reduce_fusion.2
  159.8 0.6 fusion.3
  160.4 97.2 %all-gather.5.cloned.1.call-done = bf16[1792,4096]{1,0:T(8,128)(2,1)} async-done(((bf16[112,4096]{1,0:T(8,128)(2,1)}), bf16[1792,4096]{1,0:T(8,128)(2,1)}) %all-gather.5.cloned.1.call-update) | async-done | bytes 14680080 | tf_op jit(solution)/shard_map/all_gather | solution.py:34
  257.6 9.1 %convolution_reduce_fusion = f32[1792]{0:T(1024)S(1)} fusion(bf16[4096,1]{0,1:T(2,128)(2,1)S(1)} %reshape.99, bf16[1792,4096]{1,0:T(8,128)(2,1)} %all-gather.5.cloned.1.call-done), kind=kOutput, calls=%fused_computation.3 | convolution fusion | flops 14680064 | bytes 14695424 | tf_op jit(solution)/shard_map/dot_general | solution.py:36
  266.7 0.6 select_reduce_fusion
  267.3 1.3 fusion
  270.0 7.2 %fusion.4 = f32[1,4096]{1,0:T(1,128)S(1)} fusion(bf16[1792,1]{0,1:T(2,128)(2,1)S(1)} %reshape.101, bf16[1792,4096]{1,0:T(8,128)(2,1)} %all-gather.5.cloned.1.call-done), kind=kOutput, calls=%fused_computation.17 | convolution fusion | flops 14680064 | bytes 14700032 | tf_op jit(solution)/shard_map/dot_general | solution.py:43
  277.2 1.3 broadcast_divide_fusion
  (5 shorter events, 0.0 us)
Async XLA Ops:
  7.2 136.1 %copy-start = (bf16[512,2048]{1,0:T(8,128)(2,1)S(1)}, bf16[512,2048]{1,0:T(8,128)(2,1)}, u32[]{:S(2)}) copy-start(bf16[512,2048]{1,0:T(8,128)(2,1)} %param.7) | copy-start | bytes 6291460
  7.2 136.1 %all-gather.3.cloned.1.call-start = ((), (), s32[]{:S(2)}) async-start(), calls=%async_computation | async-start | bytes 17825792 | tf_op jit(solution)/shard_map/all_gather | solution.py:18
  7.9 249.7 %all-gather.5.cloned.1.call-start = ((), (), s32[]{:S(2)}) async-start(), calls=%async_computation.1 | async-start | bytes 15597568 | tf_op jit(solution)/shard_map/all_gather | solution.py:34
  10.1 146.5 %copy-start.1 = (f32[4096]{0:T(1024)S(1)}, f32[4096]{0:T(1024)}, u32[]{:S(2)}) copy-start(f32[4096]{0:T(1024)} %param.10) | copy-start | bytes 49156
Sparse Core Ops, SparseCore 0:
  10.2 133.0 all-gather.2
  145.5 112.0 all-gather.4
where the time goes:
time: 287 us; the launch traced here: 286 us
  waiting for transfers between devices  232 us (81%)
  matrix products  29.5 us (10%)
  between operations  18 us (6%)
  other arithmetic  7.06 us (2%)
    all_gather x1, waiting for transfers between devices, per_device(): lax.all_gather(out_proj, 'dp', axis=1, tiled=True)  133 us
    all_gather x1, waiting for transfers between devices, per_device(): gathered = lax.all_gather(queries, 'dp', axis=0, tiled=True)  97.2 us
    dot_general x1, matrix products, per_device(): jnp.dot(context, lax.all_gather(out_proj, 'dp', axis=1, tiled=True), pref...  13.3 us
    dot_general x1, matrix products, per_device(): lax.dot_general(emb_half, gathered, contract, preferred_element_type=jnp....  9.07 us
    dot_general x1, matrix products, per_device(): jnp.dot(weights.astype(jnp.bfloat16), gathered, preferred_element_type=jn...  7.17 us
  transfers between devices with their start and end apart: 2, of which 2 were waited for; matrix products, arithmetic and copies ran while one was open for 6% of the time, Pallas kernels for 0%

commit v1 on v0

--- a/solution.py
+++ b/solution.py
@@ -6,6 +6,7 @@
 from jax.sharding import PartitionSpec as P
 
 QB = 256
+LANES = 128
 
 
 def per_device(context, residual, out_proj, norm_gain, lengths, queries, pattern):
@@ -13,6 +14,10 @@
     features = residual.shape[1]
     passages_here = lengths.shape[0]
     seq_len = tok_rows // passages_here
+    query_rows = queries.shape[0]
+    blocks = pattern.shape[1]
+    ranks = lax.axis_size("dp")
+    me = lax.axis_index("dp")
     branch = jnp.dot(
         context,
         lax.all_gather(out_proj, "dp", axis=1, tiled=True),
@@ -31,18 +36,31 @@
     emb_half = embedded.astype(jnp.bfloat16)
     temper = 1.0 / (0.02 * math.sqrt(features))
     contract = (((1,), (1,)), ((), ()))
-    gathered = lax.all_gather(queries, "dp", axis=0, tiled=True)
-    scores = (
-        lax.dot_general(emb_half, gathered, contract, preferred_element_type=jnp.float32) * temper
-    )
-    cand_mask = jnp.repeat(pattern, QB, axis=1) > 0
-    peak_score = jnp.max(jnp.where(cand_mask, scores, -jnp.inf), axis=1)
-    weights = jnp.where(cand_mask, jnp.exp(scores - peak_score[:, None]), 0.0)
-    totals = jnp.sum(weights, axis=1)
-    recalled = (
-        jnp.dot(weights.astype(jnp.bfloat16), gathered, preferred_element_type=jnp.float32)
-        / totals[:, None]
-    )
+
+    flags = jnp.pad(pattern.astype(jnp.bfloat16), ((0, 0), (0, LANES - blocks)))
+    everyone = lax.all_gather(jnp.concatenate([emb_half, flags], axis=1), "dp", axis=0, tiled=True)
+    emb_all = everyone[:, :features]
+    flags_all = everyone[:, features : features + blocks].astype(jnp.float32)
+    scores = lax.dot_general(emb_all, queries, contract, preferred_element_type=jnp.float32) * temper
+    row_block = (me * query_rows + jnp.arange(query_rows)) // QB
+    picks = (row_block[None, :] == jnp.arange(blocks)[:, None]).astype(jnp.float32)
+    cand_mask = jnp.dot(flags_all, picks) > 0
+    low = jnp.float32(-1e30)
+    peak_part = jnp.max(jnp.where(cand_mask, scores, low), axis=1, keepdims=True)
+    weights = jnp.where(cand_mask, jnp.exp(scores - peak_part), 0.0)
+    total_part = jnp.sum(weights, axis=1, keepdims=True)
+    mix_part = jnp.dot(weights.astype(jnp.bfloat16), queries, preferred_element_type=jnp.float32)
+
+    passages = emb_all.shape[0]
+    lane = jnp.arange(LANES)[None, :]
+    tail = jnp.where(lane == 0, peak_part, jnp.where(lane == 1, total_part, 0.0))
+    parts = jnp.concatenate([mix_part, tail], axis=1).reshape(ranks, passages // ranks, -1)
+    parts = lax.all_to_all(parts, "dp", split_axis=0, concat_axis=0, tiled=True)
+    mixes, peaks, sums = parts[:, :, :features], parts[:, :, features], parts[:, :, features + 1]
+    peak_score = jnp.max(peaks, axis=0)
+    factor = jnp.exp(peaks - peak_score[None, :])
+    totals = jnp.sum(sums * factor, axis=0)
+    recalled = jnp.sum(mixes * factor[:, :, None], axis=0) / totals[:, None]
     log_total = peak_score + jnp.log(totals)
     return (embedded, recalled, log_total)
 

time: 287 us -> 207 us (0.72)
  waiting for transfers between devices: 232 us -> 135 us
  blocking collectives: 0 us -> 32.7 us
  matrix products: 29.5 us -> 14.2 us
    all_gather x1 -> x0, waiting for transfers between devices: 97.2 us -> none  [per_device(): gathered = lax.all_gather(queries, 'dp', axis=0, tiled=True)]
    all_gather x0 -> x1, blocking collectives: none -> 20 us  [per_device(): lax.all_gather(jnp.concatenate([emb_half, flags], axis=1), 'dp', axis=0,...]
    dot_general x2 -> x3, matrix products: 16.2 us -> 0.89 us  [the longest x1 0.34 us: per_device(): lax.dot_general(emb_all, queries, contract, preferred_element_type=jnp.fl...]
    all_to_all x0 -> x1, blocking collectives: none -> 12.8 us  [per_device(): parts = lax.all_to_all(parts, 'dp', split_axis=0, concat_axis=0, tiled=True)]
  transfers between devices with their start and end apart: 2 -> 1, of which waited for: 2 -> 1; matrix products, arithmetic and copies ran while one was open for 6% -> 0% of each run, Pallas kernels for 0% -> 0%
where the time goes in v1:
time: 207 us
  waiting for transfers between devices  135 us (65%)
  blocking collectives  32.7 us (16%)
  between operations  18 us (9%)
  matrix products  14.2 us (7%)
  other arithmetic  7.23 us (3%)
    all_gather x1, waiting for transfers between devices, per_device(): lax.all_gather(out_proj, 'dp', axis=1, tiled=True)  134 us
    all_gather x1, blocking collectives, per_device(): lax.all_gather(jnp.concatenate([emb_half, flags], axis=1), 'dp', axis=0,...  20 us
    dot_general x1, matrix products, per_device(): jnp.dot(context, lax.all_gather(out_proj, 'dp', axis=1, tiled=True), pref...  13.3 us
    all_to_all x1, blocking collectives, per_device(): parts = lax.all_to_all(parts, 'dp', split_axis=0, concat_axis=0, tiled=True)  12.8 us
  transfers between devices with their start and end apart: 1, of which 1 were waited for; matrix products, arithmetic and copies ran while one was open for 0% of the time, Pallas kernels for 0%

profile of v1, /device:TPU:0, one launch (start us, length us, event | category | flops | bytes accessed | tf_op | source)
XLA Modules:
  0.0 207.2 jit_solution(9994814818101104451)
XLA Ops:
  7.2 0.0 copy-start
  7.2 0.0 all-gather.3.cloned.1.call-start
  7.2 0.7 all-gather.3.cloned.1.call-update
  8.6 0.7 convert_element_type.40
  9.3 0.0 copy-start.3
  9.3 134.0 %all-gather.3.cloned.1.call-done = bf16[2048,4096]{1,0:T(8,128)(2,1)} async-done(((bf16[2048,256]{1,0:T(8,128)(2,1)}), bf16[2048,4096]{1,0:T(8,128)(2,1)}) %all-gather.3.cloned.1.call-update) | async-done | bytes 16777232 | tf_op jit(solution)/shard_map/all_gather | solution.py:23
  143.2 0.0 copy-done
  143.2 13.3 %multiply_reduce_fusion.1 = (f32[512]{0:T(512)S(1)}, f32[512,4096]{1,0:T(8,128)S(1)}) fusion(bf16[512,2048]{1,0:T(8,128)(2,1)S(1)} %copy-done, bf16[2048,4096]{1,0:T(8,128)(2,1)} %all-gather.3.cloned.1.call-done, bf16[512,4096]{1,0:T(8,128)(2,1)} %param.8), kind=kOutput, calls=%fused_computation.1 | convolution fusion | flops 8598323200 | bytes 31459328 | tf_op jit(solution)/shard_map/dot_general | solution.py:21
  156.5 0.0 copy-start.1
  156.6 1.9 multiply_reduce_fusion
  158.5 0.6 multiply_reduce_fusion.2
  159.8 0.0 copy-start.2
  159.9 20.0 %all-gather = bf16[16,1,4224]{2,1,0:T(2,128)(2,1)S(1)} all-gather(bf16[1,1,4224]{2,1,0:T(2,128)(2,1)S(1)} %fusion.3), channel_id=1, replica_groups=mesh['groups'=2,'dp'=16] {'dp'}, dimensions={0}, use_global_device_ids=true | all-gather | bytes 143616 | tf_op jit(solution)/shard_map/all_gather | solution.py:41
  179.9 0.3 convolution_multiply_fusion
  180.2 0.2 select_reduce_fusion
  180.4 0.3 fusion.7
  180.7 0.2 fusion.5
  180.9 0.1 select_select_fusion
  181.0 0.3 copy.10
  181.3 12.8 %all_to_all.5 = f32[16,1,4224]{2,1,0:T(1,128)S(1)} all-to-all(f32[16,1,4224]{2,1,0:T(1,128)S(1)} %copy.10), channel_id=1, replica_groups=mesh['groups'=2,'dp'=16] {'dp'}, dimensions={0} | all-to-all | bytes 540672 | tf_op jit(solution)/shard_map/all_to_all | solution.py:58
  194.1 0.6 slice_reduce_fusion
  194.7 1.5 fusion.4
  197.6 0.3 fusion
  197.9 1.3 broadcast_divide_fusion
  (12 shorter events, 0.1 us)
Async XLA Ops:
  7.2 136.1 %copy-start = (bf16[512,2048]{1,0:T(8,128)(2,1)S(1)}, bf16[512,2048]{1,0:T(8,128)(2,1)}, u32[]{:S(2)}) copy-start(bf16[512,2048]{1,0:T(8,128)(2,1)} %param.7) | copy-start | bytes 6291460
  7.2 136.1 %all-gather.3.cloned.1.call-start = ((), (), s32[]{:S(2)}) async-start(), calls=%async_computation.1 | async-start | bytes 17825792 | tf_op jit(solution)/shard_map/all_gather | solution.py:23
  9.3 147.3 %copy-start.3 = (f32[4096]{0:T(1024)S(1)}, f32[4096]{0:T(1024)}, u32[]{:S(2)}) copy-start(f32[4096]{0:T(1024)} %param.10) | copy-start | bytes 49156
  156.5 23.3 %copy-start.1 = (bf16[112,4096]{1,0:T(8,128)(2,1)S(1)}, bf16[112,4096]{1,0:T(8,128)(2,1)}, u32[]{:S(2)}) copy-start(bf16[112,4096]{1,0:T(8,128)(2,1)} %param.12) | copy-start | bytes 2752516
  159.8 39.4 %copy-start.2 = (f32[4096]{0:T(1024)}, f32[4096]{0:T(1024)S(1)}, u32[]{:S(2)}) copy-start(f32[4096]{0:T(1024)S(1)} %broadcast_multiply_fusion) | copy-start | bytes 49156
Sparse Core Ops, SparseCore 0:
  10.2 133.0 all-gather.2

commit v2 on v1

--- a/solution.py
+++ b/solution.py
@@ -18,11 +18,18 @@
     blocks = pattern.shape[1]
     ranks = lax.axis_size("dp")
     me = lax.axis_index("dp")
-    branch = jnp.dot(
-        context,
-        lax.all_gather(out_proj, "dp", axis=1, tiled=True),
+    groups = lax.axis_size("groups")
+    depth = out_proj.shape[0]
+    share = depth // groups
+    piece = lax.dynamic_slice_in_dim(out_proj, lax.axis_index("groups") * share, share, 0)
+    pieces = lax.all_gather(piece, ("groups", "dp"), axis=0)
+    pieces = pieces.reshape(groups, ranks, share, out_proj.shape[1])
+    branch = jnp.einsum(
+        "tgk,grkc->trc",
+        context.reshape(tok_rows, groups, share),
+        pieces,
         preferred_element_type=jnp.float32,
-    )
+    ).reshape(tok_rows, features)
     hidden_sum = residual.astype(jnp.float32) + branch
     normed = (
         hidden_sum

time: 207 us -> 212 us (1.024)
  waiting for transfers between devices: 135 us -> 115 us
  local copies, waits for them, and re-layouts: 0.33 us -> 16.8 us
  other arithmetic: 7.23 us -> 13.6 us
    all_gather x1, waiting for transfers between devices: 134 us -> 115 us  [per_device(): pieces = lax.all_gather(piece, ('groups', 'dp'), axis=0)]
    reshape x0 -> x2, local copies, waits for them, and re-layouts: none -> 12.2 us  [the longest x1 8.95 us: per_device(): branch = jnp.einsum('tgk,grkc->trc', context.reshape(tok_rows, groups, sh...]
    reduce_sum x0 -> x1, other arithmetic: none -> 5.89 us  [per_device(): jnp.mean(hidden_sum * hidden_sum, axis=-1, keepdims=True) + 1e-05]
    unnamed x9 -> x13, local copies, waits for them, and re-layouts: 0.05 us -> 3.44 us
  transfers between devices with their start and end apart: 1 -> 1, of which waited for: 1 -> 1; matrix products, arithmetic and copies ran while one was open for 0% -> 2% of each run, Pallas kernels for 0% -> 0%
where the time goes in v2:
time: 212 us
  waiting for transfers between devices  115 us (54%)
  blocking collectives  33 us (16%)
  between operations  18 us (8%)
  local copies, waits for them, and re-layouts  16.8 us (8%)
  matrix products  15.4 us (7%)
  other arithmetic  13.6 us (6%)
    all_gather x1, waiting for transfers between devices, per_device(): pieces = lax.all_gather(piece, ('groups', 'dp'), axis=0)  115 us
    all_gather x1, blocking collectives, per_device(): lax.all_gather(jnp.concatenate([emb_half, flags], axis=1), 'dp', axis=0,...  20.3 us
    dot_general x1, matrix products, per_device(): jnp.einsum('tgk,grkc->trc', context.reshape(tok_rows, groups, share), pie...  14.6 us
    all_to_all x1, blocking collectives, per_device(): parts = lax.all_to_all(parts, 'dp', split_axis=0, concat_axis=0, tiled=True)  12.8 us
    reshape x1, local copies, waits for them, and re-layouts, per_device(): branch = jnp.einsum('tgk,grkc->trc', context.reshape(tok_rows, groups, sh...  8.95 us
    reduce_sum x1, other arithmetic, per_device(): jnp.mean(hidden_sum * hidden_sum, axis=-1, keepdims=True) + 1e-05  5.89 us
  transfers between devices with their start and end apart: 1, of which 1 were waited for; matrix products, arithmetic and copies ran while one was open for 2% of the time, Pallas kernels for 0%

profile of v2, /device:TPU:0, one launch (start us, length us, event | category | flops | bytes accessed | tf_op | source)
XLA Modules:
  0.0 211.6 jit_solution(16966097521326469420)
XLA Ops:
  7.2 1.2 copy-done
  8.4 0.8 constant_dynamic-slice_fusion
  9.2 3.3 %reshape.172 = bf16[512,2,1024]{2,1,0:T(2,128)(2,1)S(1)} reshape(bf16[512,2048]{1,0:T(8,128)(2,1)} %param.7) | data formatting | bytes 4194304 | tf_op jit(solution)/shard_map/reshape | solution.py:29
  13.2 0.7 convert_element_type.40
  13.9 114.6 %all-gather.4.cloned.1.call-done = bf16[32768,256]{1,0:T(8,128)(2,1)} async-done(((bf16[1024,256]{1,0:T(8,128)(2,1)}), bf16[32768,256]{1,0:T(8,128)(2,1)}) %all-gather.4.cloned.1.call-update) | async-done | bytes 16777232 | tf_op jit(solution)/shard_map/all_gather | solution.py:25
  128.5 14.6 %fusion = f32[16,256,512,1]{2,1,0,3:T(8,128)} fusion(bf16[2,16,1024,256]{3,2,1,0:T(8,128)(2,1)} %bitcast.30, bf16[512,2,1024,1]{2,1,0,3:T(2,128)(2,1)S(1)} %bitcast.24), kind=kOutput, calls=%fused_computation.3 | convolution fusion | flops 8589934592 | bytes 27262976 | tf_op jit(solution)/shard_map/tgk,grkc->trc/dot_general | solution.py:27
  143.1 8.9 %copy.17 = f32[512,4096]{1,0:T(8,128)} copy(f32[512,4096]{0,1:T(8,128)} %bitcast.23) | data formatting | bytes 16777216 | tf_op jit(solution)/shard_map/reshape | solution.py:32
  152.0 5.9 %multiply_reduce_fusion.1 = f32[512]{0:T(512)S(1)} fusion(f32[512,4096]{1,0:T(8,128)} %copy.17, bf16[512,4096]{1,0:T(8,128)(2,1)} %param.8), kind=kLoop, calls=%fused_computation.1 | loop fusion | flops 8388096 | bytes 12584960 | tf_op jit(solution)/shard_map/reduce_sum | solution.py:36
  157.9 1.0 copy-done.1
  159.0 1.2 copy-done.2
  160.2 2.4 %multiply_reduce_fusion = f32[4096]{0:T(1024)S(1)} fusion(f32[512,4096]{1,0:T(8,128)S(1)} %copy-done.1, bf16[512,4096]{1,0:T(8,128)(2,1)S(1)} %copy-done.2, f32[512]{0:T(512)S(1)} %fusion.15, f32[4096]{0:T(1024)S(1)} %copy-done.5, f32[512]{0:T(512)S(1)} %add_rsqrt_fusion), kind=kLoop, calls=%fused_computation | loop fusion | flops 12578816 | bytes 12619776 | tf_op jit(solution)/shard_map/reduce_sum | solution.py:41
  162.6 0.6 multiply_reduce_fusion.2
  164.0 20.3 %all-gather.1 = bf16[16,1,4224]{2,1,0:T(2,128)(2,1)S(1)} all-gather(bf16[1,1,4224]{2,1,0:T(2,128)(2,1)S(1)} %fusion.5), channel_id=1, replica_groups=mesh['groups'=2,'dp'=16] {'dp'}, dimensions={0}, use_global_device_ids=true | all-gather | bytes 143616 | tf_op jit(solution)/shard_map/all_gather | solution.py:48
  184.3 0.3 convolution_multiply_fusion
  184.6 0.2 select_reduce_fusion
  184.9 0.3 fusion.9
  185.2 0.2 fusion.7
  185.4 0.1 select_select_fusion
  185.5 0.3 copy.18
  185.8 12.8 %all_to_all.5 = f32[16,1,4224]{2,1,0:T(1,128)S(1)} all-to-all(f32[16,1,4224]{2,1,0:T(1,128)S(1)} %copy.18), channel_id=1, replica_groups=mesh['groups'=2,'dp'=16] {'dp'}, dimensions={0} | all-to-all | bytes 540672 | tf_op jit(solution)/shard_map/all_to_all | solution.py:65
  198.5 0.6 slice_reduce_fusion
  199.2 1.5 fusion.6
  202.0 0.3 fusion.2
  202.3 1.3 broadcast_divide_fusion
  (20 shorter events, 0.2 us)
Async XLA Ops:
  7.2 1.2 copy-start
  7.2 121.3 %all-gather.4.cloned.1.call-start = ((), (), s32[]{:S(2)}) async-start(), calls=%async_computation.1 | async-start | bytes 17301504 | tf_op jit(solution)/shard_map/all_gather | solution.py:25
  143.1 14.9 %copy-start.5 = (f32[4096]{0:T(1024)S(1)}, f32[4096]{0:T(1024)}, u32[]{:S(2)}) copy-start(f32[4096]{0:T(1024)} %param.10) | copy-start | bytes 49156
  152.0 7.0 %copy-start.1 = (f32[512,4096]{1,0:T(8,128)S(1)}, f32[512,4096]{1,0:T(8,128)}, u32[]{:S(2)}) copy-start(f32[512,4096]{1,0:T(8,128)} %copy.17) | copy-start | bytes 25165828
  152.0 8.2 %copy-start.2 = (bf16[512,4096]{1,0:T(8,128)(2,1)S(1)}, bf16[512,4096]{1,0:T(8,128)(2,1)}, u32[]{:S(2)}) copy-start(bf16[512,4096]{1,0:T(8,128)(2,1)} %param.8) | copy-start | bytes 12582916
  157.9 26.4 %copy-start.3 = (bf16[112,4096]{1,0:T(8,128)(2,1)S(1)}, bf16[112,4096]{1,0:T(8,128)(2,1)}, u32[]{:S(2)}) copy-start(bf16[112,4096]{1,0:T(8,128)(2,1)} %param.12) | copy-start | bytes 2752516
  163.9 39.7 %copy-start.4 = (f32[4096]{0:T(1024)}, f32[4096]{0:T(1024)S(1)}, u32[]{:S(2)}) copy-start(f32[4096]{0:T(1024)S(1)} %broadcast_multiply_fusion) | copy-start | bytes 49156
Sparse Core Ops, SparseCore 0:
  10.9 117.5 all-gather.3

commit v3 on v1

--- a/solution.py
+++ b/solution.py
@@ -1,23 +1,228 @@
+import functools
 import math
 
 import jax
 import jax.numpy as jnp
 from jax import lax
+from jax.experimental import pallas as pl
+from jax.experimental.pallas import tpu as pltpu
 from jax.sharding import PartitionSpec as P
 
 QB = 256
 LANES = 128
-
-
-def per_device(context, residual, out_proj, norm_gain, lengths, queries, pattern):
+CORES = 2
+CYCLE = (0, 2, 4, 6, 7, 5, 3, 1)
+
+
+def project_kernel(count, place, ctx, residual, *refs):
+    pieces = refs[: 2 * count]
+    hidden, squares, weights, extra, weight_sems, extra_sems = refs[2 * count :]
+    half = weights.shape[1]
+    width = weights.shape[2]
+    rows = ctx.shape[0]
+
+    def weight_copy(i):
+        return pltpu.make_async_copy(pieces[i], weights.at[i], weight_sems.at[i])
+
+    def extra_copy(j):
+        start = pl.multiple_of(place[j] * width, width)
+        return pltpu.make_async_copy(residual.at[:, pl.ds(start, width)], extra.at[j], extra_sems.at[j])
+
+    for j in range(count):
+        extra_copy(j).start()
+        weight_copy(2 * j).start()
+        weight_copy(2 * j + 1).start()
+    squares[...] = jnp.zeros_like(squares)
+    first = pl.multiple_of(place[count] * half, half)
+    second = pl.multiple_of((1 - place[count]) * half, half)
+    step = 256
+    for j in range(count):
+        extra_copy(j).wait()
+        weight_copy(2 * j).wait()
+        weight_copy(2 * j + 1).wait()
+
+        @pl.loop(0, rows // step)
+        def _(k):
+            at = pl.ds(pl.multiple_of(k * step, step), step)
+            total = jnp.dot(
+                ctx[at, pl.ds(first, half)], weights[2 * j], preferred_element_type=jnp.float32
+            )
+            total += jnp.dot(
+                ctx[at, pl.ds(second, half)], weights[2 * j + 1], preferred_element_type=jnp.float32
+            )
+            total += extra[j, at, :].astype(jnp.float32)
+            hidden[j, at, :] = total
+            square = total * total
+            for lane in range(0, width, LANES):
+                squares[at, :] += square[:, lane : lane + LANES]
+
+
+def project(place, ctx, residual, pieces):
+    count = len(pieces) // 2
+    rows = ctx.shape[0]
+    half, width = pieces[0].shape
+    return pl.pallas_call(
+        functools.partial(project_kernel, count),
+        out_shape=(
+            jax.ShapeDtypeStruct((count, rows, width), jnp.float32),
+            jax.ShapeDtypeStruct((rows, LANES), jnp.float32),
+        ),
+        in_specs=[pl.BlockSpec(memory_space=pltpu.SMEM), pl.BlockSpec(memory_space=pltpu.VMEM)]
+        + [pl.BlockSpec(memory_space=pl.ANY)] * (1 + 2 * count),
+        out_specs=(pl.BlockSpec(memory_space=pltpu.VMEM), pl.BlockSpec(memory_space=pltpu.VMEM)),
+        scratch_shapes=[
+            pltpu.VMEM((2 * count, half, width), jnp.bfloat16),
+            pltpu.VMEM((count, rows, width), jnp.bfloat16),
+            pltpu.SemaphoreType.DMA((2 * count,)),
+            pltpu.SemaphoreType.DMA((count,)),
+        ],
+        compiler_params=pltpu.CompilerParams(vmem_limit_bytes=24 << 20),
+        cost_estimate=pl.CostEstimate(
+            flops=2 * rows * 2 * half * width * count,
+            bytes_accessed=count * width * (2 * half * 2 + rows * 6),
+            transcendentals=0,
+        ),
+    )(place, ctx, residual, *pieces)
+
+
+def pool_kernel(parts, counts, place, length, gain, *refs):
+    hidden = refs[:parts]
+    squares = refs[parts : 2 * parts]
+    embedded = refs[2 * parts]
+    blocks, rows, sems = refs[2 * parts + 1 :]
+    total = sum(counts)
+    width = blocks.shape[2]
+    features = total * width
+    at = 0
+    copies = []
+    for i, n in enumerate(counts):
+        copies.append(pltpu.make_async_copy(hidden[i], blocks.at[pl.ds(at, n)], sems.at[i]))
+        copies[-1].start()
+        at += n
+    square = squares[0][...]
+    for i in range(1, parts):
+        square += squares[i][...]
+    mean = jnp.sum(square, axis=1, keepdims=True) * (1.0 / features)
+    row = lax.broadcasted_iota(jnp.int32, mean.shape, 0)
+    scale = jnp.where(row < length[0], lax.rsqrt(mean + 1e-05), 0.0)
+    rows[...] = jnp.broadcast_to(scale, rows.shape)
+    inverse = 1.0 / jnp.full((1, width), length[0], jnp.int32).astype(jnp.float32)
+    at = 0
+    for i, n in enumerate(counts):
+        copies[i].wait()
+        for j in range(at, at + n):
+            halves = [
+                jnp.sum(blocks[j, :, lane : lane + LANES] * rows[...], axis=0, keepdims=True)
+                for lane in range(0, width, LANES)
+            ]
+            summed = jnp.concatenate(halves, axis=1)
+            embedded[pl.ds(place[j], 1), :] = summed * gain[pl.ds(place[j], 1), :] * inverse
+        at += n
+    pooled = embedded[...]
+    mean = jnp.sum(jnp.sum(pooled * pooled, axis=1, keepdims=True), axis=0, keepdims=True)
+    embedded[...] = pooled * lax.rsqrt(mean * (1.0 / features) + 1e-06)
+
+
+def pool(place, lengths, gain, hidden, squares):
+    counts = tuple(part.shape[0] for part in hidden)
+    total = sum(counts)
+    rows, width = hidden[0].shape[1:]
+    parts = len(hidden)
+    return pl.pallas_call(
+        functools.partial(pool_kernel, parts, counts),
+        out_shape=jax.ShapeDtypeStruct((total, width), jnp.float32),
+        in_specs=[pl.BlockSpec(memory_space=pltpu.SMEM)] * 2
+        + [pl.BlockSpec(memory_space=pltpu.VMEM)]
+        + [pl.BlockSpec(memory_space=pl.ANY)] * parts
+        + [pl.BlockSpec(memory_space=pltpu.VMEM)] * parts,
+        out_specs=pl.BlockSpec(memory_space=pltpu.VMEM),
+        scratch_shapes=[
+            pltpu.VMEM((total, rows, width), jnp.float32),
+            pltpu.VMEM((rows, LANES), jnp.float32),
+            pltpu.SemaphoreType.DMA((parts,)),
+        ],
+        compiler_params=pltpu.CompilerParams(vmem_limit_bytes=24 << 20),
+    )(place, lengths, gain.reshape(total, width), *hidden, *squares)
+
+
+def embed_ring(context, residual, out_proj, norm_gain, lengths):
+    ranks = lax.axis_size("dp")
+    me = lax.axis_index("dp")
+    side = lax.axis_index("groups")
+    core = me % CORES
+    size = ranks // CORES
+    where = [CYCLE.index(chip) for chip in range(size)]
+
+    def ring(step):
+        return [
+            (CYCLE[r] * CORES + c, CYCLE[(r + step) % size] * CORES + c)
+            for r in range(size)
+            for c in range(CORES)
+        ]
+
+    def from_next(piece):
+        return lax.ppermute(piece, "dp", ring(-1))
+
+    def from_last(piece):
+        return lax.ppermute(piece, "dp", ring(1))
+
+    def over_x(piece):
+        return lax.ppermute(piece, "groups", [(0, 1), (1, 0)])
+
+    def other_core(piece):
+        return lax.ppermute(piece, "dp", [(i, i ^ 1) for i in range(ranks)])
+
+    half = out_proj.shape[0] // 2
+    own = lax.dynamic_slice_in_dim(out_proj, side * half, half, 0)
+    rest = lax.dynamic_slice_in_dim(out_proj, (1 - side) * half, half, 0)
+    n1, l1 = from_next(own), from_last(own)
+    own_pair = (own, rest, other_core(own), other_core(rest))
+    n2, l2 = from_next(n1), from_last(l1)
+    xn1 = over_x(n1)
+    n3, l3 = from_next(n2), from_last(l2)
+    xn2 = over_x(n2)
+    n3x, l4 = from_next(xn2), from_last(l3)
+    xl2 = over_x(l2)
+    n4x, l3x = from_next(n3x), from_last(xl2)
+    xl1 = over_x(l1)
+
+    def both(a, b):
+        return (a, b, other_core(a), other_core(b))
+
+    batches = (
+        (0, own_pair),
+        (1, both(n1, xn1)),
+        (2, both(n2, xn2)),
+        (-2, both(l2, xl2)),
+        (3, both(n3, n3x)),
+        (-1, both(l1, xl1)),
+        (-3, both(l3, l3x)),
+        (4, both(l4, n4x)),
+    )
+    cycle = jnp.array(CYCLE, jnp.int32)
+    at = jnp.array(where, jnp.int32)[me // CORES]
+
+    def place_of(group):
+        chips = cycle[(at + jnp.array([k for k, _ in group], jnp.int32)) % size]
+        return jnp.stack([chips * CORES + core, chips * CORES + 1 - core], axis=1).reshape(-1)
+
+    hidden, squares, places = [], [], []
+    for group in (batches[:1], batches[1:3], batches[3:5], batches[5:]):
+        place = place_of(group)
+        pieces = [piece for _, four in group for piece in four]
+        h, s = project(jnp.append(place, side), context, residual, pieces)
+        hidden.append(h)
+        squares.append(s)
+        places.append(place)
+    embedded = pool(jnp.concatenate(places), lengths, norm_gain, hidden, squares)
+    return embedded.reshape(1, -1)
+
+
+def embed_gather(context, residual, out_proj, norm_gain, lengths):
     tok_rows = context.shape[0]
     features = residual.shape[1]
     passages_here = lengths.shape[0]
     seq_len = tok_rows // passages_here
-    query_rows = queries.shape[0]
-    blocks = pattern.shape[1]
-    ranks = lax.axis_size("dp")
-    me = lax.axis_index("dp")
     branch = jnp.dot(
         context,
         lax.all_gather(out_proj, "dp", axis=1, tiled=True),
@@ -32,7 +237,24 @@
     shaped = normed.reshape(passages_here, seq_len, features)
     valid_mask = (jnp.arange(seq_len)[None, :] < lengths[:, None]).astype(jnp.float32)
     pooled = jnp.sum(shaped * valid_mask[:, :, None], axis=1) / lengths.astype(jnp.float32)[:, None]
-    embedded = pooled * lax.rsqrt(jnp.mean(pooled * pooled, axis=-1, keepdims=True) + 1e-06)
+    return pooled * lax.rsqrt(jnp.mean(pooled * pooled, axis=-1, keepdims=True) + 1e-06)
+
+
+def per_device(context, residual, out_proj, norm_gain, lengths, queries, pattern):
+    features = residual.shape[1]
+    query_rows = queries.shape[0]
+    blocks = pattern.shape[1]
+    ranks = lax.axis_size("dp")
+    me = lax.axis_index("dp")
+    if (
+        ranks == CORES * len(CYCLE)
+        and lax.axis_size("groups") == 2
+        and lengths.shape[0] == 1
+        and out_proj.shape[1] % LANES == 0
+    ):
+        embedded = embed_ring(context, residual, out_proj, norm_gain, lengths)
+    else:
+        embedded = embed_gather(context, residual, out_proj, norm_gain, lengths)
     emb_half = embedded.astype(jnp.bfloat16)
     temper = 1.0 / (0.02 * math.sqrt(features))
     contract = (((1,), (1,)), ((), ()))

time: 207 us -> 178 us (0.86)
  waiting for transfers between devices: 135 us -> 61.6 us
  Pallas kernels: 0 us -> 24.2 us
  starting transfers between devices: 0.04 us -> 21.7 us
  local copies, waits for them, and re-layouts: 0.33 us -> 15.4 us
  matrix products: 14.2 us -> 0.89 us
  between operations: 18 us -> 6.7 us
  other arithmetic: 7.23 us -> 12.6 us
    all_gather x1 -> x0, waiting for transfers between devices: 134 us -> none  [per_device(): lax.all_gather(out_proj, 'dp', axis=1, tiled=True)]
    ppermute x0 -> x30, waiting for transfers between devices: none -> 61.6 us  [the longest x5 24.1 us: from_next(): return lax.ppermute(piece, 'dp', ring(-1))]
    pallas_call x0 -> x5, Pallas kernels: none -> 24.2 us  [the longest x4 22 us: project(): pl.pallas_call(functools.partial(project_kernel, count), out_shape=(jax.S...]
    ppermute x0 -> x30, starting transfers between devices: none -> 21.7 us  [the longest x5 9.29 us: from_next(): return lax.ppermute(piece, 'dp', ring(-1))]
    dot_general x1 -> x0, matrix products: 13.3 us -> none  [per_device(): jnp.dot(context, lax.all_gather(out_proj, 'dp', axis=1, tiled=True), pref...]
    unnamed x9 -> x50, local copies, waits for them, and re-layouts: 0.05 us -> 6.23 us
    concatenate x0 -> x5, other arithmetic: none -> 4.29 us  [the longest x4 3.04 us: embed_ring(): h, s = project(jnp.append(place, side), context, residual, pieces)]
    gather x0 -> x4, local copies, waits for them, and re-layouts: none -> 3.06 us  [place_of(): chips = cycle[(at + jnp.array([k for k, _ in group], jnp.int32)) % size]]
  transfers between devices with their start and end apart: 1 -> 30, of which waited for: 1 -> 9; matrix products, arithmetic and copies ran while one was open for 0% -> 9% of each run, Pallas kernels for 0% -> 8%
where the time goes in v3:
time: 178 us; the launch traced here: 177 us
  waiting for transfers between devices  61.6 us (35%)
  blocking collectives  34.1 us (19%)
  Pallas kernels  24.2 us (14%)
  starting transfers between devices  21.7 us (12%)
  local copies, waits for them, and re-layouts  15.4 us (9%)
  other arithmetic  12.6 us (7%)
  between operations  6.7 us (4%)
    ppermute x5, waiting for transfers between devices, from_next(): return lax.ppermute(piece, 'dp', ring(-1))  24.1 us
    ppermute x4, waiting for transfers between devices, over_x(): return lax.ppermute(piece, 'groups', [(0, 1), (1, 0)])  23.3 us
    pallas_call x4, Pallas kernels, project(): pl.pallas_call(functools.partial(project_kernel, count), out_shape=(jax.S...  22 us
    all_gather x1, blocking collectives, per_device(): lax.all_gather(jnp.concatenate([emb_half, flags], axis=1), 'dp', axis=0,...  21.4 us
    ppermute x5, waiting for transfers between devices, from_last(): return lax.ppermute(piece, 'dp', ring(1))  14.2 us
    all_to_all x1, blocking collectives, per_device(): parts = lax.all_to_all(parts, 'dp', split_axis=0, concat_axis=0, tiled=True)  12.8 us
    ppermute x5, starting transfers between devices, from_next(): return lax.ppermute(piece, 'dp', ring(-1))  9.29 us
    unnamed x50, local copies, waits for them, and re-layouts  6.23 us
  transfers between devices with their start and end apart: 30, of which 9 were waited for; matrix products, arithmetic and copies ran while one was open for 9% of the time, Pallas kernels for 8%

profile of v3, /device:TPU:0, one launch (start us, length us, event | category | flops | bytes accessed | tf_op | source)
XLA Modules:
  0.0 177.2 jit_solution(5735381914471638287)
XLA Ops:
  0.7 2.3 %constant_dynamic-slice_fusion = (bf16[1024,256]{1,0:T(8,128)(2,1)S(1)}, bf16[1024,256]{1,0:T(8,128)(2,1)}) fusion(bf16[2048,256]{1,0:T(8,128)(2,1)} %param.15, s32[]{:T(128)S(6)} %select_n.91, s32[]{:T(128)S(6)} %select_n.90), kind=kLoop, calls=%fused_computation.68 | loop fusion | bytes 2097160 | tf_op jit(solution)/shard_map/dynamic_slice | solution.py:177
  3.0 3.0 %collective-permute-start.2 = (bf16[1024,256]{1,0:T(8,128)(2,1)}, bf16[1024,256]{1,0:T(8,128)(2,1)}, u32[]{:S(2)}, u32[]{:S(2)}) collective-permute-start(bf16[1024,256]{1,0:T(8,128)(2,1)} %get-tuple-element.42.refs_0_), channel_id=1, source_target_pairs={{0,2},{1,3},{4,0},{5,1},{8,4},{9,5},{12,8},{13,9},{14,12},{15,13},... | collective-permute-start | bytes 1572872 | tf_op jit(solution)/shard_map/ppermute | solution.py:164
  6.5 11.7 %collective-permute-done.2.refs_0_ = bf16[1024,256]{1,0:T(8,128)(2,1)} collective-permute-done((bf16[1024,256]{1,0:T(8,128)(2,1)}, bf16[1024,256]{1,0:T(8,128)(2,1)}, u32[]{:S(2)}, u32[]{:S(2)}) %collective-permute-start.2) | collective-permute-done | bytes 524320 | tf_op jit(solution)/shard_map/ppermute | solution.py:164
  18.2 1.7 collective-permute-start.6
  24.2 1.7 collective-permute-start.19
  26.3 5.4 %collective-permute-done.6.refs_4_ = bf16[1024,256]{1,0:T(8,128)(2,1)} collective-permute-done((bf16[1024,256]{1,0:T(8,128)(2,1)}, bf16[1024,256]{1,0:T(8,128)(2,1)}, u32[]{:S(2)}, u32[]{:S(2)}) %collective-permute-start.6) | collective-permute-done | bytes 524320 | tf_op jit(solution)/shard_map/ppermute | solution.py:164
  33.2 3.5 %collective-permute-done.11.refs_0_ = bf16[1024,256]{1,0:T(8,128)(2,1)} collective-permute-done((bf16[1024,256]{1,0:T(8,128)(2,1)}, bf16[1024,256]{1,0:T(8,128)(2,1)}, u32[]{:S(2)}, u32[]{:S(2)}) %collective-permute-start.11) | collective-permute-done | bytes 524320 | tf_op jit(solution)/shard_map/ppermute | solution.py:167
  39.4 1.7 collective-permute-start.22
  41.1 1.5 collective-permute-start.7
  42.6 8.0 %collective-permute-done.3.refs_1_ = bf16[1024,256]{1,0:T(8,128)(2,1)} collective-permute-done((bf16[1024,256]{1,0:T(8,128)(2,1)}, bf16[1024,256]{1,0:T(8,128)(2,1)}, u32[]{:S(2)}, u32[]{:S(2)}) %collective-permute-start.3) | collective-permute-done | bytes 524320 | tf_op jit(solution)/shard_map/ppermute | solution.py:170
  50.6 1.7 collective-permute-start.15
  56.7 14.1 %collective-permute-done.7.refs_5_ = bf16[1024,256]{1,0:T(8,128)(2,1)} collective-permute-done((bf16[1024,256]{1,0:T(8,128)(2,1)}, bf16[1024,256]{1,0:T(8,128)(2,1)}, u32[]{:S(2)}, u32[]{:S(2)}) %collective-permute-start.7) | collective-permute-done | bytes 524320 | tf_op jit(solution)/shard_map/ppermute | solution.py:170
  78.5 7.0 %collective-permute-done.16.refs_5_ = bf16[1024,256]{1,0:T(8,128)(2,1)} collective-permute-done((bf16[1024,256]{1,0:T(8,128)(2,1)}, bf16[1024,256]{1,0:T(8,128)(2,1)}, u32[]{:S(2)}, u32[]{:S(2)}) %collective-permute-start.16) | collective-permute-done | bytes 524320 | tf_op jit(solution)/shard_map/ppermute | solution.py:164
  85.5 2.3 %collective-permute-done.23.refs_5_ = bf16[1024,256]{1,0:T(8,128)(2,1)} collective-permute-done((bf16[1024,256]{1,0:T(8,128)(2,1)}, bf16[1024,256]{1,0:T(8,128)(2,1)}, u32[]{:S(2)}, u32[]{:S(2)}) %collective-permute-start.23) | collective-permute-done | bytes 524320 | tf_op jit(solution)/shard_map/ppermute | solution.py:167
  87.8 1.6 collective-permute-start.27
  89.4 8.4 %collective-permute-done.26.refs_8_ = bf16[1024,256]{1,0:T(8,128)(2,1)} collective-permute-done((bf16[1024,256]{1,0:T(8,128)(2,1)}, bf16[1024,256]{1,0:T(8,128)(2,1)}, u32[]{:S(2)}, u32[]{:S(2)}) %collective-permute-start.26) | collective-permute-done | bytes 524320 | tf_op jit(solution)/shard_map/ppermute | solution.py:167
  108.3 2.2 %copy-done.1 = bf16[512,4096]{1,0:T(8,128)(2,1)S(1)} copy-done((bf16[512,4096]{1,0:T(8,128)(2,1)S(1)}, bf16[512,4096]{1,0:T(8,128)(2,1)}, u32[]{:S(2)}) %copy-start.1) | copy-done | bytes 4194328
  111.2 3.7 %shard_map.148 = (f32[2,512,256]{2,1,0:T(8,128)S(1)}, f32[512,128]{1,0:T(8,128)S(1)}) custom-call(s32[3]{0:T(128)S(1)} %copy-done.14, bf16[512,2048]{1,0:T(8,128)(2,1)S(1)} %copy-done.3, bf16[512,4096]{1,0:T(8,128)(2,1)S(1)} %copy-done.1, bf16[1024,256]{1,0:T(8,128)(2,1)} %get-tuple-element.42.refs_0_, bf16[1024,256]{1,0:T(8,128)(2,1)S(1)} %get-tuple-element.41.refs_1_, ...), custom_call_target="tpu_custom_call" | custom-call | flops 1073741824 | bytes 3670016 | tf_op jit(solution)/shard_map/pallas_call | solution.py:64
  115.0 5.5 %shard_map.149 = (f32[4,512,256]{2,1,0:T(8,128)S(1)}, f32[512,128]{1,0:T(8,128)S(1)}) custom-call(s32[5]{0:T(128)S(1)} %copy-done.16, bf16[512,2048]{1,0:T(8,128)(2,1)S(1)} %copy-done.3, bf16[512,4096]{1,0:T(8,128)(2,1)S(1)} %copy-done.2, bf16[1024,256]{1,0:T(8,128)(2,1)} %collective-permute-done.2.refs_0_, ...), custom_call_target="tpu_custom_call" | custom-call | flops 2147483648 | bytes 7340032 | tf_op jit(solution)/shard_map/pallas_call | solution.py:64
  120.5 5.5 %shard_map.150 = (f32[4,512,256]{2,1,0:T(8,128)S(1)}, f32[512,128]{1,0:T(8,128)S(1)}) custom-call(s32[5]{0:T(128)S(1)} %copy-done.15, bf16[512,2048]{1,0:T(8,128)(2,1)S(1)} %copy-done.3, bf16[512,4096]{1,0:T(8,128)(2,1)S(1)} %copy-done.2, bf16[1024,256]{1,0:T(8,128)(2,1)} %collective-permute-done.11.refs_0_, ...), custom_call_target="tpu_custom_call" | custom-call | flops 2147483648 | bytes 7340032 | tf_op jit(solution)/shard_map/pallas_call | solution.py:64
  126.0 7.3 %shard_map.151 = (f32[6,512,256]{2,1,0:T(8,128)S(1)}, f32[512,128]{1,0:T(8,128)S(1)}) custom-call(s32[7]{0:T(128)S(1)} %copy-done.13, bf16[512,2048]{1,0:T(8,128)(2,1)S(1)} %copy-done.3, bf16[512,4096]{1,0:T(8,128)(2,1)S(1)} %copy-done.2, bf16[1024,256]{1,0:T(8,128)(2,1)} %collective-permute-done.10.refs_0_, ...), custom_call_target="tpu_custom_call" | custom-call | flops 3221225472 | bytes 11010048 | tf_op jit(solution)/shard_map/pallas_call | solution.py:64
  133.4 2.2 %shard_map.152 = f32[16,256]{1,0:T(8,128)S(1)} custom-call(s32[16]{0:T(128)S(1)} %copy-done.12, s32[1]{0:T(128)S(6)} %copy.30.length, f32[16,256]{1,0:T(8,128)S(1)} %reshape.227.gain, f32[2,512,256]{2,1,0:T(8,128)S(1)} %get-tuple-element.11.refs_0_, f32[4,512,256]{2,1,0:T(8,128)S(1)} %get-tuple-element.12.refs_1_, ...), custom_call_target="tpu_custom_call" | custom-call | tf_op jit(solution)/shard_map/pallas_call | solution.py:131
  135.7 21.4 %all-gather = bf16[16,1,4224]{2,1,0:T(2,128)(2,1)S(1)} all-gather(bf16[1,1,4224]{2,1,0:T(2,128)(2,1)S(1)} %fusion.3), channel_id=1, replica_groups=mesh['groups'=2,'dp'=16] {'dp'}, dimensions={0}, use_global_device_ids=true | all-gather | bytes 143616 | tf_op jit(solution)/shard_map/all_gather | solution.py:263
  158.6 12.8 %all_to_all.5 = f32[16,1,4224]{2,1,0:T(1,128)S(1)} all-to-all(f32[16,1,4224]{2,1,0:T(1,128)S(1)} %copy.25), channel_id=1, replica_groups=mesh['groups'=2,'dp'=16] {'dp'}, dimensions={0} | all-to-all | bytes 540672 | tf_op jit(solution)/shard_map/all_to_all | solution.py:280
  (139 shorter events, 34.6 us)
Async XLA Ops:
  3.0 15.3 %collective-permute-start.2 = (bf16[1024,256]{1,0:T(8,128)(2,1)}, bf16[1024,256]{1,0:T(8,128)(2,1)}, u32[]{:S(2)}, u32[]{:S(2)}) collective-permute-start(bf16[1024,256]{1,0:T(8,128)(2,1)} %get-tuple-element.42.refs_0_), channel_id=1, source_target_pairs={{0,2},{1,3},{4,0},{5,1},{8,4},{9,5},{12,8},{13,9},{14,12},{15,13},... | collective-permute-start | bytes 1572872 | tf_op jit(solution)/shard_map/ppermute | solution.py:164
  5.9 17.9 %collective-permute-start.10 = (bf16[1024,256]{1,0:T(8,128)(2,1)}, bf16[1024,256]{1,0:T(8,128)(2,1)}, u32[]{:S(2)}, u32[]{:S(2)}) collective-permute-start(bf16[1024,256]{1,0:T(8,128)(2,1)} %get-tuple-element.42.refs_0_), channel_id=1, source_target_pairs={{0,4},{1,5},{4,8},{5,9},{8,12},{9,13},{12,14},{13,15},{14,10},{15,... | collective-permute-start | bytes 1572872 | tf_op jit(solution)/shard_map/ppermute | solution.py:167
  6.0 19.8 %collective-permute-start = (bf16[1024,256]{1,0:T(8,128)(2,1)}, bf16[1024,256]{1,0:T(8,128)(2,1)}, u32[]{:S(2)}, u32[]{:S(2)}) collective-permute-start(bf16[1024,256]{1,0:T(8,128)(2,1)} %get-tuple-element.42.refs_0_), channel_id=1, source_target_pairs={{0,1},{1,0},{2,3},{3,2},{4,5},{5,4},{6,7},{7,6},{8,9},{9,8},{10,11... | collective-permute-start | bytes 1572872 | tf_op jit(solution)/shard_map/ppermute | solution.py:173
  6.0 19.8 %collective-permute-start.1 = (bf16[1024,256]{1,0:T(8,128)(2,1)S(1)}, bf16[1024,256]{1,0:T(8,128)(2,1)}, u32[]{:S(2)}, u32[]{:S(2)}) collective-permute-start(bf16[1024,256]{1,0:T(8,128)(2,1)S(1)} %get-tuple-element.41.refs_1_), channel_id=1, source_target_pairs={{0,1},{1,0},{2,3},{3,2},{4,5},{5,4},{6,7},{7,6},{8,9},{9,8},{10,11... | collective-permute-start | bytes 1572872 | tf_op jit(solution)/shard_map/ppermute | solution.py:173
  24.2 15.2 %collective-permute-start.19 = (bf16[1024,256]{1,0:T(8,128)(2,1)}, bf16[1024,256]{1,0:T(8,128)(2,1)}, u32[]{:S(2)}, u32[]{:S(2)}) collective-permute-start(bf16[1024,256]{1,0:T(8,128)(2,1)} %collective-permute-done.10.refs_0_), channel_id=1, source_target_pairs={{0,16},{16,0},{1,17},{17,1},{2,18},{18,2},{3,19},{19,3},{4,20},{20... | collective-permute-start | bytes 1572872 | tf_op jit(solution)/shard_map/ppermute | solution.py:170
  25.8 15.3 %collective-permute-start.20 = (bf16[1024,256]{1,0:T(8,128)(2,1)}, bf16[1024,256]{1,0:T(8,128)(2,1)}, u32[]{:S(2)}, u32[]{:S(2)}) collective-permute-start(bf16[1024,256]{1,0:T(8,128)(2,1)} %collective-permute-done.10.refs_0_), channel_id=1, source_target_pairs={{0,1},{1,0},{2,3},{3,2},{4,5},{5,4},{6,7},{7,6},{8,9},{9,8},{10,11... | collective-permute-start | bytes 1572872 | tf_op jit(solution)/shard_map/ppermute | solution.py:173
  25.8 24.7 %collective-permute-start.3 = (bf16[1024,256]{1,0:T(8,128)(2,1)}, bf16[1024,256]{1,0:T(8,128)(2,1)}, u32[]{:S(2)}, u32[]{:S(2)}) collective-permute-start(bf16[1024,256]{1,0:T(8,128)(2,1)} %collective-permute-done.2.refs_0_), channel_id=1, source_target_pairs={{0,16},{16,0},{1,17},{17,1},{2,18},{18,2},{3,19},{19,3},{4,20},{20... | collective-permute-start | bytes 1572872 | tf_op jit(solution)/shard_map/ppermute | solution.py:170
  31.7 20.6 %collective-permute-start.4 = (bf16[1024,256]{1,0:T(8,128)(2,1)}, bf16[1024,256]{1,0:T(8,128)(2,1)}, u32[]{:S(2)}, u32[]{:S(2)}) collective-permute-start(bf16[1024,256]{1,0:T(8,128)(2,1)} %collective-permute-done.2.refs_0_), channel_id=1, source_target_pairs={{0,1},{1,0},{2,3},{3,2},{4,5},{5,4},{6,7},{7,6},{8,9},{9,8},{10,11... | collective-permute-start | bytes 1572872 | tf_op jit(solution)/shard_map/ppermute | solution.py:173
  36.7 34.1 %collective-permute-start.12 = (bf16[1024,256]{1,0:T(8,128)(2,1)}, bf16[1024,256]{1,0:T(8,128)(2,1)}, u32[]{:S(2)}, u32[]{:S(2)}) collective-permute-start(bf16[1024,256]{1,0:T(8,128)(2,1)} %collective-permute-done.11.refs_0_), channel_id=1, source_target_pairs={{0,16},{16,0},{1,17},{17,1},{2,18},{18,2},{3,19},{19,3},{4,20},{20... | collective-permute-start | bytes 1572872 | tf_op jit(solution)/shard_map/ppermute | solution.py:170
  39.4 31.9 %collective-permute-start.22 = (bf16[1024,256]{1,0:T(8,128)(2,1)}, bf16[1024,256]{1,0:T(8,128)(2,1)}, u32[]{:S(2)}, u32[]{:S(2)}) collective-permute-start(bf16[1024,256]{1,0:T(8,128)(2,1)} %collective-permute-done.11.refs_0_), channel_id=1, source_target_pairs={{0,4},{1,5},{4,8},{5,9},{8,12},{9,13},{12,14},{13,15},{14,10},{15,... | collective-permute-start | bytes 1572872 | tf_op jit(solution)/shard_map/ppermute | solution.py:167
  41.1 29.6 %collective-permute-start.7 = (bf16[1024,256]{1,0:T(8,128)(2,1)}, bf16[1024,256]{1,0:T(8,128)(2,1)}, u32[]{:S(2)}, u32[]{:S(2)}) collective-permute-start(bf16[1024,256]{1,0:T(8,128)(2,1)} %collective-permute-done.6.refs_4_), channel_id=1, source_target_pairs={{0,16},{16,0},{1,17},{17,1},{2,18},{18,2},{3,19},{19,3},{4,20},{20... | collective-permute-start | bytes 1572872 | tf_op jit(solution)/shard_map/ppermute | solution.py:170
  50.6 22.1 %collective-permute-start.15 = (bf16[1024,256]{1,0:T(8,128)(2,1)}, bf16[1024,256]{1,0:T(8,128)(2,1)}, u32[]{:S(2)}, u32[]{:S(2)}) collective-permute-start(bf16[1024,256]{1,0:T(8,128)(2,1)} %collective-permute-done.6.refs_4_), channel_id=1, source_target_pairs={{0,2},{1,3},{4,0},{5,1},{8,4},{9,5},{12,8},{13,9},{14,12},{15,13},... | collective-permute-start | bytes 1572872 | tf_op jit(solution)/shard_map/ppermute | solution.py:164
  52.3 21.0 %collective-permute-start.13 = (bf16[1024,256]{1,0:T(8,128)(2,1)}, bf16[1024,256]{1,0:T(8,128)(2,1)}, u32[]{:S(2)}, u32[]{:S(2)}) collective-permute-start(bf16[1024,256]{1,0:T(8,128)(2,1)} %collective-permute-done.11.refs_0_), channel_id=1, source_target_pairs={{0,1},{1,0},{2,3},{3,2},{4,5},{5,4},{6,7},{7,6},{8,9},{9,8},{10,11... | collective-permute-start | bytes 1572872 | tf_op jit(solution)/shard_map/ppermute | solution.py:173
  72.6 15.1 %collective-permute-start.23 = (bf16[1024,256]{1,0:T(8,128)(2,1)}, bf16[1024,256]{1,0:T(8,128)(2,1)}, u32[]{:S(2)}, u32[]{:S(2)}) collective-permute-start(bf16[1024,256]{1,0:T(8,128)(2,1)} %collective-permute-done.12.refs_1_), channel_id=1, source_target_pairs={{0,4},{1,5},{4,8},{5,9},{8,12},{9,13},{12,14},{13,15},{14,10},{15,... | collective-permute-start | bytes 1572872 | tf_op jit(solution)/shard_map/ppermute | solution.py:167
  73.3 24.5 %collective-permute-start.26 = (bf16[1024,256]{1,0:T(8,128)(2,1)}, bf16[1024,256]{1,0:T(8,128)(2,1)}, u32[]{:S(2)}, u32[]{:S(2)}) collective-permute-start(bf16[1024,256]{1,0:T(8,128)(2,1)} %collective-permute-done.22.refs_4_), channel_id=1, source_target_pairs={{0,4},{1,5},{4,8},{5,9},{8,12},{9,13},{12,14},{13,15},{14,10},{15,... | collective-permute-start | bytes 1572872 | tf_op jit(solution)/shard_map/ppermute | solution.py:167
  78.0 23.0 %collective-permute-start.14 = (bf16[1024,256]{1,0:T(8,128)(2,1)}, bf16[1024,256]{1,0:T(8,128)(2,1)S(1)}, u32[]{:S(2)}, u32[]{:S(2)}) collective-permute-start(bf16[1024,256]{1,0:T(8,128)(2,1)} %collective-permute-done.12.refs_1_), channel_id=1, source_target_pairs={{0,1},{1,0},{2,3},{3,2},{4,5},{5,4},{6,7},{7,6},{8,9},{9,8},{10,11... | collective-permute-start | bytes 1572872 | tf_op jit(solution)/shard_map/ppermute | solution.py:173
  78.0 25.1 %collective-permute-start.9 = (bf16[1024,256]{1,0:T(8,128)(2,1)}, bf16[1024,256]{1,0:T(8,128)(2,1)S(1)}, u32[]{:S(2)}, u32[]{:S(2)}) collective-permute-start(bf16[1024,256]{1,0:T(8,128)(2,1)} %collective-permute-done.7.refs_5_), channel_id=1, source_target_pairs={{0,1},{1,0},{2,3},{3,2},{4,5},{5,4},{6,7},{7,6},{8,9},{9,8},{10,11... | collective-permute-start | bytes 1572872 | tf_op jit(solution)/shard_map/ppermute | solution.py:173
  85.5 16.8 %collective-permute-start.17 = (bf16[1024,256]{1,0:T(8,128)(2,1)}, bf16[1024,256]{1,0:T(8,128)(2,1)S(1)}, u32[]{:S(2)}, u32[]{:S(2)}) collective-permute-start(bf16[1024,256]{1,0:T(8,128)(2,1)} %collective-permute-done.15.refs_4_), channel_id=1, source_target_pairs={{0,1},{1,0},{2,3},{3,2},{4,5},{5,4},{6,7},{7,6},{8,9},{9,8},{10,11... | collective-permute-start | bytes 1572872 | tf_op jit(solution)/shard_map/ppermute | solution.py:173
  87.8 16.6 %collective-permute-start.27 = (bf16[1024,256]{1,0:T(8,128)(2,1)}, bf16[1024,256]{1,0:T(8,128)(2,1)}, u32[]{:S(2)}, u32[]{:S(2)}) collective-permute-start(bf16[1024,256]{1,0:T(8,128)(2,1)} %collective-permute-done.16.refs_5_), channel_id=1, source_target_pairs={{0,2},{1,3},{4,0},{5,1},{8,4},{9,5},{12,8},{13,9},{14,12},{15,13},... | collective-permute-start | bytes 1572872 | tf_op jit(solution)/shard_map/ppermute | solution.py:164
  101.8 24.2 %collective-permute-start.21 = (bf16[1024,256]{1,0:T(8,128)(2,1)}, bf16[1024,256]{1,0:T(8,128)(2,1)}, u32[]{:S(2)}, u32[]{:S(2)}) collective-permute-start(bf16[1024,256]{1,0:T(8,128)(2,1)} %collective-permute-done.19.refs_1_), channel_id=1, source_target_pairs={{0,1},{1,0},{2,3},{3,2},{4,5},{5,4},{6,7},{7,6},{8,9},{9,8},{10,11... | collective-permute-start | bytes 1572872 | tf_op jit(solution)/shard_map/ppermute | solution.py:173
  103.1 22.9 %collective-permute-start.24 = (bf16[1024,256]{1,0:T(8,128)(2,1)}, bf16[1024,256]{1,0:T(8,128)(2,1)}, u32[]{:S(2)}, u32[]{:S(2)}) collective-permute-start(bf16[1024,256]{1,0:T(8,128)(2,1)} %collective-permute-done.22.refs_4_), channel_id=1, source_target_pairs={{0,1},{1,0},{2,3},{3,2},{4,5},{5,4},{6,7},{7,6},{8,9},{9,8},{10,11... | collective-permute-start | bytes 1572872 | tf_op jit(solution)/shard_map/ppermute | solution.py:173
  103.9 22.1 %collective-permute-start.25 = (bf16[1024,256]{1,0:T(8,128)(2,1)}, bf16[1024,256]{1,0:T(8,128)(2,1)}, u32[]{:S(2)}, u32[]{:S(2)}) collective-permute-start(bf16[1024,256]{1,0:T(8,128)(2,1)} %collective-permute-done.23.refs_5_), channel_id=1, source_target_pairs={{0,1},{1,0},{2,3},{3,2},{4,5},{5,4},{6,7},{7,6},{8,9},{9,8},{10,11... | collective-permute-start | bytes 1572872 | tf_op jit(solution)/shard_map/ppermute | solution.py:173
  104.4 21.6 %collective-permute-start.28 = (bf16[1024,256]{1,0:T(8,128)(2,1)}, bf16[1024,256]{1,0:T(8,128)(2,1)}, u32[]{:S(2)}, u32[]{:S(2)}) collective-permute-start(bf16[1024,256]{1,0:T(8,128)(2,1)} %collective-permute-done.26.refs_8_), channel_id=1, source_target_pairs={{0,1},{1,0},{2,3},{3,2},{4,5},{5,4},{6,7},{7,6},{8,9},{9,8},{10,11... | collective-permute-start | bytes 1572872 | tf_op jit(solution)/shard_map/ppermute | solution.py:173
  105.3 20.8 %collective-permute-start.29 = (bf16[1024,256]{1,0:T(8,128)(2,1)}, bf16[1024,256]{1,0:T(8,128)(2,1)}, u32[]{:S(2)}, u32[]{:S(2)}) collective-permute-start(bf16[1024,256]{1,0:T(8,128)(2,1)} %collective-permute-done.27.refs_9_), channel_id=1, source_target_pairs={{0,1},{1,0},{2,3},{3,2},{4,5},{5,4},{6,7},{7,6},{8,9},{9,8},{10,11... | collective-permute-start | bytes 1572872 | tf_op jit(solution)/shard_map/ppermute | solution.py:173
  (30 other events, 546.7 us)

commit v4 on v3

--- a/solution.py
+++ b/solution.py
@@ -172,48 +172,52 @@
     def other_core(piece):
         return lax.ppermute(piece, "dp", [(i, i ^ 1) for i in range(ranks)])
 
+    def after(piece, *earlier):
+        return lax.optimization_barrier((piece, earlier))[0]
+
+    cycle = jnp.array(CYCLE, jnp.int32)
+    at = jnp.array(where, jnp.int32)[me // CORES]
+
+    def place_of(group):
+        chips = cycle[(at + jnp.array(group, jnp.int32)) % size]
+        return jnp.stack([chips * CORES + core, chips * CORES + 1 - core], axis=1).reshape(-1)
+
+    steps = ((0,), (1, 2), (-2, 3), (-1, -3, 4))
+    places = [place_of(group) for group in steps]
+    hidden, squares = [], []
+
+    def run(i, side, pieces):
+        h, s = project(jnp.append(places[i], side), context, residual, pieces)
+        hidden.append(h)
+        squares.append(s)
+        return s
+
     half = out_proj.shape[0] // 2
     own = lax.dynamic_slice_in_dim(out_proj, side * half, half, 0)
-    rest = lax.dynamic_slice_in_dim(out_proj, (1 - side) * half, half, 0)
     n1, l1 = from_next(own), from_last(own)
-    own_pair = (own, rest, other_core(own), other_core(rest))
+    other = other_core(out_proj)
+    done = run(0, 0, [out_proj[:half], out_proj[half:], other[:half], other[half:]])
+    n1, l1 = after((n1, l1), done)
     n2, l2 = from_next(n1), from_last(l1)
     xn1 = over_x(n1)
+    cn1, cl1 = other_core(n1), other_core(l1)
+    n2, l2, xn1 = after((n2, l2, xn1), cn1, cl1)
     n3, l3 = from_next(n2), from_last(l2)
     xn2 = over_x(n2)
+    cn2, cl2, cxn1 = other_core(n2), other_core(l2), other_core(xn1)
+    xn2, n3, l3 = after((xn2, n3, l3), cn2, cl2, cxn1)
     n3x, l4 = from_next(xn2), from_last(l3)
-    xl2 = over_x(l2)
+    xl2 = over_x(after(l2, xn2))
+    cn3, cl3, cxn2 = other_core(n3), other_core(l3), other_core(xn2)
+    done = run(1, side, [n1, xn1, cn1, cxn1, n2, xn2, cn2, cxn2])
+    n3x, l4, xl2 = after((n3x, l4, xl2), cn3, cl3, cxn2, done)
     n4x, l3x = from_next(n3x), from_last(xl2)
-    xl1 = over_x(l1)
-
-    def both(a, b):
-        return (a, b, other_core(a), other_core(b))
-
-    batches = (
-        (0, own_pair),
-        (1, both(n1, xn1)),
-        (2, both(n2, xn2)),
-        (-2, both(l2, xl2)),
-        (3, both(n3, n3x)),
-        (-1, both(l1, xl1)),
-        (-3, both(l3, l3x)),
-        (4, both(l4, n4x)),
-    )
-    cycle = jnp.array(CYCLE, jnp.int32)
-    at = jnp.array(where, jnp.int32)[me // CORES]
-
-    def place_of(group):
-        chips = cycle[(at + jnp.array([k for k, _ in group], jnp.int32)) % size]
-        return jnp.stack([chips * CORES + core, chips * CORES + 1 - core], axis=1).reshape(-1)
-
-    hidden, squares, places = [], [], []
-    for group in (batches[:1], batches[1:3], batches[3:5], batches[5:]):
-        place = place_of(group)
-        pieces = [piece for _, four in group for piece in four]
-        h, s = project(jnp.append(place, side), context, residual, pieces)
-        hidden.append(h)
-        squares.append(s)
-        places.append(place)
+    xl1 = over_x(after(l1, xl2))
+    cn3x, cl4, cxl2 = other_core(n3x), other_core(l4), other_core(xl2)
+    done = run(2, side, [l2, xl2, cl2, cxl2, n3, n3x, cn3, cn3x])
+    n4x, l3x, xl1 = after((n4x, l3x, xl1), cl4, done)
+    cn4x, cl3x, cxl1 = other_core(n4x), other_core(l3x), other_core(xl1)
+    run(3, side, [l1, xl1, cl1, cxl1, l3, l3x, cl3, cl3x, l4, n4x, cl4, cn4x])
     embedded = pool(jnp.concatenate(places), lengths, norm_gain, hidden, squares)
     return embedded.reshape(1, -1)
 
@@ -260,7 +264,11 @@
     contract = (((1,), (1,)), ((), ()))
 
     flags = jnp.pad(pattern.astype(jnp.bfloat16), ((0, 0), (0, LANES - blocks)))
-    everyone = lax.all_gather(jnp.concatenate([emb_half, flags], axis=1), "dp", axis=0, tiled=True)
+    everyone = jnp.broadcast_to(
+        jnp.concatenate([emb_half, flags], axis=1)[None], (ranks,) + (emb_half.shape[0], features + LANES)
+    )
+    everyone = lax.all_to_all(everyone, "dp", split_axis=0, concat_axis=0, tiled=True)
+    everyone = everyone.reshape(-1, features + LANES)
     emb_all = everyone[:, :features]
     flags_all = everyone[:, features : features + blocks].astype(jnp.float32)
     scores = lax.dot_general(emb_all, queries, contract, preferred_element_type=jnp.float32) * temper

time: 178 us -> 154 us (0.87)
  waiting for transfers between devices: 61.6 us -> 35.9 us
  local copies, waits for them, and re-layouts: 15.4 us -> 38.9 us
  blocking collectives: 34.1 us -> 12.8 us
  starting transfers between devices: 21.7 us -> 24.1 us
  other arithmetic: 12.6 us -> 10.3 us
    unnamed x50 -> x92, local copies, waits for them, and re-layouts: 6.23 us -> 29.3 us
    all_gather x1 -> x0, blocking collectives: 21.4 us -> none  [per_device(): lax.all_gather(jnp.concatenate([emb_half, flags], axis=1), 'dp', axis=0,...]
    ppermute x4, waiting for transfers between devices: 23.3 us -> 4.72 us  [over_x(): return lax.ppermute(piece, 'groups', [(0, 1), (1, 0)])]
    ppermute x5, waiting for transfers between devices: 14.2 us -> 4.57 us  [from_last(): return lax.ppermute(piece, 'dp', ring(1))]
    all_to_all x0 -> x1, waiting for transfers between devices: none -> 8.03 us  [per_device(): lax.all_to_all(everyone, 'dp', split_axis=0, concat_axis=0, tiled=True)]
    ppermute x5, waiting for transfers between devices: 24.1 us -> 18.5 us  [from_next(): return lax.ppermute(piece, 'dp', ring(-1))]
    all_to_all x0 -> x1, starting transfers between devices: none -> 4.92 us  [per_device(): lax.all_to_all(everyone, 'dp', split_axis=0, concat_axis=0, tiled=True)]
    ppermute x5, starting transfers between devices: 4.25 us -> 1.86 us  [from_last(): return lax.ppermute(piece, 'dp', ring(1))]
  transfers between devices with their start and end apart: 30 -> 30, of which waited for: 9 -> 9; matrix products, arithmetic and copies ran while one was open for 9% -> 9% of each run, Pallas kernels for 8% -> 9%
where the time goes in v4:
time: 154 us; the launch traced here: 153 us
  local copies, waits for them, and re-layouts  38.9 us (25%)
  waiting for transfers between devices  35.9 us (23%)
  starting transfers between devices  24.1 us (16%)
  Pallas kernels  23.1 us (15%)
  blocking collectives  12.8 us (8%)
  other arithmetic  10.3 us (7%)
  between operations  6.77 us (4%)
    unnamed x92, local copies, waits for them, and re-layouts  29.3 us
    pallas_call x4, Pallas kernels, project(): pl.pallas_call(functools.partial(project_kernel, count), out_shape=(jax.S...  20.8 us
    ppermute x5, waiting for transfers between devices, from_next(): return lax.ppermute(piece, 'dp', ring(-1))  18.5 us
    all_to_all x1, blocking collectives, per_device(): parts = lax.all_to_all(parts, 'dp', split_axis=0, concat_axis=0, tiled=True)  12.8 us
    ppermute x5, starting transfers between devices, from_next(): return lax.ppermute(piece, 'dp', ring(-1))  8.86 us
    all_to_all x1, waiting for transfers between devices, per_device(): lax.all_to_all(everyone, 'dp', split_axis=0, concat_axis=0, tiled=True)  8.03 us
    ppermute x4, starting transfers between devices, over_x(): return lax.ppermute(piece, 'groups', [(0, 1), (1, 0)])  5.01 us
    all_to_all x1, starting transfers between devices, per_device(): lax.all_to_all(everyone, 'dp', split_axis=0, concat_axis=0, tiled=True)  4.92 us
  transfers between devices with their start and end apart: 30, of which 9 were waited for; matrix products, arithmetic and copies ran while one was open for 9% of the time, Pallas kernels for 9%

profile of v4, /device:TPU:0, one launch (start us, length us, event | category | flops | bytes accessed | tf_op | source)
XLA Modules:
  0.0 152.7 jit_solution(12038687098529867854)
XLA Ops:
  1.2 2.6 %constant_dynamic-slice_fusion = (bf16[1024,256]{1,0:T(8,128)(2,1)}, bf16[1024,256]{1,0:T(8,128)(2,1)S(1)}, bf16[1024,256]{1,0:T(8,128)(2,1)}) fusion(bf16[2048,256]{1,0:T(8,128)(2,1)} %param.15, s32[]{:T(128)S(6)} %select_n.87), kind=kLoop, calls=%fused_computation.68 | loop fusion | bytes 3145732 | tf_op jit(solution)/shard_map/dynamic_slice | solution.py:196
  3.8 2.5 %collective-permute-start.1 = (bf16[1024,256]{1,0:T(8,128)(2,1)}, bf16[1024,256]{1,0:T(8,128)(2,1)}, u32[]{:S(2)}, u32[]{:S(2)}) collective-permute-start(bf16[1024,256]{1,0:T(8,128)(2,1)} %get-tuple-element.73), channel_id=1, source_target_pairs={{0,2},{1,3},{4,0},{5,1},{8,4},{9,5},{12,8},{13,9},{14,12},{15,13},... | collective-permute-start | bytes 1572872 | tf_op jit(solution)/shard_map/ppermute | solution.py:164
  12.1 2.2 %copy-done.1 = bf16[512,4096]{1,0:T(8,128)(2,1)S(1)} copy-done((bf16[512,4096]{1,0:T(8,128)(2,1)S(1)}, bf16[512,4096]{1,0:T(8,128)(2,1)}, u32[]{:S(2)}) %copy-start.1) | copy-done | bytes 4194328
  14.3 2.6 %shard_map.148 = (f32[2,512,256]{2,1,0:T(8,128)S(1)}, f32[512,128]{1,0:T(8,128)S(1)}) custom-call(s32[3]{0:T(128)S(1)} %pad_add_fusion.4.place, bf16[512,2048]{1,0:T(8,128)(2,1)S(1)} %copy-done.5, bf16[512,4096]{1,0:T(8,128)(2,1)S(1)} %copy-done.1, bf16[1024,256]{1,0:T(8,128)(2,1)S(1)} %copy-done.10, bf16[1024,256]{1,0:T(8,128)(2,1)S(1)} %get-tuple-element.74.refs_1_, ...), custom_call_target="tpu_custom_call" | custom-call | flops 1073741824 | bytes 3670016 | tf_op jit(solution)/shard_map/pallas_call | solution.py:64
  20.7 1.6 %collective-permute-start.3 = (bf16[1024,256]{1,0:T(8,128)(2,1)}, bf16[1024,256]{1,0:T(8,128)(2,1)S(1)}, u32[]{:S(2)}, u32[]{:S(2)}) collective-permute-start(bf16[1024,256]{1,0:T(8,128)(2,1)} %collective-permute-done.1.refs_0_), channel_id=1, source_target_pairs={{0,2},{1,3},{4,0},{5,1},{8,4},{9,5},{12,8},{13,9},{14,12},{15,13},... | collective-permute-start | bytes 1572872 | tf_op jit(solution)/shard_map/ppermute | solution.py:164
  22.7 1.5 collective-permute-start.5
  24.7 9.4 %collective-permute-done.3.refs_4_ = bf16[1024,256]{1,0:T(8,128)(2,1)S(1)} collective-permute-done((bf16[1024,256]{1,0:T(8,128)(2,1)}, bf16[1024,256]{1,0:T(8,128)(2,1)S(1)}, u32[]{:S(2)}, u32[]{:S(2)}) %collective-permute-start.3) | collective-permute-done | bytes 524320 | tf_op jit(solution)/shard_map/ppermute | solution.py:164
  36.4 1.6 %collective-permute-start.10 = (bf16[1024,256]{1,0:T(8,128)(2,1)S(1)}, bf16[1024,256]{1,0:T(8,128)(2,1)S(1)}, u32[]{:S(2)}, u32[]{:S(2)}) collective-permute-start(bf16[1024,256]{1,0:T(8,128)(2,1)S(1)} %collective-permute-done.3.refs_4_), channel_id=1, source_target_pairs={{0,2},{1,3},{4,0},{5,1},{8,4},{9,5},{12,8},{13,9},{14,12},{15,13},... | collective-permute-start | bytes 1572872 | tf_op jit(solution)/shard_map/ppermute | solution.py:164
  39.7 8.5 %collective-permute-done.10.refs_4_ = bf16[1024,256]{1,0:T(8,128)(2,1)S(1)} collective-permute-done((bf16[1024,256]{1,0:T(8,128)(2,1)S(1)}, bf16[1024,256]{1,0:T(8,128)(2,1)S(1)}, u32[]{:S(2)}, u32[]{:S(2)}) %collective-permute-start.10) | collective-permute-done | bytes 524320 | tf_op jit(solution)/shard_map/ppermute | solution.py:164
  48.2 1.5 collective-permute-start.9
  50.5 1.9 %collective-permute-done.11.refs_4_ = bf16[1024,256]{1,0:T(8,128)(2,1)} collective-permute-done((bf16[1024,256]{1,0:T(8,128)(2,1)S(1)}, bf16[1024,256]{1,0:T(8,128)(2,1)}, u32[]{:S(2)}, u32[]{:S(2)}) %collective-permute-start.11) | collective-permute-done | bytes 524320 | tf_op jit(solution)/shard_map/ppermute | solution.py:167
  54.8 4.5 %collective-permute-done.9.refs_5_ = bf16[1024,256]{1,0:T(8,128)(2,1)} collective-permute-done((bf16[1024,256]{1,0:T(8,128)(2,1)S(1)}, bf16[1024,256]{1,0:T(8,128)(2,1)}, u32[]{:S(2)}, u32[]{:S(2)}) %collective-permute-start.9) | collective-permute-done | bytes 524320 | tf_op jit(solution)/shard_map/ppermute | solution.py:170
  60.7 1.6 %collective-permute-start.15 = (bf16[1024,256]{1,0:T(8,128)(2,1)}, bf16[1024,256]{1,0:T(8,128)(2,1)}, u32[]{:S(2)}, u32[]{:S(2)}) collective-permute-start(bf16[1024,256]{1,0:T(8,128)(2,1)} %collective-permute-done.9.refs_5_), channel_id=1, source_target_pairs={{0,2},{1,3},{4,0},{5,1},{8,4},{9,5},{12,8},{13,9},{14,12},{15,13},... | collective-permute-start | bytes 1572872 | tf_op jit(solution)/shard_map/ppermute | solution.py:164
  64.7 2.2 %copy-done.2 = bf16[512,4096]{1,0:T(8,128)(2,1)S(1)} copy-done((bf16[512,4096]{1,0:T(8,128)(2,1)S(1)}, bf16[512,4096]{1,0:T(8,128)(2,1)}, u32[]{:S(2)}) %copy-start.2) | copy-done | bytes 4194328
  72.1 5.3 %shard_map.149 = (f32[4,512,256]{2,1,0:T(8,128)S(1)}, f32[512,128]{1,0:T(8,128)S(1)}) custom-call(s32[5]{0:T(128)S(1)} %pad_add_fusion.5.place, bf16[512,2048]{1,0:T(8,128)(2,1)S(1)} %copy-done.5, bf16[512,4096]{1,0:T(8,128)(2,1)S(1)} %copy-done.2, bf16[1024,256]{1,0:T(8,128)(2,1)} %collective-permute-done.1.refs_0_, bf16[1024,256]{1,0:T(8,128)(2,1)S(1)} %copy-done.22, ...), custom_call_target="tpu_custom_call" | custom-call | flops 2147483648 | bytes 7340032 | tf_op jit(solution)/shard_map/pallas_call | solution.py:64
  82.0 1.6 %collective-permute-start.22 = (bf16[1024,256]{1,0:T(8,128)(2,1)}, bf16[1024,256]{1,0:T(8,128)(2,1)}, u32[]{:S(2)}, u32[]{:S(2)}) collective-permute-start(bf16[1024,256]{1,0:T(8,128)(2,1)} %collective-permute-done.15.refs_5_), channel_id=1, source_target_pairs={{0,2},{1,3},{4,0},{5,1},{8,4},{9,5},{12,8},{13,9},{14,12},{15,13},... | collective-permute-start | bytes 1572872 | tf_op jit(solution)/shard_map/ppermute | solution.py:164
  86.1 2.2 %copy-done.3 = bf16[512,4096]{1,0:T(8,128)(2,1)S(1)} copy-done((bf16[512,4096]{1,0:T(8,128)(2,1)S(1)}, bf16[512,4096]{1,0:T(8,128)(2,1)}, u32[]{:S(2)}) %copy-start.3) | copy-done | bytes 4194328
  91.4 5.3 %shard_map.150 = (f32[4,512,256]{2,1,0:T(8,128)S(1)}, f32[512,128]{1,0:T(8,128)S(1)}) custom-call(s32[5]{0:T(128)S(1)} %pad_add_fusion.6.place, bf16[512,2048]{1,0:T(8,128)(2,1)S(1)} %copy-done.5, bf16[512,4096]{1,0:T(8,128)(2,1)S(1)} %copy-done.3, bf16[1024,256]{1,0:T(8,128)(2,1)S(1)} %copy-done.14, bf16[1024,256]{1,0:T(8,128)(2,1)} %collective-permute-done.17.refs_1_, ...), custom_call_target="tpu_custom_call" | custom-call | flops 2147483648 | bytes 7340032 | tf_op jit(solution)/shard_map/pallas_call | solution.py:64
  104.2 2.2 %copy-done.4 = bf16[512,4096]{1,0:T(8,128)(2,1)S(1)} copy-done((bf16[512,4096]{1,0:T(8,128)(2,1)S(1)}, bf16[512,4096]{1,0:T(8,128)(2,1)}, u32[]{:S(2)}) %copy-start.4) | copy-done | bytes 4194328
  106.4 7.6 %shard_map.151 = (f32[6,512,256]{2,1,0:T(8,128)S(1)}, f32[512,128]{1,0:T(8,128)S(1)}) custom-call(s32[7]{0:T(128)S(1)} %pad_add_fusion.7.place, bf16[512,2048]{1,0:T(8,128)(2,1)S(1)} %copy-done.5, bf16[512,4096]{1,0:T(8,128)(2,1)S(1)} %copy-done.4, bf16[1024,256]{1,0:T(8,128)(2,1)} %collective-permute-done.2.refs_0_, ...), custom_call_target="tpu_custom_call" | custom-call | flops 3221225472 | bytes 11010048 | tf_op jit(solution)/shard_map/pallas_call | solution.py:64
  114.1 2.2 %shard_map.152 = f32[16,256]{1,0:T(8,128)S(1)} custom-call(s32[16]{0:T(128)S(1)} %pad_add_fusion.3.place, s32[1]{0:T(128)S(6)} %copy.30.length, f32[16,256]{1,0:T(8,128)S(1)} %reshape.233.gain, f32[2,512,256]{2,1,0:T(8,128)S(1)} %copy-done.12, f32[4,512,256]{2,1,0:T(8,128)S(1)} %copy-done.7, f32[4,512,256]{2,1,0:T(8,128)S(1)} %copy-done.9, ...), custom_call_target="tpu_custom_call" | custom-call | tf_op jit(solution)/shard_map/pallas_call | solution.py:131
  119.3 4.9 %all-to-all-start = ((bf16[16,2,2112]{2,1,0:T(2,128)(2,1)}), bf16[16,2,2112]{2,1,0:T(2,128)(2,1)S(1)}, u32[]{:S(2)}, u32[]{:S(2)}) async-start(bf16[16,2,2112]{2,1,0:T(2,128)(2,1)} %reshape.292), calls=%async_computation | async-start | bytes 278528 | tf_op jit(solution)/shard_map/all_to_all | solution.py:270
  124.3 8.0 %all-to-all-done = bf16[16,2,2112]{2,1,0:T(2,128)(2,1)S(1)} async-done(((bf16[16,2,2112]{2,1,0:T(2,128)(2,1)}), bf16[16,2,2112]{2,1,0:T(2,128)(2,1)S(1)}, u32[]{:S(2)}, u32[]{:S(2)}) %all-to-all-start) | async-done | bytes 135200 | tf_op jit(solution)/shard_map/all_to_all | solution.py:270
  134.0 12.8 %all_to_all.10 = f32[16,1,4224]{2,1,0:T(1,128)S(1)} all-to-all(f32[16,1,4224]{2,1,0:T(1,128)S(1)} %copy.25), channel_id=1, replica_groups=mesh['groups'=2,'dp'=16] {'dp'}, dimensions={0} | all-to-all | bytes 540672 | tf_op jit(solution)/shard_map/all_to_all | solution.py:288
  (184 shorter events, 49.6 us)
Async XLA Ops:
  0.7 10.1 %collective-permute-start = (bf16[2048,256]{1,0:T(8,128)(2,1)}, bf16[2048,256]{1,0:T(8,128)(2,1)}, u32[]{:S(2)}, u32[]{:S(2)}) collective-permute-start(bf16[2048,256]{1,0:T(8,128)(2,1)} %param.15), channel_id=1, source_target_pairs={{0,1},{1,0},{2,3},{3,2},{4,5},{5,4},{6,7},{7,6},{8,9},{9,8},{10,11... | collective-permute-start | bytes 3145736 | tf_op jit(solution)/shard_map/ppermute | solution.py:173
  3.8 15.5 %collective-permute-start.1 = (bf16[1024,256]{1,0:T(8,128)(2,1)}, bf16[1024,256]{1,0:T(8,128)(2,1)}, u32[]{:S(2)}, u32[]{:S(2)}) collective-permute-start(bf16[1024,256]{1,0:T(8,128)(2,1)} %get-tuple-element.73), channel_id=1, source_target_pairs={{0,2},{1,3},{4,0},{5,1},{8,4},{9,5},{12,8},{13,9},{14,12},{15,13},... | collective-permute-start | bytes 1572872 | tf_op jit(solution)/shard_map/ppermute | solution.py:164
  6.3 14.3 %collective-permute-start.2 = (bf16[1024,256]{1,0:T(8,128)(2,1)}, bf16[1024,256]{1,0:T(8,128)(2,1)}, u32[]{:S(2)}, u32[]{:S(2)}) collective-permute-start(bf16[1024,256]{1,0:T(8,128)(2,1)} %get-tuple-element.73), channel_id=1, source_target_pairs={{0,4},{1,5},{4,8},{5,9},{8,12},{9,13},{12,14},{13,15},{14,10},{15,... | collective-permute-start | bytes 1572872 | tf_op jit(solution)/shard_map/ppermute | solution.py:167
  20.7 13.4 %collective-permute-start.3 = (bf16[1024,256]{1,0:T(8,128)(2,1)}, bf16[1024,256]{1,0:T(8,128)(2,1)S(1)}, u32[]{:S(2)}, u32[]{:S(2)}) collective-permute-start(bf16[1024,256]{1,0:T(8,128)(2,1)} %collective-permute-done.1.refs_0_), channel_id=1, source_target_pairs={{0,2},{1,3},{4,0},{5,1},{8,4},{9,5},{12,8},{13,9},{14,12},{15,13},... | collective-permute-start | bytes 1572872 | tf_op jit(solution)/shard_map/ppermute | solution.py:164
  22.3 13.1 %collective-permute-start.4 = (bf16[1024,256]{1,0:T(8,128)(2,1)}, bf16[1024,256]{1,0:T(8,128)(2,1)S(1)}, u32[]{:S(2)}, u32[]{:S(2)}) collective-permute-start(bf16[1024,256]{1,0:T(8,128)(2,1)} %collective-permute-done.2.refs_0_), channel_id=1, source_target_pairs={{0,4},{1,5},{4,8},{5,9},{8,12},{9,13},{12,14},{13,15},{14,10},{15,... | collective-permute-start | bytes 1572872 | tf_op jit(solution)/shard_map/ppermute | solution.py:167
  22.7 12.8 %collective-permute-start.5 = (bf16[1024,256]{1,0:T(8,128)(2,1)}, bf16[1024,256]{1,0:T(8,128)(2,1)S(1)}, u32[]{:S(2)}, u32[]{:S(2)}) collective-permute-start(bf16[1024,256]{1,0:T(8,128)(2,1)} %collective-permute-done.1.refs_0_), channel_id=1, source_target_pairs={{0,16},{16,0},{1,17},{17,1},{2,18},{18,2},{3,19},{19,3},{4,20},{20... | collective-permute-start | bytes 1572872 | tf_op jit(solution)/shard_map/ppermute | solution.py:170
  24.2 11.4 %collective-permute-start.6 = (bf16[1024,256]{1,0:T(8,128)(2,1)}, bf16[1024,256]{1,0:T(8,128)(2,1)S(1)}, u32[]{:S(2)}, u32[]{:S(2)}) collective-permute-start(bf16[1024,256]{1,0:T(8,128)(2,1)} %collective-permute-done.1.refs_0_), channel_id=1, source_target_pairs={{0,1},{1,0},{2,3},{3,2},{4,5},{5,4},{6,7},{7,6},{8,9},{9,8},{10,11... | collective-permute-start | bytes 1572872 | tf_op jit(solution)/shard_map/ppermute | solution.py:173
  24.2 12.2 %collective-permute-start.7 = (bf16[1024,256]{1,0:T(8,128)(2,1)}, bf16[1024,256]{1,0:T(8,128)(2,1)S(1)}, u32[]{:S(2)}, u32[]{:S(2)}) collective-permute-start(bf16[1024,256]{1,0:T(8,128)(2,1)} %collective-permute-done.2.refs_0_), channel_id=1, source_target_pairs={{0,1},{1,0},{2,3},{3,2},{4,5},{5,4},{6,7},{7,6},{8,9},{9,8},{10,11... | collective-permute-start | bytes 1572872 | tf_op jit(solution)/shard_map/ppermute | solution.py:173
  36.4 11.9 %collective-permute-start.10 = (bf16[1024,256]{1,0:T(8,128)(2,1)S(1)}, bf16[1024,256]{1,0:T(8,128)(2,1)S(1)}, u32[]{:S(2)}, u32[]{:S(2)}) collective-permute-start(bf16[1024,256]{1,0:T(8,128)(2,1)S(1)} %collective-permute-done.3.refs_4_), channel_id=1, source_target_pairs={{0,2},{1,3},{4,0},{5,1},{8,4},{9,5},{12,8},{13,9},{14,12},{15,13},... | collective-permute-start | bytes 1572872 | tf_op jit(solution)/shard_map/ppermute | solution.py:164
  37.9 14.4 %collective-permute-start.12 = (bf16[1024,256]{1,0:T(8,128)(2,1)S(1)}, bf16[1024,256]{1,0:T(8,128)(2,1)S(1)}, u32[]{:S(2)}, u32[]{:S(2)}) collective-permute-start(bf16[1024,256]{1,0:T(8,128)(2,1)S(1)} %collective-permute-done.3.refs_4_), channel_id=1, source_target_pairs={{0,1},{1,0},{2,3},{3,2},{4,5},{5,4},{6,7},{7,6},{8,9},{9,8},{10,11... | collective-permute-start | bytes 1572872 | tf_op jit(solution)/shard_map/ppermute | solution.py:173
  38.0 14.4 %collective-permute-start.11 = (bf16[1024,256]{1,0:T(8,128)(2,1)S(1)}, bf16[1024,256]{1,0:T(8,128)(2,1)}, u32[]{:S(2)}, u32[]{:S(2)}) collective-permute-start(bf16[1024,256]{1,0:T(8,128)(2,1)S(1)} %collective-permute-done.4.refs_0_), channel_id=1, source_target_pairs={{0,4},{1,5},{4,8},{5,9},{8,12},{9,13},{12,14},{13,15},{14,10},{15,... | collective-permute-start | bytes 1572872 | tf_op jit(solution)/shard_map/ppermute | solution.py:167
  38.4 14.8 %collective-permute-start.13 = (bf16[1024,256]{1,0:T(8,128)(2,1)S(1)}, bf16[1024,256]{1,0:T(8,128)(2,1)S(1)}, u32[]{:S(2)}, u32[]{:S(2)}) collective-permute-start(bf16[1024,256]{1,0:T(8,128)(2,1)S(1)} %collective-permute-done.4.refs_0_), channel_id=1, source_target_pairs={{0,1},{1,0},{2,3},{3,2},{4,5},{5,4},{6,7},{7,6},{8,9},{9,8},{10,11... | collective-permute-start | bytes 1572872 | tf_op jit(solution)/shard_map/ppermute | solution.py:173
  38.6 15.4 %collective-permute-start.8 = (bf16[1024,256]{1,0:T(8,128)(2,1)S(1)}, bf16[1024,256]{1,0:T(8,128)(2,1)S(1)}, u32[]{:S(2)}, u32[]{:S(2)}) collective-permute-start(bf16[1024,256]{1,0:T(8,128)(2,1)S(1)} %collective-permute-done.5.refs_1_), channel_id=1, source_target_pairs={{0,1},{1,0},{2,3},{3,2},{4,5},{5,4},{6,7},{7,6},{8,9},{9,8},{10,11... | collective-permute-start | bytes 1572872 | tf_op jit(solution)/shard_map/ppermute | solution.py:173
  48.2 11.1 %collective-permute-start.9 = (bf16[1024,256]{1,0:T(8,128)(2,1)S(1)}, bf16[1024,256]{1,0:T(8,128)(2,1)}, u32[]{:S(2)}, u32[]{:S(2)}) collective-permute-start(bf16[1024,256]{1,0:T(8,128)(2,1)S(1)} %collective-permute-done.3.refs_4_), channel_id=1, source_target_pairs={{0,16},{16,0},{1,17},{17,1},{2,18},{18,2},{3,19},{19,3},{4,20},{20... | collective-permute-start | bytes 1572872 | tf_op jit(solution)/shard_map/ppermute | solution.py:170
  60.7 18.8 %collective-permute-start.15 = (bf16[1024,256]{1,0:T(8,128)(2,1)}, bf16[1024,256]{1,0:T(8,128)(2,1)}, u32[]{:S(2)}, u32[]{:S(2)}) collective-permute-start(bf16[1024,256]{1,0:T(8,128)(2,1)} %collective-permute-done.9.refs_5_), channel_id=1, source_target_pairs={{0,2},{1,3},{4,0},{5,1},{8,4},{9,5},{12,8},{13,9},{14,12},{15,13},... | collective-permute-start | bytes 1572872 | tf_op jit(solution)/shard_map/ppermute | solution.py:164
  62.3 17.3 %collective-permute-start.16 = (bf16[1024,256]{1,0:T(8,128)(2,1)}, bf16[1024,256]{1,0:T(8,128)(2,1)}, u32[]{:S(2)}, u32[]{:S(2)}) collective-permute-start(bf16[1024,256]{1,0:T(8,128)(2,1)} %collective-permute-done.11.refs_4_), channel_id=1, source_target_pairs={{0,4},{1,5},{4,8},{5,9},{8,12},{9,13},{12,14},{13,15},{14,10},{15,... | collective-permute-start | bytes 1572872 | tf_op jit(solution)/shard_map/ppermute | solution.py:167
  62.7 16.8 %collective-permute-start.19 = (bf16[1024,256]{1,0:T(8,128)(2,1)}, bf16[1024,256]{1,0:T(8,128)(2,1)}, u32[]{:S(2)}, u32[]{:S(2)}) collective-permute-start(bf16[1024,256]{1,0:T(8,128)(2,1)} %collective-permute-done.11.refs_4_), channel_id=1, source_target_pairs={{0,1},{1,0},{2,3},{3,2},{4,5},{5,4},{6,7},{7,6},{8,9},{9,8},{10,11... | collective-permute-start | bytes 1572872 | tf_op jit(solution)/shard_map/ppermute | solution.py:173
  62.7 16.8 %collective-permute-start.17 = (bf16[1024,256]{1,0:T(8,128)(2,1)}, bf16[1024,256]{1,0:T(8,128)(2,1)}, u32[]{:S(2)}, u32[]{:S(2)}) collective-permute-start(bf16[1024,256]{1,0:T(8,128)(2,1)} %copy-done.13), channel_id=1, source_target_pairs={{0,16},{16,0},{1,17},{17,1},{2,18},{18,2},{3,19},{19,3},{4,20},{20... | collective-permute-start | bytes 1572872 | tf_op jit(solution)/shard_map/ppermute | solution.py:170
  64.2 15.3 %collective-permute-start.18 = (bf16[1024,256]{1,0:T(8,128)(2,1)}, bf16[1024,256]{1,0:T(8,128)(2,1)}, u32[]{:S(2)}, u32[]{:S(2)}) collective-permute-start(bf16[1024,256]{1,0:T(8,128)(2,1)} %copy-done.15), channel_id=1, source_target_pairs={{0,1},{1,0},{2,3},{3,2},{4,5},{5,4},{6,7},{7,6},{8,9},{9,8},{10,11... | collective-permute-start | bytes 1572872 | tf_op jit(solution)/shard_map/ppermute | solution.py:173
  82.0 16.9 %collective-permute-start.22 = (bf16[1024,256]{1,0:T(8,128)(2,1)}, bf16[1024,256]{1,0:T(8,128)(2,1)}, u32[]{:S(2)}, u32[]{:S(2)}) collective-permute-start(bf16[1024,256]{1,0:T(8,128)(2,1)} %collective-permute-done.15.refs_5_), channel_id=1, source_target_pairs={{0,2},{1,3},{4,0},{5,1},{8,4},{9,5},{12,8},{13,9},{14,12},{15,13},... | collective-permute-start | bytes 1572872 | tf_op jit(solution)/shard_map/ppermute | solution.py:164
  83.6 15.3 %collective-permute-start.23 = (bf16[1024,256]{1,0:T(8,128)(2,1)}, bf16[1024,256]{1,0:T(8,128)(2,1)}, u32[]{:S(2)}, u32[]{:S(2)}) collective-permute-start(bf16[1024,256]{1,0:T(8,128)(2,1)} %collective-permute-done.17.refs_1_), channel_id=1, source_target_pairs={{0,4},{1,5},{4,8},{5,9},{8,12},{9,13},{12,14},{13,15},{14,10},{15,... | collective-permute-start | bytes 1572872 | tf_op jit(solution)/shard_map/ppermute | solution.py:167
  84.0 14.8 %collective-permute-start.24 = (bf16[1024,256]{1,0:T(8,128)(2,1)}, bf16[1024,256]{1,0:T(8,128)(2,1)}, u32[]{:S(2)}, u32[]{:S(2)}) collective-permute-start(bf16[1024,256]{1,0:T(8,128)(2,1)} %collective-permute-done.2.refs_0_), channel_id=1, source_target_pairs={{0,16},{16,0},{1,17},{17,1},{2,18},{18,2},{3,19},{19,3},{4,20},{20... | collective-permute-start | bytes 1572872 | tf_op jit(solution)/shard_map/ppermute | solution.py:170
  84.5 14.3 %collective-permute-start.25 = (bf16[1024,256]{1,0:T(8,128)(2,1)}, bf16[1024,256]{1,0:T(8,128)(2,1)}, u32[]{:S(2)}, u32[]{:S(2)}) collective-permute-start(bf16[1024,256]{1,0:T(8,128)(2,1)} %collective-permute-done.16.refs_8_), channel_id=1, source_target_pairs={{0,1},{1,0},{2,3},{3,2},{4,5},{5,4},{6,7},{7,6},{8,9},{9,8},{10,11... | collective-permute-start | bytes 1572872 | tf_op jit(solution)/shard_map/ppermute | solution.py:173
  119.3 13.0 %all-to-all-start = ((bf16[16,2,2112]{2,1,0:T(2,128)(2,1)}), bf16[16,2,2112]{2,1,0:T(2,128)(2,1)S(1)}, u32[]{:S(2)}, u32[]{:S(2)}) async-start(bf16[16,2,2112]{2,1,0:T(2,128)(2,1)} %reshape.292), calls=%async_computation | async-start | bytes 278528 | tf_op jit(solution)/shard_map/all_to_all | solution.py:270
  (50 other events, 411.9 us)

commit v5 on v1

--- a/solution.py
+++ b/solution.py
@@ -1,15 +1,478 @@
+import functools
 import math
 
 import jax
 import jax.numpy as jnp
 from jax import lax
+from jax.experimental import pallas as pl
+from jax.experimental.pallas import tpu as pltpu
 from jax.sharding import PartitionSpec as P
 
 QB = 256
 LANES = 128
-
-
-def per_device(context, residual, out_proj, norm_gain, lengths, queries, pattern):
+CORES = 2
+STEP = 256
+VMEM_BYTES = 20 << 20
+LOW = -1e30
+CYCLE = (0, 2, 4, 6, 7, 5, 3, 1)
+WAVES = (((0,), ()), ((1,), ()), ((2,), (-1, -3)), ((-2, 3), (4,)))
+LATE = (-1, -3, 4)
+
+
+def column_block(distance, same_core):
+    me = lax.axis_index("dp")
+    core = lax.rem(me, CORES)
+    chip = lax.div(me, CORES)
+    z, y = lax.div(chip, 2), lax.rem(chip, 2)
+    size = len(CYCLE)
+    at = jnp.where(y == 0, z, size - 1 - z)
+    there = lax.rem(at + (distance + size), size)
+    chip = jnp.where(there < size // 2, 2 * there, 2 * (size - 1 - there) + 1)
+    return chip * CORES + (core if same_core else 1 - core)
+
+
+def columns(distance, same_core, width):
+    return pl.ds(pl.multiple_of(column_block(distance, same_core) * width, width), width)
+
+
+def half_rows(second, half):
+    side = lax.axis_index("groups")
+    return pl.ds(pl.multiple_of((1 - side if second else side) * half, half), half)
+
+
+def copy_in(copies, source, target, sems):
+    copies.append(pltpu.make_async_copy(source, target, sems.at[len(copies)]))
+    copies[-1].start()
+    return copies[-1]
+
+
+def add_squares(squares, at, total):
+    square = total * total
+    for lane in range(0, total.shape[1], LANES):
+        squares[at, :] += square[:, lane : lane + LANES]
+
+
+def half_kernel(whole, part, sem):
+    copy = pltpu.make_async_copy(whole.at[half_rows(False, part.shape[0])], part, sem)
+    copy.start()
+    copy.wait()
+
+
+def own_half(whole):
+    rows, width = whole.shape
+    return pl.pallas_call(
+        half_kernel,
+        out_shape=jax.ShapeDtypeStruct((rows // 2, width), whole.dtype),
+        in_specs=[pl.BlockSpec(memory_space=pl.ANY)],
+        out_specs=pl.BlockSpec(memory_space=pl.ANY),
+        scratch_shapes=[pltpu.SemaphoreType.DMA],
+        compiler_params=pltpu.CompilerParams(vmem_limit_bytes=VMEM_BYTES),
+    )(whole)
+
+
+def wave_kernel(full, part, arrived, whole, context, other_context, residual, *refs):
+    count = len(full) + len(part)
+    n_pieces = 1 if whole else 2 * len(full) + len(part)
+    pieces, refs = refs[:n_pieces], refs[n_pieces:]
+    n_given = 2 if arrived else 0
+    given, refs = refs[:n_given], refs[n_given:]
+    mine, theirs, refs = refs[0], refs[1], refs[2:]
+    if arrived:
+        finished, refs = refs[0], refs[1:]
+    squares, both, weights, extra = refs[:4]
+    sems = refs[-1]
+    half, width = weights.shape[2:]
+    rows = context.shape[0]
+    copies = []
+    for who, tokens in enumerate((context, other_context)):
+        for part_of in range(2):
+            source = tokens.at[:, half_rows(part_of, half)]
+            copy_in(copies, source, both.at[who, part_of], sems)
+    at = 0
+    for j in range(count):
+        for part_of in range(2 if j < len(full) else 1):
+            if whole:
+                source = pieces[0].at[half_rows(part_of, half)]
+            else:
+                source = pieces[at]
+                at += 1
+            copy_in(copies, source, weights.at[j, part_of], sems)
+    for j, distance in enumerate(full + part):
+        copy_in(copies, residual.at[:, columns(distance, True, width)], extra.at[j], sems)
+    if arrived:
+        landed = refs[4]
+        for j, distance in enumerate(arrived):
+            copy_in(copies, given[0].at[j], landed.at[j], sems)
+            copy_in(copies, residual.at[:, columns(distance, False, width)], extra.at[count + j], sems)
+        squares[...] = given[1][...]
+    else:
+        squares[...] = jnp.zeros_like(squares)
+    for copy in copies:
+        copy.wait()
+    if arrived:
+        for j in range(len(arrived)):
+
+            @pl.loop(0, rows // STEP)
+            def _(k):
+                at = pl.ds(pl.multiple_of(k * STEP, STEP), STEP)
+                total = landed[j, at, :] + extra[count + j, at, :].astype(jnp.float32)
+                finished[j, at, :] = total
+                add_squares(squares, at, total)
+
+    for j in range(count):
+
+        @pl.loop(0, rows // STEP)
+        def _(k):
+            at = pl.ds(pl.multiple_of(k * STEP, STEP), STEP)
+
+            def product(who):
+                total = jnp.dot(both[who, 0, at, :], weights[j, 0], preferred_element_type=jnp.float32)
+                if j < len(full):
+                    total += jnp.dot(both[who, 1, at, :], weights[j, 1], preferred_element_type=jnp.float32)
+                return total
+
+            theirs[j, at, :] = product(1)
+            total = product(0) + extra[j, at, :].astype(jnp.float32)
+            mine[j, at, :] = total
+            if j < len(full):
+                add_squares(squares, at, total)
+
+
+def wave(full, part, arrived, context, other_context, residual, pieces, received=None, squares=None):
+    count, done = len(full) + len(part), len(arrived)
+    rows = context.shape[0]
+    whole = len(pieces) == 1
+    half, width = pieces[0].shape
+    half = half // 2 if whole else half
+    given = [received, squares] if arrived else []
+    blocks = jax.ShapeDtypeStruct((count, rows, width), jnp.float32)
+    outs = [blocks, blocks]
+    scratch = [
+        pltpu.VMEM((2, 2, rows, half), jnp.bfloat16),
+        pltpu.VMEM((count, 2, half, width), jnp.bfloat16),
+        pltpu.VMEM((count + done, rows, width), jnp.bfloat16),
+    ]
+    if arrived:
+        outs.append(jax.ShapeDtypeStruct((done, rows, width), jnp.float32))
+        scratch.append(pltpu.VMEM((done, rows, width), jnp.float32))
+    outs.append(jax.ShapeDtypeStruct((rows, LANES), jnp.float32))
+    scratch.append(pltpu.SemaphoreType.DMA((4 + 3 * count + 2 * done,)))
+    out = pl.pallas_call(
+        functools.partial(wave_kernel, full, part, arrived, whole),
+        out_shape=outs,
+        in_specs=[pl.BlockSpec(memory_space=pl.ANY)] * (3 + len(pieces))
+        + ([pl.BlockSpec(memory_space=pl.ANY), pl.BlockSpec(memory_space=pltpu.VMEM)] if arrived else []),
+        out_specs=[pl.BlockSpec(memory_space=pltpu.VMEM)] * len(outs),
+        scratch_shapes=scratch,
+        compiler_params=pltpu.CompilerParams(vmem_limit_bytes=VMEM_BYTES),
+        cost_estimate=pl.CostEstimate(
+            flops=4 * rows * half * width * (2 * len(full) + len(part)),
+            bytes_accessed=8 * rows * half + count * width * (4 * half + 10 * rows),
+            transcendentals=0,
+        ),
+    )(context, other_context, residual, *pieces, *given)
+    if arrived:
+        return out
+    return out[0], out[1], None, out[2]
+
+
+def final_kernel(sources, late, plain, length, context, residual, squares, gain, flags, *refs):
+    n_late = len(late)
+    arrays = 1 + max(source for source, _, _, _ in sources)
+    pieces, refs = refs[:n_late], refs[n_late:]
+    hidden, refs = refs[:arrays], refs[arrays:]
+    embedded, payload, second, weights, extra, blocks, scale_rows, sheet, sems = refs
+    half, width = weights.shape[1:]
+    rows = context.shape[0]
+    total = len(sources)
+    features = total * width
+    copies = []
+    first = [copy_in(copies, context.at[:, half_rows(True, half)], second, sems)]
+    late_copies = []
+    for i, slot in enumerate(late):
+        source, entry, distance, same = sources[slot]
+        needed = [
+            copy_in(copies, pieces[i], weights.at[i], sems),
+            copy_in(copies, hidden[source].at[entry], blocks.at[slot], sems),
+        ]
+        if not same:
+            needed.append(copy_in(copies, residual.at[:, columns(distance, same, width)], extra.at[i], sems))
+        late_copies.append(needed)
+    plain_copies = []
+    for i, slot in enumerate(plain):
+        source, entry, distance, same = sources[slot]
+        plain_copies.append(
+            [
+                copy_in(copies, hidden[source].at[entry], blocks.at[slot], sems),
+                copy_in(copies, residual.at[:, columns(distance, same, width)], extra.at[n_late + i], sems),
+            ]
+        )
+    rest = [slot for slot in range(total) if slot not in late + plain]
+    rest_copies = [
+        copy_in(copies, hidden[sources[slot][0]].at[sources[slot][1]], blocks.at[slot], sems) for slot in rest
+    ]
+    for copy in first:
+        copy.wait()
+    for i, slot in enumerate(late):
+        for copy in late_copies[i]:
+            copy.wait()
+        same = sources[slot][3]
+
+        @pl.loop(0, rows // STEP)
+        def _(k):
+            at = pl.ds(pl.multiple_of(k * STEP, STEP), STEP)
+            value = jnp.dot(second[at, :], weights[i], preferred_element_type=jnp.float32)
+            value += blocks[slot, at, :]
+            if not same:
+                value += extra[i, at, :].astype(jnp.float32)
+            blocks[slot, at, :] = value
+            add_squares(squares, at, value)
+
+    for i, slot in enumerate(plain):
+        for copy in plain_copies[i]:
+            copy.wait()
+
+        @pl.loop(0, rows // STEP)
+        def _(k):
+            at = pl.ds(pl.multiple_of(k * STEP, STEP), STEP)
+            value = blocks[slot, at, :] + extra[n_late + i, at, :].astype(jnp.float32)
+            blocks[slot, at, :] = value
+            add_squares(squares, at, value)
+
+    mean = jnp.sum(squares[...], axis=1, keepdims=True) * (1.0 / features)
+    row = lax.broadcasted_iota(jnp.int32, mean.shape, 0)
+    scale = jnp.where(row < length[0], lax.rsqrt(mean + 1e-05), 0.0)
+    scale_rows[...] = jnp.broadcast_to(scale, scale_rows.shape)
+    for copy in rest_copies:
+        copy.wait()
+    inverse = 1.0 / jnp.full((1, width), length[0], jnp.int32).astype(jnp.float32)
+    for slot, (_, _, distance, same) in enumerate(sources):
+        parts = [
+            jnp.sum(blocks[slot, :, lane : lane + LANES] * scale_rows[...], axis=0, keepdims=True)
+            for lane in range(0, width, LANES)
+        ]
+        where = columns(distance, same, width)
+        embedded[:, where] = jnp.concatenate(parts, axis=1) * gain[:, where] * inverse
+    pooled = embedded[...]
+    mean = jnp.sum(pooled * pooled, axis=1, keepdims=True) * (1.0 / features)
+    embedded[...] = pooled * lax.rsqrt(mean + 1e-06)
+    lines = features // LANES
+    sheet[lines:, :] = jnp.zeros((sheet.shape[0] - lines, LANES), jnp.float32)
+    for line in range(lines):
+        sheet[line : line + 1, :] = embedded[:, line * LANES : (line + 1) * LANES]
+    sheet[lines : lines + 1, :] = flags[...]
+    rounded = sheet[...].astype(jnp.bfloat16)
+    for rank in range(payload.shape[0]):
+        payload[rank] = rounded
+
+
+def finish(sources, late, plain, lengths, context, residual, squares, gain, flags, pieces, hidden, ranks):
+    rows = context.shape[0]
+    half, width = pieces[0].shape
+    total = len(sources)
+    features = total * width
+    lines = -(-(features // LANES + 1) // 16) * 16
+    return pl.pallas_call(
+        functools.partial(final_kernel, sources, late, plain),
+        out_shape=(
+            jax.ShapeDtypeStruct((1, features), jnp.float32),
+            jax.ShapeDtypeStruct((ranks, lines, LANES), jnp.bfloat16),
+        ),
+        in_specs=[pl.BlockSpec(memory_space=pltpu.SMEM)]
+        + [pl.BlockSpec(memory_space=pl.ANY)] * 2
+        + [pl.BlockSpec(memory_space=pltpu.VMEM)] * 3
+        + [pl.BlockSpec(memory_space=pl.ANY)] * (len(pieces) + len(hidden)),
+        out_specs=(pl.BlockSpec(memory_space=pltpu.VMEM), pl.BlockSpec(memory_space=pltpu.VMEM)),
+        scratch_shapes=[
+            pltpu.VMEM((rows, half), jnp.bfloat16),
+            pltpu.VMEM((len(late), half, width), jnp.bfloat16),
+            pltpu.VMEM((len(late) + len(plain), rows, width), jnp.bfloat16),
+            pltpu.VMEM((total, rows, width), jnp.float32),
+            pltpu.VMEM((rows, LANES), jnp.float32),
+            pltpu.VMEM((lines, LANES), jnp.float32),
+            pltpu.SemaphoreType.DMA((1 + total + 2 * len(late) + len(plain),)),
+        ],
+        compiler_params=pltpu.CompilerParams(vmem_limit_bytes=VMEM_BYTES),
+    )(lengths, context, residual, squares, gain, flags, *pieces, *hidden)
+
+
+def score_kernel(lines, blocks, got, queries, other_queries, out, wide, emb, mix):
+    me = lax.axis_index("dp")
+    ranks = got.shape[0]
+    count = queries.shape[0]
+    wide[...] = got[...].astype(jnp.float32)
+    for line in range(lines):
+        emb[:, line * LANES : (line + 1) * LANES] = wide[:, line, :]
+    half = emb[...].astype(jnp.bfloat16)
+    flags = wide[:, lines, :].astype(jnp.bfloat16)
+    temper = 1.0 / (0.02 * math.sqrt(lines * LANES))
+    scores, masks = [], []
+    for owner, rows in ((me, queries), (me + 1 - 2 * lax.rem(me, CORES), other_queries)):
+        score = lax.dot_general(
+            half, rows[...], (((1,), (1,)), ((), ())), preferred_element_type=jnp.float32
+        )
+        scores.append(score * temper)
+        block = lax.broadcasted_iota(jnp.int32, (LANES, count), 0)
+        row = owner * count + lax.broadcasted_iota(jnp.int32, (LANES, count), 1)
+        pick = (row >= block * QB) & (row < block * QB + QB) & (block < blocks)
+        pick = jnp.where(pick, 1.0, 0.0).astype(jnp.bfloat16)
+        masks.append(jnp.dot(flags, pick, preferred_element_type=jnp.float32) > 0.5)
+    peaks = [
+        jnp.max(jnp.where(mask, score, LOW), axis=1, keepdims=True) for score, mask in zip(scores, masks)
+    ]
+    peak = jnp.maximum(*peaks)
+    weights = [jnp.where(mask, jnp.exp(score - peak), 0.0) for score, mask in zip(scores, masks)]
+    total = sum(jnp.sum(weight, axis=1, keepdims=True) for weight in weights)
+    mix[...] = jnp.dot(
+        weights[0].astype(jnp.bfloat16), queries[...], preferred_element_type=jnp.float32
+    ) + jnp.dot(weights[1].astype(jnp.bfloat16), other_queries[...], preferred_element_type=jnp.float32)
+    for line in range(lines):
+        out[:, line, :] = mix[:, line * LANES : (line + 1) * LANES]
+    lane = lax.broadcasted_iota(jnp.int32, (ranks, LANES), 1)
+    out[:, lines, :] = jnp.where(lane == 0, peak, jnp.where(lane == 1, total, 0.0))
+    for line in range(lines + 1, out.shape[1]):
+        out[:, line, :] = jnp.zeros((ranks, LANES), jnp.float32)
+
+
+def score(got, queries, other_queries, blocks):
+    ranks = got.shape[0]
+    features = queries.shape[1]
+    lines = features // LANES
+    return pl.pallas_call(
+        functools.partial(score_kernel, lines, blocks),
+        out_shape=jax.ShapeDtypeStruct((ranks, -(-(lines + 1) // 8) * 8, LANES), jnp.float32),
+        in_specs=[pl.BlockSpec(memory_space=pltpu.VMEM)] * 3,
+        out_specs=pl.BlockSpec(memory_space=pltpu.VMEM),
+        scratch_shapes=[
+            pltpu.VMEM(got.shape, jnp.float32),
+            pltpu.VMEM((ranks, features), jnp.float32),
+            pltpu.VMEM((ranks, features), jnp.float32),
+        ],
+        compiler_params=pltpu.CompilerParams(vmem_limit_bytes=VMEM_BYTES),
+    )(got, queries, other_queries)
+
+
+def combine_kernel(lines, got, recalled, log_total):
+    stats = got[:, lines, :]
+    peaks, sums = stats[:, 0:1], stats[:, 1:2]
+    peak = jnp.max(peaks, axis=0, keepdims=True)
+    factor = jnp.exp(peaks - peak)
+    total = jnp.sum(sums * factor, axis=0, keepdims=True)
+    mix = got[0, :lines, :] * factor[0:1, :]
+    for rank in range(1, got.shape[0]):
+        mix += got[rank, :lines, :] * factor[rank : rank + 1, :]
+    mix = mix / total
+    for line in range(lines):
+        recalled[:, line * LANES : (line + 1) * LANES] = mix[line : line + 1, :]
+    log_total[...] = peak + jnp.log(total)
+
+
+def combine(got, features):
+    recalled, log_total = pl.pallas_call(
+        functools.partial(combine_kernel, features // LANES),
+        out_shape=(
+            jax.ShapeDtypeStruct((1, features), jnp.float32),
+            jax.ShapeDtypeStruct((1, 1), jnp.float32),
+        ),
+        in_specs=[pl.BlockSpec(memory_space=pltpu.VMEM)],
+        out_specs=(pl.BlockSpec(memory_space=pltpu.VMEM), pl.BlockSpec(memory_space=pltpu.VMEM)),
+        compiler_params=pltpu.CompilerParams(vmem_limit_bytes=VMEM_BYTES),
+    )(got)
+    return recalled, log_total.reshape(1)
+
+
+def on_cycle(context, residual, out_proj, norm_gain, lengths, queries, pattern):
+    ranks = lax.axis_size("dp")
+    size = ranks // CORES
+    features = residual.shape[1]
+
+    def ring(step):
+        return [
+            (CYCLE[r] * CORES + c, CYCLE[(r + step) % size] * CORES + c)
+            for r in range(size)
+            for c in range(CORES)
+        ]
+
+    def from_next(piece):
+        return lax.ppermute(piece, "dp", ring(-1))
+
+    def from_last(piece):
+        return lax.ppermute(piece, "dp", ring(1))
+
+    def over_x(piece):
+        return lax.ppermute(piece, "groups", [(0, 1), (1, 0)])
+
+    def other_core(piece):
+        return lax.ppermute(piece, "dp", [(i, i ^ 1) for i in range(ranks)])
+
+    wait = lax.optimization_barrier
+    own = own_half(out_proj)
+    n1, l1, context2 = wait((from_next(own), from_last(own), other_core(context)))
+
+    def run(i, pieces, arrived=(), received=None, squares=None):
+        full, part = WAVES[i]
+        return wave(full, part, arrived, context, context2, residual, pieces, received, squares)
+
+    h0, t0, _, sq0 = run(0, [out_proj])
+    n2, l2, xn1, queries2, t0, sq0 = wait(
+        (from_next(n1), from_last(l1), over_x(n1), other_core(queries), t0, sq0)
+    )
+    h1, t1, f0, sq1 = run(1, [n1, xn1], (0,), other_core(t0), sq0)
+    n3, l3, xn2, t1, sq1 = wait((from_next(n2), from_last(l2), over_x(n2), t1, sq1))
+    h2, t2, f1, sq2 = run(2, [n2, xn2, l1, l3], (1,), other_core(t1), sq1)
+    n3x, l4, xl2, t2, sq2 = wait((from_next(xn2), from_last(l3), over_x(l2), t2, sq2))
+    r2 = other_core(t2)
+    h3, t3, f2, sq3 = run(3, [l2, xl2, n3, n3x, l4], (2,), r2, sq2)
+    n4x, l3x, xl1, t3, sq3 = wait((from_next(n3x), from_last(xl2), over_x(l1), t3, sq3))
+    late = [xl1, l3x, n4x]
+    late += [other_core(piece) for piece in late]
+    r3 = other_core(t3)
+
+    hidden = [h0, h1, h2, h3, f0, f1, f2, r2, r3]
+    sources = (
+        (2, 1, -1, True),
+        (2, 2, -3, True),
+        (3, 2, 4, True),
+        (7, 1, -1, False),
+        (7, 2, -3, False),
+        (8, 2, 4, False),
+        (8, 0, -2, False),
+        (8, 1, 3, False),
+        (0, 0, 0, True),
+        (1, 0, 1, True),
+        (2, 0, 2, True),
+        (3, 0, -2, True),
+        (3, 1, 3, True),
+        (4, 0, 0, False),
+        (5, 0, 1, False),
+        (6, 0, 2, False),
+    )
+    flags = jnp.pad(pattern.astype(jnp.float32), ((0, 0), (0, LANES - pattern.shape[1])))
+    embedded, payload = finish(
+        sources,
+        (0, 1, 2, 3, 4, 5),
+        (6, 7),
+        lengths,
+        context,
+        residual,
+        sq3,
+        norm_gain.reshape(1, -1),
+        flags,
+        late,
+        hidden,
+        size,
+    )
+    same_core = [list(range(c, ranks, CORES)) for c in range(CORES)]
+
+    def spread(blocks):
+        return lax.all_to_all(blocks, "dp", 0, 0, axis_index_groups=same_core, tiled=True)
+
+    parts = score(spread(payload), queries, queries2, pattern.shape[1])
+    recalled, log_total = combine(spread(parts), features)
+    return embedded, recalled, log_total
+
+
+def gathered(context, residual, out_proj, norm_gain, lengths, queries, pattern):
     tok_rows = context.shape[0]
     features = residual.shape[1]
     passages_here = lengths.shape[0]
@@ -45,8 +508,7 @@
     row_block = (me * query_rows + jnp.arange(query_rows)) // QB
     picks = (row_block[None, :] == jnp.arange(blocks)[:, None]).astype(jnp.float32)
     cand_mask = jnp.dot(flags_all, picks) > 0
-    low = jnp.float32(-1e30)
-    peak_part = jnp.max(jnp.where(cand_mask, scores, low), axis=1, keepdims=True)
+    peak_part = jnp.max(jnp.where(cand_mask, scores, LOW), axis=1, keepdims=True)
     weights = jnp.where(cand_mask, jnp.exp(scores - peak_part), 0.0)
     total_part = jnp.sum(weights, axis=1, keepdims=True)
     mix_part = jnp.dot(weights.astype(jnp.bfloat16), queries, preferred_element_type=jnp.float32)
@@ -65,6 +527,20 @@
     return (embedded, recalled, log_total)
 
 
+def per_device(context, residual, out_proj, norm_gain, lengths, queries, pattern):
+    fits = (
+        lax.axis_size("dp") == CORES * len(CYCLE)
+        and lax.axis_size("groups") == 2
+        and lengths.shape[0] == 1
+        and out_proj.shape[1] % LANES == 0
+        and out_proj.shape[0] % (2 * LANES) == 0
+        and context.shape[0] % STEP == 0
+        and pattern.shape[1] <= LANES
+    )
+    form = on_cycle if fits else gathered
+    return form(context, residual, out_proj, norm_gain, lengths, queries, pattern)
+
+
 def solution(mesh):
     in_specs = (
         P(("groups", "dp"), None),

time: 207 us -> 117 us (0.57)
  waiting for transfers between devices: 135 us -> 49.9 us
  Pallas kernels: 0 us -> 22.8 us
  starting transfers between devices: 0.04 us -> 17.6 us
  between operations: 18 us -> 1.39 us
  matrix products: 14.2 us -> 0 us
  blocking collectives: 32.7 us -> 19.8 us
  other arithmetic: 7.23 us -> 0.01 us
  local copies, waits for them, and re-layouts: 0.33 us -> 5.03 us
    all_gather x1 -> x0, waiting for transfers between devices: 134 us -> none  [per_device(): lax.all_gather(out_proj, 'dp', axis=1, tiled=True)]
    ppermute x0 -> x23, waiting for transfers between devices: none -> 49.9 us  [the longest x5 25.8 us: from_next(): return lax.ppermute(piece, 'dp', ring(-1))]
    pallas_call x0 -> x8, Pallas kernels: none -> 22.8 us  [the longest x4 14 us: wave(): pl.pallas_call(functools.partial(wave_kernel, full, part, arrived, whole)...]
    all_gather x1 -> x0, blocking collectives: 20 us -> none  [per_device(): lax.all_gather(jnp.concatenate([emb_half, flags], axis=1), 'dp', axis=0,...]
    ppermute x0 -> x23, starting transfers between devices: none -> 17.6 us  [the longest x5 8.89 us: from_next(): return lax.ppermute(piece, 'dp', ring(-1))]
    dot_general x4 -> x0, matrix products: 14.2 us -> none  [the longest x1 13.3 us: per_device(): jnp.dot(context, lax.all_gather(out_proj, 'dp', axis=1, tiled=True), pref...]
    all_to_all x1 -> x2, blocking collectives: 12.8 us -> 19.8 us  [spread(): lax.all_to_all(blocks, 'dp', 0, 0, axis_index_groups=same_core, tiled=True)]
    unnamed x9 -> x16, local copies, waits for them, and re-layouts: 0.05 us -> 5.02 us
  transfers between devices with their start and end apart: 1 -> 23, of which waited for: 1 -> 18; matrix products, arithmetic and copies ran while one was open for 0% -> 0% of each run, Pallas kernels for 0% -> 12%
where the time goes in v5:
time: 117 us
  waiting for transfers between devices  49.9 us (43%)
  Pallas kernels  22.8 us (19%)
  blocking collectives  19.8 us (17%)
  starting transfers between devices  17.6 us (15%)
  local copies, waits for them, and re-layouts  5.03 us (4%)
  between operations  1.39 us (1%)
    ppermute x5, waiting for transfers between devices, from_next(): return lax.ppermute(piece, 'dp', ring(-1))  25.8 us
    all_to_all x2, blocking collectives, spread(): lax.all_to_all(blocks, 'dp', 0, 0, axis_index_groups=same_core, tiled=True)  19.8 us
    pallas_call x4, Pallas kernels, wave(): pl.pallas_call(functools.partial(wave_kernel, full, part, arrived, whole)...  14 us
    ppermute x4, waiting for transfers between devices, over_x(): return lax.ppermute(piece, 'groups', [(0, 1), (1, 0)])  12.8 us
    ppermute x5, starting transfers between devices, from_next(): return lax.ppermute(piece, 'dp', ring(-1))  8.89 us
    pallas_call x1, Pallas kernels, finish(): pl.pallas_call(functools.partial(final_kernel, sources, late, plain), out...  6.94 us
    ppermute x5, waiting for transfers between devices, from_last(): return lax.ppermute(piece, 'dp', ring(1))  6.59 us
    ppermute x4, starting transfers between devices, over_x(): return lax.ppermute(piece, 'groups', [(0, 1), (1, 0)])  5.07 us
  transfers between devices with their start and end apart: 23, of which 18 were waited for; matrix products, arithmetic and copies ran while one was open for 0% of the time, Pallas kernels for 12%

profile of v5, /device:TPU:0, one launch (start us, length us, event | category | flops | bytes accessed | tf_op | source)
XLA Modules:
  0.0 116.5 jit_solution(4337602209159847424)
XLA Ops:
  2.4 2.6 %collective-permute-start = (bf16[1024,256]{1,0:T(8,128)(2,1)S(1)}, bf16[1024,256]{1,0:T(8,128)(2,1)S(1)}, u32[]{:S(2)}, u32[]{:S(2)}) collective-permute-start(bf16[1024,256]{1,0:T(8,128)(2,1)S(1)} %shard_map.94), channel_id=1, source_target_pairs={{0,2},{1,3},{4,0},{5,1},{8,4},{9,5},{12,8},{13,9},{14,12},{15,13},... | collective-permute-start | bytes 1572872 | tf_op jit(solution)/shard_map/ppermute | solution.py:397
  5.4 12.3 %collective-permute-done.refs_0_ = bf16[1024,256]{1,0:T(8,128)(2,1)S(1)} collective-permute-done((bf16[1024,256]{1,0:T(8,128)(2,1)S(1)}, bf16[1024,256]{1,0:T(8,128)(2,1)S(1)}, u32[]{:S(2)}, u32[]{:S(2)}) %collective-permute-start) | collective-permute-done | bytes 524320 | tf_op jit(solution)/shard_map/ppermute | solution.py:397
  17.7 1.4 %collective-permute-done.1.refs_2_ = bf16[1024,256]{1,0:T(8,128)(2,1)S(1)} collective-permute-done((bf16[1024,256]{1,0:T(8,128)(2,1)S(1)}, bf16[1024,256]{1,0:T(8,128)(2,1)S(1)}, u32[]{:S(2)}, u32[]{:S(2)}) %collective-permute-start.1) | collective-permute-done | bytes 524320 | tf_op jit(solution)/shard_map/ppermute | solution.py:400
  19.1 1.6 %collective-permute-start.3 = (bf16[1024,256]{1,0:T(8,128)(2,1)S(1)}, bf16[1024,256]{1,0:T(8,128)(2,1)S(1)}, u32[]{:S(2)}, u32[]{:S(2)}) collective-permute-start(bf16[1024,256]{1,0:T(8,128)(2,1)S(1)} %collective-permute-done.refs_0_), channel_id=1, source_target_pairs={{0,2},{1,3},{4,0},{5,1},{8,4},{9,5},{12,8},{13,9},{14,12},{15,13},... | collective-permute-start | bytes 1572872 | tf_op jit(solution)/shard_map/ppermute | solution.py:397
  21.1 1.5 %collective-permute-start.5 = (bf16[1024,256]{1,0:T(8,128)(2,1)S(1)}, bf16[1024,256]{1,0:T(8,128)(2,1)S(1)}, u32[]{:S(2)}, u32[]{:S(2)}) collective-permute-start(bf16[1024,256]{1,0:T(8,128)(2,1)S(1)} %collective-permute-done.refs_0_), channel_id=1, source_target_pairs={{0,16},{16,0},{1,17},{17,1},{2,18},{18,2},{3,19},{19,3},{4,20},{20... | collective-permute-start | bytes 1572872 | tf_op jit(solution)/shard_map/ppermute | solution.py:403
  22.6 2.2 %copy-done = bf16[512,4096]{1,0:T(8,128)(2,1)S(1)} copy-done((bf16[512,4096]{1,0:T(8,128)(2,1)S(1)}, bf16[512,4096]{1,0:T(8,128)(2,1)}, u32[]{:S(2)}) %copy-start) | copy-done | bytes 4194328
  24.8 1.6 %copy-done.2 = bf16[512,2048]{1,0:T(8,128)(2,1)S(1)} copy-done((bf16[512,2048]{1,0:T(8,128)(2,1)S(1)}, bf16[512,2048]{1,0:T(8,128)(2,1)}, u32[]{:S(2)}) %copy-start.2) | copy-done | bytes 2097176
  26.4 2.3 %shard_map.95 = (f32[1,512,256]{2,1,0:T(8,128)S(1)}, f32[1,512,256]{2,1,0:T(8,128)S(1)}, f32[512,128]{1,0:T(8,128)S(1)}) custom-call(bf16[512,2048]{1,0:T(8,128)(2,1)S(1)} %copy-done.2, bf16[512,2048]{1,0:T(8,128)(2,1)S(1)} %collective-permute-done.2.other_context, bf16[512,4096]{1,0:T(8,128)(2,1)S(1)} %copy-done, bf16[2048,256]{1,0:T(8,128)(2,1)S(1)} %copy-done.4), custom_call_target="tpu_custom_call" | custom-call | flops 1073741824 | bytes 6553600 | tf_op jit(solution)/shard_map/pallas_call | solution.py:160
  28.7 3.6 %collective-permute-done.3.refs_0_ = bf16[1024,256]{1,0:T(8,128)(2,1)S(1)} collective-permute-done((bf16[1024,256]{1,0:T(8,128)(2,1)S(1)}, bf16[1024,256]{1,0:T(8,128)(2,1)S(1)}, u32[]{:S(2)}, u32[]{:S(2)}) %collective-permute-start.3) | collective-permute-done | bytes 524320 | tf_op jit(solution)/shard_map/ppermute | solution.py:397
  33.8 1.6 %collective-permute-start.7 = (bf16[1024,256]{1,0:T(8,128)(2,1)S(1)}, bf16[1024,256]{1,0:T(8,128)(2,1)S(1)}, u32[]{:S(2)}, u32[]{:S(2)}) collective-permute-start(bf16[1024,256]{1,0:T(8,128)(2,1)S(1)} %collective-permute-done.3.refs_0_), channel_id=1, source_target_pairs={{0,2},{1,3},{4,0},{5,1},{8,4},{9,5},{12,8},{13,9},{14,12},{15,13},... | collective-permute-start | bytes 1572872 | tf_op jit(solution)/shard_map/ppermute | solution.py:397
  35.8 1.5 %collective-permute-start.9 = (bf16[1024,256]{1,0:T(8,128)(2,1)S(1)}, bf16[1024,256]{1,0:T(8,128)(2,1)S(1)}, u32[]{:S(2)}, u32[]{:S(2)}) collective-permute-start(bf16[1024,256]{1,0:T(8,128)(2,1)S(1)} %collective-permute-done.3.refs_0_), channel_id=1, source_target_pairs={{0,16},{16,0},{1,17},{17,1},{2,18},{18,2},{3,19},{19,3},{4,20},{20... | collective-permute-start | bytes 1572872 | tf_op jit(solution)/shard_map/ppermute | solution.py:403
  37.3 2.4 %shard_map.96 = (f32[1,512,256]{2,1,0:T(8,128)S(1)}, f32[1,512,256]{2,1,0:T(8,128)S(1)}, f32[1,512,256]{2,1,0:T(8,128)S(1)}, f32[512,128]{1,0:T(8,128)S(1)}) custom-call(bf16[512,2048]{1,0:T(8,128)(2,1)S(1)} %copy-done.3, bf16[512,2048]{1,0:T(8,128)(2,1)S(1)} %collective-permute-done.2.other_context, bf16[512,4096]{1,0:T(8,128)(2,1)S(1)} %copy-done.1, ...), custom_call_target="tpu_custom_call" | custom-call | flops 1073741824 | bytes 6553600 | tf_op jit(solution)/shard_map/pallas_call | solution.py:160
  39.7 8.4 %collective-permute-done.7.refs_2_ = bf16[1024,256]{1,0:T(8,128)(2,1)S(1)} collective-permute-done((bf16[1024,256]{1,0:T(8,128)(2,1)S(1)}, bf16[1024,256]{1,0:T(8,128)(2,1)S(1)}, u32[]{:S(2)}, u32[]{:S(2)}) %collective-permute-start.7) | collective-permute-done | bytes 524320 | tf_op jit(solution)/shard_map/ppermute | solution.py:397
  49.6 1.5 %collective-permute-start.13 = (bf16[1024,256]{1,0:T(8,128)(2,1)S(1)}, bf16[1024,256]{1,0:T(8,128)(2,1)S(1)}, u32[]{:S(2)}, u32[]{:S(2)}) collective-permute-start(bf16[1024,256]{1,0:T(8,128)(2,1)S(1)} %collective-permute-done.4.refs_0_), channel_id=1, source_target_pairs={{0,16},{16,0},{1,17},{17,1},{2,18},{18,2},{3,19},{19,3},{4,20},{20... | collective-permute-start | bytes 1572872 | tf_op jit(solution)/shard_map/ppermute | solution.py:403
  51.1 1.6 %collective-permute-start.11 = (bf16[1024,256]{1,0:T(8,128)(2,1)S(1)}, bf16[1024,256]{1,0:T(8,128)(2,1)S(1)}, u32[]{:S(2)}, u32[]{:S(2)}) collective-permute-start(bf16[1024,256]{1,0:T(8,128)(2,1)S(1)} %collective-permute-done.9.refs_1_), channel_id=1, source_target_pairs={{0,2},{1,3},{4,0},{5,1},{8,4},{9,5},{12,8},{13,9},{14,12},{15,13},... | collective-permute-start | bytes 1572872 | tf_op jit(solution)/shard_map/ppermute | solution.py:397
  53.1 4.4 %shard_map.97 = (f32[3,512,256]{2,1,0:T(8,128)S(1)}, f32[3,512,256]{2,1,0:T(8,128)S(1)}, f32[1,512,256]{2,1,0:T(8,128)S(1)}, f32[512,128]{1,0:T(8,128)S(1)}) custom-call(bf16[512,2048]{1,0:T(8,128)(2,1)S(1)} %copy-done.3, bf16[512,2048]{1,0:T(8,128)(2,1)S(1)} %collective-permute-done.2.other_context, bf16[512,4096]{1,0:T(8,128)(2,1)S(1)} %copy-done.1, ...), custom_call_target="tpu_custom_call" | custom-call | flops 2147483648 | bytes 11272192 | tf_op jit(solution)/shard_map/pallas_call | solution.py:160
  57.5 6.4 %collective-permute-done.13.refs_1_ = bf16[1024,256]{1,0:T(8,128)(2,1)S(1)} collective-permute-done((bf16[1024,256]{1,0:T(8,128)(2,1)S(1)}, bf16[1024,256]{1,0:T(8,128)(2,1)S(1)}, u32[]{:S(2)}, u32[]{:S(2)}) %collective-permute-start.13) | collective-permute-done | bytes 524320 | tf_op jit(solution)/shard_map/ppermute | solution.py:403
  67.0 1.6 %collective-permute-start.15 = (bf16[1024,256]{1,0:T(8,128)(2,1)S(1)}, bf16[1024,256]{1,0:T(8,128)(2,1)S(1)}, u32[]{:S(2)}, u32[]{:S(2)}) collective-permute-start(bf16[1024,256]{1,0:T(8,128)(2,1)S(1)} %collective-permute-done.11.refs_3_), channel_id=1, source_target_pairs={{0,2},{1,3},{4,0},{5,1},{8,4},{9,5},{12,8},{13,9},{14,12},{15,13},... | collective-permute-start | bytes 1572872 | tf_op jit(solution)/shard_map/ppermute | solution.py:397
  69.8 4.9 %shard_map.98 = (f32[3,512,256]{2,1,0:T(8,128)S(1)}, f32[3,512,256]{2,1,0:T(8,128)S(1)}, f32[1,512,256]{2,1,0:T(8,128)S(1)}, f32[512,128]{1,0:T(8,128)S(1)}) custom-call(bf16[512,2048]{1,0:T(8,128)(2,1)S(1)} %copy-done.3, bf16[512,2048]{1,0:T(8,128)(2,1)S(1)} %collective-permute-done.2.other_context, bf16[512,4096]{1,0:T(8,128)(2,1)S(1)} %copy-done.1, ...), custom_call_target="tpu_custom_call" | custom-call | flops 2684354560 | bytes 11272192 | tf_op jit(solution)/shard_map/pallas_call | solution.py:160
  74.8 6.0 %collective-permute-done.17.refs_0_ = bf16[1024,256]{1,0:T(8,128)(2,1)S(1)} collective-permute-done((bf16[1024,256]{1,0:T(8,128)(2,1)S(1)}, bf16[1024,256]{1,0:T(8,128)(2,1)S(1)}, u32[]{:S(2)}, u32[]{:S(2)}) %collective-permute-start.17) | collective-permute-done | bytes 524320 | tf_op jit(solution)/shard_map/ppermute | solution.py:403
  84.0 2.5 %collective-permute-done.19.refs_3_ = bf16[1024,256]{1,0:T(8,128)(2,1)S(1)} collective-permute-done((bf16[1024,256]{1,0:T(8,128)(2,1)S(1)}, bf16[1024,256]{1,0:T(8,128)(2,1)S(1)}, u32[]{:S(2)}, u32[]{:S(2)}) %collective-permute-start.19) | collective-permute-done | bytes 524320 | tf_op jit(solution)/shard_map/ppermute | solution.py:406
  88.0 6.9 %shard_map.99 = (f32[1,4096]{1,0:T(1,128)}, bf16[8,48,128]{2,1,0:T(8,128)(2,1)S(1)}) custom-call(s32[1]{0:T(128)S(6)} %copy.10.length, bf16[512,2048]{1,0:T(8,128)(2,1)S(1)} %copy-done.3, bf16[512,4096]{1,0:T(8,128)(2,1)S(1)} %copy-done.1, f32[512,128]{1,0:T(8,128)S(1)} %get-tuple-element.72.squares, f32[1,4096]{1,0:T(1,128)S(1)} %bitcast.2, ...), custom_call_target="tpu_custom_call" | custom-call | tf_op jit(solution)/shard_map/pallas_call | solution.py:275
  94.9 9.8 %all_to_all.10.got = bf16[8,48,128]{2,1,0:T(8,128)(2,1)S(1)} all-to-all(bf16[8,48,128]{2,1,0:T(8,128)(2,1)S(1)} %get-tuple-element.85), channel_id=1, replica_groups={{0,2,4,6,8,10,12,14},{1,3,5,7,9,11,13,15},{16,18,20,22,24,26,28,30},{17..., dimensions={0} | all-to-all | bytes 196608 | tf_op jit(solution)/shard_map/all_to_all | solution.py:468
  105.8 10.0 %all_to_all.11.got = f32[8,40,128]{2,1,0:T(8,128)S(1)} all-to-all(f32[8,40,128]{2,1,0:T(8,128)S(1)} %shard_map.100), channel_id=1, replica_groups={{0,2,4,6,8,10,12,14},{1,3,5,7,9,11,13,15},{16,18,20,22,24,26,28,30},{17..., dimensions={0} | all-to-all | bytes 327680 | tf_op jit(solution)/shard_map/all_to_all | solution.py:468
  (50 shorter events, 16.7 us)
Async XLA Ops:
  0.6 18.4 %collective-permute-start.2 = (bf16[512,2048]{1,0:T(8,128)(2,1)}, bf16[512,2048]{1,0:T(8,128)(2,1)S(1)}, u32[]{:S(2)}, u32[]{:S(2)}) collective-permute-start(bf16[512,2048]{1,0:T(8,128)(2,1)} %context.9), channel_id=1, source_target_pairs={{0,1},{1,0},{2,3},{3,2},{4,5},{5,4},{6,7},{7,6},{8,9},{9,8},{10,11... | collective-permute-start | bytes 6291464 | tf_op jit(solution)/shard_map/ppermute | solution.py:406
  2.4 15.2 %collective-permute-start = (bf16[1024,256]{1,0:T(8,128)(2,1)S(1)}, bf16[1024,256]{1,0:T(8,128)(2,1)S(1)}, u32[]{:S(2)}, u32[]{:S(2)}) collective-permute-start(bf16[1024,256]{1,0:T(8,128)(2,1)S(1)} %shard_map.94), channel_id=1, source_target_pairs={{0,2},{1,3},{4,0},{5,1},{8,4},{9,5},{12,8},{13,9},{14,12},{15,13},... | collective-permute-start | bytes 1572872 | tf_op jit(solution)/shard_map/ppermute | solution.py:397
  5.0 14.0 %collective-permute-start.1 = (bf16[1024,256]{1,0:T(8,128)(2,1)S(1)}, bf16[1024,256]{1,0:T(8,128)(2,1)S(1)}, u32[]{:S(2)}, u32[]{:S(2)}) collective-permute-start(bf16[1024,256]{1,0:T(8,128)(2,1)S(1)} %shard_map.94), channel_id=1, source_target_pairs={{0,4},{1,5},{4,8},{5,9},{8,12},{9,13},{12,14},{13,15},{14,10},{15,... | collective-permute-start | bytes 1572872 | tf_op jit(solution)/shard_map/ppermute | solution.py:400
  5.1 23.5 %collective-permute-start.6 = (bf16[112,4096]{1,0:T(8,128)(2,1)S(1)}, bf16[112,4096]{1,0:T(8,128)(2,1)S(1)}, u32[]{:S(2)}, u32[]{:S(2)}) collective-permute-start(bf16[112,4096]{1,0:T(8,128)(2,1)S(1)} %copy-done.5), channel_id=1, source_target_pairs={{0,1},{1,0},{2,3},{3,2},{4,5},{5,4},{6,7},{7,6},{8,9},{9,8},{10,11... | collective-permute-start | bytes 2752520 | tf_op jit(solution)/shard_map/ppermute | solution.py:406
  19.1 13.2 %collective-permute-start.3 = (bf16[1024,256]{1,0:T(8,128)(2,1)S(1)}, bf16[1024,256]{1,0:T(8,128)(2,1)S(1)}, u32[]{:S(2)}, u32[]{:S(2)}) collective-permute-start(bf16[1024,256]{1,0:T(8,128)(2,1)S(1)} %collective-permute-done.refs_0_), channel_id=1, source_target_pairs={{0,2},{1,3},{4,0},{5,1},{8,4},{9,5},{12,8},{13,9},{14,12},{15,13},... | collective-permute-start | bytes 1572872 | tf_op jit(solution)/shard_map/ppermute | solution.py:397
  20.6 12.9 %collective-permute-start.4 = (bf16[1024,256]{1,0:T(8,128)(2,1)S(1)}, bf16[1024,256]{1,0:T(8,128)(2,1)S(1)}, u32[]{:S(2)}, u32[]{:S(2)}) collective-permute-start(bf16[1024,256]{1,0:T(8,128)(2,1)S(1)} %collective-permute-done.1.refs_2_), channel_id=1, source_target_pairs={{0,4},{1,5},{4,8},{5,9},{8,12},{9,13},{12,14},{13,15},{14,10},{15,... | collective-permute-start | bytes 1572872 | tf_op jit(solution)/shard_map/ppermute | solution.py:400
  21.1 12.7 %collective-permute-start.5 = (bf16[1024,256]{1,0:T(8,128)(2,1)S(1)}, bf16[1024,256]{1,0:T(8,128)(2,1)S(1)}, u32[]{:S(2)}, u32[]{:S(2)}) collective-permute-start(bf16[1024,256]{1,0:T(8,128)(2,1)S(1)} %collective-permute-done.refs_0_), channel_id=1, source_target_pairs={{0,16},{16,0},{1,17},{17,1},{2,18},{18,2},{3,19},{19,3},{4,20},{20... | collective-permute-start | bytes 1572872 | tf_op jit(solution)/shard_map/ppermute | solution.py:403
  33.8 3.5 %collective-permute-start.10 = (f32[1,512,256]{2,1,0:T(8,128)S(1)}, f32[1,512,256]{2,1,0:T(8,128)S(1)}, u32[]{:S(2)}, u32[]{:S(2)}) collective-permute-start(f32[1,512,256]{2,1,0:T(8,128)S(1)} %get-tuple-element.54), channel_id=1, source_target_pairs={{0,1},{1,0},{2,3},{3,2},{4,5},{5,4},{6,7},{7,6},{8,9},{9,8},{10,11... | collective-permute-start | bytes 1572872 | tf_op jit(solution)/shard_map/ppermute | solution.py:406
  33.8 14.3 %collective-permute-start.7 = (bf16[1024,256]{1,0:T(8,128)(2,1)S(1)}, bf16[1024,256]{1,0:T(8,128)(2,1)S(1)}, u32[]{:S(2)}, u32[]{:S(2)}) collective-permute-start(bf16[1024,256]{1,0:T(8,128)(2,1)S(1)} %collective-permute-done.3.refs_0_), channel_id=1, source_target_pairs={{0,2},{1,3},{4,0},{5,1},{8,4},{9,5},{12,8},{13,9},{14,12},{15,13},... | collective-permute-start | bytes 1572872 | tf_op jit(solution)/shard_map/ppermute | solution.py:397
  35.3 14.1 %collective-permute-start.8 = (bf16[1024,256]{1,0:T(8,128)(2,1)S(1)}, bf16[1024,256]{1,0:T(8,128)(2,1)S(1)}, u32[]{:S(2)}, u32[]{:S(2)}) collective-permute-start(bf16[1024,256]{1,0:T(8,128)(2,1)S(1)} %collective-permute-done.4.refs_0_), channel_id=1, source_target_pairs={{0,4},{1,5},{4,8},{5,9},{8,12},{9,13},{12,14},{13,15},{14,10},{15,... | collective-permute-start | bytes 1572872 | tf_op jit(solution)/shard_map/ppermute | solution.py:400
  35.8 13.8 %collective-permute-start.9 = (bf16[1024,256]{1,0:T(8,128)(2,1)S(1)}, bf16[1024,256]{1,0:T(8,128)(2,1)S(1)}, u32[]{:S(2)}, u32[]{:S(2)}) collective-permute-start(bf16[1024,256]{1,0:T(8,128)(2,1)S(1)} %collective-permute-done.3.refs_0_), channel_id=1, source_target_pairs={{0,16},{16,0},{1,17},{17,1},{2,18},{18,2},{3,19},{19,3},{4,20},{20... | collective-permute-start | bytes 1572872 | tf_op jit(solution)/shard_map/ppermute | solution.py:403
  49.6 3.5 %collective-permute-start.14 = (f32[1,512,256]{2,1,0:T(8,128)S(1)}, f32[1,512,256]{2,1,0:T(8,128)S(1)}, u32[]{:S(2)}, u32[]{:S(2)}) collective-permute-start(f32[1,512,256]{2,1,0:T(8,128)S(1)} %get-tuple-element.60), channel_id=1, source_target_pairs={{0,1},{1,0},{2,3},{3,2},{4,5},{5,4},{6,7},{7,6},{8,9},{9,8},{10,11... | collective-permute-start | bytes 1572872 | tf_op jit(solution)/shard_map/ppermute | solution.py:406
  49.6 14.3 %collective-permute-start.13 = (bf16[1024,256]{1,0:T(8,128)(2,1)S(1)}, bf16[1024,256]{1,0:T(8,128)(2,1)S(1)}, u32[]{:S(2)}, u32[]{:S(2)}) collective-permute-start(bf16[1024,256]{1,0:T(8,128)(2,1)S(1)} %collective-permute-done.4.refs_0_), channel_id=1, source_target_pairs={{0,16},{16,0},{1,17},{17,1},{2,18},{18,2},{3,19},{19,3},{4,20},{20... | collective-permute-start | bytes 1572872 | tf_op jit(solution)/shard_map/ppermute | solution.py:403
  51.1 14.1 %collective-permute-start.11 = (bf16[1024,256]{1,0:T(8,128)(2,1)S(1)}, bf16[1024,256]{1,0:T(8,128)(2,1)S(1)}, u32[]{:S(2)}, u32[]{:S(2)}) collective-permute-start(bf16[1024,256]{1,0:T(8,128)(2,1)S(1)} %collective-permute-done.9.refs_1_), channel_id=1, source_target_pairs={{0,2},{1,3},{4,0},{5,1},{8,4},{9,5},{12,8},{13,9},{14,12},{15,13},... | collective-permute-start | bytes 1572872 | tf_op jit(solution)/shard_map/ppermute | solution.py:397
  52.6 13.8 %collective-permute-start.12 = (bf16[1024,256]{1,0:T(8,128)(2,1)S(1)}, bf16[1024,256]{1,0:T(8,128)(2,1)S(1)}, u32[]{:S(2)}, u32[]{:S(2)}) collective-permute-start(bf16[1024,256]{1,0:T(8,128)(2,1)S(1)} %collective-permute-done.8.refs_3_), channel_id=1, source_target_pairs={{0,4},{1,5},{4,8},{5,9},{8,12},{9,13},{12,14},{13,15},{14,10},{15,... | collective-permute-start | bytes 1572872 | tf_op jit(solution)/shard_map/ppermute | solution.py:400
  66.4 21.6 %copy-start.6 = (f32[4096]{0:T(1024)S(1)}, f32[4096]{0:T(1024)}, u32[]{:S(2)}) copy-start(f32[4096]{0:T(1024)} %param.10) | copy-start | bytes 49156
  66.4 3.4 %collective-permute-start.18 = (f32[3,512,256]{2,1,0:T(8,128)S(1)}, f32[3,512,256]{2,1,0:T(8,128)S(1)}, u32[]{:S(2)}, u32[]{:S(2)}) collective-permute-start(f32[3,512,256]{2,1,0:T(8,128)S(1)} %get-tuple-element.68), channel_id=1, source_target_pairs={{0,1},{1,0},{2,3},{3,2},{4,5},{5,4},{6,7},{7,6},{8,9},{9,8},{10,11... | collective-permute-start | bytes 4718600 | tf_op jit(solution)/shard_map/ppermute | solution.py:406
  66.4 14.3 %collective-permute-start.17 = (bf16[1024,256]{1,0:T(8,128)(2,1)S(1)}, bf16[1024,256]{1,0:T(8,128)(2,1)S(1)}, u32[]{:S(2)}, u32[]{:S(2)}) collective-permute-start(bf16[1024,256]{1,0:T(8,128)(2,1)S(1)} %collective-permute-done.1.refs_2_), channel_id=1, source_target_pairs={{0,16},{16,0},{1,17},{17,1},{2,18},{18,2},{3,19},{19,3},{4,20},{20... | collective-permute-start | bytes 1572872 | tf_op jit(solution)/shard_map/ppermute | solution.py:403
  67.0 14.0 %collective-permute-start.15 = (bf16[1024,256]{1,0:T(8,128)(2,1)S(1)}, bf16[1024,256]{1,0:T(8,128)(2,1)S(1)}, u32[]{:S(2)}, u32[]{:S(2)}) collective-permute-start(bf16[1024,256]{1,0:T(8,128)(2,1)S(1)} %collective-permute-done.11.refs_3_), channel_id=1, source_target_pairs={{0,2},{1,3},{4,0},{5,1},{8,4},{9,5},{12,8},{13,9},{14,12},{15,13},... | collective-permute-start | bytes 1572872 | tf_op jit(solution)/shard_map/ppermute | solution.py:397
  68.6 13.7 %collective-permute-start.16 = (bf16[1024,256]{1,0:T(8,128)(2,1)S(1)}, bf16[1024,256]{1,0:T(8,128)(2,1)S(1)}, u32[]{:S(2)}, u32[]{:S(2)}) collective-permute-start(bf16[1024,256]{1,0:T(8,128)(2,1)S(1)} %collective-permute-done.13.refs_1_), channel_id=1, source_target_pairs={{0,4},{1,5},{4,8},{5,9},{8,12},{9,13},{12,14},{13,15},{14,10},{15,... | collective-permute-start | bytes 1572872 | tf_op jit(solution)/shard_map/ppermute | solution.py:400
  82.3 5.7 %collective-permute-start.22 = (f32[3,512,256]{2,1,0:T(8,128)S(1)}, f32[3,512,256]{2,1,0:T(8,128)S(1)}, u32[]{:S(2)}, u32[]{:S(2)}) collective-permute-start(f32[3,512,256]{2,1,0:T(8,128)S(1)} %get-tuple-element.83), channel_id=1, source_target_pairs={{0,1},{1,0},{2,3},{3,2},{4,5},{5,4},{6,7},{7,6},{8,9},{9,8},{10,11... | collective-permute-start | bytes 4718600 | tf_op jit(solution)/shard_map/ppermute | solution.py:406
  82.3 4.2 %collective-permute-start.19 = (bf16[1024,256]{1,0:T(8,128)(2,1)S(1)}, bf16[1024,256]{1,0:T(8,128)(2,1)S(1)}, u32[]{:S(2)}, u32[]{:S(2)}) collective-permute-start(bf16[1024,256]{1,0:T(8,128)(2,1)S(1)} %collective-permute-done.17.refs_0_), channel_id=1, source_target_pairs={{0,1},{1,0},{2,3},{3,2},{4,5},{5,4},{6,7},{7,6},{8,9},{9,8},{10,11... | collective-permute-start | bytes 1572872 | tf_op jit(solution)/shard_map/ppermute | solution.py:406
  82.8 4.4 %collective-permute-start.20 = (bf16[1024,256]{1,0:T(8,128)(2,1)S(1)}, bf16[1024,256]{1,0:T(8,128)(2,1)S(1)}, u32[]{:S(2)}, u32[]{:S(2)}) collective-permute-start(bf16[1024,256]{1,0:T(8,128)(2,1)S(1)} %collective-permute-done.16.refs_1_), channel_id=1, source_target_pairs={{0,1},{1,0},{2,3},{3,2},{4,5},{5,4},{6,7},{7,6},{8,9},{9,8},{10,11... | collective-permute-start | bytes 1572872 | tf_op jit(solution)/shard_map/ppermute | solution.py:406
  82.8 5.1 %collective-permute-start.21 = (bf16[1024,256]{1,0:T(8,128)(2,1)S(1)}, bf16[1024,256]{1,0:T(8,128)(2,1)S(1)}, u32[]{:S(2)}, u32[]{:S(2)}) collective-permute-start(bf16[1024,256]{1,0:T(8,128)(2,1)S(1)} %collective-permute-done.15.refs_2_), channel_id=1, source_target_pairs={{0,1},{1,0},{2,3},{3,2},{4,5},{5,4},{6,7},{7,6},{8,9},{9,8},{10,11... | collective-permute-start | bytes 1572872 | tf_op jit(solution)/shard_map/ppermute | solution.py:406
  (7 other events, 46.5 us)

commit v6 on v5

--- a/solution.py
+++ b/solution.py
@@ -13,6 +13,7 @@
 CORES = 2
 STEP = 256
 VMEM_BYTES = 20 << 20
+FULL_VMEM_BYTES = 60 << 20
 LOW = -1e30
 CYCLE = (0, 2, 4, 6, 7, 5, 3, 1)
 WAVES = (((0,), ()), ((1,), ()), ((2,), (-1, -3)), ((-2, 3), (4,)))
@@ -26,9 +27,10 @@
     z, y = lax.div(chip, 2), lax.rem(chip, 2)
     size = len(CYCLE)
     at = jnp.where(y == 0, z, size - 1 - z)
-    there = lax.rem(at + (distance + size), size)
+    core = core if same_core else 1 - core
+    there = lax.rem(at + jnp.where(core == 0, size + distance, size - distance), size)
     chip = jnp.where(there < size // 2, 2 * there, 2 * (size - 1 - there) + 1)
-    return chip * CORES + (core if same_core else 1 - core)
+    return chip * CORES + core
 
 
 def columns(distance, same_core, width):
@@ -66,7 +68,7 @@
         in_specs=[pl.BlockSpec(memory_space=pl.ANY)],
         out_specs=pl.BlockSpec(memory_space=pl.ANY),
         scratch_shapes=[pltpu.SemaphoreType.DMA],
-        compiler_params=pltpu.CompilerParams(vmem_limit_bytes=VMEM_BYTES),
+        compiler_params=pltpu.CompilerParams(vmem_limit_bytes=FULL_VMEM_BYTES),
     )(whole)
 
 
@@ -176,6 +178,64 @@
     return out[0], out[1], None, out[2]
 
 
+def late_kernel(entries, context, given, *refs):
+    count = len(entries)
+    pieces, parts = refs[:count], refs[count : 2 * count]
+    finished, squares, second, weights, landed, sems = refs[2 * count :]
+    half, width = weights.shape[1:]
+    rows = context.shape[0]
+    copies = []
+    first = copy_in(copies, context.at[:, half_rows(True, half)], second, sems)
+    needed = [
+        (
+            copy_in(copies, pieces[i], weights.at[i], sems),
+            copy_in(copies, parts[i].at[entries[i]], landed.at[i], sems),
+        )
+        for i in range(count)
+    ]
+    squares[...] = given[...]
+    first.wait()
+    for i in range(count):
+        for copy in needed[i]:
+            copy.wait()
+
+        @pl.loop(0, rows // STEP)
+        def _(k):
+            at = pl.ds(pl.multiple_of(k * STEP, STEP), STEP)
+            value = jnp.dot(second[at, :], weights[i], preferred_element_type=jnp.float32)
+            value += landed[i, at, :]
+            finished[i, at, :] = value
+            add_squares(squares, at, value)
+
+
+def late_half(context, squares, pieces, parts, entries):
+    count = len(pieces)
+    rows = context.shape[0]
+    half, width = pieces[0].shape
+    return pl.pallas_call(
+        functools.partial(late_kernel, entries),
+        out_shape=(
+            jax.ShapeDtypeStruct((count, rows, width), jnp.float32),
+            jax.ShapeDtypeStruct(squares.shape, jnp.float32),
+        ),
+        in_specs=[pl.BlockSpec(memory_space=pl.ANY), pl.BlockSpec(memory_space=pltpu.VMEM)]
+        + [pl.BlockSpec(memory_space=pl.ANY)] * (2 * count),
+        out_specs=(pl.BlockSpec(memory_space=pltpu.VMEM), pl.BlockSpec(memory_space=pltpu.VMEM)),
+        scratch_shapes=[
+            pltpu.VMEM((rows, half), jnp.bfloat16),
+            pltpu.VMEM((count, half, width), jnp.bfloat16),
+            pltpu.VMEM((count, rows, width), jnp.float32),
+            pltpu.SemaphoreType.DMA((1 + 2 * count,)),
+        ],
+        compiler_params=pltpu.CompilerParams(vmem_limit_bytes=VMEM_BYTES),
+        cost_estimate=pl.CostEstimate(
+            flops=2 * rows * half * width * count,
+            bytes_accessed=2 * rows * half + count * width * (2 * half + 8 * rows),
+            transcendentals=0,
+        ),
+    )(context, squares, *pieces, *parts)
+
+
 def final_kernel(sources, late, plain, length, context, residual, squares, gain, flags, *refs):
     n_late = len(late)
     arrays = 1 + max(source for source, _, _, _ in sources)
@@ -191,13 +251,13 @@
     late_copies = []
     for i, slot in enumerate(late):
         source, entry, distance, same = sources[slot]
-        needed = [
-            copy_in(copies, pieces[i], weights.at[i], sems),
-            copy_in(copies, hidden[source].at[entry], blocks.at[slot], sems),
-        ]
-        if not same:
-            needed.append(copy_in(copies, residual.at[:, columns(distance, same, width)], extra.at[i], sems))
-        late_copies.append(needed)
+        late_copies.append(
+            [
+                copy_in(copies, pieces[i], weights.at[i], sems),
+                copy_in(copies, hidden[source].at[entry], blocks.at[slot], sems),
+                copy_in(copies, residual.at[:, columns(distance, same, width)], extra.at[i], sems),
+            ]
+        )
     plain_copies = []
     for i, slot in enumerate(plain):
         source, entry, distance, same = sources[slot]
@@ -216,15 +276,12 @@
     for i, slot in enumerate(late):
         for copy in late_copies[i]:
             copy.wait()
-        same = sources[slot][3]
 
         @pl.loop(0, rows // STEP)
         def _(k):
             at = pl.ds(pl.multiple_of(k * STEP, STEP), STEP)
             value = jnp.dot(second[at, :], weights[i], preferred_element_type=jnp.float32)
-            value += blocks[slot, at, :]
-            if not same:
-                value += extra[i, at, :].astype(jnp.float32)
+            value += blocks[slot, at, :] + extra[i, at, :].astype(jnp.float32)
             blocks[slot, at, :] = value
             add_squares(squares, at, value)
 
@@ -388,7 +445,7 @@
 
     def ring(step):
         return [
-            (CYCLE[r] * CORES + c, CYCLE[(r + step) % size] * CORES + c)
+            (CYCLE[r] * CORES + c, CYCLE[(r + step * (1 - 2 * c)) % size] * CORES + c)
             for r in range(size)
             for c in range(CORES)
         ]
@@ -406,56 +463,80 @@
         return lax.ppermute(piece, "dp", [(i, i ^ 1) for i in range(ranks)])
 
     wait = lax.optimization_barrier
-    own = own_half(out_proj)
-    n1, l1, context2 = wait((from_next(own), from_last(own), other_core(context)))
 
     def run(i, pieces, arrived=(), received=None, squares=None):
         full, part = WAVES[i]
         return wave(full, part, arrived, context, context2, residual, pieces, received, squares)
 
+    own = own_half(out_proj)
+    a, b, c = from_next(own), from_last(own), other_core(context)
+    n1 = wait(a)
+    a = from_next(n1)
+    l1, n1 = wait((b, n1))
+    b = from_last(l1)
+    x = over_x(n1)
+    context2, l1 = wait((c, l1))
+    c = other_core(queries)
     h0, t0, _, sq0 = run(0, [out_proj])
-    n2, l2, xn1, queries2, t0, sq0 = wait(
-        (from_next(n1), from_last(l1), over_x(n1), other_core(queries), t0, sq0)
-    )
-    h1, t1, f0, sq1 = run(1, [n1, xn1], (0,), other_core(t0), sq0)
-    n3, l3, xn2, t1, sq1 = wait((from_next(n2), from_last(l2), over_x(n2), t1, sq1))
-    h2, t2, f1, sq2 = run(2, [n2, xn2, l1, l3], (1,), other_core(t1), sq1)
-    n3x, l4, xl2, t2, sq2 = wait((from_next(xn2), from_last(l3), over_x(l2), t2, sq2))
+
+    n2, t0, sq0, queries2 = wait((a, t0, sq0, c))
+    a = from_next(n2)
+    r0 = other_core(t0)
+    l2, n2 = wait((b, n2))
+    b = from_last(l2)
+    xn1, n2, l2 = wait((x, n2, l2))
+    x = over_x(n2)
+    h1, t1, f0, sq1 = run(1, [n1, xn1], (0,), r0, sq0)
+
+    n3, t1, sq1 = wait((a, t1, sq1))
+    r1 = other_core(t1)
+    l3, n3 = wait((b, n3))
+    b = from_last(l3)
+    xn2, n3, l3, l2 = wait((x, n3, l3, l2))
+    a = from_next(xn2)
+    x = over_x(l2)
+    h2, t2, f1, sq2 = run(2, [n2, xn2, l1, l3], (1,), r1, sq1)
+
+    n3x, l4, xl2, t2, sq2 = wait((a, b, x, t2, sq2))
+    a = from_next(n3x)
     r2 = other_core(t2)
+    b = from_last(xl2)
+    x = over_x(l1)
     h3, t3, f2, sq3 = run(3, [l2, xl2, n3, n3x, l4], (2,), r2, sq2)
-    n4x, l3x, xl1, t3, sq3 = wait((from_next(n3x), from_last(xl2), over_x(l1), t3, sq3))
-    late = [xl1, l3x, n4x]
-    late += [other_core(piece) for piece in late]
+    n4x, l3x, xl1, t3, sq3 = wait((a, b, x, t3, sq3))
+    last = [xl1, l3x, n4x]
+    late = [other_core(piece) for piece in last]
     r3 = other_core(t3)
-
-    hidden = [h0, h1, h2, h3, f0, f1, f2, r2, r3]
+    h4, sq4 = late_half(context, sq3, last, [h2, h2, h3], (1, 2, 2))
+
+    hidden = [h0, h1, h2, h3, h4, f0, f1, f2, r2, r3]
     sources = (
-        (2, 1, -1, True),
-        (2, 2, -3, True),
-        (3, 2, 4, True),
-        (7, 1, -1, False),
-        (7, 2, -3, False),
-        (8, 2, 4, False),
-        (8, 0, -2, False),
-        (8, 1, 3, False),
+        (8, 1, -1, False),
+        (8, 2, -3, False),
+        (9, 2, 4, False),
+        (9, 0, -2, False),
+        (9, 1, 3, False),
         (0, 0, 0, True),
         (1, 0, 1, True),
         (2, 0, 2, True),
         (3, 0, -2, True),
         (3, 1, 3, True),
-        (4, 0, 0, False),
-        (5, 0, 1, False),
-        (6, 0, 2, False),
+        (4, 0, -1, True),
+        (4, 1, -3, True),
+        (4, 2, 4, True),
+        (5, 0, 0, False),
+        (6, 0, 1, False),
+        (7, 0, 2, False),
     )
     flags = jnp.pad(pattern.astype(jnp.float32), ((0, 0), (0, LANES - pattern.shape[1])))
     embedded, payload = finish(
         sources,
-        (0, 1, 2, 3, 4, 5),
-        (6, 7),
+        (0, 1, 2),
+        (3, 4),
         lengths,
         context,
         residual,
-        sq3,
+        sq4,
         norm_gain.reshape(1, -1),
         flags,
         late,

time: 117 us -> 129 us (1.10)
  Pallas kernels: 22.8 us -> 40.6 us
  waiting for transfers between devices: 49.9 us -> 39.1 us
  starting transfers between devices: 17.6 us -> 21.8 us
  blocking collectives: 19.8 us -> 21.6 us
    pallas_call x1, Pallas kernels: 0.05 us -> 17 us  [own_half(): pl.pallas_call(half_kernel, out_shape=jax.ShapeDtypeStruct((rows // 2, wi...]
    ppermute x5, waiting for transfers between devices: 6.59 us -> 0.55 us  [from_last(): return lax.ppermute(piece, 'dp', ring(1))]
    ppermute x4, waiting for transfers between devices: 12.8 us -> 7.21 us  [over_x(): return lax.ppermute(piece, 'groups', [(0, 1), (1, 0)])]
    ppermute x5, waiting for transfers between devices: 25.8 us -> 29.7 us  [from_next(): return lax.ppermute(piece, 'dp', ring(-1))]
    ppermute x9, waiting for transfers between devices: 4.76 us -> 1.66 us  [other_core(): return lax.ppermute(piece, 'dp', [(i, i ^ 1) for i in range(ranks)])]
    ppermute x5, starting transfers between devices: 1.92 us -> 4.74 us  [from_last(): return lax.ppermute(piece, 'dp', ring(1))]
    pallas_call x0 -> x1, Pallas kernels: none -> 2.3 us  [late_half(): pl.pallas_call(functools.partial(late_kernel, entries), out_shape=(jax.Sh...]
    pallas_call x1, Pallas kernels: 6.94 us -> 4.93 us  [finish(): pl.pallas_call(functools.partial(final_kernel, sources, late, plain), out...]
  transfers between devices with their start and end apart: 23 -> 23, of which waited for: 18 -> 12; matrix products, arithmetic and copies ran while one was open for 0% -> 0% of each run, Pallas kernels for 12% -> 26%
where the time goes in v6:
time: 129 us; the launch traced here: 128 us
  Pallas kernels  40.6 us (31%)
  waiting for transfers between devices  39.1 us (30%)
  starting transfers between devices  21.8 us (17%)
  blocking collectives  21.6 us (17%)
  local copies, waits for them, and re-layouts  3.81 us (3%)
  between operations  1.41 us (1%)
    ppermute x5, waiting for transfers between devices, from_next(): return lax.ppermute(piece, 'dp', ring(-1))  29.7 us
    all_to_all x2, blocking collectives, spread(): lax.all_to_all(blocks, 'dp', 0, 0, axis_index_groups=same_core, tiled=True)  21.6 us
    pallas_call x1, Pallas kernels, own_half(): pl.pallas_call(half_kernel, out_shape=jax.ShapeDtypeStruct((rows // 2, wi...  17 us
    pallas_call x4, Pallas kernels, wave(): pl.pallas_call(functools.partial(wave_kernel, full, part, arrived, whole)...  14.5 us
    ppermute x5, starting transfers between devices, from_next(): return lax.ppermute(piece, 'dp', ring(-1))  8.68 us
    ppermute x4, waiting for transfers between devices, over_x(): return lax.ppermute(piece, 'groups', [(0, 1), (1, 0)])  7.21 us
    ppermute x4, starting transfers between devices, over_x(): return lax.ppermute(piece, 'groups', [(0, 1), (1, 0)])  6.25 us
    pallas_call x1, Pallas kernels, finish(): pl.pallas_call(functools.partial(final_kernel, sources, late, plain), out...  4.93 us
  transfers between devices with their start and end apart: 23, of which 12 were waited for; matrix products, arithmetic and copies ran while one was open for 0% of the time, Pallas kernels for 26%

profile of v6, /device:TPU:0, one launch (start us, length us, event | category | flops | bytes accessed | tf_op | source)
XLA Modules:
  0.0 128.4 jit_solution(1974686657272743859)
XLA Ops:
  1.2 17.0 %shard_map.94 = bf16[1024,256]{1,0:T(8,128)(2,1)} custom-call(bf16[2048,256]{1,0:T(8,128)(2,1)} %refs_0_.1), custom_call_target="tpu_custom_call" | custom-call | tf_op jit(solution)/shard_map/pallas_call | solution.py:65
  18.2 2.6 %collective-permute-start.1 = (bf16[1024,256]{1,0:T(8,128)(2,1)}, bf16[1024,256]{1,0:T(8,128)(2,1)S(1)}, u32[]{:S(2)}, u32[]{:S(2)}) collective-permute-start(bf16[1024,256]{1,0:T(8,128)(2,1)} %shard_map.94), channel_id=1, source_target_pairs={{0,2},{1,5},{4,0},{5,9},{8,4},{9,13},{12,8},{13,15},{14,12},{15,11... | collective-permute-start | bytes 1572872 | tf_op jit(solution)/shard_map/ppermute | solution.py:454
  22.6 9.7 %collective-permute-done.1.refs_0_ = bf16[1024,256]{1,0:T(8,128)(2,1)S(1)} collective-permute-done((bf16[1024,256]{1,0:T(8,128)(2,1)}, bf16[1024,256]{1,0:T(8,128)(2,1)S(1)}, u32[]{:S(2)}, u32[]{:S(2)}) %collective-permute-start.1) | collective-permute-done | bytes 524320 | tf_op jit(solution)/shard_map/ppermute | solution.py:454
  32.2 2.4 %collective-permute-start.4 = (bf16[1024,256]{1,0:T(8,128)(2,1)S(1)}, bf16[1024,256]{1,0:T(8,128)(2,1)S(1)}, u32[]{:S(2)}, u32[]{:S(2)}) collective-permute-start(bf16[1024,256]{1,0:T(8,128)(2,1)S(1)} %collective-permute-done.1.refs_0_), channel_id=1, source_target_pairs={{0,2},{1,5},{4,0},{5,9},{8,4},{9,13},{12,8},{13,15},{14,12},{15,11... | collective-permute-start | bytes 1572872 | tf_op jit(solution)/shard_map/ppermute | solution.py:454
  36.8 2.2 %copy-done = bf16[512,4096]{1,0:T(8,128)(2,1)S(1)} copy-done((bf16[512,4096]{1,0:T(8,128)(2,1)S(1)}, bf16[512,4096]{1,0:T(8,128)(2,1)}, u32[]{:S(2)}) %copy-start) | copy-done | bytes 4194328
  39.0 1.6 %copy-done.2 = bf16[512,2048]{1,0:T(8,128)(2,1)S(1)} copy-done((bf16[512,2048]{1,0:T(8,128)(2,1)S(1)}, bf16[512,2048]{1,0:T(8,128)(2,1)}, u32[]{:S(2)}) %copy-start.2) | copy-done | bytes 2097176
  40.6 2.4 %shard_map.95 = (f32[1,512,256]{2,1,0:T(8,128)S(1)}, f32[1,512,256]{2,1,0:T(8,128)S(1)}, f32[512,128]{1,0:T(8,128)S(1)}) custom-call(bf16[512,2048]{1,0:T(8,128)(2,1)S(1)} %copy-done.2, bf16[512,2048]{1,0:T(8,128)(2,1)S(1)} %collective-permute-done.5.other_context, bf16[512,4096]{1,0:T(8,128)(2,1)S(1)} %copy-done, bf16[2048,256]{1,0:T(8,128)(2,1)S(1)} %copy-done.4), custom_call_target="tpu_custom_call" | custom-call | flops 1073741824 | bytes 6553600 | tf_op jit(solution)/shard_map/pallas_call | solution.py:162
  43.0 4.7 %collective-permute-done.4.refs_0_ = bf16[1024,256]{1,0:T(8,128)(2,1)S(1)} collective-permute-done((bf16[1024,256]{1,0:T(8,128)(2,1)S(1)}, bf16[1024,256]{1,0:T(8,128)(2,1)S(1)}, u32[]{:S(2)}, u32[]{:S(2)}) %collective-permute-start.4) | collective-permute-done | bytes 524320 | tf_op jit(solution)/shard_map/ppermute | solution.py:454
  47.7 1.7 %collective-permute-start.9 = (bf16[1024,256]{1,0:T(8,128)(2,1)S(1)}, bf16[1024,256]{1,0:T(8,128)(2,1)S(1)}, u32[]{:S(2)}, u32[]{:S(2)}) collective-permute-start(bf16[1024,256]{1,0:T(8,128)(2,1)S(1)} %collective-permute-done.4.refs_0_), channel_id=1, source_target_pairs={{0,2},{1,5},{4,0},{5,9},{8,4},{9,13},{12,8},{13,15},{14,12},{15,11... | collective-permute-start | bytes 1572872 | tf_op jit(solution)/shard_map/ppermute | solution.py:454
  49.8 1.7 %collective-permute-start.7 = (bf16[1024,256]{1,0:T(8,128)(2,1)S(1)}, bf16[1024,256]{1,0:T(8,128)(2,1)S(1)}, u32[]{:S(2)}, u32[]{:S(2)}) collective-permute-start(bf16[1024,256]{1,0:T(8,128)(2,1)S(1)} %collective-permute-done.4.refs_0_), channel_id=1, source_target_pairs={{0,16},{16,0},{1,17},{17,1},{2,18},{18,2},{3,19},{19,3},{4,20},{20... | collective-permute-start | bytes 1572872 | tf_op jit(solution)/shard_map/ppermute | solution.py:460
  51.4 2.5 %shard_map.96 = (f32[1,512,256]{2,1,0:T(8,128)S(1)}, f32[1,512,256]{2,1,0:T(8,128)S(1)}, f32[1,512,256]{2,1,0:T(8,128)S(1)}, f32[512,128]{1,0:T(8,128)S(1)}) custom-call(bf16[512,2048]{1,0:T(8,128)(2,1)S(1)} %copy-done.3, bf16[512,2048]{1,0:T(8,128)(2,1)S(1)} %collective-permute-done.5.other_context, bf16[512,4096]{1,0:T(8,128)(2,1)S(1)} %copy-done.1, ...), custom_call_target="tpu_custom_call" | custom-call | flops 1073741824 | bytes 6553600 | tf_op jit(solution)/shard_map/pallas_call | solution.py:162
  54.0 7.6 %collective-permute-done.9.refs_2_ = bf16[1024,256]{1,0:T(8,128)(2,1)S(1)} collective-permute-done((bf16[1024,256]{1,0:T(8,128)(2,1)S(1)}, bf16[1024,256]{1,0:T(8,128)(2,1)S(1)}, u32[]{:S(2)}, u32[]{:S(2)}) %collective-permute-start.9) | collective-permute-done | bytes 524320 | tf_op jit(solution)/shard_map/ppermute | solution.py:454
  63.6 1.6 %collective-permute-start.11 = (bf16[1024,256]{1,0:T(8,128)(2,1)S(1)}, bf16[1024,256]{1,0:T(8,128)(2,1)S(1)}, u32[]{:S(2)}, u32[]{:S(2)}) collective-permute-start(bf16[1024,256]{1,0:T(8,128)(2,1)S(1)} %collective-permute-done.7.refs_1_), channel_id=1, source_target_pairs={{0,2},{1,5},{4,0},{5,9},{8,4},{9,13},{12,8},{13,15},{14,12},{15,11... | collective-permute-start | bytes 1572872 | tf_op jit(solution)/shard_map/ppermute | solution.py:454
  67.2 4.5 %shard_map.97 = (f32[3,512,256]{2,1,0:T(8,128)S(1)}, f32[3,512,256]{2,1,0:T(8,128)S(1)}, f32[1,512,256]{2,1,0:T(8,128)S(1)}, f32[512,128]{1,0:T(8,128)S(1)}) custom-call(bf16[512,2048]{1,0:T(8,128)(2,1)S(1)} %copy-done.3, bf16[512,2048]{1,0:T(8,128)(2,1)S(1)} %collective-permute-done.5.other_context, bf16[512,4096]{1,0:T(8,128)(2,1)S(1)} %copy-done.1, ...), custom_call_target="tpu_custom_call" | custom-call | flops 2147483648 | bytes 11272192 | tf_op jit(solution)/shard_map/pallas_call | solution.py:162
  71.7 6.0 %collective-permute-done.11.refs_3_ = bf16[1024,256]{1,0:T(8,128)(2,1)S(1)} collective-permute-done((bf16[1024,256]{1,0:T(8,128)(2,1)S(1)}, bf16[1024,256]{1,0:T(8,128)(2,1)S(1)}, u32[]{:S(2)}, u32[]{:S(2)}) %collective-permute-start.11) | collective-permute-done | bytes 524320 | tf_op jit(solution)/shard_map/ppermute | solution.py:454
  78.2 1.6 %collective-permute-start.17 = (bf16[1024,256]{1,0:T(8,128)(2,1)S(1)}, bf16[1024,256]{1,0:T(8,128)(2,1)S(1)}, u32[]{:S(2)}, u32[]{:S(2)}) collective-permute-start(bf16[1024,256]{1,0:T(8,128)(2,1)S(1)} %collective-permute-done.refs_2_), channel_id=1, source_target_pairs={{0,16},{16,0},{1,17},{17,1},{2,18},{18,2},{3,19},{19,3},{4,20},{20... | collective-permute-start | bytes 1572872 | tf_op jit(solution)/shard_map/ppermute | solution.py:460
  80.2 1.6 %collective-permute-start.16 = (bf16[1024,256]{1,0:T(8,128)(2,1)S(1)}, bf16[1024,256]{1,0:T(8,128)(2,1)S(1)}, u32[]{:S(2)}, u32[]{:S(2)}) collective-permute-start(bf16[1024,256]{1,0:T(8,128)(2,1)S(1)} %collective-permute-done.13.refs_1_), channel_id=1, source_target_pairs={{0,4},{1,3},{4,8},{5,1},{8,12},{9,5},{12,14},{13,9},{14,10},{15,13... | collective-permute-start | bytes 1572872 | tf_op jit(solution)/shard_map/ppermute | solution.py:457
  81.9 5.1 %shard_map.98 = (f32[3,512,256]{2,1,0:T(8,128)S(1)}, f32[3,512,256]{2,1,0:T(8,128)S(1)}, f32[1,512,256]{2,1,0:T(8,128)S(1)}, f32[512,128]{1,0:T(8,128)S(1)}) custom-call(bf16[512,2048]{1,0:T(8,128)(2,1)S(1)} %copy-done.3, bf16[512,2048]{1,0:T(8,128)(2,1)S(1)} %collective-permute-done.5.other_context, bf16[512,4096]{1,0:T(8,128)(2,1)S(1)} %copy-done.1, ...), custom_call_target="tpu_custom_call" | custom-call | flops 2684354560 | bytes 11272192 | tf_op jit(solution)/shard_map/pallas_call | solution.py:162
  86.9 5.4 %collective-permute-done.17.refs_0_ = bf16[1024,256]{1,0:T(8,128)(2,1)S(1)} collective-permute-done((bf16[1024,256]{1,0:T(8,128)(2,1)S(1)}, bf16[1024,256]{1,0:T(8,128)(2,1)S(1)}, u32[]{:S(2)}, u32[]{:S(2)}) %collective-permute-start.17) | collective-permute-done | bytes 524320 | tf_op jit(solution)/shard_map/ppermute | solution.py:460
  92.4 1.9 %collective-permute-done.15.refs_2_ = bf16[1024,256]{1,0:T(8,128)(2,1)S(1)} collective-permute-done((bf16[1024,256]{1,0:T(8,128)(2,1)S(1)}, bf16[1024,256]{1,0:T(8,128)(2,1)S(1)}, u32[]{:S(2)}, u32[]{:S(2)}) %collective-permute-start.15) | collective-permute-done | bytes 524320 | tf_op jit(solution)/shard_map/ppermute | solution.py:454
  95.9 2.3 %shard_map.99 = (f32[3,512,256]{2,1,0:T(8,128)S(1)}, f32[512,128]{1,0:T(8,128)S(1)}) custom-call(bf16[512,2048]{1,0:T(8,128)(2,1)S(1)} %copy-done.3, f32[512,128]{1,0:T(8,128)S(1)} %get-tuple-element.90.given, bf16[1024,256]{1,0:T(8,128)(2,1)S(1)} %collective-permute-done.17.refs_0_, bf16[1024,256]{1,0:T(8,128)(2,1)S(1)} %collective-permute-done.16.refs_1_, ...), custom_call_target="tpu_custom_call" | custom-call | flops 805306368 | bytes 5767168 | tf_op jit(solution)/shard_map/pallas_call | solution.py:215
  99.9 4.9 %shard_map.100 = (f32[1,4096]{1,0:T(1,128)}, bf16[8,48,128]{2,1,0:T(8,128)(2,1)S(1)}) custom-call(s32[1]{0:T(128)S(6)} %copy.10.length, bf16[512,2048]{1,0:T(8,128)(2,1)S(1)} %copy-done.3, bf16[512,4096]{1,0:T(8,128)(2,1)S(1)} %copy-done.1, f32[512,128]{1,0:T(8,128)S(1)} %get-tuple-element.96.squares, f32[1,4096]{1,0:T(1,128)S(1)} %bitcast.2, ...), custom_call_target="tpu_custom_call" | custom-call | tf_op jit(solution)/shard_map/pallas_call | solution.py:332
  104.8 11.7 %all_to_all.10.got = bf16[8,48,128]{2,1,0:T(8,128)(2,1)S(1)} all-to-all(bf16[8,48,128]{2,1,0:T(8,128)(2,1)S(1)} %get-tuple-element.105), channel_id=1, replica_groups={{0,2,4,6,8,10,12,14},{1,3,5,7,9,11,13,15},{16,18,20,22,24,26,28,30},{17..., dimensions={0} | all-to-all | bytes 196608 | tf_op jit(solution)/shard_map/all_to_all | solution.py:549
  117.6 10.0 %all_to_all.11.got = f32[8,40,128]{2,1,0:T(8,128)S(1)} all-to-all(f32[8,40,128]{2,1,0:T(8,128)S(1)} %shard_map.101), channel_id=1, replica_groups={{0,2,4,6,8,10,12,14},{1,3,5,7,9,11,13,15},{16,18,20,22,24,26,28,30},{17..., dimensions={0} | all-to-all | bytes 327680 | tf_op jit(solution)/shard_map/all_to_all | solution.py:549
  (51 shorter events, 14.5 us)
Async XLA Ops:
  0.6 36.2 %copy-start.4 = (bf16[2048,256]{1,0:T(8,128)(2,1)S(1)}, bf16[2048,256]{1,0:T(8,128)(2,1)}, u32[]{:S(2)}) copy-start(bf16[2048,256]{1,0:T(8,128)(2,1)} %refs_0_.1) | copy-start | bytes 3145732
  0.6 36.2 %collective-permute-start.5 = (bf16[512,2048]{1,0:T(8,128)(2,1)}, bf16[512,2048]{1,0:T(8,128)(2,1)S(1)}, u32[]{:S(2)}, u32[]{:S(2)}) collective-permute-start(bf16[512,2048]{1,0:T(8,128)(2,1)} %context.11), channel_id=1, source_target_pairs={{0,1},{1,0},{2,3},{3,2},{4,5},{5,4},{6,7},{7,6},{8,9},{9,8},{10,11... | collective-permute-start | bytes 6291464 | tf_op jit(solution)/shard_map/ppermute | solution.py:463
  18.2 14.1 %collective-permute-start.1 = (bf16[1024,256]{1,0:T(8,128)(2,1)}, bf16[1024,256]{1,0:T(8,128)(2,1)S(1)}, u32[]{:S(2)}, u32[]{:S(2)}) collective-permute-start(bf16[1024,256]{1,0:T(8,128)(2,1)} %shard_map.94), channel_id=1, source_target_pairs={{0,2},{1,5},{4,0},{5,9},{8,4},{9,13},{12,8},{13,15},{14,12},{15,11... | collective-permute-start | bytes 1572872 | tf_op jit(solution)/shard_map/ppermute | solution.py:454
  20.8 22.3 %collective-permute-start.6 = (bf16[112,4096]{1,0:T(8,128)(2,1)}, bf16[112,4096]{1,0:T(8,128)(2,1)S(1)}, u32[]{:S(2)}, u32[]{:S(2)}) collective-permute-start(bf16[112,4096]{1,0:T(8,128)(2,1)} %queries.1), channel_id=1, source_target_pairs={{0,1},{1,0},{2,3},{3,2},{4,5},{5,4},{6,7},{7,6},{8,9},{9,8},{10,11... | collective-permute-start | bytes 2752520 | tf_op jit(solution)/shard_map/ppermute | solution.py:463
  21.0 13.6 %collective-permute-start = (bf16[1024,256]{1,0:T(8,128)(2,1)}, bf16[1024,256]{1,0:T(8,128)(2,1)S(1)}, u32[]{:S(2)}, u32[]{:S(2)}) collective-permute-start(bf16[1024,256]{1,0:T(8,128)(2,1)} %shard_map.94), channel_id=1, source_target_pairs={{0,4},{1,3},{4,8},{5,1},{8,12},{9,5},{12,14},{13,9},{14,10},{15,13... | collective-permute-start | bytes 1572872 | tf_op jit(solution)/shard_map/ppermute | solution.py:457
  32.2 15.5 %collective-permute-start.4 = (bf16[1024,256]{1,0:T(8,128)(2,1)S(1)}, bf16[1024,256]{1,0:T(8,128)(2,1)S(1)}, u32[]{:S(2)}, u32[]{:S(2)}) collective-permute-start(bf16[1024,256]{1,0:T(8,128)(2,1)S(1)} %collective-permute-done.1.refs_0_), channel_id=1, source_target_pairs={{0,2},{1,5},{4,0},{5,9},{8,4},{9,13},{12,8},{13,15},{14,12},{15,11... | collective-permute-start | bytes 1572872 | tf_op jit(solution)/shard_map/ppermute | solution.py:454
  34.6 14.8 %collective-permute-start.3 = (bf16[1024,256]{1,0:T(8,128)(2,1)S(1)}, bf16[1024,256]{1,0:T(8,128)(2,1)S(1)}, u32[]{:S(2)}, u32[]{:S(2)}) collective-permute-start(bf16[1024,256]{1,0:T(8,128)(2,1)S(1)} %collective-permute-done.refs_2_), channel_id=1, source_target_pairs={{0,4},{1,3},{4,8},{5,1},{8,12},{9,5},{12,14},{13,9},{14,10},{15,13... | collective-permute-start | bytes 1572872 | tf_op jit(solution)/shard_map/ppermute | solution.py:457
  35.3 14.4 %collective-permute-start.2 = (bf16[1024,256]{1,0:T(8,128)(2,1)S(1)}, bf16[1024,256]{1,0:T(8,128)(2,1)S(1)}, u32[]{:S(2)}, u32[]{:S(2)}) collective-permute-start(bf16[1024,256]{1,0:T(8,128)(2,1)S(1)} %collective-permute-done.1.refs_0_), channel_id=1, source_target_pairs={{0,16},{16,0},{1,17},{17,1},{2,18},{18,2},{3,19},{19,3},{4,20},{20... | collective-permute-start | bytes 1572872 | tf_op jit(solution)/shard_map/ppermute | solution.py:460
  47.7 3.7 %collective-permute-start.10 = (f32[1,512,256]{2,1,0:T(8,128)S(1)}, f32[1,512,256]{2,1,0:T(8,128)S(1)}, u32[]{:S(2)}, u32[]{:S(2)}) collective-permute-start(f32[1,512,256]{2,1,0:T(8,128)S(1)} %get-tuple-element.66), channel_id=1, source_target_pairs={{0,1},{1,0},{2,3},{3,2},{4,5},{5,4},{6,7},{7,6},{8,9},{9,8},{10,11... | collective-permute-start | bytes 1572872 | tf_op jit(solution)/shard_map/ppermute | solution.py:463
  47.7 13.8 %collective-permute-start.9 = (bf16[1024,256]{1,0:T(8,128)(2,1)S(1)}, bf16[1024,256]{1,0:T(8,128)(2,1)S(1)}, u32[]{:S(2)}, u32[]{:S(2)}) collective-permute-start(bf16[1024,256]{1,0:T(8,128)(2,1)S(1)} %collective-permute-done.4.refs_0_), channel_id=1, source_target_pairs={{0,2},{1,5},{4,0},{5,9},{8,4},{9,13},{12,8},{13,15},{14,12},{15,11... | collective-permute-start | bytes 1572872 | tf_op jit(solution)/shard_map/ppermute | solution.py:454
  49.4 12.6 %collective-permute-start.8 = (bf16[1024,256]{1,0:T(8,128)(2,1)S(1)}, bf16[1024,256]{1,0:T(8,128)(2,1)S(1)}, u32[]{:S(2)}, u32[]{:S(2)}) collective-permute-start(bf16[1024,256]{1,0:T(8,128)(2,1)S(1)} %collective-permute-done.3.refs_0_), channel_id=1, source_target_pairs={{0,4},{1,3},{4,8},{5,1},{8,12},{9,5},{12,14},{13,9},{14,10},{15,13... | collective-permute-start | bytes 1572872 | tf_op jit(solution)/shard_map/ppermute | solution.py:457
  49.8 13.8 %collective-permute-start.7 = (bf16[1024,256]{1,0:T(8,128)(2,1)S(1)}, bf16[1024,256]{1,0:T(8,128)(2,1)S(1)}, u32[]{:S(2)}, u32[]{:S(2)}) collective-permute-start(bf16[1024,256]{1,0:T(8,128)(2,1)S(1)} %collective-permute-done.4.refs_0_), channel_id=1, source_target_pairs={{0,16},{16,0},{1,17},{17,1},{2,18},{18,2},{3,19},{19,3},{4,20},{20... | collective-permute-start | bytes 1572872 | tf_op jit(solution)/shard_map/ppermute | solution.py:460
  61.5 5.7 %collective-permute-start.14 = (f32[1,512,256]{2,1,0:T(8,128)S(1)}, f32[1,512,256]{2,1,0:T(8,128)S(1)}, u32[]{:S(2)}, u32[]{:S(2)}) collective-permute-start(f32[1,512,256]{2,1,0:T(8,128)S(1)} %get-tuple-element.78), channel_id=1, source_target_pairs={{0,1},{1,0},{2,3},{3,2},{4,5},{5,4},{6,7},{7,6},{8,9},{9,8},{10,11... | collective-permute-start | bytes 1572872 | tf_op jit(solution)/shard_map/ppermute | solution.py:463
  63.6 14.1 %collective-permute-start.11 = (bf16[1024,256]{1,0:T(8,128)(2,1)S(1)}, bf16[1024,256]{1,0:T(8,128)(2,1)S(1)}, u32[]{:S(2)}, u32[]{:S(2)}) collective-permute-start(bf16[1024,256]{1,0:T(8,128)(2,1)S(1)} %collective-permute-done.7.refs_1_), channel_id=1, source_target_pairs={{0,2},{1,5},{4,0},{5,9},{8,4},{9,13},{12,8},{13,15},{14,12},{15,11... | collective-permute-start | bytes 1572872 | tf_op jit(solution)/shard_map/ppermute | solution.py:454
  65.2 12.7 %collective-permute-start.13 = (bf16[1024,256]{1,0:T(8,128)(2,1)S(1)}, bf16[1024,256]{1,0:T(8,128)(2,1)S(1)}, u32[]{:S(2)}, u32[]{:S(2)}) collective-permute-start(bf16[1024,256]{1,0:T(8,128)(2,1)S(1)} %collective-permute-done.3.refs_0_), channel_id=1, source_target_pairs={{0,16},{16,0},{1,17},{17,1},{2,18},{18,2},{3,19},{19,3},{4,20},{20... | collective-permute-start | bytes 1572872 | tf_op jit(solution)/shard_map/ppermute | solution.py:460
  66.7 11.2 %collective-permute-start.12 = (bf16[1024,256]{1,0:T(8,128)(2,1)S(1)}, bf16[1024,256]{1,0:T(8,128)(2,1)S(1)}, u32[]{:S(2)}, u32[]{:S(2)}) collective-permute-start(bf16[1024,256]{1,0:T(8,128)(2,1)S(1)} %collective-permute-done.8.refs_3_), channel_id=1, source_target_pairs={{0,4},{1,3},{4,8},{5,1},{8,12},{9,5},{12,14},{13,9},{14,10},{15,13... | collective-permute-start | bytes 1572872 | tf_op jit(solution)/shard_map/ppermute | solution.py:457
  77.9 3.9 %collective-permute-start.18 = (f32[3,512,256]{2,1,0:T(8,128)S(1)}, f32[3,512,256]{2,1,0:T(8,128)S(1)}, u32[]{:S(2)}, u32[]{:S(2)}) collective-permute-start(f32[3,512,256]{2,1,0:T(8,128)S(1)} %get-tuple-element.86), channel_id=1, source_target_pairs={{0,1},{1,0},{2,3},{3,2},{4,5},{5,4},{6,7},{7,6},{8,9},{9,8},{10,11... | collective-permute-start | bytes 4718600 | tf_op jit(solution)/shard_map/ppermute | solution.py:463
  78.2 14.1 %collective-permute-start.17 = (bf16[1024,256]{1,0:T(8,128)(2,1)S(1)}, bf16[1024,256]{1,0:T(8,128)(2,1)S(1)}, u32[]{:S(2)}, u32[]{:S(2)}) collective-permute-start(bf16[1024,256]{1,0:T(8,128)(2,1)S(1)} %collective-permute-done.refs_2_), channel_id=1, source_target_pairs={{0,16},{16,0},{1,17},{17,1},{2,18},{18,2},{3,19},{19,3},{4,20},{20... | collective-permute-start | bytes 1572872 | tf_op jit(solution)/shard_map/ppermute | solution.py:460
  79.8 14.4 %collective-permute-start.15 = (bf16[1024,256]{1,0:T(8,128)(2,1)S(1)}, bf16[1024,256]{1,0:T(8,128)(2,1)S(1)}, u32[]{:S(2)}, u32[]{:S(2)}) collective-permute-start(bf16[1024,256]{1,0:T(8,128)(2,1)S(1)} %collective-permute-done.11.refs_3_), channel_id=1, source_target_pairs={{0,2},{1,5},{4,0},{5,9},{8,4},{9,13},{12,8},{13,15},{14,12},{15,11... | collective-permute-start | bytes 1572872 | tf_op jit(solution)/shard_map/ppermute | solution.py:454
  80.2 14.0 %collective-permute-start.16 = (bf16[1024,256]{1,0:T(8,128)(2,1)S(1)}, bf16[1024,256]{1,0:T(8,128)(2,1)S(1)}, u32[]{:S(2)}, u32[]{:S(2)}) collective-permute-start(bf16[1024,256]{1,0:T(8,128)(2,1)S(1)} %collective-permute-done.13.refs_1_), channel_id=1, source_target_pairs={{0,4},{1,3},{4,8},{5,1},{8,12},{9,5},{12,14},{13,9},{14,10},{15,13... | collective-permute-start | bytes 1572872 | tf_op jit(solution)/shard_map/ppermute | solution.py:457
  94.2 5.7 %collective-permute-start.22 = (f32[3,512,256]{2,1,0:T(8,128)S(1)}, f32[3,512,256]{2,1,0:T(8,128)S(1)}, u32[]{:S(2)}, u32[]{:S(2)}) collective-permute-start(f32[3,512,256]{2,1,0:T(8,128)S(1)} %get-tuple-element.103), channel_id=1, source_target_pairs={{0,1},{1,0},{2,3},{3,2},{4,5},{5,4},{6,7},{7,6},{8,9},{9,8},{10,11... | collective-permute-start | bytes 4718600 | tf_op jit(solution)/shard_map/ppermute | solution.py:463
  94.5 3.9 %collective-permute-start.19 = (bf16[1024,256]{1,0:T(8,128)(2,1)S(1)}, bf16[1024,256]{1,0:T(8,128)(2,1)S(1)}, u32[]{:S(2)}, u32[]{:S(2)}) collective-permute-start(bf16[1024,256]{1,0:T(8,128)(2,1)S(1)} %collective-permute-done.17.refs_0_), channel_id=1, source_target_pairs={{0,1},{1,0},{2,3},{3,2},{4,5},{5,4},{6,7},{7,6},{8,9},{9,8},{10,11... | collective-permute-start | bytes 1572872 | tf_op jit(solution)/shard_map/ppermute | solution.py:463
  94.7 4.4 %collective-permute-start.20 = (bf16[1024,256]{1,0:T(8,128)(2,1)S(1)}, bf16[1024,256]{1,0:T(8,128)(2,1)S(1)}, u32[]{:S(2)}, u32[]{:S(2)}) collective-permute-start(bf16[1024,256]{1,0:T(8,128)(2,1)S(1)} %collective-permute-done.16.refs_1_), channel_id=1, source_target_pairs={{0,1},{1,0},{2,3},{3,2},{4,5},{5,4},{6,7},{7,6},{8,9},{9,8},{10,11... | collective-permute-start | bytes 1572872 | tf_op jit(solution)/shard_map/ppermute | solution.py:463
  95.0 4.9 %collective-permute-start.21 = (bf16[1024,256]{1,0:T(8,128)(2,1)S(1)}, bf16[1024,256]{1,0:T(8,128)(2,1)S(1)}, u32[]{:S(2)}, u32[]{:S(2)}) collective-permute-start(bf16[1024,256]{1,0:T(8,128)(2,1)S(1)} %collective-permute-done.15.refs_2_), channel_id=1, source_target_pairs={{0,1},{1,0},{2,3},{3,2},{4,5},{5,4},{6,7},{7,6},{8,9},{9,8},{10,11... | collective-permute-start | bytes 1572872 | tf_op jit(solution)/shard_map/ppermute | solution.py:463
  (7 other events, 63.3 us)

commit v7 on v1

--- a/solution.py
+++ b/solution.py
@@ -1,15 +1,469 @@
+import functools
 import math
 
 import jax
 import jax.numpy as jnp
 from jax import lax
+from jax.experimental import pallas as pl
+from jax.experimental.pallas import tpu as pltpu
 from jax.sharding import PartitionSpec as P
 
 QB = 256
 LANES = 128
-
-
-def per_device(context, residual, out_proj, norm_gain, lengths, queries, pattern):
+CORES = 2
+STEP = 256
+VMEM_BYTES = 12 << 20
+LOW = -1e30
+CYCLE = (0, 2, 4, 6, 7, 5, 3, 1)
+VMEM_SPEC = pl.BlockSpec(memory_space=pltpu.VMEM)
+SMALL = pl.CostEstimate(flops=1000, bytes_accessed=1000, transcendentals=0)
+
+
+def column_block(distance, same_core):
+    me = lax.axis_index("dp")
+    core = lax.rem(me, CORES)
+    chip = lax.div(me, CORES)
+    z, y = lax.div(chip, 2), lax.rem(chip, 2)
+    size = len(CYCLE)
+    at = jnp.where(y == 0, z, size - 1 - z)
+    core = core if same_core else 1 - core
+    there = lax.rem(at + jnp.where(core == 0, size + distance, size - distance), size)
+    chip = jnp.where(there < size // 2, 2 * there, 2 * (size - 1 - there) + 1)
+    return chip * CORES + core
+
+
+def columns(distance, same_core, width):
+    return pl.ds(pl.multiple_of(column_block(distance, same_core) * width, width), width)
+
+
+def half_slice(second, half):
+    side = lax.axis_index("groups")
+    return pl.ds(pl.multiple_of((1 - side if second else side) * half, half), half)
+
+
+def add_squares(squares, at, total):
+    square = total * total
+    for lane in range(0, total.shape[1], LANES):
+        squares[at, :] += square[:, lane : lane + LANES]
+
+
+def half_kernel(whole, part):
+    part[...] = whole[half_slice(False, part.shape[0]), :]
+
+
+def own_half(whole):
+    rows, width = whole.shape
+    return pl.pallas_call(
+        half_kernel,
+        out_shape=jax.ShapeDtypeStruct((rows // 2, width), whole.dtype),
+        in_specs=[VMEM_SPEC],
+        out_specs=VMEM_SPEC,
+        compiler_params=pltpu.CompilerParams(vmem_limit_bytes=VMEM_BYTES),
+    )(whole)
+
+
+def row_steps(rows):
+    def loop(body):
+        @pl.loop(0, rows // STEP)
+        def _(k):
+            body(pl.ds(pl.multiple_of(k * STEP, STEP), STEP))
+
+    return loop
+
+
+def product(tokens, at, pieces):
+    total = None
+    for piece, second in pieces:
+        half = piece.shape[0]
+        term = jnp.dot(tokens[at, half_slice(second, half)], piece[...], preferred_element_type=jnp.float32)
+        total = term if total is None else total + term
+    return total
+
+
+def wave_kernel(full, part, arrived, whole, tokens, *refs):
+    count = len(full) + len(part)
+    refs = list(refs)
+    context = refs.pop(0) if "mine" in tokens else None
+    other_context = refs.pop(0) if "theirs" in tokens else None
+    residual = refs.pop(0) if "mine" in tokens else None
+    if whole:
+        shard = refs.pop(0)
+        half = shard.shape[0] // 2
+        jobs = [[(shard.at[half_slice(second, half)], second) for second in (False, True)]]
+    else:
+        jobs = [[(refs.pop(0), False)] + ([(refs.pop(0), True)] if j < len(full) else []) for j in range(count)]
+    if arrived:
+        received, before = [refs.pop(0) for _ in arrived], refs.pop(0)
+    mine = refs.pop(0) if "mine" in tokens else None
+    theirs = [refs.pop(0) for _ in range(count)] if "theirs" in tokens else None
+    finished = refs.pop(0) if arrived else None
+    squares = refs.pop(0) if "mine" in tokens else None
+    rows, width = mine.shape[1:] if "mine" in tokens else theirs[0].shape
+    if arrived:
+        squares[...] = before[...]
+    elif "mine" in tokens:
+        squares[...] = jnp.zeros_like(squares)
+    for j, distance in enumerate(full + part):
+
+        @row_steps(rows)
+        def _(at):
+            if "theirs" in tokens:
+                theirs[j][at, :] = product(other_context, at, jobs[j])
+            if "mine" in tokens:
+                total = product(context, at, jobs[j])
+                total += residual[at, columns(distance, True, width)].astype(jnp.float32)
+                mine[j, at, :] = total
+                if j < len(full):
+                    add_squares(squares, at, total)
+
+    for j, distance in enumerate(arrived):
+
+        @row_steps(rows)
+        def _(at):
+            total = received[j][at, :] + residual[at, columns(distance, False, width)].astype(jnp.float32)
+            finished[j, at, :] = total
+            add_squares(squares, at, total)
+
+
+def wave(full, part, arrived, context, other_context, residual, pieces, received=None, squares=None):
+    tokens = (("mine",) if context is not None else ()) + (("theirs",) if other_context is not None else ())
+    count = len(full) + len(part)
+    rows = (context if other_context is None else other_context).shape[0]
+    whole = len(pieces) == 1
+    block = jax.ShapeDtypeStruct((rows, pieces[0].shape[1]), jnp.float32)
+    outs = [jax.ShapeDtypeStruct((count,) + block.shape, jnp.float32)] if "mine" in tokens else []
+    outs += [block] * count if "theirs" in tokens else []
+    operands = [x for x in (context, other_context) if x is not None]
+    operands += ([residual] if "mine" in tokens else []) + list(pieces)
+    if arrived:
+        operands += [*received, squares]
+        outs.append(jax.ShapeDtypeStruct((len(arrived),) + block.shape, jnp.float32))
+    if "mine" in tokens:
+        outs.append(jax.ShapeDtypeStruct((rows, LANES), jnp.float32))
+    return pl.pallas_call(
+        functools.partial(wave_kernel, full, part, arrived, whole, tokens),
+        out_shape=outs,
+        in_specs=[VMEM_SPEC] * len(operands),
+        out_specs=[VMEM_SPEC] * len(outs),
+        compiler_params=pltpu.CompilerParams(vmem_limit_bytes=VMEM_BYTES),
+        cost_estimate=SMALL,
+    )(*operands)
+
+
+def late_blocks(items, context, residual, pieces, hidden, squares, target):
+    rows, width = target.shape[1:]
+    for i, (base, parts, bare, distance, same) in enumerate(items):
+
+        @row_steps(rows)
+        def _(at):
+            value = product(context, at, [(pieces[index], second) for index, second in parts])
+            if base is not None:
+                known = hidden[base[0]][(at,) if base[1] is None else (base[1], at)]
+                value = known if value is None else value + known
+            if bare:
+                value += residual[at, columns(distance, same, width)].astype(jnp.float32)
+            target[i, at, :] = value
+            add_squares(squares, at, value)
+
+
+def late_kernel(items, n_pieces, context, residual, before, *refs):
+    pieces, hidden = refs[:n_pieces], refs[n_pieces:-2]
+    finished, squares = refs[-2:]
+    squares[...] = before[...]
+    late_blocks(items, context, residual, pieces, hidden, squares, finished)
+
+
+def late(items, context, residual, squares, pieces, hidden):
+    rows = context.shape[0]
+    operands = [context, residual, squares, *pieces, *hidden]
+    return pl.pallas_call(
+        functools.partial(late_kernel, items, len(pieces)),
+        out_shape=(
+            jax.ShapeDtypeStruct((len(items), rows, pieces[0].shape[1]), jnp.float32),
+            jax.ShapeDtypeStruct(squares.shape, jnp.float32),
+        ),
+        in_specs=[VMEM_SPEC] * len(operands),
+        out_specs=(VMEM_SPEC, VMEM_SPEC),
+        compiler_params=pltpu.CompilerParams(vmem_limit_bytes=VMEM_BYTES),
+        cost_estimate=SMALL,
+    )(*operands)
+
+
+def final_kernel(items, sources, n_pieces, length, context, residual, before, gain, flags, *refs):
+    pieces, hidden = refs[:n_pieces], refs[n_pieces:-6]
+    embedded, payload, blocks, squares, scale_rows, sheet = refs[-6:]
+    width = blocks.shape[2]
+    features = embedded.shape[1]
+    squares[...] = before[...]
+    late_blocks(items, context, residual, pieces, hidden, squares, blocks)
+    mean = jnp.sum(squares[...], axis=1, keepdims=True) * (1.0 / features)
+    row = lax.broadcasted_iota(jnp.int32, mean.shape, 0)
+    scale = jnp.where(row < length[0], lax.rsqrt(mean + 1e-05), 0.0)
+    scale_rows[...] = jnp.broadcast_to(scale, scale_rows.shape)
+    inverse = 1.0 / jnp.full((1, width), length[0], jnp.int32).astype(jnp.float32)
+    done = [(blocks.at[i], distance, same) for i, (_, _, _, distance, same) in enumerate(items)]
+    done += [(hidden[array].at[entry], distance, same) for array, entry, distance, same in sources]
+    for block, distance, same in done:
+        parts = [
+            jnp.sum(block[:, lane : lane + LANES] * scale_rows[...], axis=0, keepdims=True)
+            for lane in range(0, width, LANES)
+        ]
+        where = columns(distance, same, width)
+        embedded[:, where] = jnp.concatenate(parts, axis=1) * gain[:, where] * inverse
+    pooled = embedded[...]
+    mean = jnp.sum(pooled * pooled, axis=1, keepdims=True) * (1.0 / features)
+    embedded[...] = pooled * lax.rsqrt(mean + 1e-06)
+    lines = features // LANES
+    sheet[lines:, :] = jnp.zeros((sheet.shape[0] - lines, LANES), jnp.float32)
+    for line in range(lines):
+        sheet[line : line + 1, :] = embedded[:, line * LANES : (line + 1) * LANES]
+    sheet[lines : lines + 1, :] = flags[...]
+    rounded = sheet[...].astype(jnp.bfloat16)
+    for rank in range(payload.shape[0]):
+        payload[rank] = rounded
+
+
+def finish(items, sources, lengths, context, residual, squares, gain, flags, pieces, hidden, ranks):
+    rows = context.shape[0]
+    width = pieces[0].shape[1]
+    features = (len(items) + len(sources)) * width
+    lines = -(-(features // LANES + 1) // 16) * 16
+    operands = [context, residual, squares, gain, flags, *pieces, *hidden]
+    return pl.pallas_call(
+        functools.partial(final_kernel, items, sources, len(pieces)),
+        out_shape=(
+            jax.ShapeDtypeStruct((1, features), jnp.float32),
+            jax.ShapeDtypeStruct((ranks, lines, LANES), jnp.bfloat16),
+        ),
+        in_specs=[pl.BlockSpec(memory_space=pltpu.SMEM)] + [VMEM_SPEC] * len(operands),
+        out_specs=(VMEM_SPEC, VMEM_SPEC),
+        scratch_shapes=[
+            pltpu.VMEM((len(items), rows, width), jnp.float32),
+            pltpu.VMEM((rows, LANES), jnp.float32),
+            pltpu.VMEM((rows, LANES), jnp.float32),
+            pltpu.VMEM((lines, LANES), jnp.float32),
+        ],
+        compiler_params=pltpu.CompilerParams(vmem_limit_bytes=VMEM_BYTES),
+        cost_estimate=SMALL,
+    )(lengths, *operands)
+
+
+def score_kernel(lines, blocks, got, queries, other_queries, out, wide, emb, mix):
+    me = lax.axis_index("dp")
+    ranks = got.shape[0]
+    count = queries.shape[0]
+    wide[...] = got[...].astype(jnp.float32)
+    for line in range(lines):
+        emb[:, line * LANES : (line + 1) * LANES] = wide[:, line, :]
+    half = emb[...].astype(jnp.bfloat16)
+    flags = wide[:, lines, :].astype(jnp.bfloat16)
+    temper = 1.0 / (0.02 * math.sqrt(lines * LANES))
+    scores, masks = [], []
+    for owner, rows in ((me, queries), (me + 1 - 2 * lax.rem(me, CORES), other_queries)):
+        score = lax.dot_general(
+            half, rows[...], (((1,), (1,)), ((), ())), preferred_element_type=jnp.float32
+        )
+        scores.append(score * temper)
+        block = lax.broadcasted_iota(jnp.int32, (LANES, count), 0)
+        row = owner * count + lax.broadcasted_iota(jnp.int32, (LANES, count), 1)
+        pick = (row >= block * QB) & (row < block * QB + QB) & (block < blocks)
+        pick = jnp.where(pick, 1.0, 0.0).astype(jnp.bfloat16)
+        masks.append(jnp.dot(flags, pick, preferred_element_type=jnp.float32) > 0.5)
+    peaks = [
+        jnp.max(jnp.where(mask, score, LOW), axis=1, keepdims=True) for score, mask in zip(scores, masks)
+    ]
+    peak = jnp.maximum(*peaks)
+    weights = [jnp.where(mask, jnp.exp(score - peak), 0.0) for score, mask in zip(scores, masks)]
+    total = sum(jnp.sum(weight, axis=1, keepdims=True) for weight in weights)
+    mix[...] = jnp.dot(
+        weights[0].astype(jnp.bfloat16), queries[...], preferred_element_type=jnp.float32
+    ) + jnp.dot(weights[1].astype(jnp.bfloat16), other_queries[...], preferred_element_type=jnp.float32)
+    for line in range(lines):
+        out[:, line, :] = mix[:, line * LANES : (line + 1) * LANES]
+    lane = lax.broadcasted_iota(jnp.int32, (ranks, LANES), 1)
+    out[:, lines, :] = jnp.where(lane == 0, peak, jnp.where(lane == 1, total, 0.0))
+    for line in range(lines + 1, out.shape[1]):
+        out[:, line, :] = jnp.zeros((ranks, LANES), jnp.float32)
+
+
+def score(got, queries, other_queries, blocks):
+    ranks = got.shape[0]
+    features = queries.shape[1]
+    lines = features // LANES
+    return pl.pallas_call(
+        functools.partial(score_kernel, lines, blocks),
+        out_shape=jax.ShapeDtypeStruct((ranks, -(-(lines + 1) // 8) * 8, LANES), jnp.float32),
+        in_specs=[pl.BlockSpec(memory_space=pltpu.VMEM)] * 3,
+        out_specs=pl.BlockSpec(memory_space=pltpu.VMEM),
+        scratch_shapes=[
+            pltpu.VMEM(got.shape, jnp.float32),
+            pltpu.VMEM((ranks, features), jnp.float32),
+            pltpu.VMEM((ranks, features), jnp.float32),
+        ],
+        compiler_params=pltpu.CompilerParams(vmem_limit_bytes=VMEM_BYTES),
+    )(got, queries, other_queries)
+
+
+def combine_kernel(lines, got, recalled, log_total):
+    stats = got[:, lines, :]
+    peaks, sums = stats[:, 0:1], stats[:, 1:2]
+    peak = jnp.max(peaks, axis=0, keepdims=True)
+    factor = jnp.exp(peaks - peak)
+    total = jnp.sum(sums * factor, axis=0, keepdims=True)
+    mix = got[0, :lines, :] * factor[0:1, :]
+    for rank in range(1, got.shape[0]):
+        mix += got[rank, :lines, :] * factor[rank : rank + 1, :]
+    mix = mix / total
+    for line in range(lines):
+        recalled[:, line * LANES : (line + 1) * LANES] = mix[line : line + 1, :]
+    log_total[...] = peak + jnp.log(total)
+
+
+def combine(got, features):
+    recalled, log_total = pl.pallas_call(
+        functools.partial(combine_kernel, features // LANES),
+        out_shape=(
+            jax.ShapeDtypeStruct((1, features), jnp.float32),
+            jax.ShapeDtypeStruct((1, 1), jnp.float32),
+        ),
+        in_specs=[pl.BlockSpec(memory_space=pltpu.VMEM)],
+        out_specs=(pl.BlockSpec(memory_space=pltpu.VMEM), pl.BlockSpec(memory_space=pltpu.VMEM)),
+        compiler_params=pltpu.CompilerParams(vmem_limit_bytes=VMEM_BYTES),
+    )(got)
+    return recalled, log_total.reshape(1)
+
+
+def on_cycle(context, residual, out_proj, norm_gain, lengths, queries, pattern):
+    ranks = lax.axis_size("dp")
+    size = ranks // CORES
+    features = residual.shape[1]
+
+    def ring(step):
+        return [
+            (CYCLE[r] * CORES + c, CYCLE[(r + step * (1 - 2 * c)) % size] * CORES + c)
+            for r in range(size)
+            for c in range(CORES)
+        ]
+
+    def from_next(piece):
+        return lax.ppermute(piece, "dp", ring(-1))
+
+    def from_last(piece):
+        return lax.ppermute(piece, "dp", ring(1))
+
+    def over_x(piece):
+        return lax.ppermute(piece, "groups", [(0, 1), (1, 0)])
+
+    def other_core(piece):
+        return lax.ppermute(piece, "dp", [(i, i ^ 1) for i in range(ranks)])
+
+    wait = lax.optimization_barrier
+
+    own = own_half(out_proj)
+    a = from_next(own)
+    c = other_core(context)
+    h0, sq0 = wave((0,), (), (), context, None, residual, [out_proj])
+    own, h0, sq0 = wait((own, h0, sq0))
+    b = from_last(own)
+
+    n1, sq0 = wait((a, sq0))
+    x = over_x(n1)
+    a = from_next(n1)
+    context2, n1 = wait((c, n1))
+    (t0,) = wave((0,), (), (), None, context2, None, [out_proj])
+    l1, n1, t0 = wait((b, n1, t0))
+    b = from_last(l1)
+    r0 = other_core(t0)
+
+    n2, l1, queries = wait((a, l1, queries))
+    queries2 = other_core(queries)
+    xn1, n2 = wait((x, n2))
+    x = over_x(n2)
+    a = from_next(n2)
+    h1, t1, f0, sq1 = wave((1,), (), (0,), context, context2, residual, [n1, xn1], [r0], sq0)
+    l2, n2, t1, sq1 = wait((b, n2, t1, sq1))
+    b = from_last(l2)
+    r1 = other_core(t1)
+
+    xn2, l2, queries2 = wait((x, l2, queries2))
+    x = over_x(l2)
+    a2 = from_next(xn2)
+    n3, xn2 = wait((a, xn2))
+    h2, t2, t2p, f1, sq2 = wave((2,), (-1,), (1,), context, context2, residual, [n2, xn2, l1], [r1], sq1)
+    l3, n3, t2, t2p, sq2 = wait((b, n3, t2, t2p, sq2))
+    b = from_last(l3)
+    r2, r2p = other_core(t2), other_core(t2p)
+
+    n3x, l3 = wait((a2, l3))
+    a = from_next(n3x)
+    xl2, l1, n3x = wait((x, l1, n3x))
+    x = over_x(l1)
+    h3, t3a, t3b, t3p, f2, sq3 = wave(
+        (-2, 3), (-3,), (2,), context, context2, residual, [l2, xl2, n3, n3x, l3], [r2], sq2
+    )
+    l4, xl2, t3a, t3b, t3p, sq3, r2p = wait((b, xl2, t3a, t3b, t3p, sq3, r2p))
+    b = from_last(xl2)
+    r3a, r3b, r3p = other_core(t3a), other_core(t3b), other_core(t3p)
+    l4s = other_core(l4)
+
+    n4x, l4 = wait((a, l4))
+    n4xs = other_core(n4x)
+    xl1, n4x = wait((x, n4x))
+    xl1s = other_core(xl1)
+    l3x, xl1 = wait((b, xl1))
+    l3xs = other_core(l3x)
+
+    missing = (((0, True),), ((1, True),), ((2, False), (3, True)))
+    own_items = tuple(
+        (base, parts, base is None, distance, True)
+        for base, parts, distance in zip(((0, 1), (1, 2), None), missing, (-1, -3, 4))
+    )
+    h4, sq4 = late(own_items, context, residual, sq3, [xl1, l3x, l4, n4x], [h2, h3])
+    items = tuple(
+        (base, parts, True, distance, False)
+        for base, parts, distance in zip(
+            ((8, None), (9, None), None, (10, None), (11, None)), missing + ((), ()), (-1, -3, 4, -2, 3)
+        )
+    )
+    hidden = [h0, h1, h2, h3, h4, f0, f1, f2, r2p, r3p, r3a, r3b]
+    sources = (
+        (0, 0, 0, True),
+        (1, 0, 1, True),
+        (2, 0, 2, True),
+        (3, 0, -2, True),
+        (3, 1, 3, True),
+        (4, 0, -1, True),
+        (4, 1, -3, True),
+        (4, 2, 4, True),
+        (5, 0, 0, False),
+        (6, 0, 1, False),
+        (7, 0, 2, False),
+    )
+    flags = jnp.pad(pattern.astype(jnp.float32), ((0, 0), (0, LANES - pattern.shape[1])))
+    embedded, payload = finish(
+        items,
+        sources,
+        lengths,
+        context,
+        residual,
+        sq4,
+        norm_gain.reshape(1, -1),
+        flags,
+        [xl1s, l3xs, l4s, n4xs],
+        hidden,
+        size,
+    )
+    same_core = [list(range(c, ranks, CORES)) for c in range(CORES)]
+
+    def spread(blocks):
+        return lax.all_to_all(blocks, "dp", 0, 0, axis_index_groups=same_core, tiled=True)
+
+    parts = score(spread(payload), queries, queries2, pattern.shape[1])
+    recalled, log_total = combine(spread(parts), features)
+    return embedded, recalled, log_total
+
+
+def gathered(context, residual, out_proj, norm_gain, lengths, queries, pattern):
     tok_rows = context.shape[0]
     features = residual.shape[1]
     passages_here = lengths.shape[0]
@@ -45,8 +499,7 @@
     row_block = (me * query_rows + jnp.arange(query_rows)) // QB
     picks = (row_block[None, :] == jnp.arange(blocks)[:, None]).astype(jnp.float32)
     cand_mask = jnp.dot(flags_all, picks) > 0
-    low = jnp.float32(-1e30)
-    peak_part = jnp.max(jnp.where(cand_mask, scores, low), axis=1, keepdims=True)
+    peak_part = jnp.max(jnp.where(cand_mask, scores, LOW), axis=1, keepdims=True)
     weights = jnp.where(cand_mask, jnp.exp(scores - peak_part), 0.0)
     total_part = jnp.sum(weights, axis=1, keepdims=True)
     mix_part = jnp.dot(weights.astype(jnp.bfloat16), queries, preferred_element_type=jnp.float32)
@@ -65,6 +518,20 @@
     return (embedded, recalled, log_total)
 
 
+def per_device(context, residual, out_proj, norm_gain, lengths, queries, pattern):
+    fits = (
+        lax.axis_size("dp") == CORES * len(CYCLE)
+        and lax.axis_size("groups") == 2
+        and lengths.shape[0] == 1
+        and out_proj.shape[1] % LANES == 0
+        and out_proj.shape[0] % (2 * LANES) == 0
+        and context.shape[0] % STEP == 0
+        and pattern.shape[1] <= LANES
+    )
+    form = on_cycle if fits else gathered
+    return form(context, residual, out_proj, norm_gain, lengths, queries, pattern)
+
+
 def solution(mesh):
     in_specs = (
         P(("groups", "dp"), None),

time: 207 us -> 105 us (0.51)
  waiting for transfers between devices: 135 us -> 41.8 us
  Pallas kernels: 0 us -> 17.8 us
  starting transfers between devices: 0.04 us -> 17.6 us
  between operations: 18 us -> 1.46 us
  matrix products: 14.2 us -> 0 us
  blocking collectives: 32.7 us -> 21.3 us
  other arithmetic: 7.23 us -> 0.01 us
  local copies, waits for them, and re-layouts: 0.33 us -> 5.03 us
    all_gather x1 -> x0, waiting for transfers between devices: 134 us -> none  [per_device(): lax.all_gather(out_proj, 'dp', axis=1, tiled=True)]
    ppermute x0 -> x27, waiting for transfers between devices: none -> 41.8 us  [the longest x5 27.8 us: from_last(): return lax.ppermute(piece, 'dp', ring(1))]
    all_gather x1 -> x0, blocking collectives: 20 us -> none  [per_device(): lax.all_gather(jnp.concatenate([emb_half, flags], axis=1), 'dp', axis=0,...]
    pallas_call x0 -> x10, Pallas kernels: none -> 17.8 us  [the longest x5 9.75 us: wave(): pl.pallas_call(functools.partial(wave_kernel, full, part, arrived, whole,...]
    ppermute x0 -> x27, starting transfers between devices: none -> 17.6 us  [the longest x5 8.12 us: from_next(): return lax.ppermute(piece, 'dp', ring(-1))]
    dot_general x4 -> x0, matrix products: 14.2 us -> none  [the longest x1 13.3 us: per_device(): jnp.dot(context, lax.all_gather(out_proj, 'dp', axis=1, tiled=True), pref...]
    all_to_all x1 -> x2, blocking collectives: 12.8 us -> 21.3 us  [spread(): lax.all_to_all(blocks, 'dp', 0, 0, axis_index_groups=same_core, tiled=True)]
    unnamed x9 -> x16, local copies, waits for them, and re-layouts: 0.05 us -> 5.03 us
  transfers between devices with their start and end apart: 1 -> 27, of which waited for: 1 -> 11; matrix products, arithmetic and copies ran while one was open for 0% -> 0% of each run, Pallas kernels for 0% -> 11%
where the time goes in v7:
time: 105 us
  waiting for transfers between devices  41.8 us (40%)
  blocking collectives  21.3 us (20%)
  Pallas kernels  17.8 us (17%)
  starting transfers between devices  17.6 us (17%)
  local copies, waits for them, and re-layouts  5.03 us (5%)
  between operations  1.46 us (1%)
    ppermute x5, waiting for transfers between devices, from_last(): return lax.ppermute(piece, 'dp', ring(1))  27.8 us
    all_to_all x2, blocking collectives, spread(): lax.all_to_all(blocks, 'dp', 0, 0, axis_index_groups=same_core, tiled=True)  21.3 us
    ppermute x4, waiting for transfers between devices, over_x(): return lax.ppermute(piece, 'groups', [(0, 1), (1, 0)])  10.2 us
    pallas_call x5, Pallas kernels, wave(): pl.pallas_call(functools.partial(wave_kernel, full, part, arrived, whole,...  9.75 us
    ppermute x5, starting transfers between devices, from_next(): return lax.ppermute(piece, 'dp', ring(-1))  8.12 us
    ppermute x4, starting transfers between devices, over_x(): return lax.ppermute(piece, 'groups', [(0, 1), (1, 0)])  5.76 us
    unnamed x16, local copies, waits for them, and re-layouts  5.03 us
    pallas_call x1, Pallas kernels, finish(): pl.pallas_call(functools.partial(final_kernel, items, sources, len(pieces...  4.04 us
  transfers between devices with their start and end apart: 27, of which 11 were waited for; matrix products, arithmetic and copies ran while one was open for 0% of the time, Pallas kernels for 11%

profile of v7, /device:TPU:0, one launch (start us, length us, event | category | flops | bytes accessed | tf_op | source)
XLA Modules:
  0.0 105.1 jit_solution(16349352023980760483)
XLA Ops:
  2.4 2.6 %collective-permute-start.2 = (bf16[1024,256]{1,0:T(8,128)(2,1)S(1)}, bf16[1024,256]{1,0:T(8,128)(2,1)S(1)}, u32[]{:S(2)}, u32[]{:S(2)}) collective-permute-start(bf16[1024,256]{1,0:T(8,128)(2,1)S(1)} %shard_map.94), channel_id=1, source_target_pairs={{0,2},{1,5},{4,0},{5,9},{8,4},{9,13},{12,8},{13,15},{14,12},{15,11... | collective-permute-start | bytes 1572872 | tf_op jit(solution)/shard_map/ppermute | solution.py:349
  5.0 2.2 %copy-done = bf16[512,4096]{1,0:T(8,128)(2,1)S(1)} copy-done((bf16[512,4096]{1,0:T(8,128)(2,1)S(1)}, bf16[512,4096]{1,0:T(8,128)(2,1)}, u32[]{:S(2)}) %copy-start) | copy-done | bytes 4194328
  7.2 1.6 %copy-done.2 = bf16[512,2048]{1,0:T(8,128)(2,1)S(1)} copy-done((bf16[512,2048]{1,0:T(8,128)(2,1)S(1)}, bf16[512,2048]{1,0:T(8,128)(2,1)}, u32[]{:S(2)}) %copy-start.2) | copy-done | bytes 2097176
  9.8 3.1 %collective-permute-done.2.refs_3_ = bf16[1024,256]{1,0:T(8,128)(2,1)S(1)} collective-permute-done((bf16[1024,256]{1,0:T(8,128)(2,1)S(1)}, bf16[1024,256]{1,0:T(8,128)(2,1)S(1)}, u32[]{:S(2)}, u32[]{:S(2)}) %collective-permute-start.2) | collective-permute-done | bytes 524320 | tf_op jit(solution)/shard_map/ppermute | solution.py:349
  12.9 2.5 %collective-permute-start.5 = (bf16[1024,256]{1,0:T(8,128)(2,1)S(1)}, bf16[1024,256]{1,0:T(8,128)(2,1)S(1)}, u32[]{:S(2)}, u32[]{:S(2)}) collective-permute-start(bf16[1024,256]{1,0:T(8,128)(2,1)S(1)} %collective-permute-done.2.refs_3_), channel_id=1, source_target_pairs={{0,2},{1,5},{4,0},{5,9},{8,4},{9,13},{12,8},{13,15},{14,12},{15,11... | collective-permute-start | bytes 1572872 | tf_op jit(solution)/shard_map/ppermute | solution.py:349
  17.6 5.6 %collective-permute-done.refs_5_ = bf16[1024,256]{1,0:T(8,128)(2,1)S(1)} collective-permute-done((bf16[1024,256]{1,0:T(8,128)(2,1)S(1)}, bf16[1024,256]{1,0:T(8,128)(2,1)S(1)}, u32[]{:S(2)}, u32[]{:S(2)}) %collective-permute-start) | collective-permute-done | bytes 524320 | tf_op jit(solution)/shard_map/ppermute | solution.py:352
  24.8 2.9 %collective-permute-done.4.refs_4_ = bf16[1024,256]{1,0:T(8,128)(2,1)S(1)} collective-permute-done((bf16[1024,256]{1,0:T(8,128)(2,1)S(1)}, bf16[1024,256]{1,0:T(8,128)(2,1)S(1)}, u32[]{:S(2)}, u32[]{:S(2)}) %collective-permute-start.4) | collective-permute-done | bytes 524320 | tf_op jit(solution)/shard_map/ppermute | solution.py:355
  29.4 1.6 %shard_map.97 = (f32[1,512,256]{2,1,0:T(8,128)S(1)}, f32[512,256]{1,0:T(8,128)S(1)}, f32[1,512,256]{2,1,0:T(8,128)S(1)}, f32[512,128]{1,0:T(8,128)S(1)}) custom-call(bf16[512,2048]{1,0:T(8,128)(2,1)S(1)} %copy-done.3, bf16[512,2048]{1,0:T(8,128)(2,1)S(1)} %collective-permute-done.1.refs_0_.refs_1_, bf16[512,4096]{1,0:T(8,128)(2,1)S(1)} %copy-done.1, ...), custom_call_target="tpu_custom_call" | custom-call | flops 1000 | bytes 1000 | tf_op jit(solution)/shard_map/pallas_call | solution.py:143
  31.0 5.0 %collective-permute-done.3.refs_3_ = bf16[1024,256]{1,0:T(8,128)(2,1)S(1)} collective-permute-done((bf16[1024,256]{1,0:T(8,128)(2,1)S(1)}, bf16[1024,256]{1,0:T(8,128)(2,1)S(1)}, u32[]{:S(2)}, u32[]{:S(2)}) %collective-permute-start.3) | collective-permute-done | bytes 524320 | tf_op jit(solution)/shard_map/ppermute | solution.py:352
  36.0 3.2 %collective-permute-done.9.refs_4_ = bf16[1024,256]{1,0:T(8,128)(2,1)S(1)} collective-permute-done((bf16[1024,256]{1,0:T(8,128)(2,1)S(1)}, bf16[1024,256]{1,0:T(8,128)(2,1)S(1)}, u32[]{:S(2)}, u32[]{:S(2)}) %collective-permute-start.9) | collective-permute-done | bytes 524320 | tf_op jit(solution)/shard_map/ppermute | solution.py:355
  40.3 1.5 %collective-permute-start.13 = (bf16[1024,256]{1,0:T(8,128)(2,1)S(1)}, bf16[1024,256]{1,0:T(8,128)(2,1)S(1)}, u32[]{:S(2)}, u32[]{:S(2)}) collective-permute-start(bf16[1024,256]{1,0:T(8,128)(2,1)S(1)} %collective-permute-done.3.refs_3_), channel_id=1, source_target_pairs={{0,16},{16,0},{1,17},{17,1},{2,18},{18,2},{3,19},{19,3},{4,20},{20... | collective-permute-start | bytes 1572872 | tf_op jit(solution)/shard_map/ppermute | solution.py:355
  41.8 2.5 %shard_map.98 = (f32[2,512,256]{2,1,0:T(8,128)S(1)}, f32[512,256]{1,0:T(8,128)S(1)}, f32[512,256]{1,0:T(8,128)S(1)}, f32[1,512,256]{2,1,0:T(8,128)S(1)}, f32[512,128]{1,0:T(8,128)S(1)}) custom-call(bf16[512,2048]{1,0:T(8,128)(2,1)S(1)} %copy-done.3, bf16[512,2048]{1,0:T(8,128)(2,1)S(1)} %collective-permute-done.1.refs_0_.refs_1_, ...), custom_call_target="tpu_custom_call" | custom-call | flops 1000 | bytes 1000 | tf_op jit(solution)/shard_map/pallas_call | solution.py:143
  44.3 6.1 %collective-permute-done.7.refs_7_ = bf16[1024,256]{1,0:T(8,128)(2,1)S(1)} collective-permute-done((bf16[1024,256]{1,0:T(8,128)(2,1)S(1)}, bf16[1024,256]{1,0:T(8,128)(2,1)S(1)}, u32[]{:S(2)}, u32[]{:S(2)}) %collective-permute-start.7) | collective-permute-done | bytes 524320 | tf_op jit(solution)/shard_map/ppermute | solution.py:352
  51.4 1.4 %collective-permute-start.19 = (bf16[1024,256]{1,0:T(8,128)(2,1)S(1)}, bf16[1024,256]{1,0:T(8,128)(2,1)S(1)}, u32[]{:S(2)}, u32[]{:S(2)}) collective-permute-start(bf16[1024,256]{1,0:T(8,128)(2,1)S(1)} %collective-permute-done.14.refs_6_), channel_id=1, source_target_pairs={{0,2},{1,5},{4,0},{5,9},{8,4},{9,13},{12,8},{13,15},{14,12},{15,11... | collective-permute-start | bytes 1572872 | tf_op jit(solution)/shard_map/ppermute | solution.py:349
  52.8 1.7 %collective-permute-done.13.refs_4_ = bf16[1024,256]{1,0:T(8,128)(2,1)S(1)} collective-permute-done((bf16[1024,256]{1,0:T(8,128)(2,1)S(1)}, bf16[1024,256]{1,0:T(8,128)(2,1)S(1)}, u32[]{:S(2)}, u32[]{:S(2)}) %collective-permute-start.13) | collective-permute-done | bytes 524320 | tf_op jit(solution)/shard_map/ppermute | solution.py:355
  54.5 1.7 %collective-permute-start.18 = (bf16[1024,256]{1,0:T(8,128)(2,1)S(1)}, bf16[1024,256]{1,0:T(8,128)(2,1)S(1)}, u32[]{:S(2)}, u32[]{:S(2)}) collective-permute-start(bf16[1024,256]{1,0:T(8,128)(2,1)S(1)} %collective-permute-done.refs_5_), channel_id=1, source_target_pairs={{0,16},{16,0},{1,17},{17,1},{2,18},{18,2},{3,19},{19,3},{4,20},{20... | collective-permute-start | bytes 1572872 | tf_op jit(solution)/shard_map/ppermute | solution.py:355
  56.3 3.9 %shard_map.99 = (f32[3,512,256]{2,1,0:T(8,128)S(1)}, f32[512,256]{1,0:T(8,128)S(1)}, f32[512,256]{1,0:T(8,128)S(1)}, f32[512,256]{1,0:T(8,128)S(1)}, f32[1,512,256]{2,1,0:T(8,128)S(1)}, /*index=5*/f32[512,128]{1,0:T(8,128)S(1)}) custom-call(bf16[512,2048]{1,0:T(8,128)(2,1)S(1)} %copy-done.3, bf16[512,2048]{1,0:T(8,128)(2,1)S(1)} %collective-permute-done.1.refs_0_.refs_1_, ...), custom_call_target="tpu_custom_call" | custom-call | flops 1000 | bytes 1000 | tf_op jit(solution)/shard_map/pallas_call | solution.py:143
  60.2 5.0 %collective-permute-done.12.refs_2_ = bf16[1024,256]{1,0:T(8,128)(2,1)S(1)} collective-permute-done((bf16[1024,256]{1,0:T(8,128)(2,1)S(1)}, bf16[1024,256]{1,0:T(8,128)(2,1)S(1)}, u32[]{:S(2)}, u32[]{:S(2)}) %collective-permute-start.12) | collective-permute-done | bytes 524320 | tf_op jit(solution)/shard_map/ppermute | solution.py:352
  65.8 2.4 %collective-permute-done.18.refs_0_ = bf16[1024,256]{1,0:T(8,128)(2,1)S(1)} collective-permute-done((bf16[1024,256]{1,0:T(8,128)(2,1)S(1)}, bf16[1024,256]{1,0:T(8,128)(2,1)S(1)}, u32[]{:S(2)}, u32[]{:S(2)}) %collective-permute-start.18) | collective-permute-done | bytes 524320 | tf_op jit(solution)/shard_map/ppermute | solution.py:355
  68.1 6.2 %collective-permute-done.17.refs_1_ = bf16[1024,256]{1,0:T(8,128)(2,1)S(1)} collective-permute-done((bf16[1024,256]{1,0:T(8,128)(2,1)S(1)}, bf16[1024,256]{1,0:T(8,128)(2,1)S(1)}, u32[]{:S(2)}, u32[]{:S(2)}) %collective-permute-start.17) | collective-permute-done | bytes 524320 | tf_op jit(solution)/shard_map/ppermute | solution.py:352
  75.6 2.1 %shard_map.100 = (f32[3,512,256]{2,1,0:T(8,128)S(1)}, f32[512,128]{1,0:T(8,128)S(1)}) custom-call(bf16[512,2048]{1,0:T(8,128)(2,1)S(1)} %copy-done.3, bf16[512,4096]{1,0:T(8,128)(2,1)S(1)} %copy-done.1, f32[512,128]{1,0:T(8,128)S(1)} %get-tuple-element.115.before, bf16[1024,256]{1,0:T(8,128)(2,1)S(1)} %collective-permute-done.18.refs_0_, ...), custom_call_target="tpu_custom_call" | custom-call | flops 1000 | bytes 1000 | tf_op jit(solution)/shard_map/pallas_call | solution.py:179
  77.8 4.0 %shard_map.101 = (f32[1,4096]{1,0:T(1,128)}, bf16[8,48,128]{2,1,0:T(8,128)(2,1)S(1)}) custom-call(s32[1]{0:T(128)S(6)} %copy.10.length, bf16[512,2048]{1,0:T(8,128)(2,1)S(1)} %copy-done.3, bf16[512,4096]{1,0:T(8,128)(2,1)S(1)} %copy-done.1, f32[512,128]{1,0:T(8,128)S(1)} %get-tuple-element.127.before, f32[1,4096]{1,0:T(1,128)S(1)} %bitcast.2, ...), custom_call_target="tpu_custom_call" | custom-call | flops 1000 | bytes 1000 | tf_op jit(solution)/shard_map/pallas_call | solution.py:232
  81.9 11.4 %all_to_all.10.got = bf16[8,48,128]{2,1,0:T(8,128)(2,1)S(1)} all-to-all(bf16[8,48,128]{2,1,0:T(8,128)(2,1)S(1)} %get-tuple-element.139), channel_id=1, replica_groups={{0,2,4,6,8,10,12,14},{1,3,5,7,9,11,13,15},{16,18,20,22,24,26,28,30},{17..., dimensions={0} | all-to-all | bytes 196608 | tf_op jit(solution)/shard_map/all_to_all | solution.py:459
  94.3 10.0 %all_to_all.11.got = f32[8,40,128]{2,1,0:T(8,128)S(1)} all-to-all(f32[8,40,128]{2,1,0:T(8,128)S(1)} %shard_map.102), channel_id=1, replica_groups={{0,2,4,6,8,10,12,14},{1,3,5,7,9,11,13,15},{16,18,20,22,24,26,28,30},{17..., dimensions={0} | all-to-all | bytes 327680 | tf_op jit(solution)/shard_map/all_to_all | solution.py:459
  (60 shorter events, 13.5 us)
Async XLA Ops:
  0.6 16.1 %collective-permute-start.1 = (bf16[512,2048]{1,0:T(8,128)(2,1)}, bf16[512,2048]{1,0:T(8,128)(2,1)S(1)}, u32[]{:S(2)}, u32[]{:S(2)}) collective-permute-start(bf16[512,2048]{1,0:T(8,128)(2,1)} %context.3), channel_id=1, source_target_pairs={{0,1},{1,0},{2,3},{3,2},{4,5},{5,4},{6,7},{7,6},{8,9},{9,8},{10,11... | collective-permute-start | bytes 6291464 | tf_op jit(solution)/shard_map/ppermute | solution.py:358
  2.4 10.5 %collective-permute-start.2 = (bf16[1024,256]{1,0:T(8,128)(2,1)S(1)}, bf16[1024,256]{1,0:T(8,128)(2,1)S(1)}, u32[]{:S(2)}, u32[]{:S(2)}) collective-permute-start(bf16[1024,256]{1,0:T(8,128)(2,1)S(1)} %shard_map.94), channel_id=1, source_target_pairs={{0,2},{1,5},{4,0},{5,9},{8,4},{9,13},{12,8},{13,15},{14,12},{15,11... | collective-permute-start | bytes 1572872 | tf_op jit(solution)/shard_map/ppermute | solution.py:349
  9.7 13.5 %collective-permute-start = (bf16[1024,256]{1,0:T(8,128)(2,1)S(1)}, bf16[1024,256]{1,0:T(8,128)(2,1)S(1)}, u32[]{:S(2)}, u32[]{:S(2)}) collective-permute-start(bf16[1024,256]{1,0:T(8,128)(2,1)S(1)} %shard_map.94), channel_id=1, source_target_pairs={{0,4},{1,3},{4,8},{5,1},{8,12},{9,5},{12,14},{13,9},{14,10},{15,13... | collective-permute-start | bytes 1572872 | tf_op jit(solution)/shard_map/ppermute | solution.py:352
  12.9 11.0 %collective-permute-start.5 = (bf16[1024,256]{1,0:T(8,128)(2,1)S(1)}, bf16[1024,256]{1,0:T(8,128)(2,1)S(1)}, u32[]{:S(2)}, u32[]{:S(2)}) collective-permute-start(bf16[1024,256]{1,0:T(8,128)(2,1)S(1)} %collective-permute-done.2.refs_3_), channel_id=1, source_target_pairs={{0,2},{1,5},{4,0},{5,9},{8,4},{9,13},{12,8},{13,15},{14,12},{15,11... | collective-permute-start | bytes 1572872 | tf_op jit(solution)/shard_map/ppermute | solution.py:349
  15.4 12.3 %collective-permute-start.4 = (bf16[1024,256]{1,0:T(8,128)(2,1)S(1)}, bf16[1024,256]{1,0:T(8,128)(2,1)S(1)}, u32[]{:S(2)}, u32[]{:S(2)}) collective-permute-start(bf16[1024,256]{1,0:T(8,128)(2,1)S(1)} %collective-permute-done.2.refs_3_), channel_id=1, source_target_pairs={{0,16},{16,0},{1,17},{17,1},{2,18},{18,2},{3,19},{19,3},{4,20},{20... | collective-permute-start | bytes 1572872 | tf_op jit(solution)/shard_map/ppermute | solution.py:355
  23.2 6.2 %collective-permute-start.6 = (f32[512,256]{1,0:T(8,128)S(1)}, f32[512,256]{1,0:T(8,128)S(1)}, u32[]{:S(2)}, u32[]{:S(2)}) collective-permute-start(f32[512,256]{1,0:T(8,128)S(1)} %shard_map.96), channel_id=1, source_target_pairs={{0,1},{1,0},{2,3},{3,2},{4,5},{5,4},{6,7},{7,6},{8,9},{9,8},{10,11... | collective-permute-start | bytes 1572872 | tf_op jit(solution)/shard_map/ppermute | solution.py:358
  23.2 12.8 %collective-permute-start.3 = (bf16[1024,256]{1,0:T(8,128)(2,1)S(1)}, bf16[1024,256]{1,0:T(8,128)(2,1)S(1)}, u32[]{:S(2)}, u32[]{:S(2)}) collective-permute-start(bf16[1024,256]{1,0:T(8,128)(2,1)S(1)} %collective-permute-done.refs_5_), channel_id=1, source_target_pairs={{0,4},{1,3},{4,8},{5,1},{8,12},{9,5},{12,14},{13,9},{14,10},{15,13... | collective-permute-start | bytes 1572872 | tf_op jit(solution)/shard_map/ppermute | solution.py:352
  23.9 15.3 %collective-permute-start.10 = (bf16[112,4096]{1,0:T(8,128)(2,1)S(1)}, bf16[112,4096]{1,0:T(8,128)(2,1)S(1)}, u32[]{:S(2)}, u32[]{:S(2)}) collective-permute-start(bf16[112,4096]{1,0:T(8,128)(2,1)S(1)} %copy-done.5), channel_id=1, source_target_pairs={{0,1},{1,0},{2,3},{3,2},{4,5},{5,4},{6,7},{7,6},{8,9},{9,8},{10,11... | collective-permute-start | bytes 2752520 | tf_op jit(solution)/shard_map/ppermute | solution.py:358
  27.7 11.4 %collective-permute-start.9 = (bf16[1024,256]{1,0:T(8,128)(2,1)S(1)}, bf16[1024,256]{1,0:T(8,128)(2,1)S(1)}, u32[]{:S(2)}, u32[]{:S(2)}) collective-permute-start(bf16[1024,256]{1,0:T(8,128)(2,1)S(1)} %collective-permute-done.5.refs_3_), channel_id=1, source_target_pairs={{0,16},{16,0},{1,17},{17,1},{2,18},{18,2},{3,19},{19,3},{4,20},{20... | collective-permute-start | bytes 1572872 | tf_op jit(solution)/shard_map/ppermute | solution.py:355
  28.9 11.4 %collective-permute-start.8 = (bf16[1024,256]{1,0:T(8,128)(2,1)S(1)}, bf16[1024,256]{1,0:T(8,128)(2,1)S(1)}, u32[]{:S(2)}, u32[]{:S(2)}) collective-permute-start(bf16[1024,256]{1,0:T(8,128)(2,1)S(1)} %collective-permute-done.5.refs_3_), channel_id=1, source_target_pairs={{0,2},{1,5},{4,0},{5,9},{8,4},{9,13},{12,8},{13,15},{14,12},{15,11... | collective-permute-start | bytes 1572872 | tf_op jit(solution)/shard_map/ppermute | solution.py:349
  36.0 5.8 %collective-permute-start.11 = (f32[512,256]{1,0:T(8,128)S(1)}, f32[512,256]{1,0:T(8,128)S(1)}, u32[]{:S(2)}, u32[]{:S(2)}) collective-permute-start(f32[512,256]{1,0:T(8,128)S(1)} %get-tuple-element.96), channel_id=1, source_target_pairs={{0,1},{1,0},{2,3},{3,2},{4,5},{5,4},{6,7},{7,6},{8,9},{9,8},{10,11... | collective-permute-start | bytes 1572872 | tf_op jit(solution)/shard_map/ppermute | solution.py:358
  36.0 14.4 %collective-permute-start.7 = (bf16[1024,256]{1,0:T(8,128)(2,1)S(1)}, bf16[1024,256]{1,0:T(8,128)(2,1)S(1)}, u32[]{:S(2)}, u32[]{:S(2)}) collective-permute-start(bf16[1024,256]{1,0:T(8,128)(2,1)S(1)} %collective-permute-done.3.refs_3_), channel_id=1, source_target_pairs={{0,4},{1,3},{4,8},{5,1},{8,12},{9,5},{12,14},{13,9},{14,10},{15,13... | collective-permute-start | bytes 1572872 | tf_op jit(solution)/shard_map/ppermute | solution.py:352
  39.1 12.2 %collective-permute-start.14 = (bf16[1024,256]{1,0:T(8,128)(2,1)S(1)}, bf16[1024,256]{1,0:T(8,128)(2,1)S(1)}, u32[]{:S(2)}, u32[]{:S(2)}) collective-permute-start(bf16[1024,256]{1,0:T(8,128)(2,1)S(1)} %collective-permute-done.9.refs_4_), channel_id=1, source_target_pairs={{0,2},{1,5},{4,0},{5,9},{8,4},{9,13},{12,8},{13,15},{14,12},{15,11... | collective-permute-start | bytes 1572872 | tf_op jit(solution)/shard_map/ppermute | solution.py:349
  40.3 14.2 %collective-permute-start.13 = (bf16[1024,256]{1,0:T(8,128)(2,1)S(1)}, bf16[1024,256]{1,0:T(8,128)(2,1)S(1)}, u32[]{:S(2)}, u32[]{:S(2)}) collective-permute-start(bf16[1024,256]{1,0:T(8,128)(2,1)S(1)} %collective-permute-done.3.refs_3_), channel_id=1, source_target_pairs={{0,16},{16,0},{1,17},{17,1},{2,18},{18,2},{3,19},{19,3},{4,20},{20... | collective-permute-start | bytes 1572872 | tf_op jit(solution)/shard_map/ppermute | solution.py:355
  50.4 5.9 %collective-permute-start.15 = (f32[512,256]{1,0:T(8,128)S(1)}, f32[512,256]{1,0:T(8,128)S(1)}, u32[]{:S(2)}, u32[]{:S(2)}) collective-permute-start(f32[512,256]{1,0:T(8,128)S(1)} %get-tuple-element.108), channel_id=1, source_target_pairs={{0,1},{1,0},{2,3},{3,2},{4,5},{5,4},{6,7},{7,6},{8,9},{9,8},{10,11... | collective-permute-start | bytes 1572872 | tf_op jit(solution)/shard_map/ppermute | solution.py:358
  50.4 14.8 %collective-permute-start.12 = (bf16[1024,256]{1,0:T(8,128)(2,1)S(1)}, bf16[1024,256]{1,0:T(8,128)(2,1)S(1)}, u32[]{:S(2)}, u32[]{:S(2)}) collective-permute-start(bf16[1024,256]{1,0:T(8,128)(2,1)S(1)} %collective-permute-done.7.refs_7_), channel_id=1, source_target_pairs={{0,4},{1,3},{4,8},{5,1},{8,12},{9,5},{12,14},{13,9},{14,10},{15,13... | collective-permute-start | bytes 1572872 | tf_op jit(solution)/shard_map/ppermute | solution.py:352
  50.4 14.8 %collective-permute-start.16 = (f32[512,256]{1,0:T(8,128)S(1)}, f32[512,256]{1,0:T(8,128)S(1)}, u32[]{:S(2)}, u32[]{:S(2)}) collective-permute-start(f32[512,256]{1,0:T(8,128)S(1)} %get-tuple-element.114), channel_id=1, source_target_pairs={{0,1},{1,0},{2,3},{3,2},{4,5},{5,4},{6,7},{7,6},{8,9},{9,8},{10,11... | collective-permute-start | bytes 1572872 | tf_op jit(solution)/shard_map/ppermute | solution.py:358
  51.4 14.3 %collective-permute-start.19 = (bf16[1024,256]{1,0:T(8,128)(2,1)S(1)}, bf16[1024,256]{1,0:T(8,128)(2,1)S(1)}, u32[]{:S(2)}, u32[]{:S(2)}) collective-permute-start(bf16[1024,256]{1,0:T(8,128)(2,1)S(1)} %collective-permute-done.14.refs_6_), channel_id=1, source_target_pairs={{0,2},{1,5},{4,0},{5,9},{8,4},{9,13},{12,8},{13,15},{14,12},{15,11... | collective-permute-start | bytes 1572872 | tf_op jit(solution)/shard_map/ppermute | solution.py:349
  54.5 13.6 %collective-permute-start.18 = (bf16[1024,256]{1,0:T(8,128)(2,1)S(1)}, bf16[1024,256]{1,0:T(8,128)(2,1)S(1)}, u32[]{:S(2)}, u32[]{:S(2)}) collective-permute-start(bf16[1024,256]{1,0:T(8,128)(2,1)S(1)} %collective-permute-done.refs_5_), channel_id=1, source_target_pairs={{0,16},{16,0},{1,17},{17,1},{2,18},{18,2},{3,19},{19,3},{4,20},{20... | collective-permute-start | bytes 1572872 | tf_op jit(solution)/shard_map/ppermute | solution.py:355
  65.2 9.2 %collective-permute-start.17 = (bf16[1024,256]{1,0:T(8,128)(2,1)S(1)}, bf16[1024,256]{1,0:T(8,128)(2,1)S(1)}, u32[]{:S(2)}, u32[]{:S(2)}) collective-permute-start(bf16[1024,256]{1,0:T(8,128)(2,1)S(1)} %collective-permute-done.13.refs_4_), channel_id=1, source_target_pairs={{0,4},{1,3},{4,8},{5,1},{8,12},{9,5},{12,14},{13,9},{14,10},{15,13... | collective-permute-start | bytes 1572872 | tf_op jit(solution)/shard_map/ppermute | solution.py:352
  65.2 9.2 %collective-permute-start.22 = (bf16[1024,256]{1,0:T(8,128)(2,1)S(1)}, bf16[1024,256]{1,0:T(8,128)(2,1)S(1)}, u32[]{:S(2)}, u32[]{:S(2)}) collective-permute-start(bf16[1024,256]{1,0:T(8,128)(2,1)S(1)} %collective-permute-done.12.refs_2_), channel_id=1, source_target_pairs={{0,1},{1,0},{2,3},{3,2},{4,5},{5,4},{6,7},{7,6},{8,9},{9,8},{10,11... | collective-permute-start | bytes 1572872 | tf_op jit(solution)/shard_map/ppermute | solution.py:358
  65.2 9.7 %collective-permute-start.24 = (f32[512,256]{1,0:T(8,128)S(1)}, f32[512,256]{1,0:T(8,128)S(1)}, u32[]{:S(2)}, u32[]{:S(2)}) collective-permute-start(f32[512,256]{1,0:T(8,128)S(1)} %get-tuple-element.135), channel_id=1, source_target_pairs={{0,1},{1,0},{2,3},{3,2},{4,5},{5,4},{6,7},{7,6},{8,9},{9,8},{10,11... | collective-permute-start | bytes 1572872 | tf_op jit(solution)/shard_map/ppermute | solution.py:358
  65.7 12.1 %collective-permute-start.25 = (f32[512,256]{1,0:T(8,128)S(1)}, f32[512,256]{1,0:T(8,128)S(1)}, u32[]{:S(2)}, u32[]{:S(2)}) collective-permute-start(f32[512,256]{1,0:T(8,128)S(1)} %get-tuple-element.136), channel_id=1, source_target_pairs={{0,1},{1,0},{2,3},{3,2},{4,5},{5,4},{6,7},{7,6},{8,9},{9,8},{10,11... | collective-permute-start | bytes 1572872 | tf_op jit(solution)/shard_map/ppermute | solution.py:358
  68.1 9.6 %collective-permute-start.26 = (f32[512,256]{1,0:T(8,128)S(1)}, f32[512,256]{1,0:T(8,128)S(1)}, u32[]{:S(2)}, u32[]{:S(2)}) collective-permute-start(f32[512,256]{1,0:T(8,128)S(1)} %get-tuple-element.137), channel_id=1, source_target_pairs={{0,1},{1,0},{2,3},{3,2},{4,5},{5,4},{6,7},{7,6},{8,9},{9,8},{10,11... | collective-permute-start | bytes 1572872 | tf_op jit(solution)/shard_map/ppermute | solution.py:358
  (11 other events, 96.0 us)

commit v8 on v7

--- a/solution.py
+++ b/solution.py
@@ -362,55 +362,54 @@
     own = own_half(out_proj)
     a = from_next(own)
     c = other_core(context)
+    q = other_core(queries)
     h0, sq0 = wave((0,), (), (), context, None, residual, [out_proj])
     own, h0, sq0 = wait((own, h0, sq0))
     b = from_last(own)
 
     n1, sq0 = wait((a, sq0))
-    x = over_x(n1)
+    x1 = over_x(n1)
     a = from_next(n1)
     context2, n1 = wait((c, n1))
     (t0,) = wave((0,), (), (), None, context2, None, [out_proj])
-    l1, n1, t0 = wait((b, n1, t0))
+    l1, n1, t0, queries2 = wait((b, n1, t0, q))
     b = from_last(l1)
     r0 = other_core(t0)
 
-    n2, l1, queries = wait((a, l1, queries))
-    queries2 = other_core(queries)
-    xn1, n2 = wait((x, n2))
-    x = over_x(n2)
+    n2, l1 = wait((a, l1))
+    x2 = over_x(n2)
     a = from_next(n2)
+    xn1, n2 = wait((x1, n2))
     h1, t1, f0, sq1 = wave((1,), (), (0,), context, context2, residual, [n1, xn1], [r0], sq0)
     l2, n2, t1, sq1 = wait((b, n2, t1, sq1))
     b = from_last(l2)
+    x3 = over_x(l2)
     r1 = other_core(t1)
 
-    xn2, l2, queries2 = wait((x, l2, queries2))
-    x = over_x(l2)
-    a2 = from_next(xn2)
-    n3, xn2 = wait((a, xn2))
+    n3, l2 = wait((a, l2))
+    xn2, l2, n3 = wait((x2, l2, n3))
+    a = from_next(xn2)
     h2, t2, t2p, f1, sq2 = wave((2,), (-1,), (1,), context, context2, residual, [n2, xn2, l1], [r1], sq1)
     l3, n3, t2, t2p, sq2 = wait((b, n3, t2, t2p, sq2))
     b = from_last(l3)
     r2, r2p = other_core(t2), other_core(t2p)
 
-    n3x, l3 = wait((a2, l3))
+    n3x, l3 = wait((a, l3))
     a = from_next(n3x)
-    xl2, l1, n3x = wait((x, l1, n3x))
-    x = over_x(l1)
+    xl2, l1, n3x = wait((x3, l1, n3x))
+    x4 = over_x(l1)
     h3, t3a, t3b, t3p, f2, sq3 = wave(
         (-2, 3), (-3,), (2,), context, context2, residual, [l2, xl2, n3, n3x, l3], [r2], sq2
     )
     l4, xl2, t3a, t3b, t3p, sq3, r2p = wait((b, xl2, t3a, t3b, t3p, sq3, r2p))
-    b = from_last(xl2)
+    b2 = from_last(xl2)
+    l4s = other_core(l4)
     r3a, r3b, r3p = other_core(t3a), other_core(t3b), other_core(t3p)
-    l4s = other_core(l4)
-
     n4x, l4 = wait((a, l4))
     n4xs = other_core(n4x)
-    xl1, n4x = wait((x, n4x))
+    xl1, n4x, r3a, r3b = wait((x4, n4x, r3a, r3b))
     xl1s = other_core(xl1)
-    l3x, xl1 = wait((b, xl1))
+    l3x, xl1, r3p, l4s = wait((b2, xl1, r3p, l4s))
     l3xs = other_core(l3x)
 
     missing = (((0, True),), ((1, True),), ((2, False), (3, True)))

time: 105 us -> 108 us (1.029)
  starting transfers between devices: 17.6 us -> 19.7 us
    ppermute x5, waiting for transfers between devices: 27.8 us -> 38.7 us  [from_last(): return lax.ppermute(piece, 'dp', ring(1))]
    ppermute x4, waiting for transfers between devices: 10.2 us -> 2.08 us  [over_x(): return lax.ppermute(piece, 'groups', [(0, 1), (1, 0)])]
    ppermute x5, starting transfers between devices: 0.13 us -> 4.6 us  [from_last(): return lax.ppermute(piece, 'dp', ring(1))]
    ppermute x5, waiting for transfers between devices: 3.74 us -> 0.62 us  [from_next(): return lax.ppermute(piece, 'dp', ring(-1))]
    ppermute x13, starting transfers between devices: 3.6 us -> 2.06 us  [other_core(): return lax.ppermute(piece, 'dp', [(i, i ^ 1) for i in range(ranks)])]
  transfers between devices with their start and end apart: 27 -> 27, of which waited for: 11 -> 12; matrix products, arithmetic and copies ran while one was open for 0% -> 0% of each run, Pallas kernels for 11% -> 11%
where the time goes in v8:
time: 108 us
  waiting for transfers between devices  42.4 us (39%)
  blocking collectives  21.3 us (20%)
  starting transfers between devices  19.7 us (18%)
  Pallas kernels  17.9 us (17%)
  local copies, waits for them, and re-layouts  5.03 us (5%)
  between operations  1.44 us (1%)
    ppermute x5, waiting for transfers between devices, from_last(): return lax.ppermute(piece, 'dp', ring(1))  38.7 us
    all_to_all x2, blocking collectives, spread(): lax.all_to_all(blocks, 'dp', 0, 0, axis_index_groups=same_core, tiled=True)  21.3 us
    pallas_call x5, Pallas kernels, wave(): pl.pallas_call(functools.partial(wave_kernel, full, part, arrived, whole,...  9.76 us
    ppermute x5, starting transfers between devices, from_next(): return lax.ppermute(piece, 'dp', ring(-1))  7.21 us
    ppermute x4, starting transfers between devices, over_x(): return lax.ppermute(piece, 'groups', [(0, 1), (1, 0)])  5.87 us
    unnamed x16, local copies, waits for them, and re-layouts  5.03 us
    ppermute x5, starting transfers between devices, from_last(): return lax.ppermute(piece, 'dp', ring(1))  4.6 us
    pallas_call x1, Pallas kernels, finish(): pl.pallas_call(functools.partial(final_kernel, items, sources, len(pieces...  4.05 us
  transfers between devices with their start and end apart: 27, of which 12 were waited for; matrix products, arithmetic and copies ran while one was open for 0% of the time, Pallas kernels for 11%

profile of v8, /device:TPU:0, one launch (start us, length us, event | category | flops | bytes accessed | tf_op | source)
XLA Modules:
  0.0 107.8 jit_solution(18337512984835495180)
XLA Ops:
  1.1 1.2 %copy-done.4 = bf16[2048,256]{1,0:T(8,128)(2,1)S(1)} copy-done((bf16[2048,256]{1,0:T(8,128)(2,1)S(1)}, bf16[2048,256]{1,0:T(8,128)(2,1)}, u32[]{:S(2)}) %copy-start.4) | copy-done | bytes 1048600
  2.4 2.6 %collective-permute-start.2 = (bf16[1024,256]{1,0:T(8,128)(2,1)S(1)}, bf16[1024,256]{1,0:T(8,128)(2,1)S(1)}, u32[]{:S(2)}, u32[]{:S(2)}) collective-permute-start(bf16[1024,256]{1,0:T(8,128)(2,1)S(1)} %shard_map.94), channel_id=1, source_target_pairs={{0,2},{1,5},{4,0},{5,9},{8,4},{9,13},{12,8},{13,15},{14,12},{15,11... | collective-permute-start | bytes 1572872 | tf_op jit(solution)/shard_map/ppermute | solution.py:349
  5.3 2.2 %copy-done = bf16[512,4096]{1,0:T(8,128)(2,1)S(1)} copy-done((bf16[512,4096]{1,0:T(8,128)(2,1)S(1)}, bf16[512,4096]{1,0:T(8,128)(2,1)}, u32[]{:S(2)}) %copy-start) | copy-done | bytes 4194328
  7.5 1.6 %copy-done.2 = bf16[512,2048]{1,0:T(8,128)(2,1)S(1)} copy-done((bf16[512,2048]{1,0:T(8,128)(2,1)S(1)}, bf16[512,2048]{1,0:T(8,128)(2,1)}, u32[]{:S(2)}) %copy-start.2) | copy-done | bytes 2097176
  10.0 1.6 %collective-permute-start = (bf16[1024,256]{1,0:T(8,128)(2,1)S(1)}, bf16[1024,256]{1,0:T(8,128)(2,1)S(1)}, u32[]{:S(2)}, u32[]{:S(2)}) collective-permute-start(bf16[1024,256]{1,0:T(8,128)(2,1)S(1)} %shard_map.94), channel_id=1, source_target_pairs={{0,4},{1,3},{4,8},{5,1},{8,12},{9,5},{12,14},{13,9},{14,10},{15,13... | collective-permute-start | bytes 1572872 | tf_op jit(solution)/shard_map/ppermute | solution.py:352
  12.2 2.0 %collective-permute-start.6 = (bf16[1024,256]{1,0:T(8,128)(2,1)S(1)}, bf16[1024,256]{1,0:T(8,128)(2,1)S(1)}, u32[]{:S(2)}, u32[]{:S(2)}) collective-permute-start(bf16[1024,256]{1,0:T(8,128)(2,1)S(1)} %collective-permute-done.2.refs_3_), channel_id=1, source_target_pairs={{0,2},{1,5},{4,0},{5,9},{8,4},{9,13},{12,8},{13,15},{14,12},{15,11... | collective-permute-start | bytes 1572872 | tf_op jit(solution)/shard_map/ppermute | solution.py:349
  14.2 1.5 %collective-permute-start.5 = (bf16[1024,256]{1,0:T(8,128)(2,1)S(1)}, bf16[1024,256]{1,0:T(8,128)(2,1)S(1)}, u32[]{:S(2)}, u32[]{:S(2)}) collective-permute-start(bf16[1024,256]{1,0:T(8,128)(2,1)S(1)} %collective-permute-done.2.refs_3_), channel_id=1, source_target_pairs={{0,16},{16,0},{1,17},{17,1},{2,18},{18,2},{3,19},{19,3},{4,20},{20... | collective-permute-start | bytes 1572872 | tf_op jit(solution)/shard_map/ppermute | solution.py:355
  16.6 7.1 %collective-permute-done.refs_5_ = bf16[1024,256]{1,0:T(8,128)(2,1)S(1)} collective-permute-done((bf16[1024,256]{1,0:T(8,128)(2,1)S(1)}, bf16[1024,256]{1,0:T(8,128)(2,1)S(1)}, u32[]{:S(2)}, u32[]{:S(2)}) %collective-permute-start) | collective-permute-done | bytes 524320 | tf_op jit(solution)/shard_map/ppermute | solution.py:352
  23.7 1.3 %collective-permute-start.4 = (bf16[1024,256]{1,0:T(8,128)(2,1)S(1)}, bf16[1024,256]{1,0:T(8,128)(2,1)S(1)}, u32[]{:S(2)}, u32[]{:S(2)}) collective-permute-start(bf16[1024,256]{1,0:T(8,128)(2,1)S(1)} %collective-permute-done.refs_5_), channel_id=1, source_target_pairs={{0,4},{1,3},{4,8},{5,1},{8,12},{9,5},{12,14},{13,9},{14,10},{15,13... | collective-permute-start | bytes 1572872 | tf_op jit(solution)/shard_map/ppermute | solution.py:352
  25.8 1.4 %collective-permute-start.9 = (bf16[1024,256]{1,0:T(8,128)(2,1)S(1)}, bf16[1024,256]{1,0:T(8,128)(2,1)S(1)}, u32[]{:S(2)}, u32[]{:S(2)}) collective-permute-start(bf16[1024,256]{1,0:T(8,128)(2,1)S(1)} %collective-permute-done.6.refs_3_), channel_id=1, source_target_pairs={{0,16},{16,0},{1,17},{17,1},{2,18},{18,2},{3,19},{19,3},{4,20},{20... | collective-permute-start | bytes 1572872 | tf_op jit(solution)/shard_map/ppermute | solution.py:355
  27.4 1.6 %shard_map.97 = (f32[1,512,256]{2,1,0:T(8,128)S(1)}, f32[512,256]{1,0:T(8,128)S(1)}, f32[1,512,256]{2,1,0:T(8,128)S(1)}, f32[512,128]{1,0:T(8,128)S(1)}) custom-call(bf16[512,2048]{1,0:T(8,128)(2,1)S(1)} %copy-done.3, bf16[512,2048]{1,0:T(8,128)(2,1)S(1)} %collective-permute-done.1.refs_0_.refs_1_, bf16[512,4096]{1,0:T(8,128)(2,1)S(1)} %copy-done.1, ...), custom_call_target="tpu_custom_call" | custom-call | flops 1000 | bytes 1000 | tf_op jit(solution)/shard_map/pallas_call | solution.py:143
  29.0 9.3 %collective-permute-done.4.refs_3_ = bf16[1024,256]{1,0:T(8,128)(2,1)S(1)} collective-permute-done((bf16[1024,256]{1,0:T(8,128)(2,1)S(1)}, bf16[1024,256]{1,0:T(8,128)(2,1)S(1)}, u32[]{:S(2)}, u32[]{:S(2)}) %collective-permute-start.4) | collective-permute-done | bytes 524320 | tf_op jit(solution)/shard_map/ppermute | solution.py:352
  40.5 1.5 %collective-permute-start.13 = (bf16[1024,256]{1,0:T(8,128)(2,1)S(1)}, bf16[1024,256]{1,0:T(8,128)(2,1)S(1)}, u32[]{:S(2)}, u32[]{:S(2)}) collective-permute-start(bf16[1024,256]{1,0:T(8,128)(2,1)S(1)} %collective-permute-done.4.refs_3_), channel_id=1, source_target_pairs={{0,16},{16,0},{1,17},{17,1},{2,18},{18,2},{3,19},{19,3},{4,20},{20... | collective-permute-start | bytes 1572872 | tf_op jit(solution)/shard_map/ppermute | solution.py:355
  42.0 2.5 %shard_map.98 = (f32[2,512,256]{2,1,0:T(8,128)S(1)}, f32[512,256]{1,0:T(8,128)S(1)}, f32[512,256]{1,0:T(8,128)S(1)}, f32[1,512,256]{2,1,0:T(8,128)S(1)}, f32[512,128]{1,0:T(8,128)S(1)}) custom-call(bf16[512,2048]{1,0:T(8,128)(2,1)S(1)} %copy-done.3, bf16[512,2048]{1,0:T(8,128)(2,1)S(1)} %collective-permute-done.1.refs_0_.refs_1_, ...), custom_call_target="tpu_custom_call" | custom-call | flops 1000 | bytes 1000 | tf_op jit(solution)/shard_map/pallas_call | solution.py:143
  44.5 8.2 %collective-permute-done.8.refs_7_ = bf16[1024,256]{1,0:T(8,128)(2,1)S(1)} collective-permute-done((bf16[1024,256]{1,0:T(8,128)(2,1)S(1)}, bf16[1024,256]{1,0:T(8,128)(2,1)S(1)}, u32[]{:S(2)}, u32[]{:S(2)}) %collective-permute-start.8) | collective-permute-done | bytes 524320 | tf_op jit(solution)/shard_map/ppermute | solution.py:352
  53.2 1.5 %collective-permute-start.19 = (bf16[1024,256]{1,0:T(8,128)(2,1)S(1)}, bf16[1024,256]{1,0:T(8,128)(2,1)S(1)}, u32[]{:S(2)}, u32[]{:S(2)}) collective-permute-start(bf16[1024,256]{1,0:T(8,128)(2,1)S(1)} %collective-permute-done.14.refs_6_), channel_id=1, source_target_pairs={{0,2},{1,5},{4,0},{5,9},{8,4},{9,13},{12,8},{13,15},{14,12},{15,11... | collective-permute-start | bytes 1572872 | tf_op jit(solution)/shard_map/ppermute | solution.py:349
  55.1 1.5 %collective-permute-start.18 = (bf16[1024,256]{1,0:T(8,128)(2,1)S(1)}, bf16[1024,256]{1,0:T(8,128)(2,1)S(1)}, u32[]{:S(2)}, u32[]{:S(2)}) collective-permute-start(bf16[1024,256]{1,0:T(8,128)(2,1)S(1)} %collective-permute-done.refs_5_), channel_id=1, source_target_pairs={{0,16},{16,0},{1,17},{17,1},{2,18},{18,2},{3,19},{19,3},{4,20},{20... | collective-permute-start | bytes 1572872 | tf_op jit(solution)/shard_map/ppermute | solution.py:355
  56.5 3.9 %shard_map.99 = (f32[3,512,256]{2,1,0:T(8,128)S(1)}, f32[512,256]{1,0:T(8,128)S(1)}, f32[512,256]{1,0:T(8,128)S(1)}, f32[512,256]{1,0:T(8,128)S(1)}, f32[1,512,256]{2,1,0:T(8,128)S(1)}, /*index=5*/f32[512,128]{1,0:T(8,128)S(1)}) custom-call(bf16[512,2048]{1,0:T(8,128)(2,1)S(1)} %copy-done.3, bf16[512,2048]{1,0:T(8,128)(2,1)S(1)} %collective-permute-done.1.refs_0_.refs_1_, ...), custom_call_target="tpu_custom_call" | custom-call | flops 1000 | bytes 1000 | tf_op jit(solution)/shard_map/pallas_call | solution.py:143
  60.5 7.0 %collective-permute-done.12.refs_2_ = bf16[1024,256]{1,0:T(8,128)(2,1)S(1)} collective-permute-done((bf16[1024,256]{1,0:T(8,128)(2,1)S(1)}, bf16[1024,256]{1,0:T(8,128)(2,1)S(1)}, u32[]{:S(2)}, u32[]{:S(2)}) %collective-permute-start.12) | collective-permute-done | bytes 524320 | tf_op jit(solution)/shard_map/ppermute | solution.py:352
  70.1 7.0 %collective-permute-done.17.refs_1_ = bf16[1024,256]{1,0:T(8,128)(2,1)S(1)} collective-permute-done((bf16[1024,256]{1,0:T(8,128)(2,1)S(1)}, bf16[1024,256]{1,0:T(8,128)(2,1)S(1)}, u32[]{:S(2)}, u32[]{:S(2)}) %collective-permute-start.17) | collective-permute-done | bytes 524320 | tf_op jit(solution)/shard_map/ppermute | solution.py:352
  78.4 2.1 %shard_map.100 = (f32[3,512,256]{2,1,0:T(8,128)S(1)}, f32[512,128]{1,0:T(8,128)S(1)}) custom-call(bf16[512,2048]{1,0:T(8,128)(2,1)S(1)} %copy-done.3, bf16[512,4096]{1,0:T(8,128)(2,1)S(1)} %copy-done.1, f32[512,128]{1,0:T(8,128)S(1)} %get-tuple-element.119.before, bf16[1024,256]{1,0:T(8,128)(2,1)S(1)} %collective-permute-done.18.refs_0_, ...), custom_call_target="tpu_custom_call" | custom-call | flops 1000 | bytes 1000 | tf_op jit(solution)/shard_map/pallas_call | solution.py:179
  80.6 4.0 %shard_map.101 = (f32[1,4096]{1,0:T(1,128)}, bf16[8,48,128]{2,1,0:T(8,128)(2,1)S(1)}) custom-call(s32[1]{0:T(128)S(6)} %copy.10.length, bf16[512,2048]{1,0:T(8,128)(2,1)S(1)} %copy-done.3, bf16[512,4096]{1,0:T(8,128)(2,1)S(1)} %copy-done.1, f32[512,128]{1,0:T(8,128)S(1)} %get-tuple-element.134.before, f32[1,4096]{1,0:T(1,128)S(1)} %bitcast.2, ...), custom_call_target="tpu_custom_call" | custom-call | flops 1000 | bytes 1000 | tf_op jit(solution)/shard_map/pallas_call | solution.py:232
  84.6 11.3 %all_to_all.10.got = bf16[8,48,128]{2,1,0:T(8,128)(2,1)S(1)} all-to-all(bf16[8,48,128]{2,1,0:T(8,128)(2,1)S(1)} %get-tuple-element.147), channel_id=1, replica_groups={{0,2,4,6,8,10,12,14},{1,3,5,7,9,11,13,15},{16,18,20,22,24,26,28,30},{17..., dimensions={0} | all-to-all | bytes 196608 | tf_op jit(solution)/shard_map/all_to_all | solution.py:458
  97.1 10.0 %all_to_all.11.got = f32[8,40,128]{2,1,0:T(8,128)S(1)} all-to-all(f32[8,40,128]{2,1,0:T(8,128)S(1)} %shard_map.102), channel_id=1, replica_groups={{0,2,4,6,8,10,12,14},{1,3,5,7,9,11,13,15},{16,18,20,22,24,26,28,30},{17..., dimensions={0} | all-to-all | bytes 327680 | tf_op jit(solution)/shard_map/all_to_all | solution.py:458
  (60 shorter events, 12.4 us)
Async XLA Ops:
  0.6 15.0 %collective-permute-start.1 = (bf16[512,2048]{1,0:T(8,128)(2,1)}, bf16[512,2048]{1,0:T(8,128)(2,1)S(1)}, u32[]{:S(2)}, u32[]{:S(2)}) collective-permute-start(bf16[512,2048]{1,0:T(8,128)(2,1)} %context.3), channel_id=1, source_target_pairs={{0,1},{1,0},{2,3},{3,2},{4,5},{5,4},{6,7},{7,6},{8,9},{9,8},{10,11... | collective-permute-start | bytes 6291464 | tf_op jit(solution)/shard_map/ppermute | solution.py:358
  2.4 9.8 %collective-permute-start.2 = (bf16[1024,256]{1,0:T(8,128)(2,1)S(1)}, bf16[1024,256]{1,0:T(8,128)(2,1)S(1)}, u32[]{:S(2)}, u32[]{:S(2)}) collective-permute-start(bf16[1024,256]{1,0:T(8,128)(2,1)S(1)} %shard_map.94), channel_id=1, source_target_pairs={{0,2},{1,5},{4,0},{5,9},{8,4},{9,13},{12,8},{13,15},{14,12},{15,11... | collective-permute-start | bytes 1572872 | tf_op jit(solution)/shard_map/ppermute | solution.py:349
  5.0 18.7 %collective-permute-start.3 = (bf16[112,4096]{1,0:T(8,128)(2,1)}, bf16[112,4096]{1,0:T(8,128)(2,1)S(1)}, u32[]{:S(2)}, u32[]{:S(2)}) collective-permute-start(bf16[112,4096]{1,0:T(8,128)(2,1)} %queries.1), channel_id=1, source_target_pairs={{0,1},{1,0},{2,3},{3,2},{4,5},{5,4},{6,7},{7,6},{8,9},{9,8},{10,11... | collective-permute-start | bytes 2752520 | tf_op jit(solution)/shard_map/ppermute | solution.py:358
  10.0 13.8 %collective-permute-start = (bf16[1024,256]{1,0:T(8,128)(2,1)S(1)}, bf16[1024,256]{1,0:T(8,128)(2,1)S(1)}, u32[]{:S(2)}, u32[]{:S(2)}) collective-permute-start(bf16[1024,256]{1,0:T(8,128)(2,1)S(1)} %shard_map.94), channel_id=1, source_target_pairs={{0,4},{1,3},{4,8},{5,1},{8,12},{9,5},{12,14},{13,9},{14,10},{15,13... | collective-permute-start | bytes 1572872 | tf_op jit(solution)/shard_map/ppermute | solution.py:352
  12.2 12.9 %collective-permute-start.6 = (bf16[1024,256]{1,0:T(8,128)(2,1)S(1)}, bf16[1024,256]{1,0:T(8,128)(2,1)S(1)}, u32[]{:S(2)}, u32[]{:S(2)}) collective-permute-start(bf16[1024,256]{1,0:T(8,128)(2,1)S(1)} %collective-permute-done.2.refs_3_), channel_id=1, source_target_pairs={{0,2},{1,5},{4,0},{5,9},{8,4},{9,13},{12,8},{13,15},{14,12},{15,11... | collective-permute-start | bytes 1572872 | tf_op jit(solution)/shard_map/ppermute | solution.py:349
  14.2 13.2 %collective-permute-start.5 = (bf16[1024,256]{1,0:T(8,128)(2,1)S(1)}, bf16[1024,256]{1,0:T(8,128)(2,1)S(1)}, u32[]{:S(2)}, u32[]{:S(2)}) collective-permute-start(bf16[1024,256]{1,0:T(8,128)(2,1)S(1)} %collective-permute-done.2.refs_3_), channel_id=1, source_target_pairs={{0,16},{16,0},{1,17},{17,1},{2,18},{18,2},{3,19},{19,3},{4,20},{20... | collective-permute-start | bytes 1572872 | tf_op jit(solution)/shard_map/ppermute | solution.py:355
  23.7 3.7 %collective-permute-start.7 = (f32[512,256]{1,0:T(8,128)S(1)}, f32[512,256]{1,0:T(8,128)S(1)}, u32[]{:S(2)}, u32[]{:S(2)}) collective-permute-start(f32[512,256]{1,0:T(8,128)S(1)} %shard_map.96), channel_id=1, source_target_pairs={{0,1},{1,0},{2,3},{3,2},{4,5},{5,4},{6,7},{7,6},{8,9},{9,8},{10,11... | collective-permute-start | bytes 1572872 | tf_op jit(solution)/shard_map/ppermute | solution.py:358
  23.7 14.6 %collective-permute-start.4 = (bf16[1024,256]{1,0:T(8,128)(2,1)S(1)}, bf16[1024,256]{1,0:T(8,128)(2,1)S(1)}, u32[]{:S(2)}, u32[]{:S(2)}) collective-permute-start(bf16[1024,256]{1,0:T(8,128)(2,1)S(1)} %collective-permute-done.refs_5_), channel_id=1, source_target_pairs={{0,4},{1,3},{4,8},{5,1},{8,12},{9,5},{12,14},{13,9},{14,10},{15,13... | collective-permute-start | bytes 1572872 | tf_op jit(solution)/shard_map/ppermute | solution.py:352
  25.1 14.4 %collective-permute-start.10 = (bf16[1024,256]{1,0:T(8,128)(2,1)S(1)}, bf16[1024,256]{1,0:T(8,128)(2,1)S(1)}, u32[]{:S(2)}, u32[]{:S(2)}) collective-permute-start(bf16[1024,256]{1,0:T(8,128)(2,1)S(1)} %collective-permute-done.6.refs_3_), channel_id=1, source_target_pairs={{0,2},{1,5},{4,0},{5,9},{8,4},{9,13},{12,8},{13,15},{14,12},{15,11... | collective-permute-start | bytes 1572872 | tf_op jit(solution)/shard_map/ppermute | solution.py:349
  25.8 14.3 %collective-permute-start.9 = (bf16[1024,256]{1,0:T(8,128)(2,1)S(1)}, bf16[1024,256]{1,0:T(8,128)(2,1)S(1)}, u32[]{:S(2)}, u32[]{:S(2)}) collective-permute-start(bf16[1024,256]{1,0:T(8,128)(2,1)S(1)} %collective-permute-done.6.refs_3_), channel_id=1, source_target_pairs={{0,16},{16,0},{1,17},{17,1},{2,18},{18,2},{3,19},{19,3},{4,20},{20... | collective-permute-start | bytes 1572872 | tf_op jit(solution)/shard_map/ppermute | solution.py:355
  38.3 3.7 %collective-permute-start.11 = (f32[512,256]{1,0:T(8,128)S(1)}, f32[512,256]{1,0:T(8,128)S(1)}, u32[]{:S(2)}, u32[]{:S(2)}) collective-permute-start(f32[512,256]{1,0:T(8,128)S(1)} %get-tuple-element.100), channel_id=1, source_target_pairs={{0,1},{1,0},{2,3},{3,2},{4,5},{5,4},{6,7},{7,6},{8,9},{9,8},{10,11... | collective-permute-start | bytes 1572872 | tf_op jit(solution)/shard_map/ppermute | solution.py:358
  38.3 14.4 %collective-permute-start.8 = (bf16[1024,256]{1,0:T(8,128)(2,1)S(1)}, bf16[1024,256]{1,0:T(8,128)(2,1)S(1)}, u32[]{:S(2)}, u32[]{:S(2)}) collective-permute-start(bf16[1024,256]{1,0:T(8,128)(2,1)S(1)} %collective-permute-done.4.refs_3_), channel_id=1, source_target_pairs={{0,4},{1,3},{4,8},{5,1},{8,12},{9,5},{12,14},{13,9},{14,10},{15,13... | collective-permute-start | bytes 1572872 | tf_op jit(solution)/shard_map/ppermute | solution.py:352
  40.1 13.1 %collective-permute-start.14 = (bf16[1024,256]{1,0:T(8,128)(2,1)S(1)}, bf16[1024,256]{1,0:T(8,128)(2,1)S(1)}, u32[]{:S(2)}, u32[]{:S(2)}) collective-permute-start(bf16[1024,256]{1,0:T(8,128)(2,1)S(1)} %collective-permute-done.9.refs_4_), channel_id=1, source_target_pairs={{0,2},{1,5},{4,0},{5,9},{8,4},{9,13},{12,8},{13,15},{14,12},{15,11... | collective-permute-start | bytes 1572872 | tf_op jit(solution)/shard_map/ppermute | solution.py:349
  40.5 14.5 %collective-permute-start.13 = (bf16[1024,256]{1,0:T(8,128)(2,1)S(1)}, bf16[1024,256]{1,0:T(8,128)(2,1)S(1)}, u32[]{:S(2)}, u32[]{:S(2)}) collective-permute-start(bf16[1024,256]{1,0:T(8,128)(2,1)S(1)} %collective-permute-done.4.refs_3_), channel_id=1, source_target_pairs={{0,16},{16,0},{1,17},{17,1},{2,18},{18,2},{3,19},{19,3},{4,20},{20... | collective-permute-start | bytes 1572872 | tf_op jit(solution)/shard_map/ppermute | solution.py:355
  52.7 3.9 %collective-permute-start.15 = (f32[512,256]{1,0:T(8,128)S(1)}, f32[512,256]{1,0:T(8,128)S(1)}, u32[]{:S(2)}, u32[]{:S(2)}) collective-permute-start(f32[512,256]{1,0:T(8,128)S(1)} %get-tuple-element.112), channel_id=1, source_target_pairs={{0,1},{1,0},{2,3},{3,2},{4,5},{5,4},{6,7},{7,6},{8,9},{9,8},{10,11... | collective-permute-start | bytes 1572872 | tf_op jit(solution)/shard_map/ppermute | solution.py:358
  52.7 14.8 %collective-permute-start.12 = (bf16[1024,256]{1,0:T(8,128)(2,1)S(1)}, bf16[1024,256]{1,0:T(8,128)(2,1)S(1)}, u32[]{:S(2)}, u32[]{:S(2)}) collective-permute-start(bf16[1024,256]{1,0:T(8,128)(2,1)S(1)} %collective-permute-done.8.refs_7_), channel_id=1, source_target_pairs={{0,4},{1,3},{4,8},{5,1},{8,12},{9,5},{12,14},{13,9},{14,10},{15,13... | collective-permute-start | bytes 1572872 | tf_op jit(solution)/shard_map/ppermute | solution.py:352
  53.2 14.3 %collective-permute-start.16 = (f32[512,256]{1,0:T(8,128)S(1)}, f32[512,256]{1,0:T(8,128)S(1)}, u32[]{:S(2)}, u32[]{:S(2)}) collective-permute-start(f32[512,256]{1,0:T(8,128)S(1)} %get-tuple-element.118), channel_id=1, source_target_pairs={{0,1},{1,0},{2,3},{3,2},{4,5},{5,4},{6,7},{7,6},{8,9},{9,8},{10,11... | collective-permute-start | bytes 1572872 | tf_op jit(solution)/shard_map/ppermute | solution.py:358
  53.2 14.8 %collective-permute-start.19 = (bf16[1024,256]{1,0:T(8,128)(2,1)S(1)}, bf16[1024,256]{1,0:T(8,128)(2,1)S(1)}, u32[]{:S(2)}, u32[]{:S(2)}) collective-permute-start(bf16[1024,256]{1,0:T(8,128)(2,1)S(1)} %collective-permute-done.14.refs_6_), channel_id=1, source_target_pairs={{0,2},{1,5},{4,0},{5,9},{8,4},{9,13},{12,8},{13,15},{14,12},{15,11... | collective-permute-start | bytes 1572872 | tf_op jit(solution)/shard_map/ppermute | solution.py:349
  55.1 13.9 %collective-permute-start.18 = (bf16[1024,256]{1,0:T(8,128)(2,1)S(1)}, bf16[1024,256]{1,0:T(8,128)(2,1)S(1)}, u32[]{:S(2)}, u32[]{:S(2)}) collective-permute-start(bf16[1024,256]{1,0:T(8,128)(2,1)S(1)} %collective-permute-done.refs_5_), channel_id=1, source_target_pairs={{0,16},{16,0},{1,17},{17,1},{2,18},{18,2},{3,19},{19,3},{4,20},{20... | collective-permute-start | bytes 1572872 | tf_op jit(solution)/shard_map/ppermute | solution.py:355
  68.0 9.2 %collective-permute-start.17 = (bf16[1024,256]{1,0:T(8,128)(2,1)S(1)}, bf16[1024,256]{1,0:T(8,128)(2,1)S(1)}, u32[]{:S(2)}, u32[]{:S(2)}) collective-permute-start(bf16[1024,256]{1,0:T(8,128)(2,1)S(1)} %collective-permute-done.13.refs_4_), channel_id=1, source_target_pairs={{0,4},{1,3},{4,8},{5,1},{8,12},{9,5},{12,14},{13,9},{14,10},{15,13... | collective-permute-start | bytes 1572872 | tf_op jit(solution)/shard_map/ppermute | solution.py:352
  68.0 9.2 %collective-permute-start.22 = (f32[512,256]{1,0:T(8,128)S(1)}, f32[512,256]{1,0:T(8,128)S(1)}, u32[]{:S(2)}, u32[]{:S(2)}) collective-permute-start(f32[512,256]{1,0:T(8,128)S(1)} %get-tuple-element.127), channel_id=1, source_target_pairs={{0,1},{1,0},{2,3},{3,2},{4,5},{5,4},{6,7},{7,6},{8,9},{9,8},{10,11... | collective-permute-start | bytes 1572872 | tf_op jit(solution)/shard_map/ppermute | solution.py:358
  69.0 8.2 %collective-permute-start.23 = (bf16[1024,256]{1,0:T(8,128)(2,1)S(1)}, bf16[1024,256]{1,0:T(8,128)(2,1)S(1)}, u32[]{:S(2)}, u32[]{:S(2)}) collective-permute-start(bf16[1024,256]{1,0:T(8,128)(2,1)S(1)} %collective-permute-done.12.refs_2_), channel_id=1, source_target_pairs={{0,1},{1,0},{2,3},{3,2},{4,5},{5,4},{6,7},{7,6},{8,9},{9,8},{10,11... | collective-permute-start | bytes 1572872 | tf_op jit(solution)/shard_map/ppermute | solution.py:358
  69.4 11.1 %collective-permute-start.26 = (bf16[1024,256]{1,0:T(8,128)(2,1)S(1)}, bf16[1024,256]{1,0:T(8,128)(2,1)S(1)}, u32[]{:S(2)}, u32[]{:S(2)}) collective-permute-start(bf16[1024,256]{1,0:T(8,128)(2,1)S(1)} %collective-permute-done.19.refs_3_), channel_id=1, source_target_pairs={{0,1},{1,0},{2,3},{3,2},{4,5},{5,4},{6,7},{7,6},{8,9},{9,8},{10,11... | collective-permute-start | bytes 1572872 | tf_op jit(solution)/shard_map/ppermute | solution.py:358
  77.2 3.4 %collective-permute-start.24 = (bf16[1024,256]{1,0:T(8,128)(2,1)S(1)}, bf16[1024,256]{1,0:T(8,128)(2,1)S(1)}, u32[]{:S(2)}, u32[]{:S(2)}) collective-permute-start(bf16[1024,256]{1,0:T(8,128)(2,1)S(1)} %collective-permute-done.18.refs_0_), channel_id=1, source_target_pairs={{0,1},{1,0},{2,3},{3,2},{4,5},{5,4},{6,7},{7,6},{8,9},{9,8},{10,11... | collective-permute-start | bytes 1572872 | tf_op jit(solution)/shard_map/ppermute | solution.py:358
  (11 other events, 91.4 us)

commit v9 on v8

--- a/solution.py
+++ b/solution.py
@@ -80,7 +80,7 @@
     return total
 
 
-def wave_kernel(full, part, arrived, whole, tokens, *refs):
+def wave_kernel(full, part, arrived, whole, tokens, stacked, *refs):
     count = len(full) + len(part)
     refs = list(refs)
     context = refs.pop(0) if "mine" in tokens else None
@@ -95,7 +95,12 @@
     if arrived:
         received, before = [refs.pop(0) for _ in arrived], refs.pop(0)
     mine = refs.pop(0) if "mine" in tokens else None
-    theirs = [refs.pop(0) for _ in range(count)] if "theirs" in tokens else None
+    theirs = None
+    if "theirs" in tokens:
+        stacks = [refs.pop(0) for _ in range(2 if stacked else count)]
+        theirs = stacks
+        if stacked:
+            theirs = [stacks[0].at[j] for j in range(len(full))] + [stacks[1].at[j] for j in range(len(part))]
     finished = refs.pop(0) if arrived else None
     squares = refs.pop(0) if "mine" in tokens else None
     rows, width = mine.shape[1:] if "mine" in tokens else theirs[0].shape
@@ -125,14 +130,21 @@
             add_squares(squares, at, total)
 
 
-def wave(full, part, arrived, context, other_context, residual, pieces, received=None, squares=None):
+def wave(
+    full, part, arrived, context, other_context, residual, pieces, received=None, squares=None, stacked=False
+):
     tokens = (("mine",) if context is not None else ()) + (("theirs",) if other_context is not None else ())
     count = len(full) + len(part)
     rows = (context if other_context is None else other_context).shape[0]
     whole = len(pieces) == 1
     block = jax.ShapeDtypeStruct((rows, pieces[0].shape[1]), jnp.float32)
-    outs = [jax.ShapeDtypeStruct((count,) + block.shape, jnp.float32)] if "mine" in tokens else []
-    outs += [block] * count if "theirs" in tokens else []
+
+    def stack(n):
+        return jax.ShapeDtypeStruct((n,) + block.shape, jnp.float32)
+
+    outs = [stack(count)] if "mine" in tokens else []
+    if "theirs" in tokens:
+        outs += [stack(len(full)), stack(len(part))] if stacked else [block] * count
     operands = [x for x in (context, other_context) if x is not None]
     operands += ([residual] if "mine" in tokens else []) + list(pieces)
     if arrived:
@@ -141,7 +153,7 @@
     if "mine" in tokens:
         outs.append(jax.ShapeDtypeStruct((rows, LANES), jnp.float32))
     return pl.pallas_call(
-        functools.partial(wave_kernel, full, part, arrived, whole, tokens),
+        functools.partial(wave_kernel, full, part, arrived, whole, tokens, stacked),
         out_shape=outs,
         in_specs=[VMEM_SPEC] * len(operands),
         out_specs=[VMEM_SPEC] * len(outs),
@@ -360,83 +372,80 @@
     wait = lax.optimization_barrier
 
     own = own_half(out_proj)
-    a = from_next(own)
-    c = other_core(context)
-    q = other_core(queries)
+    a, b = from_next(own), from_last(own)
+    c, q = other_core(context), other_core(queries)
     h0, sq0 = wave((0,), (), (), context, None, residual, [out_proj])
-    own, h0, sq0 = wait((own, h0, sq0))
-    b = from_last(own)
 
     n1, sq0 = wait((a, sq0))
     x1 = over_x(n1)
     a = from_next(n1)
-    context2, n1 = wait((c, n1))
+    l1, n1, context2 = wait((b, n1, c))
+    b = from_last(l1)
     (t0,) = wave((0,), (), (), None, context2, None, [out_proj])
-    l1, n1, t0, queries2 = wait((b, n1, t0, q))
-    b = from_last(l1)
-    r0 = other_core(t0)
-
-    n2, l1 = wait((a, l1))
+
+    n2, t0, queries2 = wait((a, t0, q))
     x2 = over_x(n2)
     a = from_next(n2)
-    xn1, n2 = wait((x1, n2))
+    r0 = other_core(t0)
+    l2, n2 = wait((b, n2))
+    b = from_last(l2)
+    xn1, n2, l2 = wait((x1, n2, l2))
     h1, t1, f0, sq1 = wave((1,), (), (0,), context, context2, residual, [n1, xn1], [r0], sq0)
-    l2, n2, t1, sq1 = wait((b, n2, t1, sq1))
-    b = from_last(l2)
+
+    xn2, l2, t1, sq1 = wait((x2, l2, t1, sq1))
     x3 = over_x(l2)
+    a2 = from_next(xn2)
     r1 = other_core(t1)
-
-    n3, l2 = wait((a, l2))
-    xn2, l2, n3 = wait((x2, l2, n3))
-    a = from_next(xn2)
+    n3, xn2 = wait((a, xn2))
+    l3, n3, xn2 = wait((b, n3, xn2))
+    b = from_last(l3)
     h2, t2, t2p, f1, sq2 = wave((2,), (-1,), (1,), context, context2, residual, [n2, xn2, l1], [r1], sq1)
-    l3, n3, t2, t2p, sq2 = wait((b, n3, t2, t2p, sq2))
-    b = from_last(l3)
+
+    n3x, t2, t2p, sq2 = wait((a2, t2, t2p, sq2))
+    a = from_next(n3x)
     r2, r2p = other_core(t2), other_core(t2p)
-
-    n3x, l3 = wait((a, l3))
-    a = from_next(n3x)
-    xl2, l1, n3x = wait((x3, l1, n3x))
+    xl2, n3x, l1 = wait((x3, n3x, l1))
     x4 = over_x(l1)
-    h3, t3a, t3b, t3p, f2, sq3 = wave(
-        (-2, 3), (-3,), (2,), context, context2, residual, [l2, xl2, n3, n3x, l3], [r2], sq2
-    )
-    l4, xl2, t3a, t3b, t3p, sq3, r2p = wait((b, xl2, t3a, t3b, t3p, sq3, r2p))
-    b2 = from_last(xl2)
-    l4s = other_core(l4)
-    r3a, r3b, r3p = other_core(t3a), other_core(t3b), other_core(t3p)
-    n4x, l4 = wait((a, l4))
+    l4, xl2, n3x = wait((b, xl2, n3x))
+    b = from_last(xl2)
+    h3, t3a, t3b, f2, sq3 = wave(
+        (-2, 3), (-3, 4), (2,), context, context2, residual, [l2, xl2, n3, n3x, l3, l4], [r2], sq2, stacked=True
+    )
+
+    r3a, r3b = other_core(t3a), other_core(t3b)
+    n4x, sq3, r2p = wait((a, sq3, r2p))
     n4xs = other_core(n4x)
-    xl1, n4x, r3a, r3b = wait((x4, n4x, r3a, r3b))
+    xl1, n4x = wait((x4, n4x))
     xl1s = other_core(xl1)
-    l3x, xl1, r3p, l4s = wait((b2, xl1, r3p, l4s))
+    l3x, xl1 = wait((b, xl1))
     l3xs = other_core(l3x)
 
-    missing = (((0, True),), ((1, True),), ((2, False), (3, True)))
-    own_items = tuple(
-        (base, parts, base is None, distance, True)
-        for base, parts, distance in zip(((0, 1), (1, 2), None), missing, (-1, -3, 4))
-    )
-    h4, sq4 = late(own_items, context, residual, sq3, [xl1, l3x, l4, n4x], [h2, h3])
-    items = tuple(
-        (base, parts, True, distance, False)
-        for base, parts, distance in zip(
-            ((8, None), (9, None), None, (10, None), (11, None)), missing + ((), ()), (-1, -3, 4, -2, 3)
-        )
-    )
-    hidden = [h0, h1, h2, h3, h4, f0, f1, f2, r2p, r3p, r3a, r3b]
+    first_items = (
+        ((0, 1), ((0, True),), False, -1, True),
+        ((1, 2), ((1, True),), False, -3, True),
+        ((1, 3), ((2, True),), False, 4, True),
+    )
+    h4, sq4 = late(first_items, context, residual, sq3, [xl1, l3x, n4x], [h2, h3])
+    items = (
+        ((8, None), ((0, True),), True, -1, False),
+        ((10, 0), ((1, True),), True, -3, False),
+        ((10, 1), ((2, True),), True, 4, False),
+        ((9, 0), (), True, -2, False),
+        ((9, 1), (), True, 3, False),
+    )
+    hidden = [h0, h1, h2, h3, h4, f0, f1, f2, r2p, r3a, r3b]
     sources = (
         (0, 0, 0, True),
         (1, 0, 1, True),
         (2, 0, 2, True),
         (3, 0, -2, True),
         (3, 1, 3, True),
+        (5, 0, 0, False),
+        (6, 0, 1, False),
+        (7, 0, 2, False),
         (4, 0, -1, True),
         (4, 1, -3, True),
         (4, 2, 4, True),
-        (5, 0, 0, False),
-        (6, 0, 1, False),
-        (7, 0, 2, False),
     )
     flags = jnp.pad(pattern.astype(jnp.float32), ((0, 0), (0, LANES - pattern.shape[1])))
     embedded, payload = finish(
@@ -448,7 +457,7 @@
         sq4,
         norm_gain.reshape(1, -1),
         flags,
-        [xl1s, l3xs, l4s, n4xs],
+        [xl1s, l3xs, n4xs],
         hidden,
         size,
     )

time: 108 us -> 108 us (level)
  waiting for transfers between devices: 42.4 us -> 36.4 us
  starting transfers between devices: 19.7 us -> 24.2 us
    ppermute x5, waiting for transfers between devices: 38.7 us -> 0.01 us  [from_last(): return lax.ppermute(piece, 'dp', ring(1))]
    ppermute x5, waiting for transfers between devices: 0.62 us -> 21.6 us  [from_next(): return lax.ppermute(piece, 'dp', ring(-1))]
    ppermute x4, waiting for transfers between devices: 2.08 us -> 14.8 us  [over_x(): return lax.ppermute(piece, 'groups', [(0, 1), (1, 0)])]
    ppermute x5, starting transfers between devices: 7.21 us -> 10.7 us  [from_next(): return lax.ppermute(piece, 'dp', ring(-1))]
    ppermute x13 -> x11, starting transfers between devices: 2.06 us -> 2.69 us  [other_core(): return lax.ppermute(piece, 'dp', [(i, i ^ 1) for i in range(ranks)])]
  transfers between devices with their start and end apart: 27 -> 25, of which waited for: 12 -> 7; matrix products, arithmetic and copies ran while one was open for 0% -> 0% of each run, Pallas kernels for 11% -> 12%
where the time goes in v9:
time: 108 us; the launch traced here: 107 us
  waiting for transfers between devices  36.4 us (34%)
  starting transfers between devices  24.2 us (22%)
  blocking collectives  21.9 us (20%)
  Pallas kernels  18.3 us (17%)
  local copies, waits for them, and re-layouts  5.03 us (5%)
  between operations  1.47 us (1%)
    all_to_all x2, blocking collectives, spread(): lax.all_to_all(blocks, 'dp', 0, 0, axis_index_groups=same_core, tiled=True)  21.9 us
    ppermute x5, waiting for transfers between devices, from_next(): return lax.ppermute(piece, 'dp', ring(-1))  21.6 us
    ppermute x4, waiting for transfers between devices, over_x(): return lax.ppermute(piece, 'groups', [(0, 1), (1, 0)])  14.8 us
    ppermute x5, starting transfers between devices, from_next(): return lax.ppermute(piece, 'dp', ring(-1))  10.7 us
    pallas_call x5, Pallas kernels, wave(): pl.pallas_call(functools.partial(wave_kernel, full, part, arrived, whole,...  10.6 us
    ppermute x4, starting transfers between devices, over_x(): return lax.ppermute(piece, 'groups', [(0, 1), (1, 0)])  6.68 us
    unnamed x16, local copies, waits for them, and re-layouts  5.03 us
    ppermute x5, starting transfers between devices, from_last(): return lax.ppermute(piece, 'dp', ring(1))  4.18 us
  transfers between devices with their start and end apart: 25, of which 7 were waited for; matrix products, arithmetic and copies ran while one was open for 0% of the time, Pallas kernels for 12%

profile of v9, /device:TPU:0, one launch (start us, length us, event | category | flops | bytes accessed | tf_op | source)
XLA Modules:
  0.0 107.4 jit_solution(6887287642950534134)
XLA Ops:
  2.4 2.6 %collective-permute-start = (bf16[1024,256]{1,0:T(8,128)(2,1)S(1)}, bf16[1024,256]{1,0:T(8,128)(2,1)S(1)}, u32[]{:S(2)}, u32[]{:S(2)}) collective-permute-start(bf16[1024,256]{1,0:T(8,128)(2,1)S(1)} %shard_map.94), channel_id=1, source_target_pairs={{0,2},{1,5},{4,0},{5,9},{8,4},{9,13},{12,8},{13,15},{14,12},{15,11... | collective-permute-start | bytes 1572872 | tf_op jit(solution)/shard_map/ppermute | solution.py:361
  5.3 1.6 %collective-permute-start.2 = (bf16[1024,256]{1,0:T(8,128)(2,1)S(1)}, bf16[1024,256]{1,0:T(8,128)(2,1)S(1)}, u32[]{:S(2)}, u32[]{:S(2)}) collective-permute-start(bf16[1024,256]{1,0:T(8,128)(2,1)S(1)} %shard_map.94), channel_id=1, source_target_pairs={{0,4},{1,3},{4,8},{5,1},{8,12},{9,5},{12,14},{13,9},{14,10},{15,13... | collective-permute-start | bytes 1572872 | tf_op jit(solution)/shard_map/ppermute | solution.py:364
  6.8 2.2 %copy-done = bf16[512,4096]{1,0:T(8,128)(2,1)S(1)} copy-done((bf16[512,4096]{1,0:T(8,128)(2,1)S(1)}, bf16[512,4096]{1,0:T(8,128)(2,1)}, u32[]{:S(2)}) %copy-start) | copy-done | bytes 4194328
  9.0 1.6 %copy-done.2 = bf16[512,2048]{1,0:T(8,128)(2,1)S(1)} copy-done((bf16[512,2048]{1,0:T(8,128)(2,1)S(1)}, bf16[512,2048]{1,0:T(8,128)(2,1)}, u32[]{:S(2)}) %copy-start.2) | copy-done | bytes 2097176
  11.5 4.7 %collective-permute-done.refs_3_ = bf16[1024,256]{1,0:T(8,128)(2,1)S(1)} collective-permute-done((bf16[1024,256]{1,0:T(8,128)(2,1)S(1)}, bf16[1024,256]{1,0:T(8,128)(2,1)S(1)}, u32[]{:S(2)}, u32[]{:S(2)}) %collective-permute-start) | collective-permute-done | bytes 524320 | tf_op jit(solution)/shard_map/ppermute | solution.py:361
  16.3 2.4 %collective-permute-start.1 = (bf16[1024,256]{1,0:T(8,128)(2,1)S(1)}, bf16[1024,256]{1,0:T(8,128)(2,1)S(1)}, u32[]{:S(2)}, u32[]{:S(2)}) collective-permute-start(bf16[1024,256]{1,0:T(8,128)(2,1)S(1)} %collective-permute-done.refs_3_), channel_id=1, source_target_pairs={{0,2},{1,5},{4,0},{5,9},{8,4},{9,13},{12,8},{13,15},{14,12},{15,11... | collective-permute-start | bytes 1572872 | tf_op jit(solution)/shard_map/ppermute | solution.py:361
  19.4 1.5 %collective-permute-start.6 = (bf16[1024,256]{1,0:T(8,128)(2,1)S(1)}, bf16[1024,256]{1,0:T(8,128)(2,1)S(1)}, u32[]{:S(2)}, u32[]{:S(2)}) collective-permute-start(bf16[1024,256]{1,0:T(8,128)(2,1)S(1)} %collective-permute-done.refs_3_), channel_id=1, source_target_pairs={{0,16},{16,0},{1,17},{17,1},{2,18},{18,2},{3,19},{19,3},{4,20},{20... | collective-permute-start | bytes 1572872 | tf_op jit(solution)/shard_map/ppermute | solution.py:367
  21.8 10.0 %collective-permute-done.1.refs_3_ = bf16[1024,256]{1,0:T(8,128)(2,1)S(1)} collective-permute-done((bf16[1024,256]{1,0:T(8,128)(2,1)S(1)}, bf16[1024,256]{1,0:T(8,128)(2,1)S(1)}, u32[]{:S(2)}, u32[]{:S(2)}) %collective-permute-start.1) | collective-permute-done | bytes 524320 | tf_op jit(solution)/shard_map/ppermute | solution.py:361
  31.8 1.7 %collective-permute-start.5 = (bf16[1024,256]{1,0:T(8,128)(2,1)S(1)}, bf16[1024,256]{1,0:T(8,128)(2,1)S(1)}, u32[]{:S(2)}, u32[]{:S(2)}) collective-permute-start(bf16[1024,256]{1,0:T(8,128)(2,1)S(1)} %collective-permute-done.1.refs_3_), channel_id=1, source_target_pairs={{0,16},{16,0},{1,17},{17,1},{2,18},{18,2},{3,19},{19,3},{4,20},{20... | collective-permute-start | bytes 1572872 | tf_op jit(solution)/shard_map/ppermute | solution.py:367
  33.4 1.5 %collective-permute-start.11 = (bf16[1024,256]{1,0:T(8,128)(2,1)S(1)}, bf16[1024,256]{1,0:T(8,128)(2,1)S(1)}, u32[]{:S(2)}, u32[]{:S(2)}) collective-permute-start(bf16[1024,256]{1,0:T(8,128)(2,1)S(1)} %collective-permute-done.1.refs_3_), channel_id=1, source_target_pairs={{0,2},{1,5},{4,0},{5,9},{8,4},{9,13},{12,8},{13,15},{14,12},{15,11... | collective-permute-start | bytes 1572872 | tf_op jit(solution)/shard_map/ppermute | solution.py:361
  35.5 1.6 %shard_map.97 = (f32[1,512,256]{2,1,0:T(8,128)S(1)}, f32[512,256]{1,0:T(8,128)S(1)}, f32[1,512,256]{2,1,0:T(8,128)S(1)}, f32[512,128]{1,0:T(8,128)S(1)}) custom-call(bf16[512,2048]{1,0:T(8,128)(2,1)S(1)} %copy-done.3, bf16[512,2048]{1,0:T(8,128)(2,1)S(1)} %collective-permute-done.3.refs_0_.refs_1_, bf16[512,4096]{1,0:T(8,128)(2,1)S(1)} %copy-done.1, ...), custom_call_target="tpu_custom_call" | custom-call | flops 1000 | bytes 1000 | tf_op jit(solution)/shard_map/pallas_call | solution.py:155
  37.1 9.0 %collective-permute-done.5.refs_4_ = bf16[1024,256]{1,0:T(8,128)(2,1)S(1)} collective-permute-done((bf16[1024,256]{1,0:T(8,128)(2,1)S(1)}, bf16[1024,256]{1,0:T(8,128)(2,1)S(1)}, u32[]{:S(2)}, u32[]{:S(2)}) %collective-permute-start.5) | collective-permute-done | bytes 524320 | tf_op jit(solution)/shard_map/ppermute | solution.py:367
  46.1 1.7 %collective-permute-start.9 = (bf16[1024,256]{1,0:T(8,128)(2,1)S(1)}, bf16[1024,256]{1,0:T(8,128)(2,1)S(1)}, u32[]{:S(2)}, u32[]{:S(2)}) collective-permute-start(bf16[1024,256]{1,0:T(8,128)(2,1)S(1)} %collective-permute-done.5.refs_4_), channel_id=1, source_target_pairs={{0,2},{1,5},{4,0},{5,9},{8,4},{9,13},{12,8},{13,15},{14,12},{15,11... | collective-permute-start | bytes 1572872 | tf_op jit(solution)/shard_map/ppermute | solution.py:361
  47.8 1.5 %collective-permute-start.15 = (bf16[1024,256]{1,0:T(8,128)(2,1)S(1)}, bf16[1024,256]{1,0:T(8,128)(2,1)S(1)}, u32[]{:S(2)}, u32[]{:S(2)}) collective-permute-start(bf16[1024,256]{1,0:T(8,128)(2,1)S(1)} %collective-permute-done.7.refs_3_), channel_id=1, source_target_pairs={{0,16},{16,0},{1,17},{17,1},{2,18},{18,2},{3,19},{19,3},{4,20},{20... | collective-permute-start | bytes 1572872 | tf_op jit(solution)/shard_map/ppermute | solution.py:367
  49.8 2.5 %shard_map.98 = (f32[2,512,256]{2,1,0:T(8,128)S(1)}, f32[512,256]{1,0:T(8,128)S(1)}, f32[512,256]{1,0:T(8,128)S(1)}, f32[1,512,256]{2,1,0:T(8,128)S(1)}, f32[512,128]{1,0:T(8,128)S(1)}) custom-call(bf16[512,2048]{1,0:T(8,128)(2,1)S(1)} %copy-done.3, bf16[512,2048]{1,0:T(8,128)(2,1)S(1)} %collective-permute-done.3.refs_0_.refs_1_, ...), custom_call_target="tpu_custom_call" | custom-call | flops 1000 | bytes 1000 | tf_op jit(solution)/shard_map/pallas_call | solution.py:155
  52.3 6.8 %collective-permute-done.9.refs_6_ = bf16[1024,256]{1,0:T(8,128)(2,1)S(1)} collective-permute-done((bf16[1024,256]{1,0:T(8,128)(2,1)S(1)}, bf16[1024,256]{1,0:T(8,128)(2,1)S(1)}, u32[]{:S(2)}, u32[]{:S(2)}) %collective-permute-start.9) | collective-permute-done | bytes 524320 | tf_op jit(solution)/shard_map/ppermute | solution.py:361
  59.1 2.5 %collective-permute-start.13 = (bf16[1024,256]{1,0:T(8,128)(2,1)S(1)}, bf16[1024,256]{1,0:T(8,128)(2,1)S(1)}, u32[]{:S(2)}, u32[]{:S(2)}) collective-permute-start(bf16[1024,256]{1,0:T(8,128)(2,1)S(1)} %collective-permute-done.9.refs_6_), channel_id=1, source_target_pairs={{0,2},{1,5},{4,0},{5,9},{8,4},{9,13},{12,8},{13,15},{14,12},{15,11... | collective-permute-start | bytes 1572872 | tf_op jit(solution)/shard_map/ppermute | solution.py:361
  61.9 2.0 %collective-permute-start.19 = (bf16[1024,256]{1,0:T(8,128)(2,1)S(1)}, bf16[1024,256]{1,0:T(8,128)(2,1)S(1)}, u32[]{:S(2)}, u32[]{:S(2)}) collective-permute-start(bf16[1024,256]{1,0:T(8,128)(2,1)S(1)} %collective-permute-done.2.refs_5_), channel_id=1, source_target_pairs={{0,16},{16,0},{1,17},{17,1},{2,18},{18,2},{3,19},{19,3},{4,20},{20... | collective-permute-start | bytes 1572872 | tf_op jit(solution)/shard_map/ppermute | solution.py:367
  64.8 4.8 %shard_map.99 = (f32[4,512,256]{2,1,0:T(8,128)S(1)}, f32[2,512,256]{2,1,0:T(8,128)S(1)}, f32[2,512,256]{2,1,0:T(8,128)S(1)}, f32[1,512,256]{2,1,0:T(8,128)S(1)}, f32[512,128]{1,0:T(8,128)S(1)}) custom-call(bf16[512,2048]{1,0:T(8,128)(2,1)S(1)} %copy-done.3, bf16[512,2048]{1,0:T(8,128)(2,1)S(1)} %collective-permute-done.3.refs_0_.refs_1_, ...), custom_call_target="tpu_custom_call" | custom-call | flops 1000 | bytes 1000 | tf_op jit(solution)/shard_map/pallas_call | solution.py:155
  71.1 5.5 %collective-permute-done.19.refs_0_ = bf16[1024,256]{1,0:T(8,128)(2,1)S(1)} collective-permute-done((bf16[1024,256]{1,0:T(8,128)(2,1)S(1)}, bf16[1024,256]{1,0:T(8,128)(2,1)S(1)}, u32[]{:S(2)}, u32[]{:S(2)}) %collective-permute-start.19) | collective-permute-done | bytes 524320 | tf_op jit(solution)/shard_map/ppermute | solution.py:367
  77.7 1.9 %shard_map.100 = (f32[3,512,256]{2,1,0:T(8,128)S(1)}, f32[512,128]{1,0:T(8,128)S(1)}) custom-call(bf16[512,2048]{1,0:T(8,128)(2,1)S(1)} %copy-done.3, bf16[512,4096]{1,0:T(8,128)(2,1)S(1)} %copy-done.1, f32[512,128]{1,0:T(8,128)S(1)} %get-tuple-element.101.before, bf16[1024,256]{1,0:T(8,128)(2,1)S(1)} %collective-permute-done.19.refs_0_, ...), custom_call_target="tpu_custom_call" | custom-call | flops 1000 | bytes 1000 | tf_op jit(solution)/shard_map/pallas_call | solution.py:191
  79.7 3.9 %shard_map.101 = (f32[1,4096]{1,0:T(1,128)}, bf16[8,48,128]{2,1,0:T(8,128)(2,1)S(1)}) custom-call(s32[1]{0:T(128)S(6)} %copy.10.length, bf16[512,2048]{1,0:T(8,128)(2,1)S(1)} %copy-done.3, bf16[512,4096]{1,0:T(8,128)(2,1)S(1)} %copy-done.1, f32[512,128]{1,0:T(8,128)S(1)} %get-tuple-element.110.before, f32[1,4096]{1,0:T(1,128)S(1)} %bitcast.2, ...), custom_call_target="tpu_custom_call" | custom-call | flops 1000 | bytes 1000 | tf_op jit(solution)/shard_map/pallas_call | solution.py:244
  83.5 12.0 %all_to_all.10.got = bf16[8,48,128]{2,1,0:T(8,128)(2,1)S(1)} all-to-all(bf16[8,48,128]{2,1,0:T(8,128)(2,1)S(1)} %get-tuple-element.121), channel_id=1, replica_groups={{0,2,4,6,8,10,12,14},{1,3,5,7,9,11,13,15},{16,18,20,22,24,26,28,30},{17..., dimensions={0} | all-to-all | bytes 196608 | tf_op jit(solution)/shard_map/all_to_all | solution.py:467
  96.6 10.0 %all_to_all.11.got = f32[8,40,128]{2,1,0:T(8,128)S(1)} all-to-all(f32[8,40,128]{2,1,0:T(8,128)S(1)} %shard_map.102), channel_id=1, replica_groups={{0,2,4,6,8,10,12,14},{1,3,5,7,9,11,13,15},{16,18,20,22,24,26,28,30},{17..., dimensions={0} | all-to-all | bytes 327680 | tf_op jit(solution)/shard_map/all_to_all | solution.py:467
  (56 shorter events, 10.7 us)
Async XLA Ops:
  0.6 18.0 %collective-permute-start.3 = (bf16[512,2048]{1,0:T(8,128)(2,1)}, bf16[512,2048]{1,0:T(8,128)(2,1)S(1)}, u32[]{:S(2)}, u32[]{:S(2)}) collective-permute-start(bf16[512,2048]{1,0:T(8,128)(2,1)} %context.3), channel_id=1, source_target_pairs={{0,1},{1,0},{2,3},{3,2},{4,5},{5,4},{6,7},{7,6},{8,9},{9,8},{10,11... | collective-permute-start | bytes 6291464 | tf_op jit(solution)/shard_map/ppermute | solution.py:370
  2.4 13.8 %collective-permute-start = (bf16[1024,256]{1,0:T(8,128)(2,1)S(1)}, bf16[1024,256]{1,0:T(8,128)(2,1)S(1)}, u32[]{:S(2)}, u32[]{:S(2)}) collective-permute-start(bf16[1024,256]{1,0:T(8,128)(2,1)S(1)} %shard_map.94), channel_id=1, source_target_pairs={{0,2},{1,5},{4,0},{5,9},{8,4},{9,13},{12,8},{13,15},{14,12},{15,11... | collective-permute-start | bytes 1572872 | tf_op jit(solution)/shard_map/ppermute | solution.py:361
  5.0 16.8 %collective-permute-start.4 = (bf16[112,4096]{1,0:T(8,128)(2,1)}, bf16[112,4096]{1,0:T(8,128)(2,1)S(1)}, u32[]{:S(2)}, u32[]{:S(2)}) collective-permute-start(bf16[112,4096]{1,0:T(8,128)(2,1)} %queries.1), channel_id=1, source_target_pairs={{0,1},{1,0},{2,3},{3,2},{4,5},{5,4},{6,7},{7,6},{8,9},{9,8},{10,11... | collective-permute-start | bytes 2752520 | tf_op jit(solution)/shard_map/ppermute | solution.py:370
  5.3 13.4 %collective-permute-start.2 = (bf16[1024,256]{1,0:T(8,128)(2,1)S(1)}, bf16[1024,256]{1,0:T(8,128)(2,1)S(1)}, u32[]{:S(2)}, u32[]{:S(2)}) collective-permute-start(bf16[1024,256]{1,0:T(8,128)(2,1)S(1)} %shard_map.94), channel_id=1, source_target_pairs={{0,4},{1,3},{4,8},{5,1},{8,12},{9,5},{12,14},{13,9},{14,10},{15,13... | collective-permute-start | bytes 1572872 | tf_op jit(solution)/shard_map/ppermute | solution.py:364
  16.3 15.5 %collective-permute-start.1 = (bf16[1024,256]{1,0:T(8,128)(2,1)S(1)}, bf16[1024,256]{1,0:T(8,128)(2,1)S(1)}, u32[]{:S(2)}, u32[]{:S(2)}) collective-permute-start(bf16[1024,256]{1,0:T(8,128)(2,1)S(1)} %collective-permute-done.refs_3_), channel_id=1, source_target_pairs={{0,2},{1,5},{4,0},{5,9},{8,4},{9,13},{12,8},{13,15},{14,12},{15,11... | collective-permute-start | bytes 1572872 | tf_op jit(solution)/shard_map/ppermute | solution.py:361
  18.7 16.3 %collective-permute-start.7 = (bf16[1024,256]{1,0:T(8,128)(2,1)S(1)}, bf16[1024,256]{1,0:T(8,128)(2,1)S(1)}, u32[]{:S(2)}, u32[]{:S(2)}) collective-permute-start(bf16[1024,256]{1,0:T(8,128)(2,1)S(1)} %collective-permute-done.2.refs_5_), channel_id=1, source_target_pairs={{0,4},{1,3},{4,8},{5,1},{8,12},{9,5},{12,14},{13,9},{14,10},{15,13... | collective-permute-start | bytes 1572872 | tf_op jit(solution)/shard_map/ppermute | solution.py:364
  19.4 16.1 %collective-permute-start.6 = (bf16[1024,256]{1,0:T(8,128)(2,1)S(1)}, bf16[1024,256]{1,0:T(8,128)(2,1)S(1)}, u32[]{:S(2)}, u32[]{:S(2)}) collective-permute-start(bf16[1024,256]{1,0:T(8,128)(2,1)S(1)} %collective-permute-done.refs_3_), channel_id=1, source_target_pairs={{0,16},{16,0},{1,17},{17,1},{2,18},{18,2},{3,19},{19,3},{4,20},{20... | collective-permute-start | bytes 1572872 | tf_op jit(solution)/shard_map/ppermute | solution.py:367
  31.8 3.7 %collective-permute-start.8 = (f32[512,256]{1,0:T(8,128)S(1)}, f32[512,256]{1,0:T(8,128)S(1)}, u32[]{:S(2)}, u32[]{:S(2)}) collective-permute-start(f32[512,256]{1,0:T(8,128)S(1)} %shard_map.96), channel_id=1, source_target_pairs={{0,1},{1,0},{2,3},{3,2},{4,5},{5,4},{6,7},{7,6},{8,9},{9,8},{10,11... | collective-permute-start | bytes 1572872 | tf_op jit(solution)/shard_map/ppermute | solution.py:370
  31.8 14.3 %collective-permute-start.5 = (bf16[1024,256]{1,0:T(8,128)(2,1)S(1)}, bf16[1024,256]{1,0:T(8,128)(2,1)S(1)}, u32[]{:S(2)}, u32[]{:S(2)}) collective-permute-start(bf16[1024,256]{1,0:T(8,128)(2,1)S(1)} %collective-permute-done.1.refs_3_), channel_id=1, source_target_pairs={{0,16},{16,0},{1,17},{17,1},{2,18},{18,2},{3,19},{19,3},{4,20},{20... | collective-permute-start | bytes 1572872 | tf_op jit(solution)/shard_map/ppermute | solution.py:367
  33.4 14.4 %collective-permute-start.11 = (bf16[1024,256]{1,0:T(8,128)(2,1)S(1)}, bf16[1024,256]{1,0:T(8,128)(2,1)S(1)}, u32[]{:S(2)}, u32[]{:S(2)}) collective-permute-start(bf16[1024,256]{1,0:T(8,128)(2,1)S(1)} %collective-permute-done.1.refs_3_), channel_id=1, source_target_pairs={{0,2},{1,5},{4,0},{5,9},{8,4},{9,13},{12,8},{13,15},{14,12},{15,11... | collective-permute-start | bytes 1572872 | tf_op jit(solution)/shard_map/ppermute | solution.py:361
  34.9 14.3 %collective-permute-start.10 = (bf16[1024,256]{1,0:T(8,128)(2,1)S(1)}, bf16[1024,256]{1,0:T(8,128)(2,1)S(1)}, u32[]{:S(2)}, u32[]{:S(2)}) collective-permute-start(bf16[1024,256]{1,0:T(8,128)(2,1)S(1)} %collective-permute-done.7.refs_3_), channel_id=1, source_target_pairs={{0,4},{1,3},{4,8},{5,1},{8,12},{9,5},{12,14},{13,9},{14,10},{15,13... | collective-permute-start | bytes 1572872 | tf_op jit(solution)/shard_map/ppermute | solution.py:364
  46.1 3.7 %collective-permute-start.12 = (f32[512,256]{1,0:T(8,128)S(1)}, f32[512,256]{1,0:T(8,128)S(1)}, u32[]{:S(2)}, u32[]{:S(2)}) collective-permute-start(f32[512,256]{1,0:T(8,128)S(1)} %get-tuple-element.83), channel_id=1, source_target_pairs={{0,1},{1,0},{2,3},{3,2},{4,5},{5,4},{6,7},{7,6},{8,9},{9,8},{10,11... | collective-permute-start | bytes 1572872 | tf_op jit(solution)/shard_map/ppermute | solution.py:370
  46.1 13.0 %collective-permute-start.9 = (bf16[1024,256]{1,0:T(8,128)(2,1)S(1)}, bf16[1024,256]{1,0:T(8,128)(2,1)S(1)}, u32[]{:S(2)}, u32[]{:S(2)}) collective-permute-start(bf16[1024,256]{1,0:T(8,128)(2,1)S(1)} %collective-permute-done.5.refs_4_), channel_id=1, source_target_pairs={{0,2},{1,5},{4,0},{5,9},{8,4},{9,13},{12,8},{13,15},{14,12},{15,11... | collective-permute-start | bytes 1572872 | tf_op jit(solution)/shard_map/ppermute | solution.py:361
  47.8 14.1 %collective-permute-start.15 = (bf16[1024,256]{1,0:T(8,128)(2,1)S(1)}, bf16[1024,256]{1,0:T(8,128)(2,1)S(1)}, u32[]{:S(2)}, u32[]{:S(2)}) collective-permute-start(bf16[1024,256]{1,0:T(8,128)(2,1)S(1)} %collective-permute-done.7.refs_3_), channel_id=1, source_target_pairs={{0,16},{16,0},{1,17},{17,1},{2,18},{18,2},{3,19},{19,3},{4,20},{20... | collective-permute-start | bytes 1572872 | tf_op jit(solution)/shard_map/ppermute | solution.py:367
  49.3 14.7 %collective-permute-start.14 = (bf16[1024,256]{1,0:T(8,128)(2,1)S(1)}, bf16[1024,256]{1,0:T(8,128)(2,1)S(1)}, u32[]{:S(2)}, u32[]{:S(2)}) collective-permute-start(bf16[1024,256]{1,0:T(8,128)(2,1)S(1)} %collective-permute-done.10.refs_7_), channel_id=1, source_target_pairs={{0,4},{1,3},{4,8},{5,1},{8,12},{9,5},{12,14},{13,9},{14,10},{15,13... | collective-permute-start | bytes 1572872 | tf_op jit(solution)/shard_map/ppermute | solution.py:364
  59.1 5.7 %collective-permute-start.16 = (f32[512,256]{1,0:T(8,128)S(1)}, f32[512,256]{1,0:T(8,128)S(1)}, u32[]{:S(2)}, u32[]{:S(2)}) collective-permute-start(f32[512,256]{1,0:T(8,128)S(1)} %get-tuple-element.97), channel_id=1, source_target_pairs={{0,1},{1,0},{2,3},{3,2},{4,5},{5,4},{6,7},{7,6},{8,9},{9,8},{10,11... | collective-permute-start | bytes 1572872 | tf_op jit(solution)/shard_map/ppermute | solution.py:370
  59.1 11.4 %collective-permute-start.13 = (bf16[1024,256]{1,0:T(8,128)(2,1)S(1)}, bf16[1024,256]{1,0:T(8,128)(2,1)S(1)}, u32[]{:S(2)}, u32[]{:S(2)}) collective-permute-start(bf16[1024,256]{1,0:T(8,128)(2,1)S(1)} %collective-permute-done.9.refs_6_), channel_id=1, source_target_pairs={{0,2},{1,5},{4,0},{5,9},{8,4},{9,13},{12,8},{13,15},{14,12},{15,11... | collective-permute-start | bytes 1572872 | tf_op jit(solution)/shard_map/ppermute | solution.py:361
  61.9 8.7 %collective-permute-start.17 = (f32[512,256]{1,0:T(8,128)S(1)}, f32[512,256]{1,0:T(8,128)S(1)}, u32[]{:S(2)}, u32[]{:S(2)}) collective-permute-start(f32[512,256]{1,0:T(8,128)S(1)} %get-tuple-element.100), channel_id=1, source_target_pairs={{0,1},{1,0},{2,3},{3,2},{4,5},{5,4},{6,7},{7,6},{8,9},{9,8},{10,11... | collective-permute-start | bytes 1572872 | tf_op jit(solution)/shard_map/ppermute | solution.py:370
  61.9 14.6 %collective-permute-start.19 = (bf16[1024,256]{1,0:T(8,128)(2,1)S(1)}, bf16[1024,256]{1,0:T(8,128)(2,1)S(1)}, u32[]{:S(2)}, u32[]{:S(2)}) collective-permute-start(bf16[1024,256]{1,0:T(8,128)(2,1)S(1)} %collective-permute-done.2.refs_5_), channel_id=1, source_target_pairs={{0,16},{16,0},{1,17},{17,1},{2,18},{18,2},{3,19},{19,3},{4,20},{20... | collective-permute-start | bytes 1572872 | tf_op jit(solution)/shard_map/ppermute | solution.py:367
  64.0 12.6 %collective-permute-start.18 = (bf16[1024,256]{1,0:T(8,128)(2,1)S(1)}, bf16[1024,256]{1,0:T(8,128)(2,1)S(1)}, u32[]{:S(2)}, u32[]{:S(2)}) collective-permute-start(bf16[1024,256]{1,0:T(8,128)(2,1)S(1)} %collective-permute-done.15.refs_4_), channel_id=1, source_target_pairs={{0,4},{1,3},{4,8},{5,1},{8,12},{9,5},{12,14},{13,9},{14,10},{15,13... | collective-permute-start | bytes 1572872 | tf_op jit(solution)/shard_map/ppermute | solution.py:364
  69.6 10.1 %collective-permute-start.23 = (f32[2,512,256]{2,1,0:T(8,128)S(1)}, f32[2,512,256]{2,1,0:T(8,128)S(1)}, u32[]{:S(2)}, u32[]{:S(2)}) collective-permute-start(f32[2,512,256]{2,1,0:T(8,128)S(1)} %get-tuple-element.118), channel_id=1, source_target_pairs={{0,1},{1,0},{2,3},{3,2},{4,5},{5,4},{6,7},{7,6},{8,9},{9,8},{10,11... | collective-permute-start | bytes 3145736 | tf_op jit(solution)/shard_map/ppermute | solution.py:370
  70.6 9.1 %collective-permute-start.24 = (f32[2,512,256]{2,1,0:T(8,128)S(1)}, f32[2,512,256]{2,1,0:T(8,128)S(1)}, u32[]{:S(2)}, u32[]{:S(2)}) collective-permute-start(f32[2,512,256]{2,1,0:T(8,128)S(1)} %get-tuple-element.119), channel_id=1, source_target_pairs={{0,1},{1,0},{2,3},{3,2},{4,5},{5,4},{6,7},{7,6},{8,9},{9,8},{10,11... | collective-permute-start | bytes 3145736 | tf_op jit(solution)/shard_map/ppermute | solution.py:370
  70.6 9.0 %collective-permute-start.22 = (bf16[1024,256]{1,0:T(8,128)(2,1)S(1)}, bf16[1024,256]{1,0:T(8,128)(2,1)S(1)}, u32[]{:S(2)}, u32[]{:S(2)}) collective-permute-start(bf16[1024,256]{1,0:T(8,128)(2,1)S(1)} %collective-permute-done.13.refs_2_), channel_id=1, source_target_pairs={{0,1},{1,0},{2,3},{3,2},{4,5},{5,4},{6,7},{7,6},{8,9},{9,8},{10,11... | collective-permute-start | bytes 1572872 | tf_op jit(solution)/shard_map/ppermute | solution.py:370
  76.6 3.1 %collective-permute-start.21 = (bf16[1024,256]{1,0:T(8,128)(2,1)S(1)}, bf16[1024,256]{1,0:T(8,128)(2,1)S(1)}, u32[]{:S(2)}, u32[]{:S(2)}) collective-permute-start(bf16[1024,256]{1,0:T(8,128)(2,1)S(1)} %collective-permute-done.18.refs_1_), channel_id=1, source_target_pairs={{0,1},{1,0},{2,3},{3,2},{4,5},{5,4},{6,7},{7,6},{8,9},{9,8},{10,11... | collective-permute-start | bytes 1572872 | tf_op jit(solution)/shard_map/ppermute | solution.py:370
  (9 other events, 92.6 us)

commit v10 on v7

--- a/solution.py
+++ b/solution.py
@@ -80,7 +80,7 @@
     return total
 
 
-def wave_kernel(full, part, arrived, whole, tokens, *refs):
+def wave_kernel(full, part, arrived, whole, tokens, chained, stacked, *refs):
     count = len(full) + len(part)
     refs = list(refs)
     context = refs.pop(0) if "mine" in tokens else None
@@ -92,14 +92,19 @@
         jobs = [[(shard.at[half_slice(second, half)], second) for second in (False, True)]]
     else:
         jobs = [[(refs.pop(0), False)] + ([(refs.pop(0), True)] if j < len(full) else []) for j in range(count)]
-    if arrived:
-        received, before = [refs.pop(0) for _ in arrived], refs.pop(0)
+    received = [refs.pop(0) for _ in arrived]
+    before = refs.pop(0) if chained else None
     mine = refs.pop(0) if "mine" in tokens else None
-    theirs = [refs.pop(0) for _ in range(count)] if "theirs" in tokens else None
+    theirs = None
+    if "theirs" in tokens:
+        stacks = [refs.pop(0) for _ in range(2 if stacked else count)]
+        theirs = stacks
+        if stacked:
+            theirs = [stacks[0].at[j] for j in range(len(full))] + [stacks[1].at[j] for j in range(len(part))]
     finished = refs.pop(0) if arrived else None
     squares = refs.pop(0) if "mine" in tokens else None
     rows, width = mine.shape[1:] if "mine" in tokens else theirs[0].shape
-    if arrived:
+    if chained:
         squares[...] = before[...]
     elif "mine" in tokens:
         squares[...] = jnp.zeros_like(squares)
@@ -116,32 +121,39 @@
                 if j < len(full):
                     add_squares(squares, at, total)
 
-    for j, distance in enumerate(arrived):
+    for j, (distance, same) in enumerate(arrived):
 
         @row_steps(rows)
         def _(at):
-            total = received[j][at, :] + residual[at, columns(distance, False, width)].astype(jnp.float32)
+            total = received[j][at, :] + residual[at, columns(distance, same, width)].astype(jnp.float32)
             finished[j, at, :] = total
             add_squares(squares, at, total)
 
 
-def wave(full, part, arrived, context, other_context, residual, pieces, received=None, squares=None):
+def wave(
+    full, part, arrived, context, other_context, residual, pieces, received=None, squares=None, stacked=False
+):
     tokens = (("mine",) if context is not None else ()) + (("theirs",) if other_context is not None else ())
     count = len(full) + len(part)
     rows = (context if other_context is None else other_context).shape[0]
     whole = len(pieces) == 1
     block = jax.ShapeDtypeStruct((rows, pieces[0].shape[1]), jnp.float32)
-    outs = [jax.ShapeDtypeStruct((count,) + block.shape, jnp.float32)] if "mine" in tokens else []
-    outs += [block] * count if "theirs" in tokens else []
+
+    def stack(n):
+        return jax.ShapeDtypeStruct((n,) + block.shape, jnp.float32)
+
+    outs = [stack(count)] if "mine" in tokens else []
+    if "theirs" in tokens:
+        outs += [stack(len(full)), stack(len(part))] if stacked else [block] * count
     operands = [x for x in (context, other_context) if x is not None]
     operands += ([residual] if "mine" in tokens else []) + list(pieces)
     if arrived:
-        operands += [*received, squares]
+        operands += [*received] + ([] if squares is None else [squares])
         outs.append(jax.ShapeDtypeStruct((len(arrived),) + block.shape, jnp.float32))
     if "mine" in tokens:
         outs.append(jax.ShapeDtypeStruct((rows, LANES), jnp.float32))
     return pl.pallas_call(
-        functools.partial(wave_kernel, full, part, arrived, whole, tokens),
+        functools.partial(wave_kernel, full, part, arrived, whole, tokens, squares is not None, stacked),
         out_shape=outs,
         in_specs=[VMEM_SPEC] * len(operands),
         out_specs=[VMEM_SPEC] * len(outs),
@@ -361,35 +373,36 @@
 
     own = own_half(out_proj)
     a = from_next(own)
-    c = other_core(context)
-    h0, sq0 = wave((0,), (), (), context, None, residual, [out_proj])
-    own, h0, sq0 = wait((own, h0, sq0))
+    c, q = other_core(context), other_core(queries)
+    (p0,) = wave((0,), (), (), None, context, None, [out_proj])
+    own, p0 = wait((own, p0))
     b = from_last(own)
 
-    n1, sq0 = wait((a, sq0))
+    n1, p0 = wait((a, p0))
     x = over_x(n1)
     a = from_next(n1)
     context2, n1 = wait((c, n1))
     (t0,) = wave((0,), (), (), None, context2, None, [out_proj])
-    l1, n1, t0 = wait((b, n1, t0))
+    l1, n1, t0, queries2 = wait((b, n1, t0, q))
     b = from_last(l1)
     r0 = other_core(t0)
 
-    n2, l1, queries = wait((a, l1, queries))
-    queries2 = other_core(queries)
+    n2, l1 = wait((a, l1))
     xn1, n2 = wait((x, n2))
     x = over_x(n2)
     a = from_next(n2)
-    h1, t1, f0, sq1 = wave((1,), (), (0,), context, context2, residual, [n1, xn1], [r0], sq0)
+    h1, t1, f0, sq1 = wave(
+        (1,), (), ((0, True), (0, False)), context, context2, residual, [n1, xn1], [p0, r0], None
+    )
     l2, n2, t1, sq1 = wait((b, n2, t1, sq1))
     b = from_last(l2)
     r1 = other_core(t1)
 
-    xn2, l2, queries2 = wait((x, l2, queries2))
+    xn2, l2 = wait((x, l2))
     x = over_x(l2)
     a2 = from_next(xn2)
     n3, xn2 = wait((a, xn2))
-    h2, t2, t2p, f1, sq2 = wave((2,), (-1,), (1,), context, context2, residual, [n2, xn2, l1], [r1], sq1)
+    h2, t2, t2p, f1, sq2 = wave((2,), (-1,), ((1, False),), context, context2, residual, [n2, xn2, l1], [r1], sq1)
     l3, n3, t2, t2p, sq2 = wait((b, n3, t2, t2p, sq2))
     b = from_last(l3)
     r2, r2p = other_core(t2), other_core(t2p)
@@ -398,17 +411,17 @@
     a = from_next(n3x)
     xl2, l1, n3x = wait((x, l1, n3x))
     x = over_x(l1)
-    h3, t3a, t3b, t3p, f2, sq3 = wave(
-        (-2, 3), (-3,), (2,), context, context2, residual, [l2, xl2, n3, n3x, l3], [r2], sq2
-    )
-    l4, xl2, t3a, t3b, t3p, sq3, r2p = wait((b, xl2, t3a, t3b, t3p, sq3, r2p))
+    h3, t3a, t3p, f2, sq3 = wave(
+        (-2, 3), (-3,), ((2, False),), context, context2, residual, [l2, xl2, n3, n3x, l3], [r2], sq2, stacked=True
+    )
+    l4, xl2, t3a, t3p, sq3, r2p = wait((b, xl2, t3a, t3p, sq3, r2p))
     b = from_last(xl2)
-    r3a, r3b, r3p = other_core(t3a), other_core(t3b), other_core(t3p)
+    r3a, r3p = other_core(t3a), other_core(t3p)
     l4s = other_core(l4)
 
     n4x, l4 = wait((a, l4))
     n4xs = other_core(n4x)
-    xl1, n4x = wait((x, n4x))
+    xl1, n4x, r3p, l4s = wait((x, n4x, r3p, l4s))
     xl1s = other_core(xl1)
     l3x, xl1 = wait((b, xl1))
     l3xs = other_core(l3x)
@@ -422,10 +435,10 @@
     items = tuple(
         (base, parts, True, distance, False)
         for base, parts, distance in zip(
-            ((8, None), (9, None), None, (10, None), (11, None)), missing + ((), ()), (-1, -3, 4, -2, 3)
+            ((8, None), (9, 0), None, (10, 0), (10, 1)), missing + ((), ()), (-1, -3, 4, -2, 3)
         )
     )
-    hidden = [h0, h1, h2, h3, h4, f0, f1, f2, r2p, r3p, r3a, r3b]
+    hidden = [f0, h1, h2, h3, h4, f0, f1, f2, r2p, r3p, r3a]
     sources = (
         (0, 0, 0, True),
         (1, 0, 1, True),
@@ -435,7 +448,7 @@
         (4, 0, -1, True),
         (4, 1, -3, True),
         (4, 2, 4, True),
-        (5, 0, 0, False),
+        (0, 1, 0, False),
         (6, 0, 1, False),
         (7, 0, 2, False),
     )

time: 105 us -> 104 us (level)
  waiting for transfers between devices: 41.8 us -> 34.6 us
  starting transfers between devices: 17.6 us -> 23.9 us
  local copies, waits for them, and re-layouts: 5.03 us -> 2.85 us
  blocking collectives: 21.3 us -> 22.6 us
    ppermute x5, waiting for transfers between devices: 27.8 us -> 11 us  [from_last(): return lax.ppermute(piece, 'dp', ring(1))]
    ppermute x5, waiting for transfers between devices: 3.74 us -> 11.1 us  [from_next(): return lax.ppermute(piece, 'dp', ring(-1))]
    ppermute x5, starting transfers between devices: 0.13 us -> 5.87 us  [from_last(): return lax.ppermute(piece, 'dp', ring(1))]
    ppermute x13 -> x12, starting transfers between devices: 3.6 us -> 7.28 us  [other_core(): return lax.ppermute(piece, 'dp', [(i, i ^ 1) for i in range(ranks)])]
    ppermute x4, waiting for transfers between devices: 10.2 us -> 12.5 us  [over_x(): return lax.ppermute(piece, 'groups', [(0, 1), (1, 0)])]
    unnamed x16 -> x14, local copies, waits for them, and re-layouts: 5.03 us -> 2.84 us
    ppermute x4, starting transfers between devices: 5.76 us -> 4.13 us  [over_x(): return lax.ppermute(piece, 'groups', [(0, 1), (1, 0)])]
    ppermute x5, starting transfers between devices: 8.12 us -> 6.63 us  [from_next(): return lax.ppermute(piece, 'dp', ring(-1))]
  transfers between devices with their start and end apart: 27 -> 26, of which waited for: 11 -> 13; matrix products, arithmetic and copies ran while one was open for 0% -> 0% of each run, Pallas kernels for 11% -> 12%
where the time goes in v10:
time: 104 us; the launch traced here: 103 us
  waiting for transfers between devices  34.6 us (33%)
  starting transfers between devices  23.9 us (23%)
  blocking collectives  22.6 us (22%)
  Pallas kernels  18 us (17%)
  local copies, waits for them, and re-layouts  2.85 us (3%)
  between operations  1.46 us (1%)
    all_to_all x2, blocking collectives, spread(): lax.all_to_all(blocks, 'dp', 0, 0, axis_index_groups=same_core, tiled=True)  22.6 us
    ppermute x4, waiting for transfers between devices, over_x(): return lax.ppermute(piece, 'groups', [(0, 1), (1, 0)])  12.5 us
    ppermute x5, waiting for transfers between devices, from_next(): return lax.ppermute(piece, 'dp', ring(-1))  11.1 us
    ppermute x5, waiting for transfers between devices, from_last(): return lax.ppermute(piece, 'dp', ring(1))  11 us
    pallas_call x5, Pallas kernels, wave(): pl.pallas_call(functools.partial(wave_kernel, full, part, arrived, whole,...  9.94 us
    ppermute x12, starting transfers between devices, other_core(): return lax.ppermute(piece, 'dp', [(i, i ^ 1) for i in range(ranks)])  7.28 us
    ppermute x5, starting transfers between devices, from_next(): return lax.ppermute(piece, 'dp', ring(-1))  6.63 us
    ppermute x5, starting transfers between devices, from_last(): return lax.ppermute(piece, 'dp', ring(1))  5.87 us
  transfers between devices with their start and end apart: 26, of which 13 were waited for; matrix products, arithmetic and copies ran while one was open for 0% of the time, Pallas kernels for 12%

profile of v10, /device:TPU:0, one launch (start us, length us, event | category | flops | bytes accessed | tf_op | source)
XLA Modules:
  0.0 103.4 jit_solution(10935472079113355279)
XLA Ops:
  2.4 2.6 %collective-permute-start.2 = (bf16[1024,256]{1,0:T(8,128)(2,1)S(1)}, bf16[1024,256]{1,0:T(8,128)(2,1)S(1)}, u32[]{:S(2)}, u32[]{:S(2)}) collective-permute-start(bf16[1024,256]{1,0:T(8,128)(2,1)S(1)} %shard_map.94), channel_id=1, source_target_pairs={{0,2},{1,5},{4,0},{5,9},{8,4},{9,13},{12,8},{13,15},{14,12},{15,11... | collective-permute-start | bytes 1572872 | tf_op jit(solution)/shard_map/ppermute | solution.py:361
  5.3 1.6 %copy-done.1 = bf16[512,2048]{1,0:T(8,128)(2,1)S(1)} copy-done((bf16[512,2048]{1,0:T(8,128)(2,1)S(1)}, bf16[512,2048]{1,0:T(8,128)(2,1)}, u32[]{:S(2)}) %copy-start.1) | copy-done | bytes 2097176
  7.8 1.6 %collective-permute-start = (bf16[1024,256]{1,0:T(8,128)(2,1)S(1)}, bf16[1024,256]{1,0:T(8,128)(2,1)S(1)}, u32[]{:S(2)}, u32[]{:S(2)}) collective-permute-start(bf16[1024,256]{1,0:T(8,128)(2,1)S(1)} %shard_map.94), channel_id=1, source_target_pairs={{0,4},{1,3},{4,8},{5,1},{8,12},{9,5},{12,14},{13,9},{14,10},{15,13... | collective-permute-start | bytes 1572872 | tf_op jit(solution)/shard_map/ppermute | solution.py:364
  9.4 4.3 %collective-permute-done.2.refs_3_ = bf16[1024,256]{1,0:T(8,128)(2,1)S(1)} collective-permute-done((bf16[1024,256]{1,0:T(8,128)(2,1)S(1)}, bf16[1024,256]{1,0:T(8,128)(2,1)S(1)}, u32[]{:S(2)}, u32[]{:S(2)}) %collective-permute-start.2) | collective-permute-done | bytes 524320 | tf_op jit(solution)/shard_map/ppermute | solution.py:361
  13.7 2.3 %collective-permute-start.6 = (bf16[1024,256]{1,0:T(8,128)(2,1)S(1)}, bf16[1024,256]{1,0:T(8,128)(2,1)S(1)}, u32[]{:S(2)}, u32[]{:S(2)}) collective-permute-start(bf16[1024,256]{1,0:T(8,128)(2,1)S(1)} %collective-permute-done.2.refs_3_), channel_id=1, source_target_pairs={{0,2},{1,5},{4,0},{5,9},{8,4},{9,13},{12,8},{13,15},{14,12},{15,11... | collective-permute-start | bytes 1572872 | tf_op jit(solution)/shard_map/ppermute | solution.py:361
  16.1 1.5 %collective-permute-start.5 = (bf16[1024,256]{1,0:T(8,128)(2,1)S(1)}, bf16[1024,256]{1,0:T(8,128)(2,1)S(1)}, u32[]{:S(2)}, u32[]{:S(2)}) collective-permute-start(bf16[1024,256]{1,0:T(8,128)(2,1)S(1)} %collective-permute-done.2.refs_3_), channel_id=1, source_target_pairs={{0,16},{16,0},{1,17},{17,1},{2,18},{18,2},{3,19},{19,3},{4,20},{20... | collective-permute-start | bytes 1572872 | tf_op jit(solution)/shard_map/ppermute | solution.py:367
  19.5 2.0 %collective-permute-start.4 = (bf16[1024,256]{1,0:T(8,128)(2,1)S(1)}, bf16[1024,256]{1,0:T(8,128)(2,1)S(1)}, u32[]{:S(2)}, u32[]{:S(2)}) collective-permute-start(bf16[1024,256]{1,0:T(8,128)(2,1)S(1)} %collective-permute-done.refs_5_), channel_id=1, source_target_pairs={{0,4},{1,3},{4,8},{5,1},{8,12},{9,5},{12,14},{13,9},{14,10},{15,13... | collective-permute-start | bytes 1572872 | tf_op jit(solution)/shard_map/ppermute | solution.py:364
  21.5 2.8 %collective-permute-done.6.refs_3_ = bf16[1024,256]{1,0:T(8,128)(2,1)S(1)} collective-permute-done((bf16[1024,256]{1,0:T(8,128)(2,1)S(1)}, bf16[1024,256]{1,0:T(8,128)(2,1)S(1)}, u32[]{:S(2)}, u32[]{:S(2)}) %collective-permute-start.6) | collective-permute-done | bytes 524320 | tf_op jit(solution)/shard_map/ppermute | solution.py:361
  24.2 3.9 %collective-permute-done.5.refs_4_ = bf16[1024,256]{1,0:T(8,128)(2,1)S(1)} collective-permute-done((bf16[1024,256]{1,0:T(8,128)(2,1)S(1)}, bf16[1024,256]{1,0:T(8,128)(2,1)S(1)}, u32[]{:S(2)}, u32[]{:S(2)}) %collective-permute-start.5) | collective-permute-done | bytes 524320 | tf_op jit(solution)/shard_map/ppermute | solution.py:367
  30.9 1.8 %shard_map.97 = (f32[1,512,256]{2,1,0:T(8,128)S(1)}, f32[512,256]{1,0:T(8,128)S(1)}, f32[2,512,256]{2,1,0:T(8,128)S(1)}, f32[512,128]{1,0:T(8,128)S(1)}) custom-call(bf16[512,2048]{1,0:T(8,128)(2,1)S(1)} %copy-done.2, bf16[512,2048]{1,0:T(8,128)(2,1)S(1)} %collective-permute-done.1.refs_0_.refs_1_, bf16[512,4096]{1,0:T(8,128)(2,1)S(1)} %copy-done, ...), custom_call_target="tpu_custom_call" | custom-call | flops 1000 | bytes 1000 | tf_op jit(solution)/shard_map/pallas_call | solution.py:155
  33.6 5.8 %collective-permute-done.10.refs_4_ = bf16[1024,256]{1,0:T(8,128)(2,1)S(1)} collective-permute-done((bf16[1024,256]{1,0:T(8,128)(2,1)S(1)}, bf16[1024,256]{1,0:T(8,128)(2,1)S(1)}, u32[]{:S(2)}, u32[]{:S(2)}) %collective-permute-start.10) | collective-permute-done | bytes 524320 | tf_op jit(solution)/shard_map/ppermute | solution.py:367
  39.8 1.9 %collective-permute-done.9.refs_5_ = bf16[1024,256]{1,0:T(8,128)(2,1)S(1)} collective-permute-done((bf16[1024,256]{1,0:T(8,128)(2,1)S(1)}, bf16[1024,256]{1,0:T(8,128)(2,1)S(1)}, u32[]{:S(2)}, u32[]{:S(2)}) %collective-permute-start.9) | collective-permute-done | bytes 524320 | tf_op jit(solution)/shard_map/ppermute | solution.py:361
  42.3 2.5 %shard_map.98 = (f32[2,512,256]{2,1,0:T(8,128)S(1)}, f32[512,256]{1,0:T(8,128)S(1)}, f32[512,256]{1,0:T(8,128)S(1)}, f32[1,512,256]{2,1,0:T(8,128)S(1)}, f32[512,128]{1,0:T(8,128)S(1)}) custom-call(bf16[512,2048]{1,0:T(8,128)(2,1)S(1)} %copy-done.2, bf16[512,2048]{1,0:T(8,128)(2,1)S(1)} %collective-permute-done.1.refs_0_.refs_1_, ...), custom_call_target="tpu_custom_call" | custom-call | flops 1000 | bytes 1000 | tf_op jit(solution)/shard_map/pallas_call | solution.py:155
  47.0 2.5 %collective-permute-start.16 = (f32[512,256]{1,0:T(8,128)S(1)}, f32[512,256]{1,0:T(8,128)S(1)}, u32[]{:S(2)}, u32[]{:S(2)}) collective-permute-start(f32[512,256]{1,0:T(8,128)S(1)} %get-tuple-element.106), channel_id=1, source_target_pairs={{0,1},{1,0},{2,3},{3,2},{4,5},{5,4},{6,7},{7,6},{8,9},{9,8},{10,11... | collective-permute-start | bytes 1572872 | tf_op jit(solution)/shard_map/ppermute | solution.py:370
  49.5 2.0 %collective-permute-done.14.refs_6_ = bf16[1024,256]{1,0:T(8,128)(2,1)S(1)} collective-permute-done((bf16[1024,256]{1,0:T(8,128)(2,1)S(1)}, bf16[1024,256]{1,0:T(8,128)(2,1)S(1)}, u32[]{:S(2)}, u32[]{:S(2)}) %collective-permute-start.14) | collective-permute-done | bytes 524320 | tf_op jit(solution)/shard_map/ppermute | solution.py:361
  51.5 2.3 %collective-permute-done.13.refs_4_ = bf16[1024,256]{1,0:T(8,128)(2,1)S(1)} collective-permute-done((bf16[1024,256]{1,0:T(8,128)(2,1)S(1)}, bf16[1024,256]{1,0:T(8,128)(2,1)S(1)}, u32[]{:S(2)}, u32[]{:S(2)}) %collective-permute-start.13) | collective-permute-done | bytes 524320 | tf_op jit(solution)/shard_map/ppermute | solution.py:367
  54.4 3.9 %shard_map.99 = (f32[3,512,256]{2,1,0:T(8,128)S(1)}, f32[2,512,256]{2,1,0:T(8,128)S(1)}, f32[1,512,256]{2,1,0:T(8,128)S(1)}, f32[1,512,256]{2,1,0:T(8,128)S(1)}, f32[512,128]{1,0:T(8,128)S(1)}) custom-call(bf16[512,2048]{1,0:T(8,128)(2,1)S(1)} %copy-done.2, bf16[512,2048]{1,0:T(8,128)(2,1)S(1)} %collective-permute-done.1.refs_0_.refs_1_, ...), custom_call_target="tpu_custom_call" | custom-call | flops 1000 | bytes 1000 | tf_op jit(solution)/shard_map/pallas_call | solution.py:155
  58.3 2.3 %collective-permute-done.12.refs_2_ = bf16[1024,256]{1,0:T(8,128)(2,1)S(1)} collective-permute-done((bf16[1024,256]{1,0:T(8,128)(2,1)S(1)}, bf16[1024,256]{1,0:T(8,128)(2,1)S(1)}, u32[]{:S(2)}, u32[]{:S(2)}) %collective-permute-start.12) | collective-permute-done | bytes 524320 | tf_op jit(solution)/shard_map/ppermute | solution.py:364
  61.3 2.8 %collective-permute-start.25 = (f32[2,512,256]{2,1,0:T(8,128)S(1)}, f32[2,512,256]{2,1,0:T(8,128)S(1)}, u32[]{:S(2)}, u32[]{:S(2)}) collective-permute-start(f32[2,512,256]{2,1,0:T(8,128)S(1)} %get-tuple-element.129), channel_id=1, source_target_pairs={{0,1},{1,0},{2,3},{3,2},{4,5},{5,4},{6,7},{7,6},{8,9},{9,8},{10,11... | collective-permute-start | bytes 3145736 | tf_op jit(solution)/shard_map/ppermute | solution.py:370
  64.6 7.0 %collective-permute-done.17.refs_1_ = bf16[1024,256]{1,0:T(8,128)(2,1)S(1)} collective-permute-done((bf16[1024,256]{1,0:T(8,128)(2,1)S(1)}, bf16[1024,256]{1,0:T(8,128)(2,1)S(1)}, u32[]{:S(2)}, u32[]{:S(2)}) %collective-permute-start.17) | collective-permute-done | bytes 524320 | tf_op jit(solution)/shard_map/ppermute | solution.py:364
  72.7 2.2 %shard_map.100 = (f32[3,512,256]{2,1,0:T(8,128)S(1)}, f32[512,128]{1,0:T(8,128)S(1)}) custom-call(bf16[512,2048]{1,0:T(8,128)(2,1)S(1)} %copy-done.2, bf16[512,4096]{1,0:T(8,128)(2,1)S(1)} %copy-done, f32[512,128]{1,0:T(8,128)S(1)} %get-tuple-element.107.before, bf16[1024,256]{1,0:T(8,128)(2,1)S(1)} %collective-permute-done.18.refs_0_, ...), custom_call_target="tpu_custom_call" | custom-call | flops 1000 | bytes 1000 | tf_op jit(solution)/shard_map/pallas_call | solution.py:191
  75.0 4.0 %shard_map.101 = (f32[1,4096]{1,0:T(1,128)}, bf16[8,48,128]{2,1,0:T(8,128)(2,1)S(1)}) custom-call(s32[1]{0:T(128)S(6)} %copy.10.length, bf16[512,2048]{1,0:T(8,128)(2,1)S(1)} %copy-done.2, bf16[512,4096]{1,0:T(8,128)(2,1)S(1)} %copy-done, f32[512,128]{1,0:T(8,128)S(1)} %get-tuple-element.120.before, f32[1,4096]{1,0:T(1,128)S(1)} %bitcast.2, ...), custom_call_target="tpu_custom_call" | custom-call | flops 1000 | bytes 1000 | tf_op jit(solution)/shard_map/pallas_call | solution.py:244
  79.0 12.6 %all_to_all.10.got = bf16[8,48,128]{2,1,0:T(8,128)(2,1)S(1)} all-to-all(bf16[8,48,128]{2,1,0:T(8,128)(2,1)S(1)} %get-tuple-element.131), channel_id=1, replica_groups={{0,2,4,6,8,10,12,14},{1,3,5,7,9,11,13,15},{16,18,20,22,24,26,28,30},{17..., dimensions={0} | all-to-all | bytes 196608 | tf_op jit(solution)/shard_map/all_to_all | solution.py:472
  92.6 10.0 %all_to_all.11.got = f32[8,40,128]{2,1,0:T(8,128)S(1)} all-to-all(f32[8,40,128]{2,1,0:T(8,128)S(1)} %shard_map.102), channel_id=1, replica_groups={{0,2,4,6,8,10,12,14},{1,3,5,7,9,11,13,15},{16,18,20,22,24,26,28,30},{17..., dimensions={0} | all-to-all | bytes 327680 | tf_op jit(solution)/shard_map/all_to_all | solution.py:472
  (56 shorter events, 15.7 us)
Async XLA Ops:
  0.6 16.9 %collective-permute-start.1 = (bf16[512,2048]{1,0:T(8,128)(2,1)}, bf16[512,2048]{1,0:T(8,128)(2,1)S(1)}, u32[]{:S(2)}, u32[]{:S(2)}) collective-permute-start(bf16[512,2048]{1,0:T(8,128)(2,1)} %context.3), channel_id=1, source_target_pairs={{0,1},{1,0},{2,3},{3,2},{4,5},{5,4},{6,7},{7,6},{8,9},{9,8},{10,11... | collective-permute-start | bytes 6291464 | tf_op jit(solution)/shard_map/ppermute | solution.py:370
  2.4 11.3 %collective-permute-start.2 = (bf16[1024,256]{1,0:T(8,128)(2,1)S(1)}, bf16[1024,256]{1,0:T(8,128)(2,1)S(1)}, u32[]{:S(2)}, u32[]{:S(2)}) collective-permute-start(bf16[1024,256]{1,0:T(8,128)(2,1)S(1)} %shard_map.94), channel_id=1, source_target_pairs={{0,2},{1,5},{4,0},{5,9},{8,4},{9,13},{12,8},{13,15},{14,12},{15,11... | collective-permute-start | bytes 1572872 | tf_op jit(solution)/shard_map/ppermute | solution.py:361
  5.0 14.5 %collective-permute-start.3 = (bf16[112,4096]{1,0:T(8,128)(2,1)}, bf16[112,4096]{1,0:T(8,128)(2,1)S(1)}, u32[]{:S(2)}, u32[]{:S(2)}) collective-permute-start(bf16[112,4096]{1,0:T(8,128)(2,1)} %queries.1), channel_id=1, source_target_pairs={{0,1},{1,0},{2,3},{3,2},{4,5},{5,4},{6,7},{7,6},{8,9},{9,8},{10,11... | collective-permute-start | bytes 2752520 | tf_op jit(solution)/shard_map/ppermute | solution.py:370
  7.8 11.7 %collective-permute-start = (bf16[1024,256]{1,0:T(8,128)(2,1)S(1)}, bf16[1024,256]{1,0:T(8,128)(2,1)S(1)}, u32[]{:S(2)}, u32[]{:S(2)}) collective-permute-start(bf16[1024,256]{1,0:T(8,128)(2,1)S(1)} %shard_map.94), channel_id=1, source_target_pairs={{0,4},{1,3},{4,8},{5,1},{8,12},{9,5},{12,14},{13,9},{14,10},{15,13... | collective-permute-start | bytes 1572872 | tf_op jit(solution)/shard_map/ppermute | solution.py:364
  13.7 10.5 %collective-permute-start.6 = (bf16[1024,256]{1,0:T(8,128)(2,1)S(1)}, bf16[1024,256]{1,0:T(8,128)(2,1)S(1)}, u32[]{:S(2)}, u32[]{:S(2)}) collective-permute-start(bf16[1024,256]{1,0:T(8,128)(2,1)S(1)} %collective-permute-done.2.refs_3_), channel_id=1, source_target_pairs={{0,2},{1,5},{4,0},{5,9},{8,4},{9,13},{12,8},{13,15},{14,12},{15,11... | collective-permute-start | bytes 1572872 | tf_op jit(solution)/shard_map/ppermute | solution.py:361
  16.1 12.1 %collective-permute-start.5 = (bf16[1024,256]{1,0:T(8,128)(2,1)S(1)}, bf16[1024,256]{1,0:T(8,128)(2,1)S(1)}, u32[]{:S(2)}, u32[]{:S(2)}) collective-permute-start(bf16[1024,256]{1,0:T(8,128)(2,1)S(1)} %collective-permute-done.2.refs_3_), channel_id=1, source_target_pairs={{0,16},{16,0},{1,17},{17,1},{2,18},{18,2},{3,19},{19,3},{4,20},{20... | collective-permute-start | bytes 1572872 | tf_op jit(solution)/shard_map/ppermute | solution.py:367
  19.5 11.4 %collective-permute-start.7 = (f32[512,256]{1,0:T(8,128)S(1)}, f32[512,256]{1,0:T(8,128)S(1)}, u32[]{:S(2)}, u32[]{:S(2)}) collective-permute-start(f32[512,256]{1,0:T(8,128)S(1)} %shard_map.96), channel_id=1, source_target_pairs={{0,1},{1,0},{2,3},{3,2},{4,5},{5,4},{6,7},{7,6},{8,9},{9,8},{10,11... | collective-permute-start | bytes 1572872 | tf_op jit(solution)/shard_map/ppermute | solution.py:370
  19.5 13.2 %collective-permute-start.4 = (bf16[1024,256]{1,0:T(8,128)(2,1)S(1)}, bf16[1024,256]{1,0:T(8,128)(2,1)S(1)}, u32[]{:S(2)}, u32[]{:S(2)}) collective-permute-start(bf16[1024,256]{1,0:T(8,128)(2,1)S(1)} %collective-permute-done.refs_5_), channel_id=1, source_target_pairs={{0,4},{1,3},{4,8},{5,1},{8,12},{9,5},{12,14},{13,9},{14,10},{15,13... | collective-permute-start | bytes 1572872 | tf_op jit(solution)/shard_map/ppermute | solution.py:364
  28.2 11.2 %collective-permute-start.10 = (bf16[1024,256]{1,0:T(8,128)(2,1)S(1)}, bf16[1024,256]{1,0:T(8,128)(2,1)S(1)}, u32[]{:S(2)}, u32[]{:S(2)}) collective-permute-start(bf16[1024,256]{1,0:T(8,128)(2,1)S(1)} %collective-permute-done.6.refs_3_), channel_id=1, source_target_pairs={{0,16},{16,0},{1,17},{17,1},{2,18},{18,2},{3,19},{19,3},{4,20},{20... | collective-permute-start | bytes 1572872 | tf_op jit(solution)/shard_map/ppermute | solution.py:367
  29.7 12.1 %collective-permute-start.9 = (bf16[1024,256]{1,0:T(8,128)(2,1)S(1)}, bf16[1024,256]{1,0:T(8,128)(2,1)S(1)}, u32[]{:S(2)}, u32[]{:S(2)}) collective-permute-start(bf16[1024,256]{1,0:T(8,128)(2,1)S(1)} %collective-permute-done.6.refs_3_), channel_id=1, source_target_pairs={{0,2},{1,5},{4,0},{5,9},{8,4},{9,13},{12,8},{13,15},{14,12},{15,11... | collective-permute-start | bytes 1572872 | tf_op jit(solution)/shard_map/ppermute | solution.py:361
  32.7 9.6 %collective-permute-start.11 = (f32[512,256]{1,0:T(8,128)S(1)}, f32[512,256]{1,0:T(8,128)S(1)}, u32[]{:S(2)}, u32[]{:S(2)}) collective-permute-start(f32[512,256]{1,0:T(8,128)S(1)} %get-tuple-element.89), channel_id=1, source_target_pairs={{0,1},{1,0},{2,3},{3,2},{4,5},{5,4},{6,7},{7,6},{8,9},{9,8},{10,11... | collective-permute-start | bytes 1572872 | tf_op jit(solution)/shard_map/ppermute | solution.py:370
  32.8 12.7 %collective-permute-start.8 = (bf16[1024,256]{1,0:T(8,128)(2,1)S(1)}, bf16[1024,256]{1,0:T(8,128)(2,1)S(1)}, u32[]{:S(2)}, u32[]{:S(2)}) collective-permute-start(bf16[1024,256]{1,0:T(8,128)(2,1)S(1)} %collective-permute-done.4.refs_3_), channel_id=1, source_target_pairs={{0,4},{1,3},{4,8},{5,1},{8,12},{9,5},{12,14},{13,9},{14,10},{15,13... | collective-permute-start | bytes 1572872 | tf_op jit(solution)/shard_map/ppermute | solution.py:364
  39.4 12.1 %collective-permute-start.14 = (bf16[1024,256]{1,0:T(8,128)(2,1)S(1)}, bf16[1024,256]{1,0:T(8,128)(2,1)S(1)}, u32[]{:S(2)}, u32[]{:S(2)}) collective-permute-start(bf16[1024,256]{1,0:T(8,128)(2,1)S(1)} %collective-permute-done.10.refs_4_), channel_id=1, source_target_pairs={{0,2},{1,5},{4,0},{5,9},{8,4},{9,13},{12,8},{13,15},{14,12},{15,11... | collective-permute-start | bytes 1572872 | tf_op jit(solution)/shard_map/ppermute | solution.py:361
  41.7 12.1 %collective-permute-start.13 = (bf16[1024,256]{1,0:T(8,128)(2,1)S(1)}, bf16[1024,256]{1,0:T(8,128)(2,1)S(1)}, u32[]{:S(2)}, u32[]{:S(2)}) collective-permute-start(bf16[1024,256]{1,0:T(8,128)(2,1)S(1)} %collective-permute-done.4.refs_3_), channel_id=1, source_target_pairs={{0,16},{16,0},{1,17},{17,1},{2,18},{18,2},{3,19},{19,3},{4,20},{20... | collective-permute-start | bytes 1572872 | tf_op jit(solution)/shard_map/ppermute | solution.py:367
  45.5 8.9 %collective-permute-start.15 = (f32[512,256]{1,0:T(8,128)S(1)}, f32[512,256]{1,0:T(8,128)S(1)}, u32[]{:S(2)}, u32[]{:S(2)}) collective-permute-start(f32[512,256]{1,0:T(8,128)S(1)} %get-tuple-element.101), channel_id=1, source_target_pairs={{0,1},{1,0},{2,3},{3,2},{4,5},{5,4},{6,7},{7,6},{8,9},{9,8},{10,11... | collective-permute-start | bytes 1572872 | tf_op jit(solution)/shard_map/ppermute | solution.py:370
  45.6 15.1 %collective-permute-start.12 = (bf16[1024,256]{1,0:T(8,128)(2,1)S(1)}, bf16[1024,256]{1,0:T(8,128)(2,1)S(1)}, u32[]{:S(2)}, u32[]{:S(2)}) collective-permute-start(bf16[1024,256]{1,0:T(8,128)(2,1)S(1)} %collective-permute-done.8.refs_7_), channel_id=1, source_target_pairs={{0,4},{1,3},{4,8},{5,1},{8,12},{9,5},{12,14},{13,9},{14,10},{15,13... | collective-permute-start | bytes 1572872 | tf_op jit(solution)/shard_map/ppermute | solution.py:364
  47.0 13.7 %collective-permute-start.16 = (f32[512,256]{1,0:T(8,128)S(1)}, f32[512,256]{1,0:T(8,128)S(1)}, u32[]{:S(2)}, u32[]{:S(2)}) collective-permute-start(f32[512,256]{1,0:T(8,128)S(1)} %get-tuple-element.106), channel_id=1, source_target_pairs={{0,1},{1,0},{2,3},{3,2},{4,5},{5,4},{6,7},{7,6},{8,9},{9,8},{10,11... | collective-permute-start | bytes 1572872 | tf_op jit(solution)/shard_map/ppermute | solution.py:370
  51.5 9.8 %collective-permute-start.19 = (bf16[1024,256]{1,0:T(8,128)(2,1)S(1)}, bf16[1024,256]{1,0:T(8,128)(2,1)S(1)}, u32[]{:S(2)}, u32[]{:S(2)}) collective-permute-start(bf16[1024,256]{1,0:T(8,128)(2,1)S(1)} %collective-permute-done.14.refs_6_), channel_id=1, source_target_pairs={{0,2},{1,5},{4,0},{5,9},{8,4},{9,13},{12,8},{13,15},{14,12},{15,11... | collective-permute-start | bytes 1572872 | tf_op jit(solution)/shard_map/ppermute | solution.py:361
  53.8 10.7 %collective-permute-start.18 = (bf16[1024,256]{1,0:T(8,128)(2,1)S(1)}, bf16[1024,256]{1,0:T(8,128)(2,1)S(1)}, u32[]{:S(2)}, u32[]{:S(2)}) collective-permute-start(bf16[1024,256]{1,0:T(8,128)(2,1)S(1)} %collective-permute-done.refs_5_), channel_id=1, source_target_pairs={{0,16},{16,0},{1,17},{17,1},{2,18},{18,2},{3,19},{19,3},{4,20},{20... | collective-permute-start | bytes 1572872 | tf_op jit(solution)/shard_map/ppermute | solution.py:367
  60.7 3.9 %collective-permute-start.20 = (f32[1,512,256]{2,1,0:T(8,128)S(1)}, f32[1,512,256]{2,1,0:T(8,128)S(1)}, u32[]{:S(2)}, u32[]{:S(2)}) collective-permute-start(f32[1,512,256]{2,1,0:T(8,128)S(1)} %get-tuple-element.112), channel_id=1, source_target_pairs={{0,1},{1,0},{2,3},{3,2},{4,5},{5,4},{6,7},{7,6},{8,9},{9,8},{10,11... | collective-permute-start | bytes 1572872 | tf_op jit(solution)/shard_map/ppermute | solution.py:370
  60.7 3.9 %collective-permute-start.21 = (bf16[1024,256]{1,0:T(8,128)(2,1)S(1)}, bf16[1024,256]{1,0:T(8,128)(2,1)S(1)}, u32[]{:S(2)}, u32[]{:S(2)}) collective-permute-start(bf16[1024,256]{1,0:T(8,128)(2,1)S(1)} %collective-permute-done.12.refs_2_), channel_id=1, source_target_pairs={{0,1},{1,0},{2,3},{3,2},{4,5},{5,4},{6,7},{7,6},{8,9},{9,8},{10,11... | collective-permute-start | bytes 1572872 | tf_op jit(solution)/shard_map/ppermute | solution.py:370
  61.2 10.3 %collective-permute-start.17 = (bf16[1024,256]{1,0:T(8,128)(2,1)S(1)}, bf16[1024,256]{1,0:T(8,128)(2,1)S(1)}, u32[]{:S(2)}, u32[]{:S(2)}) collective-permute-start(bf16[1024,256]{1,0:T(8,128)(2,1)S(1)} %collective-permute-done.13.refs_4_), channel_id=1, source_target_pairs={{0,4},{1,3},{4,8},{5,1},{8,12},{9,5},{12,14},{13,9},{14,10},{15,13... | collective-permute-start | bytes 1572872 | tf_op jit(solution)/shard_map/ppermute | solution.py:364
  61.3 13.6 %collective-permute-start.25 = (f32[2,512,256]{2,1,0:T(8,128)S(1)}, f32[2,512,256]{2,1,0:T(8,128)S(1)}, u32[]{:S(2)}, u32[]{:S(2)}) collective-permute-start(f32[2,512,256]{2,1,0:T(8,128)S(1)} %get-tuple-element.129), channel_id=1, source_target_pairs={{0,1},{1,0},{2,3},{3,2},{4,5},{5,4},{6,7},{7,6},{8,9},{9,8},{10,11... | collective-permute-start | bytes 3145736 | tf_op jit(solution)/shard_map/ppermute | solution.py:370
  64.6 10.3 %collective-permute-start.24 = (bf16[1024,256]{1,0:T(8,128)(2,1)S(1)}, bf16[1024,256]{1,0:T(8,128)(2,1)S(1)}, u32[]{:S(2)}, u32[]{:S(2)}) collective-permute-start(bf16[1024,256]{1,0:T(8,128)(2,1)S(1)} %collective-permute-done.19.refs_3_), channel_id=1, source_target_pairs={{0,1},{1,0},{2,3},{3,2},{4,5},{5,4},{6,7},{7,6},{8,9},{9,8},{10,11... | collective-permute-start | bytes 1572872 | tf_op jit(solution)/shard_map/ppermute | solution.py:370
  (9 other events, 102.2 us)

commit v11 on v10

--- a/solution.py
+++ b/solution.py
@@ -388,9 +388,10 @@
     r0 = other_core(t0)
 
     n2, l1 = wait((a, l1))
+    x2 = over_x(n2)
+    a = from_next(n2)
     xn1, n2 = wait((x, n2))
-    x = over_x(n2)
-    a = from_next(n2)
+    x = x2
     h1, t1, f0, sq1 = wave(
         (1,), (), ((0, True), (0, False)), context, context2, residual, [n1, xn1], [p0, r0], None
     )
@@ -421,7 +422,7 @@
 
     n4x, l4 = wait((a, l4))
     n4xs = other_core(n4x)
-    xl1, n4x, r3p, l4s = wait((x, n4x, r3p, l4s))
+    xl1, n4x = wait((x, n4x))
     xl1s = other_core(xl1)
     l3x, xl1 = wait((b, xl1))
     l3xs = other_core(l3x)

time: 104 us -> 102 us (0.981)
  waiting for transfers between devices: 34.6 us -> 31.9 us
  blocking collectives: 22.6 us -> 23.7 us
    ppermute x5, waiting for transfers between devices: 11 us -> 3.57 us  [from_last(): return lax.ppermute(piece, 'dp', ring(1))]
    ppermute x12, starting transfers between devices: 7.28 us -> 2.78 us  [other_core(): return lax.ppermute(piece, 'dp', [(i, i ^ 1) for i in range(ranks)])]
    ppermute x4, waiting for transfers between devices: 12.5 us -> 15.6 us  [over_x(): return lax.ppermute(piece, 'groups', [(0, 1), (1, 0)])]
    ppermute x4, starting transfers between devices: 4.13 us -> 6.24 us  [over_x(): return lax.ppermute(piece, 'groups', [(0, 1), (1, 0)])]
    ppermute x5, starting transfers between devices: 5.87 us -> 7.88 us  [from_last(): return lax.ppermute(piece, 'dp', ring(1))]
    ppermute x5, waiting for transfers between devices: 11.1 us -> 12.7 us  [from_next(): return lax.ppermute(piece, 'dp', ring(-1))]
    all_to_all x2, blocking collectives: 22.6 us -> 23.7 us  [spread(): lax.all_to_all(blocks, 'dp', 0, 0, axis_index_groups=same_core, tiled=True)]
  transfers between devices with their start and end apart: 26 -> 26, of which waited for: 13 -> 10; matrix products, arithmetic and copies ran while one was open for 0% -> 0% of each run, Pallas kernels for 12% -> 12%
where the time goes in v11:
time: 102 us
  waiting for transfers between devices  31.9 us (31%)
  starting transfers between devices  24 us (24%)
  blocking collectives  23.7 us (23%)
  Pallas kernels  18 us (18%)
  local copies, waits for them, and re-layouts  2.85 us (3%)
  between operations  1.5 us (1%)
    all_to_all x2, blocking collectives, spread(): lax.all_to_all(blocks, 'dp', 0, 0, axis_index_groups=same_core, tiled=True)  23.7 us
    ppermute x4, waiting for transfers between devices, over_x(): return lax.ppermute(piece, 'groups', [(0, 1), (1, 0)])  15.6 us
    ppermute x5, waiting for transfers between devices, from_next(): return lax.ppermute(piece, 'dp', ring(-1))  12.7 us
    pallas_call x5, Pallas kernels, wave(): pl.pallas_call(functools.partial(wave_kernel, full, part, arrived, whole,...  9.98 us
    ppermute x5, starting transfers between devices, from_last(): return lax.ppermute(piece, 'dp', ring(1))  7.88 us
    ppermute x5, starting transfers between devices, from_next(): return lax.ppermute(piece, 'dp', ring(-1))  7.1 us
    ppermute x4, starting transfers between devices, over_x(): return lax.ppermute(piece, 'groups', [(0, 1), (1, 0)])  6.24 us
    pallas_call x1, Pallas kernels, finish(): pl.pallas_call(functools.partial(final_kernel, items, sources, len(pieces...  4.03 us
  transfers between devices with their start and end apart: 26, of which 10 were waited for; matrix products, arithmetic and copies ran while one was open for 0% of the time, Pallas kernels for 12%

profile of v11, /device:TPU:0, one launch (start us, length us, event | category | flops | bytes accessed | tf_op | source)
XLA Modules:
  0.0 102.0 jit_solution(3285453017210036113)
XLA Ops:
  2.4 2.6 %collective-permute-start.2 = (bf16[1024,256]{1,0:T(8,128)(2,1)S(1)}, bf16[1024,256]{1,0:T(8,128)(2,1)S(1)}, u32[]{:S(2)}, u32[]{:S(2)}) collective-permute-start(bf16[1024,256]{1,0:T(8,128)(2,1)S(1)} %shard_map.94), channel_id=1, source_target_pairs={{0,2},{1,5},{4,0},{5,9},{8,4},{9,13},{12,8},{13,15},{14,12},{15,11... | collective-permute-start | bytes 1572872 | tf_op jit(solution)/shard_map/ppermute | solution.py:361
  5.3 1.6 %copy-done.1 = bf16[512,2048]{1,0:T(8,128)(2,1)S(1)} copy-done((bf16[512,2048]{1,0:T(8,128)(2,1)S(1)}, bf16[512,2048]{1,0:T(8,128)(2,1)}, u32[]{:S(2)}) %copy-start.1) | copy-done | bytes 2097176
  7.8 1.6 %collective-permute-start = (bf16[1024,256]{1,0:T(8,128)(2,1)S(1)}, bf16[1024,256]{1,0:T(8,128)(2,1)S(1)}, u32[]{:S(2)}, u32[]{:S(2)}) collective-permute-start(bf16[1024,256]{1,0:T(8,128)(2,1)S(1)} %shard_map.94), channel_id=1, source_target_pairs={{0,4},{1,3},{4,8},{5,1},{8,12},{9,5},{12,14},{13,9},{14,10},{15,13... | collective-permute-start | bytes 1572872 | tf_op jit(solution)/shard_map/ppermute | solution.py:364
  9.4 4.3 %collective-permute-done.2.refs_3_ = bf16[1024,256]{1,0:T(8,128)(2,1)S(1)} collective-permute-done((bf16[1024,256]{1,0:T(8,128)(2,1)S(1)}, bf16[1024,256]{1,0:T(8,128)(2,1)S(1)}, u32[]{:S(2)}, u32[]{:S(2)}) %collective-permute-start.2) | collective-permute-done | bytes 524320 | tf_op jit(solution)/shard_map/ppermute | solution.py:361
  13.7 2.3 %collective-permute-start.6 = (bf16[1024,256]{1,0:T(8,128)(2,1)S(1)}, bf16[1024,256]{1,0:T(8,128)(2,1)S(1)}, u32[]{:S(2)}, u32[]{:S(2)}) collective-permute-start(bf16[1024,256]{1,0:T(8,128)(2,1)S(1)} %collective-permute-done.2.refs_3_), channel_id=1, source_target_pairs={{0,2},{1,5},{4,0},{5,9},{8,4},{9,13},{12,8},{13,15},{14,12},{15,11... | collective-permute-start | bytes 1572872 | tf_op jit(solution)/shard_map/ppermute | solution.py:361
  19.5 2.0 %collective-permute-start.4 = (bf16[1024,256]{1,0:T(8,128)(2,1)S(1)}, bf16[1024,256]{1,0:T(8,128)(2,1)S(1)}, u32[]{:S(2)}, u32[]{:S(2)}) collective-permute-start(bf16[1024,256]{1,0:T(8,128)(2,1)S(1)} %collective-permute-done.refs_5_), channel_id=1, source_target_pairs={{0,4},{1,3},{4,8},{5,1},{8,12},{9,5},{12,14},{13,9},{14,10},{15,13... | collective-permute-start | bytes 1572872 | tf_op jit(solution)/shard_map/ppermute | solution.py:364
  21.5 2.8 %collective-permute-done.6.refs_3_ = bf16[1024,256]{1,0:T(8,128)(2,1)S(1)} collective-permute-done((bf16[1024,256]{1,0:T(8,128)(2,1)S(1)}, bf16[1024,256]{1,0:T(8,128)(2,1)S(1)}, u32[]{:S(2)}, u32[]{:S(2)}) %collective-permute-start.6) | collective-permute-done | bytes 524320 | tf_op jit(solution)/shard_map/ppermute | solution.py:361
  24.2 2.0 %collective-permute-start.10 = (bf16[1024,256]{1,0:T(8,128)(2,1)S(1)}, bf16[1024,256]{1,0:T(8,128)(2,1)S(1)}, u32[]{:S(2)}, u32[]{:S(2)}) collective-permute-start(bf16[1024,256]{1,0:T(8,128)(2,1)S(1)} %collective-permute-done.6.refs_3_), channel_id=1, source_target_pairs={{0,16},{16,0},{1,17},{17,1},{2,18},{18,2},{3,19},{19,3},{4,20},{20... | collective-permute-start | bytes 1572872 | tf_op jit(solution)/shard_map/ppermute | solution.py:367
  26.2 1.7 %collective-permute-start.9 = (bf16[1024,256]{1,0:T(8,128)(2,1)S(1)}, bf16[1024,256]{1,0:T(8,128)(2,1)S(1)}, u32[]{:S(2)}, u32[]{:S(2)}) collective-permute-start(bf16[1024,256]{1,0:T(8,128)(2,1)S(1)} %collective-permute-done.6.refs_3_), channel_id=1, source_target_pairs={{0,2},{1,5},{4,0},{5,9},{8,4},{9,13},{12,8},{13,15},{14,12},{15,11... | collective-permute-start | bytes 1572872 | tf_op jit(solution)/shard_map/ppermute | solution.py:361
  27.9 2.3 %collective-permute-done.5.refs_4_ = bf16[1024,256]{1,0:T(8,128)(2,1)S(1)} collective-permute-done((bf16[1024,256]{1,0:T(8,128)(2,1)S(1)}, bf16[1024,256]{1,0:T(8,128)(2,1)S(1)}, u32[]{:S(2)}, u32[]{:S(2)}) %collective-permute-start.5) | collective-permute-done | bytes 524320 | tf_op jit(solution)/shard_map/ppermute | solution.py:367
  30.3 1.8 %shard_map.97 = (f32[1,512,256]{2,1,0:T(8,128)S(1)}, f32[512,256]{1,0:T(8,128)S(1)}, f32[2,512,256]{2,1,0:T(8,128)S(1)}, f32[512,128]{1,0:T(8,128)S(1)}) custom-call(bf16[512,2048]{1,0:T(8,128)(2,1)S(1)} %copy-done.2, bf16[512,2048]{1,0:T(8,128)(2,1)S(1)} %collective-permute-done.1.refs_0_.refs_1_, bf16[512,4096]{1,0:T(8,128)(2,1)S(1)} %copy-done, ...), custom_call_target="tpu_custom_call" | custom-call | flops 1000 | bytes 1000 | tf_op jit(solution)/shard_map/pallas_call | solution.py:155
  33.2 6.2 %collective-permute-done.10.refs_4_ = bf16[1024,256]{1,0:T(8,128)(2,1)S(1)} collective-permute-done((bf16[1024,256]{1,0:T(8,128)(2,1)S(1)}, bf16[1024,256]{1,0:T(8,128)(2,1)S(1)}, u32[]{:S(2)}, u32[]{:S(2)}) %collective-permute-start.10) | collective-permute-done | bytes 524320 | tf_op jit(solution)/shard_map/ppermute | solution.py:367
  41.3 2.5 %shard_map.98 = (f32[2,512,256]{2,1,0:T(8,128)S(1)}, f32[512,256]{1,0:T(8,128)S(1)}, f32[512,256]{1,0:T(8,128)S(1)}, f32[1,512,256]{2,1,0:T(8,128)S(1)}, f32[512,128]{1,0:T(8,128)S(1)}) custom-call(bf16[512,2048]{1,0:T(8,128)(2,1)S(1)} %copy-done.2, bf16[512,2048]{1,0:T(8,128)(2,1)S(1)} %collective-permute-done.1.refs_0_.refs_1_, ...), custom_call_target="tpu_custom_call" | custom-call | flops 1000 | bytes 1000 | tf_op jit(solution)/shard_map/pallas_call | solution.py:155
  44.0 1.6 %collective-permute-start.12 = (bf16[1024,256]{1,0:T(8,128)(2,1)S(1)}, bf16[1024,256]{1,0:T(8,128)(2,1)S(1)}, u32[]{:S(2)}, u32[]{:S(2)}) collective-permute-start(bf16[1024,256]{1,0:T(8,128)(2,1)S(1)} %collective-permute-done.8.refs_7_), channel_id=1, source_target_pairs={{0,4},{1,3},{4,8},{5,1},{8,12},{9,5},{12,14},{13,9},{14,10},{15,13... | collective-permute-start | bytes 1572872 | tf_op jit(solution)/shard_map/ppermute | solution.py:364
  45.9 4.1 %collective-permute-done.14.refs_6_ = bf16[1024,256]{1,0:T(8,128)(2,1)S(1)} collective-permute-done((bf16[1024,256]{1,0:T(8,128)(2,1)S(1)}, bf16[1024,256]{1,0:T(8,128)(2,1)S(1)}, u32[]{:S(2)}, u32[]{:S(2)}) %collective-permute-start.14) | collective-permute-done | bytes 524320 | tf_op jit(solution)/shard_map/ppermute | solution.py:361
  50.0 3.0 %collective-permute-done.13.refs_4_ = bf16[1024,256]{1,0:T(8,128)(2,1)S(1)} collective-permute-done((bf16[1024,256]{1,0:T(8,128)(2,1)S(1)}, bf16[1024,256]{1,0:T(8,128)(2,1)S(1)}, u32[]{:S(2)}, u32[]{:S(2)}) %collective-permute-start.13) | collective-permute-done | bytes 524320 | tf_op jit(solution)/shard_map/ppermute | solution.py:367
  54.4 3.9 %shard_map.99 = (f32[3,512,256]{2,1,0:T(8,128)S(1)}, f32[2,512,256]{2,1,0:T(8,128)S(1)}, f32[1,512,256]{2,1,0:T(8,128)S(1)}, f32[1,512,256]{2,1,0:T(8,128)S(1)}, f32[512,128]{1,0:T(8,128)S(1)}) custom-call(bf16[512,2048]{1,0:T(8,128)(2,1)S(1)} %copy-done.2, bf16[512,2048]{1,0:T(8,128)(2,1)S(1)} %collective-permute-done.1.refs_0_.refs_1_, ...), custom_call_target="tpu_custom_call" | custom-call | flops 1000 | bytes 1000 | tf_op jit(solution)/shard_map/pallas_call | solution.py:155
  59.8 1.6 %collective-permute-start.17 = (bf16[1024,256]{1,0:T(8,128)(2,1)S(1)}, bf16[1024,256]{1,0:T(8,128)(2,1)S(1)}, u32[]{:S(2)}, u32[]{:S(2)}) collective-permute-start(bf16[1024,256]{1,0:T(8,128)(2,1)S(1)} %collective-permute-done.13.refs_4_), channel_id=1, source_target_pairs={{0,4},{1,3},{4,8},{5,1},{8,12},{9,5},{12,14},{13,9},{14,10},{15,13... | collective-permute-start | bytes 1572872 | tf_op jit(solution)/shard_map/ppermute | solution.py:364
  61.4 4.0 %collective-permute-done.18.refs_0_ = bf16[1024,256]{1,0:T(8,128)(2,1)S(1)} collective-permute-done((bf16[1024,256]{1,0:T(8,128)(2,1)S(1)}, bf16[1024,256]{1,0:T(8,128)(2,1)S(1)}, u32[]{:S(2)}, u32[]{:S(2)}) %collective-permute-start.18) | collective-permute-done | bytes 524320 | tf_op jit(solution)/shard_map/ppermute | solution.py:367
  66.5 2.5 %collective-permute-done.17.refs_1_ = bf16[1024,256]{1,0:T(8,128)(2,1)S(1)} collective-permute-done((bf16[1024,256]{1,0:T(8,128)(2,1)S(1)}, bf16[1024,256]{1,0:T(8,128)(2,1)S(1)}, u32[]{:S(2)}, u32[]{:S(2)}) %collective-permute-start.17) | collective-permute-done | bytes 524320 | tf_op jit(solution)/shard_map/ppermute | solution.py:364
  70.2 2.2 %shard_map.100 = (f32[3,512,256]{2,1,0:T(8,128)S(1)}, f32[512,128]{1,0:T(8,128)S(1)}) custom-call(bf16[512,2048]{1,0:T(8,128)(2,1)S(1)} %copy-done.2, bf16[512,4096]{1,0:T(8,128)(2,1)S(1)} %copy-done, f32[512,128]{1,0:T(8,128)S(1)} %get-tuple-element.105.before, bf16[1024,256]{1,0:T(8,128)(2,1)S(1)} %collective-permute-done.18.refs_0_, ...), custom_call_target="tpu_custom_call" | custom-call | flops 1000 | bytes 1000 | tf_op jit(solution)/shard_map/pallas_call | solution.py:191
  72.4 4.0 %shard_map.101 = (f32[1,4096]{1,0:T(1,128)}, bf16[8,48,128]{2,1,0:T(8,128)(2,1)S(1)}) custom-call(s32[1]{0:T(128)S(6)} %copy.10.length, bf16[512,2048]{1,0:T(8,128)(2,1)S(1)} %copy-done.2, bf16[512,4096]{1,0:T(8,128)(2,1)S(1)} %copy-done, f32[512,128]{1,0:T(8,128)S(1)} %get-tuple-element.117.before, f32[1,4096]{1,0:T(1,128)S(1)} %bitcast.2, ...), custom_call_target="tpu_custom_call" | custom-call | flops 1000 | bytes 1000 | tf_op jit(solution)/shard_map/pallas_call | solution.py:244
  76.5 13.7 %all_to_all.10.got = bf16[8,48,128]{2,1,0:T(8,128)(2,1)S(1)} all-to-all(bf16[8,48,128]{2,1,0:T(8,128)(2,1)S(1)} %get-tuple-element.127), channel_id=1, replica_groups={{0,2,4,6,8,10,12,14},{1,3,5,7,9,11,13,15},{16,18,20,22,24,26,28,30},{17..., dimensions={0} | all-to-all | bytes 196608 | tf_op jit(solution)/shard_map/all_to_all | solution.py:473
  91.2 10.0 %all_to_all.11.got = f32[8,40,128]{2,1,0:T(8,128)S(1)} all-to-all(f32[8,40,128]{2,1,0:T(8,128)S(1)} %shard_map.102), channel_id=1, replica_groups={{0,2,4,6,8,10,12,14},{1,3,5,7,9,11,13,15},{16,18,20,22,24,26,28,30},{17..., dimensions={0} | all-to-all | bytes 327680 | tf_op jit(solution)/shard_map/all_to_all | solution.py:473
  (56 shorter events, 16.0 us)
Async XLA Ops:
  0.6 16.9 %collective-permute-start.1 = (bf16[512,2048]{1,0:T(8,128)(2,1)}, bf16[512,2048]{1,0:T(8,128)(2,1)S(1)}, u32[]{:S(2)}, u32[]{:S(2)}) collective-permute-start(bf16[512,2048]{1,0:T(8,128)(2,1)} %context.3), channel_id=1, source_target_pairs={{0,1},{1,0},{2,3},{3,2},{4,5},{5,4},{6,7},{7,6},{8,9},{9,8},{10,11... | collective-permute-start | bytes 6291464 | tf_op jit(solution)/shard_map/ppermute | solution.py:370
  2.4 11.3 %collective-permute-start.2 = (bf16[1024,256]{1,0:T(8,128)(2,1)S(1)}, bf16[1024,256]{1,0:T(8,128)(2,1)S(1)}, u32[]{:S(2)}, u32[]{:S(2)}) collective-permute-start(bf16[1024,256]{1,0:T(8,128)(2,1)S(1)} %shard_map.94), channel_id=1, source_target_pairs={{0,2},{1,5},{4,0},{5,9},{8,4},{9,13},{12,8},{13,15},{14,12},{15,11... | collective-permute-start | bytes 1572872 | tf_op jit(solution)/shard_map/ppermute | solution.py:361
  5.0 14.5 %collective-permute-start.3 = (bf16[112,4096]{1,0:T(8,128)(2,1)}, bf16[112,4096]{1,0:T(8,128)(2,1)S(1)}, u32[]{:S(2)}, u32[]{:S(2)}) collective-permute-start(bf16[112,4096]{1,0:T(8,128)(2,1)} %queries.1), channel_id=1, source_target_pairs={{0,1},{1,0},{2,3},{3,2},{4,5},{5,4},{6,7},{7,6},{8,9},{9,8},{10,11... | collective-permute-start | bytes 2752520 | tf_op jit(solution)/shard_map/ppermute | solution.py:370
  7.8 11.7 %collective-permute-start = (bf16[1024,256]{1,0:T(8,128)(2,1)S(1)}, bf16[1024,256]{1,0:T(8,128)(2,1)S(1)}, u32[]{:S(2)}, u32[]{:S(2)}) collective-permute-start(bf16[1024,256]{1,0:T(8,128)(2,1)S(1)} %shard_map.94), channel_id=1, source_target_pairs={{0,4},{1,3},{4,8},{5,1},{8,12},{9,5},{12,14},{13,9},{14,10},{15,13... | collective-permute-start | bytes 1572872 | tf_op jit(solution)/shard_map/ppermute | solution.py:364
  13.7 10.5 %collective-permute-start.6 = (bf16[1024,256]{1,0:T(8,128)(2,1)S(1)}, bf16[1024,256]{1,0:T(8,128)(2,1)S(1)}, u32[]{:S(2)}, u32[]{:S(2)}) collective-permute-start(bf16[1024,256]{1,0:T(8,128)(2,1)S(1)} %collective-permute-done.2.refs_3_), channel_id=1, source_target_pairs={{0,2},{1,5},{4,0},{5,9},{8,4},{9,13},{12,8},{13,15},{14,12},{15,11... | collective-permute-start | bytes 1572872 | tf_op jit(solution)/shard_map/ppermute | solution.py:361
  16.1 14.2 %collective-permute-start.5 = (bf16[1024,256]{1,0:T(8,128)(2,1)S(1)}, bf16[1024,256]{1,0:T(8,128)(2,1)S(1)}, u32[]{:S(2)}, u32[]{:S(2)}) collective-permute-start(bf16[1024,256]{1,0:T(8,128)(2,1)S(1)} %collective-permute-done.2.refs_3_), channel_id=1, source_target_pairs={{0,16},{16,0},{1,17},{17,1},{2,18},{18,2},{3,19},{19,3},{4,20},{20... | collective-permute-start | bytes 1572872 | tf_op jit(solution)/shard_map/ppermute | solution.py:367
  19.5 10.8 %collective-permute-start.7 = (f32[512,256]{1,0:T(8,128)S(1)}, f32[512,256]{1,0:T(8,128)S(1)}, u32[]{:S(2)}, u32[]{:S(2)}) collective-permute-start(f32[512,256]{1,0:T(8,128)S(1)} %shard_map.96), channel_id=1, source_target_pairs={{0,1},{1,0},{2,3},{3,2},{4,5},{5,4},{6,7},{7,6},{8,9},{9,8},{10,11... | collective-permute-start | bytes 1572872 | tf_op jit(solution)/shard_map/ppermute | solution.py:370
  19.5 12.6 %collective-permute-start.4 = (bf16[1024,256]{1,0:T(8,128)(2,1)S(1)}, bf16[1024,256]{1,0:T(8,128)(2,1)S(1)}, u32[]{:S(2)}, u32[]{:S(2)}) collective-permute-start(bf16[1024,256]{1,0:T(8,128)(2,1)S(1)} %collective-permute-done.refs_5_), channel_id=1, source_target_pairs={{0,4},{1,3},{4,8},{5,1},{8,12},{9,5},{12,14},{13,9},{14,10},{15,13... | collective-permute-start | bytes 1572872 | tf_op jit(solution)/shard_map/ppermute | solution.py:364
  24.2 15.2 %collective-permute-start.10 = (bf16[1024,256]{1,0:T(8,128)(2,1)S(1)}, bf16[1024,256]{1,0:T(8,128)(2,1)S(1)}, u32[]{:S(2)}, u32[]{:S(2)}) collective-permute-start(bf16[1024,256]{1,0:T(8,128)(2,1)S(1)} %collective-permute-done.6.refs_3_), channel_id=1, source_target_pairs={{0,16},{16,0},{1,17},{17,1},{2,18},{18,2},{3,19},{19,3},{4,20},{20... | collective-permute-start | bytes 1572872 | tf_op jit(solution)/shard_map/ppermute | solution.py:367
  26.2 15.1 %collective-permute-start.9 = (bf16[1024,256]{1,0:T(8,128)(2,1)S(1)}, bf16[1024,256]{1,0:T(8,128)(2,1)S(1)}, u32[]{:S(2)}, u32[]{:S(2)}) collective-permute-start(bf16[1024,256]{1,0:T(8,128)(2,1)S(1)} %collective-permute-done.6.refs_3_), channel_id=1, source_target_pairs={{0,2},{1,5},{4,0},{5,9},{8,4},{9,13},{12,8},{13,15},{14,12},{15,11... | collective-permute-start | bytes 1572872 | tf_op jit(solution)/shard_map/ppermute | solution.py:361
  32.1 9.3 %collective-permute-start.11 = (f32[512,256]{1,0:T(8,128)S(1)}, f32[512,256]{1,0:T(8,128)S(1)}, u32[]{:S(2)}, u32[]{:S(2)}) collective-permute-start(f32[512,256]{1,0:T(8,128)S(1)} %get-tuple-element.87), channel_id=1, source_target_pairs={{0,1},{1,0},{2,3},{3,2},{4,5},{5,4},{6,7},{7,6},{8,9},{9,8},{10,11... | collective-permute-start | bytes 1572872 | tf_op jit(solution)/shard_map/ppermute | solution.py:370
  32.2 11.7 %collective-permute-start.8 = (bf16[1024,256]{1,0:T(8,128)(2,1)S(1)}, bf16[1024,256]{1,0:T(8,128)(2,1)S(1)}, u32[]{:S(2)}, u32[]{:S(2)}) collective-permute-start(bf16[1024,256]{1,0:T(8,128)(2,1)S(1)} %collective-permute-done.4.refs_3_), channel_id=1, source_target_pairs={{0,4},{1,3},{4,8},{5,1},{8,12},{9,5},{12,14},{13,9},{14,10},{15,13... | collective-permute-start | bytes 1572872 | tf_op jit(solution)/shard_map/ppermute | solution.py:364
  39.4 10.6 %collective-permute-start.14 = (bf16[1024,256]{1,0:T(8,128)(2,1)S(1)}, bf16[1024,256]{1,0:T(8,128)(2,1)S(1)}, u32[]{:S(2)}, u32[]{:S(2)}) collective-permute-start(bf16[1024,256]{1,0:T(8,128)(2,1)S(1)} %collective-permute-done.10.refs_4_), channel_id=1, source_target_pairs={{0,2},{1,5},{4,0},{5,9},{8,4},{9,13},{12,8},{13,15},{14,12},{15,11... | collective-permute-start | bytes 1572872 | tf_op jit(solution)/shard_map/ppermute | solution.py:361
  39.8 13.3 %collective-permute-start.13 = (bf16[1024,256]{1,0:T(8,128)(2,1)S(1)}, bf16[1024,256]{1,0:T(8,128)(2,1)S(1)}, u32[]{:S(2)}, u32[]{:S(2)}) collective-permute-start(bf16[1024,256]{1,0:T(8,128)(2,1)S(1)} %collective-permute-done.4.refs_3_), channel_id=1, source_target_pairs={{0,16},{16,0},{1,17},{17,1},{2,18},{18,2},{3,19},{19,3},{4,20},{20... | collective-permute-start | bytes 1572872 | tf_op jit(solution)/shard_map/ppermute | solution.py:367
  43.9 10.5 %collective-permute-start.15 = (f32[512,256]{1,0:T(8,128)S(1)}, f32[512,256]{1,0:T(8,128)S(1)}, u32[]{:S(2)}, u32[]{:S(2)}) collective-permute-start(f32[512,256]{1,0:T(8,128)S(1)} %get-tuple-element.99), channel_id=1, source_target_pairs={{0,1},{1,0},{2,3},{3,2},{4,5},{5,4},{6,7},{7,6},{8,9},{9,8},{10,11... | collective-permute-start | bytes 1572872 | tf_op jit(solution)/shard_map/ppermute | solution.py:370
  44.0 14.4 %collective-permute-start.12 = (bf16[1024,256]{1,0:T(8,128)(2,1)S(1)}, bf16[1024,256]{1,0:T(8,128)(2,1)S(1)}, u32[]{:S(2)}, u32[]{:S(2)}) collective-permute-start(bf16[1024,256]{1,0:T(8,128)(2,1)S(1)} %collective-permute-done.8.refs_7_), channel_id=1, source_target_pairs={{0,4},{1,3},{4,8},{5,1},{8,12},{9,5},{12,14},{13,9},{14,10},{15,13... | collective-permute-start | bytes 1572872 | tf_op jit(solution)/shard_map/ppermute | solution.py:364
  45.6 12.7 %collective-permute-start.16 = (f32[512,256]{1,0:T(8,128)S(1)}, f32[512,256]{1,0:T(8,128)S(1)}, u32[]{:S(2)}, u32[]{:S(2)}) collective-permute-start(f32[512,256]{1,0:T(8,128)S(1)} %get-tuple-element.104), channel_id=1, source_target_pairs={{0,1},{1,0},{2,3},{3,2},{4,5},{5,4},{6,7},{7,6},{8,9},{9,8},{10,11... | collective-permute-start | bytes 1572872 | tf_op jit(solution)/shard_map/ppermute | solution.py:370
  50.0 9.8 %collective-permute-start.19 = (bf16[1024,256]{1,0:T(8,128)(2,1)S(1)}, bf16[1024,256]{1,0:T(8,128)(2,1)S(1)}, u32[]{:S(2)}, u32[]{:S(2)}) collective-permute-start(bf16[1024,256]{1,0:T(8,128)(2,1)S(1)} %collective-permute-done.14.refs_6_), channel_id=1, source_target_pairs={{0,2},{1,5},{4,0},{5,9},{8,4},{9,13},{12,8},{13,15},{14,12},{15,11... | collective-permute-start | bytes 1572872 | tf_op jit(solution)/shard_map/ppermute | solution.py:361
  53.1 12.3 %collective-permute-start.18 = (bf16[1024,256]{1,0:T(8,128)(2,1)S(1)}, bf16[1024,256]{1,0:T(8,128)(2,1)S(1)}, u32[]{:S(2)}, u32[]{:S(2)}) collective-permute-start(bf16[1024,256]{1,0:T(8,128)(2,1)S(1)} %collective-permute-done.refs_5_), channel_id=1, source_target_pairs={{0,16},{16,0},{1,17},{17,1},{2,18},{18,2},{3,19},{19,3},{4,20},{20... | collective-permute-start | bytes 1572872 | tf_op jit(solution)/shard_map/ppermute | solution.py:367
  59.8 9.2 %collective-permute-start.17 = (bf16[1024,256]{1,0:T(8,128)(2,1)S(1)}, bf16[1024,256]{1,0:T(8,128)(2,1)S(1)}, u32[]{:S(2)}, u32[]{:S(2)}) collective-permute-start(bf16[1024,256]{1,0:T(8,128)(2,1)S(1)} %collective-permute-done.13.refs_4_), channel_id=1, source_target_pairs={{0,4},{1,3},{4,8},{5,1},{8,12},{9,5},{12,14},{13,9},{14,10},{15,13... | collective-permute-start | bytes 1572872 | tf_op jit(solution)/shard_map/ppermute | solution.py:364
  65.4 3.6 %collective-permute-start.20 = (bf16[1024,256]{1,0:T(8,128)(2,1)S(1)}, bf16[1024,256]{1,0:T(8,128)(2,1)S(1)}, u32[]{:S(2)}, u32[]{:S(2)}) collective-permute-start(bf16[1024,256]{1,0:T(8,128)(2,1)S(1)} %collective-permute-done.18.refs_0_), channel_id=1, source_target_pairs={{0,1},{1,0},{2,3},{3,2},{4,5},{5,4},{6,7},{7,6},{8,9},{9,8},{10,11... | collective-permute-start | bytes 1572872 | tf_op jit(solution)/shard_map/ppermute | solution.py:370
  65.4 7.0 %collective-permute-start.25 = (f32[2,512,256]{2,1,0:T(8,128)S(1)}, f32[2,512,256]{2,1,0:T(8,128)S(1)}, u32[]{:S(2)}, u32[]{:S(2)}) collective-permute-start(f32[2,512,256]{2,1,0:T(8,128)S(1)} %get-tuple-element.125), channel_id=1, source_target_pairs={{0,1},{1,0},{2,3},{3,2},{4,5},{5,4},{6,7},{7,6},{8,9},{9,8},{10,11... | collective-permute-start | bytes 3145736 | tf_op jit(solution)/shard_map/ppermute | solution.py:370
  65.9 6.4 %collective-permute-start.23 = (bf16[1024,256]{1,0:T(8,128)(2,1)S(1)}, bf16[1024,256]{1,0:T(8,128)(2,1)S(1)}, u32[]{:S(2)}, u32[]{:S(2)}) collective-permute-start(bf16[1024,256]{1,0:T(8,128)(2,1)S(1)} %collective-permute-done.19.refs_3_), channel_id=1, source_target_pairs={{0,1},{1,0},{2,3},{3,2},{4,5},{5,4},{6,7},{7,6},{8,9},{9,8},{10,11... | collective-permute-start | bytes 1572872 | tf_op jit(solution)/shard_map/ppermute | solution.py:370
  65.9 6.4 %collective-permute-start.22 = (bf16[1024,256]{1,0:T(8,128)(2,1)S(1)}, bf16[1024,256]{1,0:T(8,128)(2,1)S(1)}, u32[]{:S(2)}, u32[]{:S(2)}) collective-permute-start(bf16[1024,256]{1,0:T(8,128)(2,1)S(1)} %collective-permute-done.12.refs_2_), channel_id=1, source_target_pairs={{0,1},{1,0},{2,3},{3,2},{4,5},{5,4},{6,7},{7,6},{8,9},{9,8},{10,11... | collective-permute-start | bytes 1572872 | tf_op jit(solution)/shard_map/ppermute | solution.py:370
  (9 other events, 101.2 us)

commit v12 on v11

--- a/solution.py
+++ b/solution.py
@@ -201,7 +201,7 @@
     )(*operands)
 
 
-def final_kernel(items, sources, n_pieces, length, context, residual, before, gain, flags, *refs):
+def final_kernel(items, sources, n_pieces, context, residual, before, gain, flags, *refs):
     pieces, hidden = refs[:n_pieces], refs[n_pieces:-6]
     embedded, payload, blocks, squares, scale_rows, sheet = refs[-6:]
     width = blocks.shape[2]
@@ -209,10 +209,11 @@
     squares[...] = before[...]
     late_blocks(items, context, residual, pieces, hidden, squares, blocks)
     mean = jnp.sum(squares[...], axis=1, keepdims=True) * (1.0 / features)
-    row = lax.broadcasted_iota(jnp.int32, mean.shape, 0)
-    scale = jnp.where(row < length[0], lax.rsqrt(mean + 1e-05), 0.0)
+    length = flags[:, LANES - 1 : LANES]
+    row = lax.broadcasted_iota(jnp.int32, mean.shape, 0).astype(jnp.float32)
+    scale = jnp.where(row < length, lax.rsqrt(mean + 1e-05), 0.0)
     scale_rows[...] = jnp.broadcast_to(scale, scale_rows.shape)
-    inverse = 1.0 / jnp.full((1, width), length[0], jnp.int32).astype(jnp.float32)
+    inverse = 1.0 / length
     done = [(blocks.at[i], distance, same) for i, (_, _, _, distance, same) in enumerate(items)]
     done += [(hidden[array].at[entry], distance, same) for array, entry, distance, same in sources]
     for block, distance, same in done:
@@ -230,12 +231,10 @@
     for line in range(lines):
         sheet[line : line + 1, :] = embedded[:, line * LANES : (line + 1) * LANES]
     sheet[lines : lines + 1, :] = flags[...]
-    rounded = sheet[...].astype(jnp.bfloat16)
-    for rank in range(payload.shape[0]):
-        payload[rank] = rounded
-
-
-def finish(items, sources, lengths, context, residual, squares, gain, flags, pieces, hidden, ranks):
+    payload[...] = sheet[...].astype(jnp.bfloat16)
+
+
+def finish(items, sources, context, residual, squares, gain, flags, pieces, hidden):
     rows = context.shape[0]
     width = pieces[0].shape[1]
     features = (len(items) + len(sources)) * width
@@ -245,9 +244,9 @@
         functools.partial(final_kernel, items, sources, len(pieces)),
         out_shape=(
             jax.ShapeDtypeStruct((1, features), jnp.float32),
-            jax.ShapeDtypeStruct((ranks, lines, LANES), jnp.bfloat16),
+            jax.ShapeDtypeStruct((lines, LANES), jnp.bfloat16),
         ),
-        in_specs=[pl.BlockSpec(memory_space=pltpu.SMEM)] + [VMEM_SPEC] * len(operands),
+        in_specs=[VMEM_SPEC] * len(operands),
         out_specs=(VMEM_SPEC, VMEM_SPEC),
         scratch_shapes=[
             pltpu.VMEM((len(items), rows, width), jnp.float32),
@@ -257,14 +256,17 @@
         ],
         compiler_params=pltpu.CompilerParams(vmem_limit_bytes=VMEM_BYTES),
         cost_estimate=SMALL,
-    )(lengths, *operands)
-
-
-def score_kernel(lines, blocks, got, queries, other_queries, out, wide, emb, mix):
+    )(*operands)
+
+
+def score_kernel(lines, blocks, lists, *refs):
+    got, (queries, other_queries), outs = refs[:lists], refs[lists : lists + 2], refs[lists + 2 : 2 * lists + 2]
+    wide, emb, mix = refs[2 * lists + 2 :]
     me = lax.axis_index("dp")
-    ranks = got.shape[0]
+    each = got[0].shape[0]
     count = queries.shape[0]
-    wide[...] = got[...].astype(jnp.float32)
+    for i in range(lists):
+        wide[i * each : (i + 1) * each] = got[i][...].astype(jnp.float32)
     for line in range(lines):
         emb[:, line * LANES : (line + 1) * LANES] = wide[:, line, :]
     half = emb[...].astype(jnp.bfloat16)
@@ -290,58 +292,83 @@
     mix[...] = jnp.dot(
         weights[0].astype(jnp.bfloat16), queries[...], preferred_element_type=jnp.float32
     ) + jnp.dot(weights[1].astype(jnp.bfloat16), other_queries[...], preferred_element_type=jnp.float32)
-    for line in range(lines):
-        out[:, line, :] = mix[:, line * LANES : (line + 1) * LANES]
-    lane = lax.broadcasted_iota(jnp.int32, (ranks, LANES), 1)
-    out[:, lines, :] = jnp.where(lane == 0, peak, jnp.where(lane == 1, total, 0.0))
-    for line in range(lines + 1, out.shape[1]):
-        out[:, line, :] = jnp.zeros((ranks, LANES), jnp.float32)
+    lane = lax.broadcasted_iota(jnp.int32, (lists * each, LANES), 1)
+    stats = jnp.where(lane == 0, peak, jnp.where(lane == 1, total, 0.0))
+    for i in range(lists):
+        here = slice(i * each, (i + 1) * each)
+        for line in range(lines):
+            outs[i][:, line, :] = mix[here, line * LANES : (line + 1) * LANES]
+        outs[i][:, lines, :] = stats[here, :]
+        for line in range(lines + 1, outs[i].shape[1]):
+            outs[i][:, line, :] = jnp.zeros((each, LANES), jnp.float32)
 
 
 def score(got, queries, other_queries, blocks):
-    ranks = got.shape[0]
+    lists, each = len(got), got[0].shape[0]
     features = queries.shape[1]
     lines = features // LANES
+    out = jax.ShapeDtypeStruct((each, -(-(lines + 1) // 8) * 8, LANES), jnp.float32)
     return pl.pallas_call(
-        functools.partial(score_kernel, lines, blocks),
-        out_shape=jax.ShapeDtypeStruct((ranks, -(-(lines + 1) // 8) * 8, LANES), jnp.float32),
-        in_specs=[pl.BlockSpec(memory_space=pltpu.VMEM)] * 3,
-        out_specs=pl.BlockSpec(memory_space=pltpu.VMEM),
+        functools.partial(score_kernel, lines, blocks, lists),
+        out_shape=[out] * lists,
+        in_specs=[VMEM_SPEC] * (lists + 2),
+        out_specs=[VMEM_SPEC] * lists,
         scratch_shapes=[
-            pltpu.VMEM(got.shape, jnp.float32),
-            pltpu.VMEM((ranks, features), jnp.float32),
-            pltpu.VMEM((ranks, features), jnp.float32),
+            pltpu.VMEM((lists * each,) + got[0].shape[1:], jnp.float32),
+            pltpu.VMEM((lists * each, features), jnp.float32),
+            pltpu.VMEM((lists * each, features), jnp.float32),
         ],
         compiler_params=pltpu.CompilerParams(vmem_limit_bytes=VMEM_BYTES),
-    )(got, queries, other_queries)
-
-
-def combine_kernel(lines, got, recalled, log_total):
-    stats = got[:, lines, :]
-    peaks, sums = stats[:, 0:1], stats[:, 1:2]
-    peak = jnp.max(peaks, axis=0, keepdims=True)
-    factor = jnp.exp(peaks - peak)
-    total = jnp.sum(sums * factor, axis=0, keepdims=True)
-    mix = got[0, :lines, :] * factor[0:1, :]
-    for rank in range(1, got.shape[0]):
-        mix += got[rank, :lines, :] * factor[rank : rank + 1, :]
+    )(*got, queries, other_queries)
+
+
+def joined(parts, lines):
+    peaks = [part[lines : lines + 1, 0:1] for part in parts]
+    peak = functools.reduce(jnp.maximum, peaks)
+    factors = [jnp.exp(own - peak) for own in peaks]
+    mix = sum(part[:lines, :] * factor for part, factor in zip(parts, factors))
+    total = sum(part[lines : lines + 1, 1:2] * factor for part, factor in zip(parts, factors))
+    return mix, peak, total
+
+
+def join_kernel(lines, lists, *refs):
+    for j, out in enumerate(refs[lists:]):
+        mix, peak, total = joined([ref[j] for ref in refs[:lists]], lines)
+        out[:lines, :] = mix
+        lane = lax.broadcasted_iota(jnp.int32, (out.shape[0] - lines, LANES), 1)
+        out[lines:, :] = jnp.where(lane == 0, peak, jnp.where(lane == 1, total, 0.0))
+
+
+def join(parts, features):
+    out = jax.ShapeDtypeStruct(parts[0].shape[1:], jnp.float32)
+    return pl.pallas_call(
+        functools.partial(join_kernel, features // LANES, len(parts)),
+        out_shape=[out] * parts[0].shape[0],
+        in_specs=[VMEM_SPEC] * len(parts),
+        out_specs=[VMEM_SPEC] * parts[0].shape[0],
+        compiler_params=pltpu.CompilerParams(vmem_limit_bytes=VMEM_BYTES),
+    )(*parts)
+
+
+def combine_kernel(lines, first, second, recalled, log_total):
+    mix, peak, total = joined([first[...], second[...]], lines)
     mix = mix / total
     for line in range(lines):
         recalled[:, line * LANES : (line + 1) * LANES] = mix[line : line + 1, :]
     log_total[...] = peak + jnp.log(total)
 
 
-def combine(got, features):
+def combine(first, second, features):
     recalled, log_total = pl.pallas_call(
         functools.partial(combine_kernel, features // LANES),
         out_shape=(
             jax.ShapeDtypeStruct((1, features), jnp.float32),
             jax.ShapeDtypeStruct((1, 1), jnp.float32),
         ),
-        in_specs=[pl.BlockSpec(memory_space=pltpu.VMEM)],
-        out_specs=(pl.BlockSpec(memory_space=pltpu.VMEM), pl.BlockSpec(memory_space=pltpu.VMEM)),
-        compiler_params=pltpu.CompilerParams(vmem_limit_bytes=VMEM_BYTES),
-    )(got)
+        in_specs=[VMEM_SPEC] * 2,
+        out_specs=(VMEM_SPEC, VMEM_SPEC),
+        compiler_params=pltpu.CompilerParams(vmem_limit_bytes=VMEM_BYTES),
+    )(first, second)
     return recalled, log_total.reshape(1)
 
 
@@ -422,58 +449,59 @@
 
     n4x, l4 = wait((a, l4))
     n4xs = other_core(n4x)
-    xl1, n4x = wait((x, n4x))
+    items = ((None, ((0, False), (1, True)), True, 4, True),)
+    h4, sq4 = late(items, context, residual, sq3, [l4, n4x], [])
+    xl1, n4x, sq4 = wait((x, n4x, sq4))
     xl1s = other_core(xl1)
-    l3x, xl1 = wait((b, xl1))
+    items = (((0, 1), ((0, True),), False, -1, True),)
+    h5, sq5 = late(items, context, residual, sq4, [xl1], [h2])
+    l3x, xl1, sq5 = wait((b, xl1, sq5))
     l3xs = other_core(l3x)
-
-    missing = (((0, True),), ((1, True),), ((2, False), (3, True)))
-    own_items = tuple(
-        (base, parts, base is None, distance, True)
-        for base, parts, distance in zip(((0, 1), (1, 2), None), missing, (-1, -3, 4))
-    )
-    h4, sq4 = late(own_items, context, residual, sq3, [xl1, l3x, l4, n4x], [h2, h3])
-    items = tuple(
-        (base, parts, True, distance, False)
-        for base, parts, distance in zip(
-            ((8, None), (9, 0), None, (10, 0), (10, 1)), missing + ((), ()), (-1, -3, 4, -2, 3)
-        )
-    )
-    hidden = [f0, h1, h2, h3, h4, f0, f1, f2, r2p, r3p, r3a]
+    items = (
+        ((0, 2), ((0, True),), False, -3, True),
+        ((1, 0), (), True, -2, False),
+        ((1, 1), (), True, 3, False),
+        (None, ((1, False), (2, True)), True, 4, False),
+    )
+    h6, sq6 = late(items, context, residual, sq5, [l3x, l4s, n4xs], [h3, r3a])
+    items = (((0, None), ((0, True),), True, -1, False), ((1, 0), ((1, True),), True, -3, False))
+    hidden = [r2p, r3p, h1, h2, h3, h4, h5, h6, f0, f1, f2]
     sources = (
-        (0, 0, 0, True),
-        (1, 0, 1, True),
-        (2, 0, 2, True),
-        (3, 0, -2, True),
-        (3, 1, 3, True),
-        (4, 0, -1, True),
-        (4, 1, -3, True),
-        (4, 2, 4, True),
-        (0, 1, 0, False),
-        (6, 0, 1, False),
-        (7, 0, 2, False),
-    )
-    flags = jnp.pad(pattern.astype(jnp.float32), ((0, 0), (0, LANES - pattern.shape[1])))
+        (2, 0, 1, True),
+        (3, 0, 2, True),
+        (4, 0, -2, True),
+        (4, 1, 3, True),
+        (5, 0, 4, True),
+        (6, 0, -1, True),
+        (8, 0, 0, True),
+        (8, 1, 0, False),
+        (9, 0, 1, False),
+        (10, 0, 2, False),
+        (7, 0, -3, True),
+        (7, 1, -2, False),
+        (7, 2, 3, False),
+        (7, 3, 4, False),
+    )
+    flags = jnp.pad(pattern.astype(jnp.float32), ((0, 0), (0, LANES - 1 - pattern.shape[1])))
+    flags = jnp.concatenate([flags, lengths.astype(jnp.float32)[:, None]], axis=1)
     embedded, payload = finish(
-        items,
-        sources,
-        lengths,
-        context,
-        residual,
-        sq4,
-        norm_gain.reshape(1, -1),
-        flags,
-        [xl1s, l3xs, l4s, n4xs],
-        hidden,
-        size,
-    )
-    same_core = [list(range(c, ranks, CORES)) for c in range(CORES)]
-
-    def spread(blocks):
-        return lax.all_to_all(blocks, "dp", 0, 0, axis_index_groups=same_core, tiled=True)
-
-    parts = score(spread(payload), queries, queries2, pattern.shape[1])
-    recalled, log_total = combine(spread(parts), features)
+        items, sources, context, residual, sq6, norm_gain.reshape(1, -1), flags, [xl1s, l3xs], hidden
+    )
+
+    line_z = size // 2
+
+    def along_z(block, k):
+        return lax.ppermute(block, "dp", [(i, (i + k * 2 * CORES) % ranks) for i in range(ranks)])
+
+    def over_y(block):
+        return lax.ppermute(block, "dp", [(i, i ^ CORES) for i in range(ranks)])
+
+    both = jnp.stack([payload, over_y(payload)])
+    got = [both] + [along_z(both, k) for k in range(1, line_z)]
+    parts = score(got, queries, queries2, pattern.shape[1])
+    parts = [parts[0]] + [along_z(parts[k], -k) for k in range(1, line_z)]
+    mine, theirs = join(parts, features)
+    recalled, log_total = combine(mine, over_y(theirs), features)
     return embedded, recalled, log_total
 
 
@@ -540,7 +568,7 @@
         and out_proj.shape[1] % LANES == 0
         and out_proj.shape[0] % (2 * LANES) == 0
         and context.shape[0] % STEP == 0
-        and pattern.shape[1] <= LANES
+        and pattern.shape[1] < LANES
     )
     form = on_cycle if fits else gathered
     return form(context, residual, out_proj, norm_gain, lengths, queries, pattern)

time: 102 us -> 102 us (level)
  blocking collectives: 23.7 us -> 0 us
  starting transfers between devices: 24 us -> 37.2 us
  waiting for transfers between devices: 31.9 us -> 42.2 us
    all_to_all x2 -> x0, blocking collectives: 23.7 us -> none  [spread(): lax.all_to_all(blocks, 'dp', 0, 0, axis_index_groups=same_core, tiled=True)]
    ppermute x0 -> x8, starting transfers between devices: none -> 13.5 us  [the longest x6 12.2 us: along_z(): lax.ppermute(block, 'dp', [(i, (i + k * 2 * CORES) % ranks) for i in rang...]
    ppermute x0 -> x8, waiting for transfers between devices: none -> 12.8 us  [the longest x6 6.68 us: along_z(): lax.ppermute(block, 'dp', [(i, (i + k * 2 * CORES) % ranks) for i in rang...]
    pallas_call x1 -> x3, Pallas kernels: 2.15 us -> 3.35 us  [late(): pl.pallas_call(functools.partial(late_kernel, items, len(pieces)), out_sh...]
    pallas_call x1, Pallas kernels: 4.03 us -> 2.9 us  [finish(): pl.pallas_call(functools.partial(final_kernel, items, sources, len(pieces...]
    ppermute x5, waiting for transfers between devices: 3.57 us -> 2.49 us  [from_last(): return lax.ppermute(piece, 'dp', ring(1))]
  transfers between devices with their start and end apart: 26 -> 34, of which waited for: 10 -> 16; matrix products, arithmetic and copies ran while one was open for 0% -> 0% of each run, Pallas kernels for 12% -> 13%
where the time goes in v12:
time: 102 us
  waiting for transfers between devices  42.2 us (41%)
  starting transfers between devices  37.2 us (36%)
  Pallas kernels  18.2 us (18%)
  local copies, waits for them, and re-layouts  2.84 us (3%)
  between operations  1.51 us (1%)
    ppermute x4, waiting for transfers between devices, over_x(): return lax.ppermute(piece, 'groups', [(0, 1), (1, 0)])  15 us
    ppermute x6, starting transfers between devices, along_z(): lax.ppermute(block, 'dp', [(i, (i + k * 2 * CORES) % ranks) for i in rang...  12.2 us
    ppermute x5, waiting for transfers between devices, from_next(): return lax.ppermute(piece, 'dp', ring(-1))  11.9 us
    pallas_call x5, Pallas kernels, wave(): pl.pallas_call(functools.partial(wave_kernel, full, part, arrived, whole,...  9.86 us
    ppermute x5, starting transfers between devices, from_last(): return lax.ppermute(piece, 'dp', ring(1))  8.05 us
    ppermute x5, starting transfers between devices, from_next(): return lax.ppermute(piece, 'dp', ring(-1))  7.1 us
    ppermute x6, waiting for transfers between devices, along_z(): lax.ppermute(block, 'dp', [(i, (i + k * 2 * CORES) % ranks) for i in rang...  6.68 us
    ppermute x4, starting transfers between devices, over_x(): return lax.ppermute(piece, 'groups', [(0, 1), (1, 0)])  6.24 us
  transfers between devices with their start and end apart: 34, of which 16 were waited for; matrix products, arithmetic and copies ran while one was open for 0% of the time, Pallas kernels for 13%

profile of v12, /device:TPU:0, one launch (start us, length us, event | category | flops | bytes accessed | tf_op | source)
XLA Modules:
  0.0 102.1 jit_solution(7838651336807835917)
XLA Ops:
  2.4 2.6 %collective-permute-start.2 = (bf16[1024,256]{1,0:T(8,128)(2,1)S(1)}, bf16[1024,256]{1,0:T(8,128)(2,1)S(1)}, u32[]{:S(2)}, u32[]{:S(2)}) collective-permute-start(bf16[1024,256]{1,0:T(8,128)(2,1)S(1)} %shard_map.94), channel_id=1, source_target_pairs={{0,2},{1,5},{4,0},{5,9},{8,4},{9,13},{12,8},{13,15},{14,12},{15,11... | collective-permute-start | bytes 1572872 | tf_op jit(solution)/shard_map/ppermute | solution.py:388
  9.4 4.3 %collective-permute-done.2.refs_3_ = bf16[1024,256]{1,0:T(8,128)(2,1)S(1)} collective-permute-done((bf16[1024,256]{1,0:T(8,128)(2,1)S(1)}, bf16[1024,256]{1,0:T(8,128)(2,1)S(1)}, u32[]{:S(2)}, u32[]{:S(2)}) %collective-permute-start.2) | collective-permute-done | bytes 524320 | tf_op jit(solution)/shard_map/ppermute | solution.py:388
  13.7 2.3 %collective-permute-start.6 = (bf16[1024,256]{1,0:T(8,128)(2,1)S(1)}, bf16[1024,256]{1,0:T(8,128)(2,1)S(1)}, u32[]{:S(2)}, u32[]{:S(2)}) collective-permute-start(bf16[1024,256]{1,0:T(8,128)(2,1)S(1)} %collective-permute-done.2.refs_3_), channel_id=1, source_target_pairs={{0,2},{1,5},{4,0},{5,9},{8,4},{9,13},{12,8},{13,15},{14,12},{15,11... | collective-permute-start | bytes 1572872 | tf_op jit(solution)/shard_map/ppermute | solution.py:388
  19.5 2.0 %collective-permute-start.4 = (bf16[1024,256]{1,0:T(8,128)(2,1)S(1)}, bf16[1024,256]{1,0:T(8,128)(2,1)S(1)}, u32[]{:S(2)}, u32[]{:S(2)}) collective-permute-start(bf16[1024,256]{1,0:T(8,128)(2,1)S(1)} %collective-permute-done.refs_5_), channel_id=1, source_target_pairs={{0,4},{1,3},{4,8},{5,1},{8,12},{9,5},{12,14},{13,9},{14,10},{15,13... | collective-permute-start | bytes 1572872 | tf_op jit(solution)/shard_map/ppermute | solution.py:391
  21.5 2.8 %collective-permute-done.6.refs_3_ = bf16[1024,256]{1,0:T(8,128)(2,1)S(1)} collective-permute-done((bf16[1024,256]{1,0:T(8,128)(2,1)S(1)}, bf16[1024,256]{1,0:T(8,128)(2,1)S(1)}, u32[]{:S(2)}, u32[]{:S(2)}) %collective-permute-start.6) | collective-permute-done | bytes 524320 | tf_op jit(solution)/shard_map/ppermute | solution.py:388
  24.2 2.0 %collective-permute-start.10 = (bf16[1024,256]{1,0:T(8,128)(2,1)S(1)}, bf16[1024,256]{1,0:T(8,128)(2,1)S(1)}, u32[]{:S(2)}, u32[]{:S(2)}) collective-permute-start(bf16[1024,256]{1,0:T(8,128)(2,1)S(1)} %collective-permute-done.6.refs_3_), channel_id=1, source_target_pairs={{0,16},{16,0},{1,17},{17,1},{2,18},{18,2},{3,19},{19,3},{4,20},{20... | collective-permute-start | bytes 1572872 | tf_op jit(solution)/shard_map/ppermute | solution.py:394
  26.2 1.7 %collective-permute-start.9 = (bf16[1024,256]{1,0:T(8,128)(2,1)S(1)}, bf16[1024,256]{1,0:T(8,128)(2,1)S(1)}, u32[]{:S(2)}, u32[]{:S(2)}) collective-permute-start(bf16[1024,256]{1,0:T(8,128)(2,1)S(1)} %collective-permute-done.6.refs_3_), channel_id=1, source_target_pairs={{0,2},{1,5},{4,0},{5,9},{8,4},{9,13},{12,8},{13,15},{14,12},{15,11... | collective-permute-start | bytes 1572872 | tf_op jit(solution)/shard_map/ppermute | solution.py:388
  27.9 2.3 %collective-permute-done.5.refs_4_ = bf16[1024,256]{1,0:T(8,128)(2,1)S(1)} collective-permute-done((bf16[1024,256]{1,0:T(8,128)(2,1)S(1)}, bf16[1024,256]{1,0:T(8,128)(2,1)S(1)}, u32[]{:S(2)}, u32[]{:S(2)}) %collective-permute-start.5) | collective-permute-done | bytes 524320 | tf_op jit(solution)/shard_map/ppermute | solution.py:394
  30.3 1.7 %shard_map.97 = (f32[1,512,256]{2,1,0:T(8,128)S(1)}, f32[512,256]{1,0:T(8,128)S(1)}, f32[2,512,256]{2,1,0:T(8,128)S(1)}, f32[512,128]{1,0:T(8,128)S(1)}) custom-call(bf16[512,2048]{1,0:T(8,128)(2,1)S(1)} %copy-done.2, bf16[512,2048]{1,0:T(8,128)(2,1)S(1)} %collective-permute-done.1.refs_0_.refs_1_, bf16[512,4096]{1,0:T(8,128)(2,1)S(1)} %copy-done, ...), custom_call_target="tpu_custom_call" | custom-call | flops 1000 | bytes 1000 | tf_op jit(solution)/shard_map/pallas_call | solution.py:155
  33.2 6.2 %collective-permute-done.10.refs_4_ = bf16[1024,256]{1,0:T(8,128)(2,1)S(1)} collective-permute-done((bf16[1024,256]{1,0:T(8,128)(2,1)S(1)}, bf16[1024,256]{1,0:T(8,128)(2,1)S(1)}, u32[]{:S(2)}, u32[]{:S(2)}) %collective-permute-start.10) | collective-permute-done | bytes 524320 | tf_op jit(solution)/shard_map/ppermute | solution.py:394
  41.3 2.5 %shard_map.98 = (f32[2,512,256]{2,1,0:T(8,128)S(1)}, f32[512,256]{1,0:T(8,128)S(1)}, f32[512,256]{1,0:T(8,128)S(1)}, f32[1,512,256]{2,1,0:T(8,128)S(1)}, f32[512,128]{1,0:T(8,128)S(1)}) custom-call(bf16[512,2048]{1,0:T(8,128)(2,1)S(1)} %copy-done.2, bf16[512,2048]{1,0:T(8,128)(2,1)S(1)} %collective-permute-done.1.refs_0_.refs_1_, ...), custom_call_target="tpu_custom_call" | custom-call | flops 1000 | bytes 1000 | tf_op jit(solution)/shard_map/pallas_call | solution.py:155
  45.8 4.2 %collective-permute-done.14.refs_6_ = bf16[1024,256]{1,0:T(8,128)(2,1)S(1)} collective-permute-done((bf16[1024,256]{1,0:T(8,128)(2,1)S(1)}, bf16[1024,256]{1,0:T(8,128)(2,1)S(1)}, u32[]{:S(2)}, u32[]{:S(2)}) %collective-permute-start.14) | collective-permute-done | bytes 524320 | tf_op jit(solution)/shard_map/ppermute | solution.py:388
  50.1 3.0 %collective-permute-done.13.refs_4_ = bf16[1024,256]{1,0:T(8,128)(2,1)S(1)} collective-permute-done((bf16[1024,256]{1,0:T(8,128)(2,1)S(1)}, bf16[1024,256]{1,0:T(8,128)(2,1)S(1)}, u32[]{:S(2)}, u32[]{:S(2)}) %collective-permute-start.13) | collective-permute-done | bytes 524320 | tf_op jit(solution)/shard_map/ppermute | solution.py:394
  54.4 3.9 %shard_map.99 = (f32[3,512,256]{2,1,0:T(8,128)S(1)}, f32[2,512,256]{2,1,0:T(8,128)S(1)}, f32[1,512,256]{2,1,0:T(8,128)S(1)}, f32[1,512,256]{2,1,0:T(8,128)S(1)}, f32[512,128]{1,0:T(8,128)S(1)}) custom-call(bf16[512,2048]{1,0:T(8,128)(2,1)S(1)} %copy-done.2, bf16[512,2048]{1,0:T(8,128)(2,1)S(1)} %collective-permute-done.1.refs_0_.refs_1_, ...), custom_call_target="tpu_custom_call" | custom-call | flops 1000 | bytes 1000 | tf_op jit(solution)/shard_map/pallas_call | solution.py:155
  62.0 3.4 %collective-permute-done.18.refs_0_ = bf16[1024,256]{1,0:T(8,128)(2,1)S(1)} collective-permute-done((bf16[1024,256]{1,0:T(8,128)(2,1)S(1)}, bf16[1024,256]{1,0:T(8,128)(2,1)S(1)}, u32[]{:S(2)}, u32[]{:S(2)}) %collective-permute-start.18) | collective-permute-done | bytes 524320 | tf_op jit(solution)/shard_map/ppermute | solution.py:394
  68.8 1.8 %shard_map.102 = (f32[4,512,256]{2,1,0:T(8,128)S(1)}, f32[512,128]{1,0:T(8,128)S(1)}) custom-call(bf16[512,2048]{1,0:T(8,128)(2,1)S(1)} %copy-done.2, bf16[512,4096]{1,0:T(8,128)(2,1)S(1)} %copy-done, f32[512,128]{1,0:T(8,128)S(1)} %get-tuple-element.126.before, bf16[1024,256]{1,0:T(8,128)(2,1)S(1)} %collective-permute-done.17.refs_0_, ...), custom_call_target="tpu_custom_call" | custom-call | flops 1000 | bytes 1000 | tf_op jit(solution)/shard_map/pallas_call | solution.py:191
  70.7 2.9 %shard_map.103 = (f32[1,4096]{1,0:T(1,128)}, bf16[48,128]{1,0:T(8,128)(2,1)S(1)}) custom-call(bf16[512,2048]{1,0:T(8,128)(2,1)S(1)} %copy-done.2, bf16[512,4096]{1,0:T(8,128)(2,1)S(1)} %copy-done, f32[512,128]{1,0:T(8,128)S(1)} %get-tuple-element.130.before, f32[1,4096]{1,0:T(1,128)S(1)} %bitcast.5, f32[1,128]{1,0:T(1,128)S(1)} %fusion.flags, ...), custom_call_target="tpu_custom_call" | custom-call | flops 1000 | bytes 1000 | tf_op jit(solution)/shard_map/pallas_call | solution.py:243
  74.6 2.7 %collective-permute-done.26 = bf16[48,128]{1,0:T(8,128)(2,1)S(1)} collective-permute-done((bf16[48,128]{1,0:T(8,128)(2,1)S(1)}, bf16[48,128]{1,0:T(8,128)(2,1)S(1)}, u32[]{:S(2)}, u32[]{:S(2)}) %collective-permute-start.26) | collective-permute-done | bytes 12320 | tf_op jit(solution)/shard_map/ppermute | solution.py:497
  77.3 2.2 %collective-permute-start.27 = (bf16[2,48,128]{2,1,0:T(8,128)(2,1)S(1)}, bf16[2,48,128]{2,1,0:T(8,128)(2,1)S(1)}, u32[]{:S(2)}, u32[]{:S(2)}) collective-permute-start(bf16[2,48,128]{2,1,0:T(8,128)(2,1)S(1)} %pad_maximum_fusion.refs_0_), channel_id=1, source_target_pairs={{0,4},{1,5},{2,6},{3,7},{4,8},{5,9},{6,10},{7,11},{8,12},{9,13},{1... | collective-permute-start | bytes 73736 | tf_op jit(solution)/shard_map/ppermute | solution.py:494
  79.5 2.6 %collective-permute-start.28 = (bf16[2,48,128]{2,1,0:T(8,128)(2,1)S(1)}, bf16[2,48,128]{2,1,0:T(8,128)(2,1)S(1)}, u32[]{:S(2)}, u32[]{:S(2)}) collective-permute-start(bf16[2,48,128]{2,1,0:T(8,128)(2,1)S(1)} %pad_maximum_fusion.refs_0_), channel_id=1, source_target_pairs={{0,8},{1,9},{2,10},{3,11},{4,12},{5,13},{6,14},{7,15},{8,0},{9,1},... | collective-permute-start | bytes 73736 | tf_op jit(solution)/shard_map/ppermute | solution.py:494
  82.1 2.5 %collective-permute-start.29 = (bf16[2,48,128]{2,1,0:T(8,128)(2,1)S(1)}, bf16[2,48,128]{2,1,0:T(8,128)(2,1)S(1)}, u32[]{:S(2)}, u32[]{:S(2)}) collective-permute-start(bf16[2,48,128]{2,1,0:T(8,128)(2,1)S(1)} %pad_maximum_fusion.refs_0_), channel_id=1, source_target_pairs={{0,12},{1,13},{2,14},{3,15},{4,0},{5,1},{6,2},{7,3},{8,4},{9,5},{1... | collective-permute-start | bytes 73736 | tf_op jit(solution)/shard_map/ppermute | solution.py:494
  87.3 4.2 %collective-permute-start.30 = (f32[2,40,128]{2,1,0:T(8,128)S(1)}, f32[2,40,128]{2,1,0:T(8,128)S(1)}, u32[]{:S(2)}, u32[]{:S(2)}) collective-permute-start(f32[2,40,128]{2,1,0:T(8,128)S(1)} %get-tuple-element.144), channel_id=1, source_target_pairs={{0,12},{1,13},{2,14},{3,15},{4,0},{5,1},{6,2},{7,3},{8,4},{9,5},{1... | collective-permute-start | bytes 122888 | tf_op jit(solution)/shard_map/ppermute | solution.py:494
  93.1 3.2 %collective-permute-done.31.refs_2_ = f32[2,40,128]{2,1,0:T(8,128)S(1)} collective-permute-done((f32[2,40,128]{2,1,0:T(8,128)S(1)}, f32[2,40,128]{2,1,0:T(8,128)S(1)}, u32[]{:S(2)}, u32[]{:S(2)}) %collective-permute-start.31) | collective-permute-done | bytes 40992 | tf_op jit(solution)/shard_map/ppermute | solution.py:494
  97.8 3.4 %collective-permute-done.33.second = f32[40,128]{1,0:T(8,128)S(1)} collective-permute-done((f32[40,128]{1,0:T(8,128)S(1)}, f32[40,128]{1,0:T(8,128)S(1)}, u32[]{:S(2)}, u32[]{:S(2)}) %collective-permute-start.33) | collective-permute-done | bytes 20512 | tf_op jit(solution)/shard_map/ppermute | solution.py:497
  (74 shorter events, 30.0 us)
Async XLA Ops:
  0.6 16.9 %collective-permute-start.1 = (bf16[512,2048]{1,0:T(8,128)(2,1)}, bf16[512,2048]{1,0:T(8,128)(2,1)S(1)}, u32[]{:S(2)}, u32[]{:S(2)}) collective-permute-start(bf16[512,2048]{1,0:T(8,128)(2,1)} %context.7), channel_id=1, source_target_pairs={{0,1},{1,0},{2,3},{3,2},{4,5},{5,4},{6,7},{7,6},{8,9},{9,8},{10,11... | collective-permute-start | bytes 6291464 | tf_op jit(solution)/shard_map/ppermute | solution.py:397
  2.4 11.3 %collective-permute-start.2 = (bf16[1024,256]{1,0:T(8,128)(2,1)S(1)}, bf16[1024,256]{1,0:T(8,128)(2,1)S(1)}, u32[]{:S(2)}, u32[]{:S(2)}) collective-permute-start(bf16[1024,256]{1,0:T(8,128)(2,1)S(1)} %shard_map.94), channel_id=1, source_target_pairs={{0,2},{1,5},{4,0},{5,9},{8,4},{9,13},{12,8},{13,15},{14,12},{15,11... | collective-permute-start | bytes 1572872 | tf_op jit(solution)/shard_map/ppermute | solution.py:388
  5.0 14.5 %collective-permute-start.3 = (bf16[112,4096]{1,0:T(8,128)(2,1)}, bf16[112,4096]{1,0:T(8,128)(2,1)S(1)}, u32[]{:S(2)}, u32[]{:S(2)}) collective-permute-start(bf16[112,4096]{1,0:T(8,128)(2,1)} %refs_4_.1), channel_id=1, source_target_pairs={{0,1},{1,0},{2,3},{3,2},{4,5},{5,4},{6,7},{7,6},{8,9},{9,8},{10,11... | collective-permute-start | bytes 2752520 | tf_op jit(solution)/shard_map/ppermute | solution.py:397
  7.8 11.7 %collective-permute-start = (bf16[1024,256]{1,0:T(8,128)(2,1)S(1)}, bf16[1024,256]{1,0:T(8,128)(2,1)S(1)}, u32[]{:S(2)}, u32[]{:S(2)}) collective-permute-start(bf16[1024,256]{1,0:T(8,128)(2,1)S(1)} %shard_map.94), channel_id=1, source_target_pairs={{0,4},{1,3},{4,8},{5,1},{8,12},{9,5},{12,14},{13,9},{14,10},{15,13... | collective-permute-start | bytes 1572872 | tf_op jit(solution)/shard_map/ppermute | solution.py:391
  13.7 10.5 %collective-permute-start.6 = (bf16[1024,256]{1,0:T(8,128)(2,1)S(1)}, bf16[1024,256]{1,0:T(8,128)(2,1)S(1)}, u32[]{:S(2)}, u32[]{:S(2)}) collective-permute-start(bf16[1024,256]{1,0:T(8,128)(2,1)S(1)} %collective-permute-done.2.refs_3_), channel_id=1, source_target_pairs={{0,2},{1,5},{4,0},{5,9},{8,4},{9,13},{12,8},{13,15},{14,12},{15,11... | collective-permute-start | bytes 1572872 | tf_op jit(solution)/shard_map/ppermute | solution.py:388
  16.1 14.2 %collective-permute-start.5 = (bf16[1024,256]{1,0:T(8,128)(2,1)S(1)}, bf16[1024,256]{1,0:T(8,128)(2,1)S(1)}, u32[]{:S(2)}, u32[]{:S(2)}) collective-permute-start(bf16[1024,256]{1,0:T(8,128)(2,1)S(1)} %collective-permute-done.2.refs_3_), channel_id=1, source_target_pairs={{0,16},{16,0},{1,17},{17,1},{2,18},{18,2},{3,19},{19,3},{4,20},{20... | collective-permute-start | bytes 1572872 | tf_op jit(solution)/shard_map/ppermute | solution.py:394
  19.5 10.8 %collective-permute-start.7 = (f32[512,256]{1,0:T(8,128)S(1)}, f32[512,256]{1,0:T(8,128)S(1)}, u32[]{:S(2)}, u32[]{:S(2)}) collective-permute-start(f32[512,256]{1,0:T(8,128)S(1)} %shard_map.96), channel_id=1, source_target_pairs={{0,1},{1,0},{2,3},{3,2},{4,5},{5,4},{6,7},{7,6},{8,9},{9,8},{10,11... | collective-permute-start | bytes 1572872 | tf_op jit(solution)/shard_map/ppermute | solution.py:397
  19.5 12.6 %collective-permute-start.4 = (bf16[1024,256]{1,0:T(8,128)(2,1)S(1)}, bf16[1024,256]{1,0:T(8,128)(2,1)S(1)}, u32[]{:S(2)}, u32[]{:S(2)}) collective-permute-start(bf16[1024,256]{1,0:T(8,128)(2,1)S(1)} %collective-permute-done.refs_5_), channel_id=1, source_target_pairs={{0,4},{1,3},{4,8},{5,1},{8,12},{9,5},{12,14},{13,9},{14,10},{15,13... | collective-permute-start | bytes 1572872 | tf_op jit(solution)/shard_map/ppermute | solution.py:391
  24.2 15.2 %collective-permute-start.10 = (bf16[1024,256]{1,0:T(8,128)(2,1)S(1)}, bf16[1024,256]{1,0:T(8,128)(2,1)S(1)}, u32[]{:S(2)}, u32[]{:S(2)}) collective-permute-start(bf16[1024,256]{1,0:T(8,128)(2,1)S(1)} %collective-permute-done.6.refs_3_), channel_id=1, source_target_pairs={{0,16},{16,0},{1,17},{17,1},{2,18},{18,2},{3,19},{19,3},{4,20},{20... | collective-permute-start | bytes 1572872 | tf_op jit(solution)/shard_map/ppermute | solution.py:394
  26.2 13.6 %collective-permute-start.9 = (bf16[1024,256]{1,0:T(8,128)(2,1)S(1)}, bf16[1024,256]{1,0:T(8,128)(2,1)S(1)}, u32[]{:S(2)}, u32[]{:S(2)}) collective-permute-start(bf16[1024,256]{1,0:T(8,128)(2,1)S(1)} %collective-permute-done.6.refs_3_), channel_id=1, source_target_pairs={{0,2},{1,5},{4,0},{5,9},{8,4},{9,13},{12,8},{13,15},{14,12},{15,11... | collective-permute-start | bytes 1572872 | tf_op jit(solution)/shard_map/ppermute | solution.py:388
  32.0 9.3 %collective-permute-start.11 = (f32[512,256]{1,0:T(8,128)S(1)}, f32[512,256]{1,0:T(8,128)S(1)}, u32[]{:S(2)}, u32[]{:S(2)}) collective-permute-start(f32[512,256]{1,0:T(8,128)S(1)} %get-tuple-element.97), channel_id=1, source_target_pairs={{0,1},{1,0},{2,3},{3,2},{4,5},{5,4},{6,7},{7,6},{8,9},{9,8},{10,11... | collective-permute-start | bytes 1572872 | tf_op jit(solution)/shard_map/ppermute | solution.py:397
  32.1 11.7 %collective-permute-start.8 = (bf16[1024,256]{1,0:T(8,128)(2,1)S(1)}, bf16[1024,256]{1,0:T(8,128)(2,1)S(1)}, u32[]{:S(2)}, u32[]{:S(2)}) collective-permute-start(bf16[1024,256]{1,0:T(8,128)(2,1)S(1)} %collective-permute-done.4.refs_3_), channel_id=1, source_target_pairs={{0,4},{1,3},{4,8},{5,1},{8,12},{9,5},{12,14},{13,9},{14,10},{15,13... | collective-permute-start | bytes 1572872 | tf_op jit(solution)/shard_map/ppermute | solution.py:391
  39.4 10.7 %collective-permute-start.14 = (bf16[1024,256]{1,0:T(8,128)(2,1)S(1)}, bf16[1024,256]{1,0:T(8,128)(2,1)S(1)}, u32[]{:S(2)}, u32[]{:S(2)}) collective-permute-start(bf16[1024,256]{1,0:T(8,128)(2,1)S(1)} %collective-permute-done.10.refs_4_), channel_id=1, source_target_pairs={{0,2},{1,5},{4,0},{5,9},{8,4},{9,13},{12,8},{13,15},{14,12},{15,11... | collective-permute-start | bytes 1572872 | tf_op jit(solution)/shard_map/ppermute | solution.py:388
  39.8 13.3 %collective-permute-start.13 = (bf16[1024,256]{1,0:T(8,128)(2,1)S(1)}, bf16[1024,256]{1,0:T(8,128)(2,1)S(1)}, u32[]{:S(2)}, u32[]{:S(2)}) collective-permute-start(bf16[1024,256]{1,0:T(8,128)(2,1)S(1)} %collective-permute-done.4.refs_3_), channel_id=1, source_target_pairs={{0,16},{16,0},{1,17},{17,1},{2,18},{18,2},{3,19},{19,3},{4,20},{20... | collective-permute-start | bytes 1572872 | tf_op jit(solution)/shard_map/ppermute | solution.py:394
  43.8 10.6 %collective-permute-start.15 = (f32[512,256]{1,0:T(8,128)S(1)}, f32[512,256]{1,0:T(8,128)S(1)}, u32[]{:S(2)}, u32[]{:S(2)}) collective-permute-start(f32[512,256]{1,0:T(8,128)S(1)} %get-tuple-element.109), channel_id=1, source_target_pairs={{0,1},{1,0},{2,3},{3,2},{4,5},{5,4},{6,7},{7,6},{8,9},{9,8},{10,11... | collective-permute-start | bytes 1572872 | tf_op jit(solution)/shard_map/ppermute | solution.py:397
  43.9 14.4 %collective-permute-start.12 = (bf16[1024,256]{1,0:T(8,128)(2,1)S(1)}, bf16[1024,256]{1,0:T(8,128)(2,1)S(1)}, u32[]{:S(2)}, u32[]{:S(2)}) collective-permute-start(bf16[1024,256]{1,0:T(8,128)(2,1)S(1)} %collective-permute-done.8.refs_7_), channel_id=1, source_target_pairs={{0,4},{1,3},{4,8},{5,1},{8,12},{9,5},{12,14},{13,9},{14,10},{15,13... | collective-permute-start | bytes 1572872 | tf_op jit(solution)/shard_map/ppermute | solution.py:391
  45.5 12.8 %collective-permute-start.16 = (f32[512,256]{1,0:T(8,128)S(1)}, f32[512,256]{1,0:T(8,128)S(1)}, u32[]{:S(2)}, u32[]{:S(2)}) collective-permute-start(f32[512,256]{1,0:T(8,128)S(1)} %get-tuple-element.114), channel_id=1, source_target_pairs={{0,1},{1,0},{2,3},{3,2},{4,5},{5,4},{6,7},{7,6},{8,9},{9,8},{10,11... | collective-permute-start | bytes 1572872 | tf_op jit(solution)/shard_map/ppermute | solution.py:397
  50.1 10.5 %collective-permute-start.19 = (bf16[1024,256]{1,0:T(8,128)(2,1)S(1)}, bf16[1024,256]{1,0:T(8,128)(2,1)S(1)}, u32[]{:S(2)}, u32[]{:S(2)}) collective-permute-start(bf16[1024,256]{1,0:T(8,128)(2,1)S(1)} %collective-permute-done.14.refs_6_), channel_id=1, source_target_pairs={{0,2},{1,5},{4,0},{5,9},{8,4},{9,13},{12,8},{13,15},{14,12},{15,11... | collective-permute-start | bytes 1572872 | tf_op jit(solution)/shard_map/ppermute | solution.py:388
  53.1 12.3 %collective-permute-start.18 = (bf16[1024,256]{1,0:T(8,128)(2,1)S(1)}, bf16[1024,256]{1,0:T(8,128)(2,1)S(1)}, u32[]{:S(2)}, u32[]{:S(2)}) collective-permute-start(bf16[1024,256]{1,0:T(8,128)(2,1)S(1)} %collective-permute-done.refs_5_), channel_id=1, source_target_pairs={{0,16},{16,0},{1,17},{17,1},{2,18},{18,2},{3,19},{19,3},{4,20},{20... | collective-permute-start | bytes 1572872 | tf_op jit(solution)/shard_map/ppermute | solution.py:394
  58.3 9.2 %collective-permute-start.17 = (bf16[1024,256]{1,0:T(8,128)(2,1)S(1)}, bf16[1024,256]{1,0:T(8,128)(2,1)S(1)}, u32[]{:S(2)}, u32[]{:S(2)}) collective-permute-start(bf16[1024,256]{1,0:T(8,128)(2,1)S(1)} %collective-permute-done.13.refs_4_), channel_id=1, source_target_pairs={{0,4},{1,3},{4,8},{5,1},{8,12},{9,5},{12,14},{13,9},{14,10},{15,13... | collective-permute-start | bytes 1572872 | tf_op jit(solution)/shard_map/ppermute | solution.py:391
  60.0 8.8 %collective-permute-start.22 = (f32[2,512,256]{2,1,0:T(8,128)S(1)}, f32[2,512,256]{2,1,0:T(8,128)S(1)}, u32[]{:S(2)}, u32[]{:S(2)}) collective-permute-start(f32[2,512,256]{2,1,0:T(8,128)S(1)} %get-tuple-element.129), channel_id=1, source_target_pairs={{0,1},{1,0},{2,3},{3,2},{4,5},{5,4},{6,7},{7,6},{8,9},{9,8},{10,11... | collective-permute-start | bytes 3145736 | tf_op jit(solution)/shard_map/ppermute | solution.py:397
  60.6 7.0 %collective-permute-start.21 = (bf16[1024,256]{1,0:T(8,128)(2,1)S(1)}, bf16[1024,256]{1,0:T(8,128)(2,1)S(1)}, u32[]{:S(2)}, u32[]{:S(2)}) collective-permute-start(bf16[1024,256]{1,0:T(8,128)(2,1)S(1)} %collective-permute-done.19.refs_1_), channel_id=1, source_target_pairs={{0,1},{1,0},{2,3},{3,2},{4,5},{5,4},{6,7},{7,6},{8,9},{9,8},{10,11... | collective-permute-start | bytes 1572872 | tf_op jit(solution)/shard_map/ppermute | solution.py:397
  60.6 8.2 %collective-permute-start.20 = (bf16[1024,256]{1,0:T(8,128)(2,1)S(1)}, bf16[1024,256]{1,0:T(8,128)(2,1)S(1)}, u32[]{:S(2)}, u32[]{:S(2)}) collective-permute-start(bf16[1024,256]{1,0:T(8,128)(2,1)S(1)} %collective-permute-done.12.refs_0_), channel_id=1, source_target_pairs={{0,1},{1,0},{2,3},{3,2},{4,5},{5,4},{6,7},{7,6},{8,9},{9,8},{10,11... | collective-permute-start | bytes 1572872 | tf_op jit(solution)/shard_map/ppermute | solution.py:397
  77.3 7.4 %collective-permute-start.27 = (bf16[2,48,128]{2,1,0:T(8,128)(2,1)S(1)}, bf16[2,48,128]{2,1,0:T(8,128)(2,1)S(1)}, u32[]{:S(2)}, u32[]{:S(2)}) collective-permute-start(bf16[2,48,128]{2,1,0:T(8,128)(2,1)S(1)} %pad_maximum_fusion.refs_0_), channel_id=1, source_target_pairs={{0,4},{1,5},{2,6},{3,7},{4,8},{5,9},{6,10},{7,11},{8,12},{9,13},{1... | collective-permute-start | bytes 73736 | tf_op jit(solution)/shard_map/ppermute | solution.py:494
  (17 other events, 114.1 us)

commit v13 on v11

--- a/solution.py
+++ b/solution.py
@@ -201,7 +201,7 @@
     )(*operands)
 
 
-def final_kernel(items, sources, n_pieces, length, context, residual, before, gain, flags, *refs):
+def final_kernel(items, sources, n_pieces, context, residual, before, gain, flags, *refs):
     pieces, hidden = refs[:n_pieces], refs[n_pieces:-6]
     embedded, payload, blocks, squares, scale_rows, sheet = refs[-6:]
     width = blocks.shape[2]
@@ -209,10 +209,11 @@
     squares[...] = before[...]
     late_blocks(items, context, residual, pieces, hidden, squares, blocks)
     mean = jnp.sum(squares[...], axis=1, keepdims=True) * (1.0 / features)
-    row = lax.broadcasted_iota(jnp.int32, mean.shape, 0)
-    scale = jnp.where(row < length[0], lax.rsqrt(mean + 1e-05), 0.0)
+    length = flags[:, LANES - 1 : LANES]
+    row = lax.broadcasted_iota(jnp.int32, mean.shape, 0).astype(jnp.float32)
+    scale = jnp.where(row < length, lax.rsqrt(mean + 1e-05), 0.0)
     scale_rows[...] = jnp.broadcast_to(scale, scale_rows.shape)
-    inverse = 1.0 / jnp.full((1, width), length[0], jnp.int32).astype(jnp.float32)
+    inverse = 1.0 / length
     done = [(blocks.at[i], distance, same) for i, (_, _, _, distance, same) in enumerate(items)]
     done += [(hidden[array].at[entry], distance, same) for array, entry, distance, same in sources]
     for block, distance, same in done:
@@ -235,7 +236,7 @@
         payload[rank] = rounded
 
 
-def finish(items, sources, lengths, context, residual, squares, gain, flags, pieces, hidden, ranks):
+def finish(items, sources, context, residual, squares, gain, flags, pieces, hidden, ranks):
     rows = context.shape[0]
     width = pieces[0].shape[1]
     features = (len(items) + len(sources)) * width
@@ -247,7 +248,7 @@
             jax.ShapeDtypeStruct((1, features), jnp.float32),
             jax.ShapeDtypeStruct((ranks, lines, LANES), jnp.bfloat16),
         ),
-        in_specs=[pl.BlockSpec(memory_space=pltpu.SMEM)] + [VMEM_SPEC] * len(operands),
+        in_specs=[VMEM_SPEC] * len(operands),
         out_specs=(VMEM_SPEC, VMEM_SPEC),
         scratch_shapes=[
             pltpu.VMEM((len(items), rows, width), jnp.float32),
@@ -257,7 +258,7 @@
         ],
         compiler_params=pltpu.CompilerParams(vmem_limit_bytes=VMEM_BYTES),
         cost_estimate=SMALL,
-    )(lengths, *operands)
+    )(*operands)
 
 
 def score_kernel(lines, blocks, got, queries, other_queries, out, wide, emb, mix):
@@ -422,51 +423,45 @@
 
     n4x, l4 = wait((a, l4))
     n4xs = other_core(n4x)
-    xl1, n4x = wait((x, n4x))
+    items = ((None, ((0, False), (1, True)), True, 4, True),)
+    h4, sq4 = late(items, context, residual, sq3, [l4, n4x], [])
+    xl1, n4x, sq4 = wait((x, n4x, sq4))
     xl1s = other_core(xl1)
-    l3x, xl1 = wait((b, xl1))
+    items = (((0, 1), ((0, True),), False, -1, True),)
+    h5, sq5 = late(items, context, residual, sq4, [xl1], [h2])
+    l3x, xl1, sq5 = wait((b, xl1, sq5))
     l3xs = other_core(l3x)
-
-    missing = (((0, True),), ((1, True),), ((2, False), (3, True)))
-    own_items = tuple(
-        (base, parts, base is None, distance, True)
-        for base, parts, distance in zip(((0, 1), (1, 2), None), missing, (-1, -3, 4))
-    )
-    h4, sq4 = late(own_items, context, residual, sq3, [xl1, l3x, l4, n4x], [h2, h3])
-    items = tuple(
-        (base, parts, True, distance, False)
-        for base, parts, distance in zip(
-            ((8, None), (9, 0), None, (10, 0), (10, 1)), missing + ((), ()), (-1, -3, 4, -2, 3)
-        )
-    )
-    hidden = [f0, h1, h2, h3, h4, f0, f1, f2, r2p, r3p, r3a]
+    items = (
+        ((0, 2), ((0, True),), False, -3, True),
+        ((1, 0), (), True, -2, False),
+        ((1, 1), (), True, 3, False),
+        (None, ((1, False), (2, True)), True, 4, False),
+    )
+    h6, sq6 = late(items, context, residual, sq5, [l3x, l4s, n4xs], [h3, r3a])
+    items = (((0, None), ((0, True),), True, -1, False), ((1, 0), ((1, True),), True, -3, False))
+    hidden = [r2p, r3p, h1, h2, h3, h4, h5, h6, f0, f1, f2]
     sources = (
-        (0, 0, 0, True),
-        (1, 0, 1, True),
-        (2, 0, 2, True),
-        (3, 0, -2, True),
-        (3, 1, 3, True),
-        (4, 0, -1, True),
-        (4, 1, -3, True),
-        (4, 2, 4, True),
-        (0, 1, 0, False),
-        (6, 0, 1, False),
-        (7, 0, 2, False),
-    )
-    flags = jnp.pad(pattern.astype(jnp.float32), ((0, 0), (0, LANES - pattern.shape[1])))
+        (2, 0, 1, True),
+        (3, 0, 2, True),
+        (4, 0, -2, True),
+        (4, 1, 3, True),
+        (5, 0, 4, True),
+        (6, 0, -1, True),
+        (8, 0, 0, True),
+        (8, 1, 0, False),
+        (9, 0, 1, False),
+        (10, 0, 2, False),
+        (7, 0, -3, True),
+        (7, 1, -2, False),
+        (7, 2, 3, False),
+        (7, 3, 4, False),
+    )
+    flags = jnp.pad(pattern.astype(jnp.float32), ((0, 0), (0, LANES - 1 - pattern.shape[1])))
+    flags = jnp.concatenate([flags, lengths.astype(jnp.float32)[:, None]], axis=1)
     embedded, payload = finish(
-        items,
-        sources,
-        lengths,
-        context,
-        residual,
-        sq4,
-        norm_gain.reshape(1, -1),
-        flags,
-        [xl1s, l3xs, l4s, n4xs],
-        hidden,
-        size,
-    )
+        items, sources, context, residual, sq6, norm_gain.reshape(1, -1), flags, [xl1s, l3xs], hidden, size
+    )
+
     same_core = [list(range(c, ranks, CORES)) for c in range(CORES)]
 
     def spread(blocks):
@@ -540,7 +535,7 @@
         and out_proj.shape[1] % LANES == 0
         and out_proj.shape[0] % (2 * LANES) == 0
         and context.shape[0] % STEP == 0
-        and pattern.shape[1] <= LANES
+        and pattern.shape[1] < LANES
     )
     form = on_cycle if fits else gathered
     return form(context, residual, out_proj, norm_gain, lengths, queries, pattern)

time: 102 us -> 99.3 us (0.974)
  waiting for transfers between devices: 31.9 us -> 29.3 us
    pallas_call x1 -> x3, Pallas kernels: 2.15 us -> 3.38 us  [late(): pl.pallas_call(functools.partial(late_kernel, items, len(pieces)), out_sh...]
    pallas_call x1, Pallas kernels: 4.03 us -> 2.94 us  [finish(): pl.pallas_call(functools.partial(final_kernel, items, sources, len(pieces...]
    ppermute x5, waiting for transfers between devices: 3.57 us -> 2.52 us  [from_last(): return lax.ppermute(piece, 'dp', ring(1))]
  transfers between devices with their start and end apart: 26 -> 26, of which waited for: 10 -> 10; matrix products, arithmetic and copies ran while one was open for 0% -> 0% of each run, Pallas kernels for 12% -> 13%
where the time goes in v13:
time: 99.3 us; the launch traced here: 99.1 us
  waiting for transfers between devices  29.3 us (30%)
  starting transfers between devices  23.7 us (24%)
  blocking collectives  23.5 us (24%)
  Pallas kernels  18.2 us (18%)
  local copies, waits for them, and re-layouts  2.84 us (3%)
  between operations  1.5 us (2%)
    all_to_all x2, blocking collectives, spread(): lax.all_to_all(blocks, 'dp', 0, 0, axis_index_groups=same_core, tiled=True)  23.5 us
    ppermute x4, waiting for transfers between devices, over_x(): return lax.ppermute(piece, 'groups', [(0, 1), (1, 0)])  15 us
    ppermute x5, waiting for transfers between devices, from_next(): return lax.ppermute(piece, 'dp', ring(-1))  11.8 us
    pallas_call x5, Pallas kernels, wave(): pl.pallas_call(functools.partial(wave_kernel, full, part, arrived, whole,...  9.95 us
    ppermute x5, starting transfers between devices, from_last(): return lax.ppermute(piece, 'dp', ring(1))  8.04 us
    ppermute x5, starting transfers between devices, from_next(): return lax.ppermute(piece, 'dp', ring(-1))  7.1 us
    ppermute x4, starting transfers between devices, over_x(): return lax.ppermute(piece, 'groups', [(0, 1), (1, 0)])  6.24 us
    pallas_call x3, Pallas kernels, late(): pl.pallas_call(functools.partial(late_kernel, items, len(pieces)), out_sh...  3.38 us
  transfers between devices with their start and end apart: 26, of which 10 were waited for; matrix products, arithmetic and copies ran while one was open for 0% of the time, Pallas kernels for 13%

profile of v13, /device:TPU:0, one launch (start us, length us, event | category | flops | bytes accessed | tf_op | source)
XLA Modules:
  0.0 99.1 jit_solution(6327903821598974124)
XLA Ops:
  2.4 2.6 %collective-permute-start.2 = (bf16[1024,256]{1,0:T(8,128)(2,1)S(1)}, bf16[1024,256]{1,0:T(8,128)(2,1)S(1)}, u32[]{:S(2)}, u32[]{:S(2)}) collective-permute-start(bf16[1024,256]{1,0:T(8,128)(2,1)S(1)} %shard_map.94), channel_id=1, source_target_pairs={{0,2},{1,5},{4,0},{5,9},{8,4},{9,13},{12,8},{13,15},{14,12},{15,11... | collective-permute-start | bytes 1572872 | tf_op jit(solution)/shard_map/ppermute | solution.py:362
  5.3 1.6 %copy-done.1 = bf16[512,2048]{1,0:T(8,128)(2,1)S(1)} copy-done((bf16[512,2048]{1,0:T(8,128)(2,1)S(1)}, bf16[512,2048]{1,0:T(8,128)(2,1)}, u32[]{:S(2)}) %copy-start.1) | copy-done | bytes 2097176
  7.8 1.6 %collective-permute-start = (bf16[1024,256]{1,0:T(8,128)(2,1)S(1)}, bf16[1024,256]{1,0:T(8,128)(2,1)S(1)}, u32[]{:S(2)}, u32[]{:S(2)}) collective-permute-start(bf16[1024,256]{1,0:T(8,128)(2,1)S(1)} %shard_map.94), channel_id=1, source_target_pairs={{0,4},{1,3},{4,8},{5,1},{8,12},{9,5},{12,14},{13,9},{14,10},{15,13... | collective-permute-start | bytes 1572872 | tf_op jit(solution)/shard_map/ppermute | solution.py:365
  9.4 4.3 %collective-permute-done.2.refs_3_ = bf16[1024,256]{1,0:T(8,128)(2,1)S(1)} collective-permute-done((bf16[1024,256]{1,0:T(8,128)(2,1)S(1)}, bf16[1024,256]{1,0:T(8,128)(2,1)S(1)}, u32[]{:S(2)}, u32[]{:S(2)}) %collective-permute-start.2) | collective-permute-done | bytes 524320 | tf_op jit(solution)/shard_map/ppermute | solution.py:362
  13.7 2.3 %collective-permute-start.6 = (bf16[1024,256]{1,0:T(8,128)(2,1)S(1)}, bf16[1024,256]{1,0:T(8,128)(2,1)S(1)}, u32[]{:S(2)}, u32[]{:S(2)}) collective-permute-start(bf16[1024,256]{1,0:T(8,128)(2,1)S(1)} %collective-permute-done.2.refs_3_), channel_id=1, source_target_pairs={{0,2},{1,5},{4,0},{5,9},{8,4},{9,13},{12,8},{13,15},{14,12},{15,11... | collective-permute-start | bytes 1572872 | tf_op jit(solution)/shard_map/ppermute | solution.py:362
  19.5 2.0 %collective-permute-start.4 = (bf16[1024,256]{1,0:T(8,128)(2,1)S(1)}, bf16[1024,256]{1,0:T(8,128)(2,1)S(1)}, u32[]{:S(2)}, u32[]{:S(2)}) collective-permute-start(bf16[1024,256]{1,0:T(8,128)(2,1)S(1)} %collective-permute-done.refs_5_), channel_id=1, source_target_pairs={{0,4},{1,3},{4,8},{5,1},{8,12},{9,5},{12,14},{13,9},{14,10},{15,13... | collective-permute-start | bytes 1572872 | tf_op jit(solution)/shard_map/ppermute | solution.py:365
  21.5 2.8 %collective-permute-done.6.refs_3_ = bf16[1024,256]{1,0:T(8,128)(2,1)S(1)} collective-permute-done((bf16[1024,256]{1,0:T(8,128)(2,1)S(1)}, bf16[1024,256]{1,0:T(8,128)(2,1)S(1)}, u32[]{:S(2)}, u32[]{:S(2)}) %collective-permute-start.6) | collective-permute-done | bytes 524320 | tf_op jit(solution)/shard_map/ppermute | solution.py:362
  24.2 2.0 %collective-permute-start.10 = (bf16[1024,256]{1,0:T(8,128)(2,1)S(1)}, bf16[1024,256]{1,0:T(8,128)(2,1)S(1)}, u32[]{:S(2)}, u32[]{:S(2)}) collective-permute-start(bf16[1024,256]{1,0:T(8,128)(2,1)S(1)} %collective-permute-done.6.refs_3_), channel_id=1, source_target_pairs={{0,16},{16,0},{1,17},{17,1},{2,18},{18,2},{3,19},{19,3},{4,20},{20... | collective-permute-start | bytes 1572872 | tf_op jit(solution)/shard_map/ppermute | solution.py:368
  26.2 1.7 %collective-permute-start.9 = (bf16[1024,256]{1,0:T(8,128)(2,1)S(1)}, bf16[1024,256]{1,0:T(8,128)(2,1)S(1)}, u32[]{:S(2)}, u32[]{:S(2)}) collective-permute-start(bf16[1024,256]{1,0:T(8,128)(2,1)S(1)} %collective-permute-done.6.refs_3_), channel_id=1, source_target_pairs={{0,2},{1,5},{4,0},{5,9},{8,4},{9,13},{12,8},{13,15},{14,12},{15,11... | collective-permute-start | bytes 1572872 | tf_op jit(solution)/shard_map/ppermute | solution.py:362
  27.9 2.3 %collective-permute-done.5.refs_4_ = bf16[1024,256]{1,0:T(8,128)(2,1)S(1)} collective-permute-done((bf16[1024,256]{1,0:T(8,128)(2,1)S(1)}, bf16[1024,256]{1,0:T(8,128)(2,1)S(1)}, u32[]{:S(2)}, u32[]{:S(2)}) %collective-permute-start.5) | collective-permute-done | bytes 524320 | tf_op jit(solution)/shard_map/ppermute | solution.py:368
  30.3 1.8 %shard_map.97 = (f32[1,512,256]{2,1,0:T(8,128)S(1)}, f32[512,256]{1,0:T(8,128)S(1)}, f32[2,512,256]{2,1,0:T(8,128)S(1)}, f32[512,128]{1,0:T(8,128)S(1)}) custom-call(bf16[512,2048]{1,0:T(8,128)(2,1)S(1)} %copy-done.2, bf16[512,2048]{1,0:T(8,128)(2,1)S(1)} %collective-permute-done.1.refs_0_.refs_1_, bf16[512,4096]{1,0:T(8,128)(2,1)S(1)} %copy-done, ...), custom_call_target="tpu_custom_call" | custom-call | flops 1000 | bytes 1000 | tf_op jit(solution)/shard_map/pallas_call | solution.py:155
  33.2 6.2 %collective-permute-done.10.refs_4_ = bf16[1024,256]{1,0:T(8,128)(2,1)S(1)} collective-permute-done((bf16[1024,256]{1,0:T(8,128)(2,1)S(1)}, bf16[1024,256]{1,0:T(8,128)(2,1)S(1)}, u32[]{:S(2)}, u32[]{:S(2)}) %collective-permute-start.10) | collective-permute-done | bytes 524320 | tf_op jit(solution)/shard_map/ppermute | solution.py:368
  39.8 1.5 %collective-permute-start.13 = (bf16[1024,256]{1,0:T(8,128)(2,1)S(1)}, bf16[1024,256]{1,0:T(8,128)(2,1)S(1)}, u32[]{:S(2)}, u32[]{:S(2)}) collective-permute-start(bf16[1024,256]{1,0:T(8,128)(2,1)S(1)} %collective-permute-done.4.refs_3_), channel_id=1, source_target_pairs={{0,16},{16,0},{1,17},{17,1},{2,18},{18,2},{3,19},{19,3},{4,20},{20... | collective-permute-start | bytes 1572872 | tf_op jit(solution)/shard_map/ppermute | solution.py:368
  41.3 2.5 %shard_map.98 = (f32[2,512,256]{2,1,0:T(8,128)S(1)}, f32[512,256]{1,0:T(8,128)S(1)}, f32[512,256]{1,0:T(8,128)S(1)}, f32[1,512,256]{2,1,0:T(8,128)S(1)}, f32[512,128]{1,0:T(8,128)S(1)}) custom-call(bf16[512,2048]{1,0:T(8,128)(2,1)S(1)} %copy-done.2, bf16[512,2048]{1,0:T(8,128)(2,1)S(1)} %collective-permute-done.1.refs_0_.refs_1_, ...), custom_call_target="tpu_custom_call" | custom-call | flops 1000 | bytes 1000 | tf_op jit(solution)/shard_map/pallas_call | solution.py:155
  43.9 1.6 %collective-permute-start.12 = (bf16[1024,256]{1,0:T(8,128)(2,1)S(1)}, bf16[1024,256]{1,0:T(8,128)(2,1)S(1)}, u32[]{:S(2)}, u32[]{:S(2)}) collective-permute-start(bf16[1024,256]{1,0:T(8,128)(2,1)S(1)} %collective-permute-done.8.refs_7_), channel_id=1, source_target_pairs={{0,4},{1,3},{4,8},{5,1},{8,12},{9,5},{12,14},{13,9},{14,10},{15,13... | collective-permute-start | bytes 1572872 | tf_op jit(solution)/shard_map/ppermute | solution.py:365
  45.9 4.2 %collective-permute-done.14.refs_6_ = bf16[1024,256]{1,0:T(8,128)(2,1)S(1)} collective-permute-done((bf16[1024,256]{1,0:T(8,128)(2,1)S(1)}, bf16[1024,256]{1,0:T(8,128)(2,1)S(1)}, u32[]{:S(2)}, u32[]{:S(2)}) %collective-permute-start.14) | collective-permute-done | bytes 524320 | tf_op jit(solution)/shard_map/ppermute | solution.py:362
  50.1 3.0 %collective-permute-done.13.refs_4_ = bf16[1024,256]{1,0:T(8,128)(2,1)S(1)} collective-permute-done((bf16[1024,256]{1,0:T(8,128)(2,1)S(1)}, bf16[1024,256]{1,0:T(8,128)(2,1)S(1)}, u32[]{:S(2)}, u32[]{:S(2)}) %collective-permute-start.13) | collective-permute-done | bytes 524320 | tf_op jit(solution)/shard_map/ppermute | solution.py:368
  54.4 3.9 %shard_map.99 = (f32[3,512,256]{2,1,0:T(8,128)S(1)}, f32[2,512,256]{2,1,0:T(8,128)S(1)}, f32[1,512,256]{2,1,0:T(8,128)S(1)}, f32[1,512,256]{2,1,0:T(8,128)S(1)}, f32[512,128]{1,0:T(8,128)S(1)}) custom-call(bf16[512,2048]{1,0:T(8,128)(2,1)S(1)} %copy-done.2, bf16[512,2048]{1,0:T(8,128)(2,1)S(1)} %collective-permute-done.1.refs_0_.refs_1_, ...), custom_call_target="tpu_custom_call" | custom-call | flops 1000 | bytes 1000 | tf_op jit(solution)/shard_map/pallas_call | solution.py:155
  58.3 1.7 %collective-permute-start.17 = (bf16[1024,256]{1,0:T(8,128)(2,1)S(1)}, bf16[1024,256]{1,0:T(8,128)(2,1)S(1)}, u32[]{:S(2)}, u32[]{:S(2)}) collective-permute-start(bf16[1024,256]{1,0:T(8,128)(2,1)S(1)} %collective-permute-done.13.refs_4_), channel_id=1, source_target_pairs={{0,4},{1,3},{4,8},{5,1},{8,12},{9,5},{12,14},{13,9},{14,10},{15,13... | collective-permute-start | bytes 1572872 | tf_op jit(solution)/shard_map/ppermute | solution.py:365
  62.0 3.4 %collective-permute-done.18.refs_0_ = bf16[1024,256]{1,0:T(8,128)(2,1)S(1)} collective-permute-done((bf16[1024,256]{1,0:T(8,128)(2,1)S(1)}, bf16[1024,256]{1,0:T(8,128)(2,1)S(1)}, u32[]{:S(2)}, u32[]{:S(2)}) %collective-permute-start.18) | collective-permute-done | bytes 524320 | tf_op jit(solution)/shard_map/ppermute | solution.py:368
  68.8 1.8 %shard_map.102 = (f32[4,512,256]{2,1,0:T(8,128)S(1)}, f32[512,128]{1,0:T(8,128)S(1)}) custom-call(bf16[512,2048]{1,0:T(8,128)(2,1)S(1)} %copy-done.2, bf16[512,4096]{1,0:T(8,128)(2,1)S(1)} %copy-done, f32[512,128]{1,0:T(8,128)S(1)} %get-tuple-element.120.before, bf16[1024,256]{1,0:T(8,128)(2,1)S(1)} %collective-permute-done.17.refs_0_, ...), custom_call_target="tpu_custom_call" | custom-call | flops 1000 | bytes 1000 | tf_op jit(solution)/shard_map/pallas_call | solution.py:191
  70.7 2.9 %shard_map.103 = (f32[1,4096]{1,0:T(1,128)}, bf16[8,48,128]{2,1,0:T(8,128)(2,1)S(1)}) custom-call(bf16[512,2048]{1,0:T(8,128)(2,1)S(1)} %copy-done.2, bf16[512,4096]{1,0:T(8,128)(2,1)S(1)} %copy-done, f32[512,128]{1,0:T(8,128)S(1)} %get-tuple-element.124.before, f32[1,4096]{1,0:T(1,128)S(1)} %bitcast.3, f32[1,128]{1,0:T(1,128)S(1)} %fusion.flags, ...), custom_call_target="tpu_custom_call" | custom-call | flops 1000 | bytes 1000 | tf_op jit(solution)/shard_map/pallas_call | solution.py:245
  73.7 13.5 %all_to_all.10.got = bf16[8,48,128]{2,1,0:T(8,128)(2,1)S(1)} all-to-all(bf16[8,48,128]{2,1,0:T(8,128)(2,1)S(1)} %get-tuple-element.135), channel_id=1, replica_groups={{0,2,4,6,8,10,12,14},{1,3,5,7,9,11,13,15},{16,18,20,22,24,26,28,30},{17..., dimensions={0} | all-to-all | bytes 196608 | tf_op jit(solution)/shard_map/all_to_all | solution.py:468
  88.3 10.0 %all_to_all.11.got = f32[8,40,128]{2,1,0:T(8,128)S(1)} all-to-all(f32[8,40,128]{2,1,0:T(8,128)S(1)} %shard_map.104), channel_id=1, replica_groups={{0,2,4,6,8,10,12,14},{1,3,5,7,9,11,13,15},{16,18,20,22,24,26,28,30},{17..., dimensions={0} | all-to-all | bytes 327680 | tf_op jit(solution)/shard_map/all_to_all | solution.py:468
  (58 shorter events, 16.1 us)
Async XLA Ops:
  0.6 16.9 %collective-permute-start.1 = (bf16[512,2048]{1,0:T(8,128)(2,1)}, bf16[512,2048]{1,0:T(8,128)(2,1)S(1)}, u32[]{:S(2)}, u32[]{:S(2)}) collective-permute-start(bf16[512,2048]{1,0:T(8,128)(2,1)} %context.7), channel_id=1, source_target_pairs={{0,1},{1,0},{2,3},{3,2},{4,5},{5,4},{6,7},{7,6},{8,9},{9,8},{10,11... | collective-permute-start | bytes 6291464 | tf_op jit(solution)/shard_map/ppermute | solution.py:371
  2.4 11.3 %collective-permute-start.2 = (bf16[1024,256]{1,0:T(8,128)(2,1)S(1)}, bf16[1024,256]{1,0:T(8,128)(2,1)S(1)}, u32[]{:S(2)}, u32[]{:S(2)}) collective-permute-start(bf16[1024,256]{1,0:T(8,128)(2,1)S(1)} %shard_map.94), channel_id=1, source_target_pairs={{0,2},{1,5},{4,0},{5,9},{8,4},{9,13},{12,8},{13,15},{14,12},{15,11... | collective-permute-start | bytes 1572872 | tf_op jit(solution)/shard_map/ppermute | solution.py:362
  5.0 14.5 %collective-permute-start.3 = (bf16[112,4096]{1,0:T(8,128)(2,1)}, bf16[112,4096]{1,0:T(8,128)(2,1)S(1)}, u32[]{:S(2)}, u32[]{:S(2)}) collective-permute-start(bf16[112,4096]{1,0:T(8,128)(2,1)} %queries.1), channel_id=1, source_target_pairs={{0,1},{1,0},{2,3},{3,2},{4,5},{5,4},{6,7},{7,6},{8,9},{9,8},{10,11... | collective-permute-start | bytes 2752520 | tf_op jit(solution)/shard_map/ppermute | solution.py:371
  7.8 11.7 %collective-permute-start = (bf16[1024,256]{1,0:T(8,128)(2,1)S(1)}, bf16[1024,256]{1,0:T(8,128)(2,1)S(1)}, u32[]{:S(2)}, u32[]{:S(2)}) collective-permute-start(bf16[1024,256]{1,0:T(8,128)(2,1)S(1)} %shard_map.94), channel_id=1, source_target_pairs={{0,4},{1,3},{4,8},{5,1},{8,12},{9,5},{12,14},{13,9},{14,10},{15,13... | collective-permute-start | bytes 1572872 | tf_op jit(solution)/shard_map/ppermute | solution.py:365
  13.7 10.5 %collective-permute-start.6 = (bf16[1024,256]{1,0:T(8,128)(2,1)S(1)}, bf16[1024,256]{1,0:T(8,128)(2,1)S(1)}, u32[]{:S(2)}, u32[]{:S(2)}) collective-permute-start(bf16[1024,256]{1,0:T(8,128)(2,1)S(1)} %collective-permute-done.2.refs_3_), channel_id=1, source_target_pairs={{0,2},{1,5},{4,0},{5,9},{8,4},{9,13},{12,8},{13,15},{14,12},{15,11... | collective-permute-start | bytes 1572872 | tf_op jit(solution)/shard_map/ppermute | solution.py:362
  16.1 14.2 %collective-permute-start.5 = (bf16[1024,256]{1,0:T(8,128)(2,1)S(1)}, bf16[1024,256]{1,0:T(8,128)(2,1)S(1)}, u32[]{:S(2)}, u32[]{:S(2)}) collective-permute-start(bf16[1024,256]{1,0:T(8,128)(2,1)S(1)} %collective-permute-done.2.refs_3_), channel_id=1, source_target_pairs={{0,16},{16,0},{1,17},{17,1},{2,18},{18,2},{3,19},{19,3},{4,20},{20... | collective-permute-start | bytes 1572872 | tf_op jit(solution)/shard_map/ppermute | solution.py:368
  19.5 10.8 %collective-permute-start.7 = (f32[512,256]{1,0:T(8,128)S(1)}, f32[512,256]{1,0:T(8,128)S(1)}, u32[]{:S(2)}, u32[]{:S(2)}) collective-permute-start(f32[512,256]{1,0:T(8,128)S(1)} %shard_map.96), channel_id=1, source_target_pairs={{0,1},{1,0},{2,3},{3,2},{4,5},{5,4},{6,7},{7,6},{8,9},{9,8},{10,11... | collective-permute-start | bytes 1572872 | tf_op jit(solution)/shard_map/ppermute | solution.py:371
  19.5 12.6 %collective-permute-start.4 = (bf16[1024,256]{1,0:T(8,128)(2,1)S(1)}, bf16[1024,256]{1,0:T(8,128)(2,1)S(1)}, u32[]{:S(2)}, u32[]{:S(2)}) collective-permute-start(bf16[1024,256]{1,0:T(8,128)(2,1)S(1)} %collective-permute-done.refs_5_), channel_id=1, source_target_pairs={{0,4},{1,3},{4,8},{5,1},{8,12},{9,5},{12,14},{13,9},{14,10},{15,13... | collective-permute-start | bytes 1572872 | tf_op jit(solution)/shard_map/ppermute | solution.py:365
  24.2 15.2 %collective-permute-start.10 = (bf16[1024,256]{1,0:T(8,128)(2,1)S(1)}, bf16[1024,256]{1,0:T(8,128)(2,1)S(1)}, u32[]{:S(2)}, u32[]{:S(2)}) collective-permute-start(bf16[1024,256]{1,0:T(8,128)(2,1)S(1)} %collective-permute-done.6.refs_3_), channel_id=1, source_target_pairs={{0,16},{16,0},{1,17},{17,1},{2,18},{18,2},{3,19},{19,3},{4,20},{20... | collective-permute-start | bytes 1572872 | tf_op jit(solution)/shard_map/ppermute | solution.py:368
  26.2 13.6 %collective-permute-start.9 = (bf16[1024,256]{1,0:T(8,128)(2,1)S(1)}, bf16[1024,256]{1,0:T(8,128)(2,1)S(1)}, u32[]{:S(2)}, u32[]{:S(2)}) collective-permute-start(bf16[1024,256]{1,0:T(8,128)(2,1)S(1)} %collective-permute-done.6.refs_3_), channel_id=1, source_target_pairs={{0,2},{1,5},{4,0},{5,9},{8,4},{9,13},{12,8},{13,15},{14,12},{15,11... | collective-permute-start | bytes 1572872 | tf_op jit(solution)/shard_map/ppermute | solution.py:362
  32.1 9.3 %collective-permute-start.11 = (f32[512,256]{1,0:T(8,128)S(1)}, f32[512,256]{1,0:T(8,128)S(1)}, u32[]{:S(2)}, u32[]{:S(2)}) collective-permute-start(f32[512,256]{1,0:T(8,128)S(1)} %get-tuple-element.91), channel_id=1, source_target_pairs={{0,1},{1,0},{2,3},{3,2},{4,5},{5,4},{6,7},{7,6},{8,9},{9,8},{10,11... | collective-permute-start | bytes 1572872 | tf_op jit(solution)/shard_map/ppermute | solution.py:371
  32.2 11.7 %collective-permute-start.8 = (bf16[1024,256]{1,0:T(8,128)(2,1)S(1)}, bf16[1024,256]{1,0:T(8,128)(2,1)S(1)}, u32[]{:S(2)}, u32[]{:S(2)}) collective-permute-start(bf16[1024,256]{1,0:T(8,128)(2,1)S(1)} %collective-permute-done.4.refs_3_), channel_id=1, source_target_pairs={{0,4},{1,3},{4,8},{5,1},{8,12},{9,5},{12,14},{13,9},{14,10},{15,13... | collective-permute-start | bytes 1572872 | tf_op jit(solution)/shard_map/ppermute | solution.py:365
  39.4 10.7 %collective-permute-start.14 = (bf16[1024,256]{1,0:T(8,128)(2,1)S(1)}, bf16[1024,256]{1,0:T(8,128)(2,1)S(1)}, u32[]{:S(2)}, u32[]{:S(2)}) collective-permute-start(bf16[1024,256]{1,0:T(8,128)(2,1)S(1)} %collective-permute-done.10.refs_4_), channel_id=1, source_target_pairs={{0,2},{1,5},{4,0},{5,9},{8,4},{9,13},{12,8},{13,15},{14,12},{15,11... | collective-permute-start | bytes 1572872 | tf_op jit(solution)/shard_map/ppermute | solution.py:362
  39.8 13.3 %collective-permute-start.13 = (bf16[1024,256]{1,0:T(8,128)(2,1)S(1)}, bf16[1024,256]{1,0:T(8,128)(2,1)S(1)}, u32[]{:S(2)}, u32[]{:S(2)}) collective-permute-start(bf16[1024,256]{1,0:T(8,128)(2,1)S(1)} %collective-permute-done.4.refs_3_), channel_id=1, source_target_pairs={{0,16},{16,0},{1,17},{17,1},{2,18},{18,2},{3,19},{19,3},{4,20},{20... | collective-permute-start | bytes 1572872 | tf_op jit(solution)/shard_map/ppermute | solution.py:368
  43.8 10.5 %collective-permute-start.15 = (f32[512,256]{1,0:T(8,128)S(1)}, f32[512,256]{1,0:T(8,128)S(1)}, u32[]{:S(2)}, u32[]{:S(2)}) collective-permute-start(f32[512,256]{1,0:T(8,128)S(1)} %get-tuple-element.103), channel_id=1, source_target_pairs={{0,1},{1,0},{2,3},{3,2},{4,5},{5,4},{6,7},{7,6},{8,9},{9,8},{10,11... | collective-permute-start | bytes 1572872 | tf_op jit(solution)/shard_map/ppermute | solution.py:371
  43.9 14.4 %collective-permute-start.12 = (bf16[1024,256]{1,0:T(8,128)(2,1)S(1)}, bf16[1024,256]{1,0:T(8,128)(2,1)S(1)}, u32[]{:S(2)}, u32[]{:S(2)}) collective-permute-start(bf16[1024,256]{1,0:T(8,128)(2,1)S(1)} %collective-permute-done.8.refs_7_), channel_id=1, source_target_pairs={{0,4},{1,3},{4,8},{5,1},{8,12},{9,5},{12,14},{13,9},{14,10},{15,13... | collective-permute-start | bytes 1572872 | tf_op jit(solution)/shard_map/ppermute | solution.py:365
  45.6 12.8 %collective-permute-start.16 = (f32[512,256]{1,0:T(8,128)S(1)}, f32[512,256]{1,0:T(8,128)S(1)}, u32[]{:S(2)}, u32[]{:S(2)}) collective-permute-start(f32[512,256]{1,0:T(8,128)S(1)} %get-tuple-element.108), channel_id=1, source_target_pairs={{0,1},{1,0},{2,3},{3,2},{4,5},{5,4},{6,7},{7,6},{8,9},{9,8},{10,11... | collective-permute-start | bytes 1572872 | tf_op jit(solution)/shard_map/ppermute | solution.py:371
  50.1 10.5 %collective-permute-start.19 = (bf16[1024,256]{1,0:T(8,128)(2,1)S(1)}, bf16[1024,256]{1,0:T(8,128)(2,1)S(1)}, u32[]{:S(2)}, u32[]{:S(2)}) collective-permute-start(bf16[1024,256]{1,0:T(8,128)(2,1)S(1)} %collective-permute-done.14.refs_6_), channel_id=1, source_target_pairs={{0,2},{1,5},{4,0},{5,9},{8,4},{9,13},{12,8},{13,15},{14,12},{15,11... | collective-permute-start | bytes 1572872 | tf_op jit(solution)/shard_map/ppermute | solution.py:362
  53.1 12.3 %collective-permute-start.18 = (bf16[1024,256]{1,0:T(8,128)(2,1)S(1)}, bf16[1024,256]{1,0:T(8,128)(2,1)S(1)}, u32[]{:S(2)}, u32[]{:S(2)}) collective-permute-start(bf16[1024,256]{1,0:T(8,128)(2,1)S(1)} %collective-permute-done.refs_5_), channel_id=1, source_target_pairs={{0,16},{16,0},{1,17},{17,1},{2,18},{18,2},{3,19},{19,3},{4,20},{20... | collective-permute-start | bytes 1572872 | tf_op jit(solution)/shard_map/ppermute | solution.py:368
  58.3 9.2 %collective-permute-start.17 = (bf16[1024,256]{1,0:T(8,128)(2,1)S(1)}, bf16[1024,256]{1,0:T(8,128)(2,1)S(1)}, u32[]{:S(2)}, u32[]{:S(2)}) collective-permute-start(bf16[1024,256]{1,0:T(8,128)(2,1)S(1)} %collective-permute-done.13.refs_4_), channel_id=1, source_target_pairs={{0,4},{1,3},{4,8},{5,1},{8,12},{9,5},{12,14},{13,9},{14,10},{15,13... | collective-permute-start | bytes 1572872 | tf_op jit(solution)/shard_map/ppermute | solution.py:365
  60.1 8.8 %collective-permute-start.22 = (f32[2,512,256]{2,1,0:T(8,128)S(1)}, f32[2,512,256]{2,1,0:T(8,128)S(1)}, u32[]{:S(2)}, u32[]{:S(2)}) collective-permute-start(f32[2,512,256]{2,1,0:T(8,128)S(1)} %get-tuple-element.123), channel_id=1, source_target_pairs={{0,1},{1,0},{2,3},{3,2},{4,5},{5,4},{6,7},{7,6},{8,9},{9,8},{10,11... | collective-permute-start | bytes 3145736 | tf_op jit(solution)/shard_map/ppermute | solution.py:371
  60.6 7.0 %collective-permute-start.21 = (bf16[1024,256]{1,0:T(8,128)(2,1)S(1)}, bf16[1024,256]{1,0:T(8,128)(2,1)S(1)}, u32[]{:S(2)}, u32[]{:S(2)}) collective-permute-start(bf16[1024,256]{1,0:T(8,128)(2,1)S(1)} %collective-permute-done.19.refs_1_), channel_id=1, source_target_pairs={{0,1},{1,0},{2,3},{3,2},{4,5},{5,4},{6,7},{7,6},{8,9},{9,8},{10,11... | collective-permute-start | bytes 1572872 | tf_op jit(solution)/shard_map/ppermute | solution.py:371
  60.6 8.3 %collective-permute-start.20 = (bf16[1024,256]{1,0:T(8,128)(2,1)S(1)}, bf16[1024,256]{1,0:T(8,128)(2,1)S(1)}, u32[]{:S(2)}, u32[]{:S(2)}) collective-permute-start(bf16[1024,256]{1,0:T(8,128)(2,1)S(1)} %collective-permute-done.12.refs_0_), channel_id=1, source_target_pairs={{0,1},{1,0},{2,3},{3,2},{4,5},{5,4},{6,7},{7,6},{8,9},{9,8},{10,11... | collective-permute-start | bytes 1572872 | tf_op jit(solution)/shard_map/ppermute | solution.py:371
  65.4 5.3 %collective-permute-start.23 = (bf16[1024,256]{1,0:T(8,128)(2,1)S(1)}, bf16[1024,256]{1,0:T(8,128)(2,1)S(1)}, u32[]{:S(2)}, u32[]{:S(2)}) collective-permute-start(bf16[1024,256]{1,0:T(8,128)(2,1)S(1)} %collective-permute-done.18.refs_0_), channel_id=1, source_target_pairs={{0,1},{1,0},{2,3},{3,2},{4,5},{5,4},{6,7},{7,6},{8,9},{9,8},{10,11... | collective-permute-start | bytes 1572872 | tf_op jit(solution)/shard_map/ppermute | solution.py:371
  (9 other events, 76.7 us)

commit v14 on v13

--- a/solution.py
+++ b/solution.py
@@ -375,9 +375,8 @@
     own = own_half(out_proj)
     a = from_next(own)
     c, q = other_core(context), other_core(queries)
+    b = from_last(own)
     (p0,) = wave((0,), (), (), None, context, None, [out_proj])
-    own, p0 = wait((own, p0))
-    b = from_last(own)
 
     n1, p0 = wait((a, p0))
     x = over_x(n1)

time: 99.3 us -> 105 us (1.057)
  waiting for transfers between devices: 29.3 us -> 34.4 us
  blocking collectives: 23.5 us -> 25 us
    ppermute x4, waiting for transfers between devices: 15 us -> 7.89 us  [over_x(): return lax.ppermute(piece, 'groups', [(0, 1), (1, 0)])]
    ppermute x5, waiting for transfers between devices: 2.52 us -> 8.98 us  [from_last(): return lax.ppermute(piece, 'dp', ring(1))]
    ppermute x5, waiting for transfers between devices: 11.8 us -> 17.5 us  [from_next(): return lax.ppermute(piece, 'dp', ring(-1))]
    all_to_all x2, blocking collectives: 23.5 us -> 25 us  [spread(): lax.all_to_all(blocks, 'dp', 0, 0, axis_index_groups=same_core, tiled=True)]
  transfers between devices with their start and end apart: 26 -> 26, of which waited for: 10 -> 11; matrix products, arithmetic and copies ran while one was open for 0% -> 0% of each run, Pallas kernels for 13% -> 13%
where the time goes in v14:
time: 105 us
  waiting for transfers between devices  34.4 us (33%)
  blocking collectives  25 us (24%)
  starting transfers between devices  22.9 us (22%)
  Pallas kernels  18.2 us (17%)
  local copies, waits for them, and re-layouts  2.84 us (3%)
  between operations  1.5 us (1%)
    all_to_all x2, blocking collectives, spread(): lax.all_to_all(blocks, 'dp', 0, 0, axis_index_groups=same_core, tiled=True)  25 us
    ppermute x5, waiting for transfers between devices, from_next(): return lax.ppermute(piece, 'dp', ring(-1))  17.5 us
    pallas_call x5, Pallas kernels, wave(): pl.pallas_call(functools.partial(wave_kernel, full, part, arrived, whole,...  9.95 us
    ppermute x5, waiting for transfers between devices, from_last(): return lax.ppermute(piece, 'dp', ring(1))  8.98 us
    ppermute x4, waiting for transfers between devices, over_x(): return lax.ppermute(piece, 'groups', [(0, 1), (1, 0)])  7.89 us
    ppermute x5, starting transfers between devices, from_last(): return lax.ppermute(piece, 'dp', ring(1))  7.66 us
    ppermute x5, starting transfers between devices, from_next(): return lax.ppermute(piece, 'dp', ring(-1))  6.76 us
    ppermute x4, starting transfers between devices, over_x(): return lax.ppermute(piece, 'groups', [(0, 1), (1, 0)])  5.47 us
  transfers between devices with their start and end apart: 26, of which 11 were waited for; matrix products, arithmetic and copies ran while one was open for 0% of the time, Pallas kernels for 13%

profile of v14, /device:TPU:0, one launch (start us, length us, event | category | flops | bytes accessed | tf_op | source)
XLA Modules:
  0.0 104.9 jit_solution(2371433310990300019)
XLA Ops:
  2.4 2.6 %collective-permute-start.2 = (bf16[1024,256]{1,0:T(8,128)(2,1)S(1)}, bf16[1024,256]{1,0:T(8,128)(2,1)S(1)}, u32[]{:S(2)}, u32[]{:S(2)}) collective-permute-start(bf16[1024,256]{1,0:T(8,128)(2,1)S(1)} %shard_map.94), channel_id=1, source_target_pairs={{0,2},{1,5},{4,0},{5,9},{8,4},{9,13},{12,8},{13,15},{14,12},{15,11... | collective-permute-start | bytes 1572872 | tf_op jit(solution)/shard_map/ppermute | solution.py:362
  5.3 1.6 %collective-permute-start = (bf16[1024,256]{1,0:T(8,128)(2,1)S(1)}, bf16[1024,256]{1,0:T(8,128)(2,1)S(1)}, u32[]{:S(2)}, u32[]{:S(2)}) collective-permute-start(bf16[1024,256]{1,0:T(8,128)(2,1)S(1)} %shard_map.94), channel_id=1, source_target_pairs={{0,4},{1,3},{4,8},{5,1},{8,12},{9,5},{12,14},{13,9},{14,10},{15,13... | collective-permute-start | bytes 1572872 | tf_op jit(solution)/shard_map/ppermute | solution.py:365
  6.8 1.6 %copy-done.1 = bf16[512,2048]{1,0:T(8,128)(2,1)S(1)} copy-done((bf16[512,2048]{1,0:T(8,128)(2,1)S(1)}, bf16[512,2048]{1,0:T(8,128)(2,1)}, u32[]{:S(2)}) %copy-start.1) | copy-done | bytes 2097176
  9.3 6.9 %collective-permute-done.2.refs_3_ = bf16[1024,256]{1,0:T(8,128)(2,1)S(1)} collective-permute-done((bf16[1024,256]{1,0:T(8,128)(2,1)S(1)}, bf16[1024,256]{1,0:T(8,128)(2,1)S(1)}, u32[]{:S(2)}, u32[]{:S(2)}) %collective-permute-start.2) | collective-permute-done | bytes 524320 | tf_op jit(solution)/shard_map/ppermute | solution.py:362
  16.3 2.4 %collective-permute-start.6 = (bf16[1024,256]{1,0:T(8,128)(2,1)S(1)}, bf16[1024,256]{1,0:T(8,128)(2,1)S(1)}, u32[]{:S(2)}, u32[]{:S(2)}) collective-permute-start(bf16[1024,256]{1,0:T(8,128)(2,1)S(1)} %collective-permute-done.2.refs_3_), channel_id=1, source_target_pairs={{0,2},{1,5},{4,0},{5,9},{8,4},{9,13},{12,8},{13,15},{14,12},{15,11... | collective-permute-start | bytes 1572872 | tf_op jit(solution)/shard_map/ppermute | solution.py:362
  18.7 1.5 %collective-permute-start.5 = (bf16[1024,256]{1,0:T(8,128)(2,1)S(1)}, bf16[1024,256]{1,0:T(8,128)(2,1)S(1)}, u32[]{:S(2)}, u32[]{:S(2)}) collective-permute-start(bf16[1024,256]{1,0:T(8,128)(2,1)S(1)} %collective-permute-done.2.refs_3_), channel_id=1, source_target_pairs={{0,16},{16,0},{1,17},{17,1},{2,18},{18,2},{3,19},{19,3},{4,20},{20... | collective-permute-start | bytes 1572872 | tf_op jit(solution)/shard_map/ppermute | solution.py:368
  21.8 6.4 %collective-permute-done.6.refs_3_ = bf16[1024,256]{1,0:T(8,128)(2,1)S(1)} collective-permute-done((bf16[1024,256]{1,0:T(8,128)(2,1)S(1)}, bf16[1024,256]{1,0:T(8,128)(2,1)S(1)}, u32[]{:S(2)}, u32[]{:S(2)}) %collective-permute-start.6) | collective-permute-done | bytes 524320 | tf_op jit(solution)/shard_map/ppermute | solution.py:362
  28.1 2.8 %collective-permute-start.10 = (bf16[1024,256]{1,0:T(8,128)(2,1)S(1)}, bf16[1024,256]{1,0:T(8,128)(2,1)S(1)}, u32[]{:S(2)}, u32[]{:S(2)}) collective-permute-start(bf16[1024,256]{1,0:T(8,128)(2,1)S(1)} %collective-permute-done.6.refs_3_), channel_id=1, source_target_pairs={{0,16},{16,0},{1,17},{17,1},{2,18},{18,2},{3,19},{19,3},{4,20},{20... | collective-permute-start | bytes 1572872 | tf_op jit(solution)/shard_map/ppermute | solution.py:368
  30.9 1.3 %collective-permute-start.9 = (bf16[1024,256]{1,0:T(8,128)(2,1)S(1)}, bf16[1024,256]{1,0:T(8,128)(2,1)S(1)}, u32[]{:S(2)}, u32[]{:S(2)}) collective-permute-start(bf16[1024,256]{1,0:T(8,128)(2,1)S(1)} %collective-permute-done.6.refs_3_), channel_id=1, source_target_pairs={{0,2},{1,5},{4,0},{5,9},{8,4},{9,13},{12,8},{13,15},{14,12},{15,11... | collective-permute-start | bytes 1572872 | tf_op jit(solution)/shard_map/ppermute | solution.py:362
  32.3 1.3 %collective-permute-done.5.refs_4_ = bf16[1024,256]{1,0:T(8,128)(2,1)S(1)} collective-permute-done((bf16[1024,256]{1,0:T(8,128)(2,1)S(1)}, bf16[1024,256]{1,0:T(8,128)(2,1)S(1)}, u32[]{:S(2)}, u32[]{:S(2)}) %collective-permute-start.5) | collective-permute-done | bytes 524320 | tf_op jit(solution)/shard_map/ppermute | solution.py:368
  33.5 1.8 %shard_map.97 = (f32[1,512,256]{2,1,0:T(8,128)S(1)}, f32[512,256]{1,0:T(8,128)S(1)}, f32[2,512,256]{2,1,0:T(8,128)S(1)}, f32[512,128]{1,0:T(8,128)S(1)}) custom-call(bf16[512,2048]{1,0:T(8,128)(2,1)S(1)} %copy-done.2, bf16[512,2048]{1,0:T(8,128)(2,1)S(1)} %collective-permute-done.1.refs_0_.refs_1_, bf16[512,4096]{1,0:T(8,128)(2,1)S(1)} %copy-done, ...), custom_call_target="tpu_custom_call" | custom-call | flops 1000 | bytes 1000 | tf_op jit(solution)/shard_map/pallas_call | solution.py:155
  35.9 6.0 %collective-permute-done.10.refs_4_ = bf16[1024,256]{1,0:T(8,128)(2,1)S(1)} collective-permute-done((bf16[1024,256]{1,0:T(8,128)(2,1)S(1)}, bf16[1024,256]{1,0:T(8,128)(2,1)S(1)}, u32[]{:S(2)}, u32[]{:S(2)}) %collective-permute-start.10) | collective-permute-done | bytes 524320 | tf_op jit(solution)/shard_map/ppermute | solution.py:368
  42.4 1.3 %collective-permute-done.9.refs_5_ = bf16[1024,256]{1,0:T(8,128)(2,1)S(1)} collective-permute-done((bf16[1024,256]{1,0:T(8,128)(2,1)S(1)}, bf16[1024,256]{1,0:T(8,128)(2,1)S(1)}, u32[]{:S(2)}, u32[]{:S(2)}) %collective-permute-start.9) | collective-permute-done | bytes 524320 | tf_op jit(solution)/shard_map/ppermute | solution.py:362
  43.9 2.5 %shard_map.98 = (f32[2,512,256]{2,1,0:T(8,128)S(1)}, f32[512,256]{1,0:T(8,128)S(1)}, f32[512,256]{1,0:T(8,128)S(1)}, f32[1,512,256]{2,1,0:T(8,128)S(1)}, f32[512,128]{1,0:T(8,128)S(1)}) custom-call(bf16[512,2048]{1,0:T(8,128)(2,1)S(1)} %copy-done.2, bf16[512,2048]{1,0:T(8,128)(2,1)S(1)} %collective-permute-done.1.refs_0_.refs_1_, ...), custom_call_target="tpu_custom_call" | custom-call | flops 1000 | bytes 1000 | tf_op jit(solution)/shard_map/pallas_call | solution.py:155
  48.0 2.5 %collective-permute-start.12 = (bf16[1024,256]{1,0:T(8,128)(2,1)S(1)}, bf16[1024,256]{1,0:T(8,128)(2,1)S(1)}, u32[]{:S(2)}, u32[]{:S(2)}) collective-permute-start(bf16[1024,256]{1,0:T(8,128)(2,1)S(1)} %collective-permute-done.8.refs_7_), channel_id=1, source_target_pairs={{0,4},{1,3},{4,8},{5,1},{8,12},{9,5},{12,14},{13,9},{14,10},{15,13... | collective-permute-start | bytes 1572872 | tf_op jit(solution)/shard_map/ppermute | solution.py:365
  50.5 2.8 %collective-permute-done.14.refs_6_ = bf16[1024,256]{1,0:T(8,128)(2,1)S(1)} collective-permute-done((bf16[1024,256]{1,0:T(8,128)(2,1)S(1)}, bf16[1024,256]{1,0:T(8,128)(2,1)S(1)}, u32[]{:S(2)}, u32[]{:S(2)}) %collective-permute-start.14) | collective-permute-done | bytes 524320 | tf_op jit(solution)/shard_map/ppermute | solution.py:362
  54.9 3.9 %shard_map.99 = (f32[3,512,256]{2,1,0:T(8,128)S(1)}, f32[2,512,256]{2,1,0:T(8,128)S(1)}, f32[1,512,256]{2,1,0:T(8,128)S(1)}, f32[1,512,256]{2,1,0:T(8,128)S(1)}, f32[512,128]{1,0:T(8,128)S(1)}) custom-call(bf16[512,2048]{1,0:T(8,128)(2,1)S(1)} %copy-done.2, bf16[512,2048]{1,0:T(8,128)(2,1)S(1)} %collective-permute-done.1.refs_0_.refs_1_, ...), custom_call_target="tpu_custom_call" | custom-call | flops 1000 | bytes 1000 | tf_op jit(solution)/shard_map/pallas_call | solution.py:155
  58.8 3.9 %collective-permute-done.12.refs_0_ = bf16[1024,256]{1,0:T(8,128)(2,1)S(1)} collective-permute-done((bf16[1024,256]{1,0:T(8,128)(2,1)S(1)}, bf16[1024,256]{1,0:T(8,128)(2,1)S(1)}, u32[]{:S(2)}, u32[]{:S(2)}) %collective-permute-start.12) | collective-permute-done | bytes 524320 | tf_op jit(solution)/shard_map/ppermute | solution.py:365
  62.7 2.5 %collective-permute-start.17 = (bf16[1024,256]{1,0:T(8,128)(2,1)S(1)}, bf16[1024,256]{1,0:T(8,128)(2,1)S(1)}, u32[]{:S(2)}, u32[]{:S(2)}) collective-permute-start(bf16[1024,256]{1,0:T(8,128)(2,1)S(1)} %collective-permute-done.13.refs_4_), channel_id=1, source_target_pairs={{0,4},{1,3},{4,8},{5,1},{8,12},{9,5},{12,14},{13,9},{14,10},{15,13... | collective-permute-start | bytes 1572872 | tf_op jit(solution)/shard_map/ppermute | solution.py:365
  67.9 4.0 %collective-permute-done.17.refs_0_ = bf16[1024,256]{1,0:T(8,128)(2,1)S(1)} collective-permute-done((bf16[1024,256]{1,0:T(8,128)(2,1)S(1)}, bf16[1024,256]{1,0:T(8,128)(2,1)S(1)}, u32[]{:S(2)}, u32[]{:S(2)}) %collective-permute-start.17) | collective-permute-done | bytes 524320 | tf_op jit(solution)/shard_map/ppermute | solution.py:365
  73.2 1.8 %shard_map.102 = (f32[4,512,256]{2,1,0:T(8,128)S(1)}, f32[512,128]{1,0:T(8,128)S(1)}) custom-call(bf16[512,2048]{1,0:T(8,128)(2,1)S(1)} %copy-done.2, bf16[512,4096]{1,0:T(8,128)(2,1)S(1)} %copy-done, f32[512,128]{1,0:T(8,128)S(1)} %get-tuple-element.116.before, bf16[1024,256]{1,0:T(8,128)(2,1)S(1)} %collective-permute-done.17.refs_0_, ...), custom_call_target="tpu_custom_call" | custom-call | flops 1000 | bytes 1000 | tf_op jit(solution)/shard_map/pallas_call | solution.py:191
  75.1 2.9 %shard_map.103 = (f32[1,4096]{1,0:T(1,128)}, bf16[8,48,128]{2,1,0:T(8,128)(2,1)S(1)}) custom-call(bf16[512,2048]{1,0:T(8,128)(2,1)S(1)} %copy-done.2, bf16[512,4096]{1,0:T(8,128)(2,1)S(1)} %copy-done, f32[512,128]{1,0:T(8,128)S(1)} %get-tuple-element.120.before, f32[1,4096]{1,0:T(1,128)S(1)} %bitcast.3, f32[1,128]{1,0:T(1,128)S(1)} %fusion.flags, ...), custom_call_target="tpu_custom_call" | custom-call | flops 1000 | bytes 1000 | tf_op jit(solution)/shard_map/pallas_call | solution.py:245
  78.0 15.1 %all_to_all.10.got = bf16[8,48,128]{2,1,0:T(8,128)(2,1)S(1)} all-to-all(bf16[8,48,128]{2,1,0:T(8,128)(2,1)S(1)} %get-tuple-element.131), channel_id=1, replica_groups={{0,2,4,6,8,10,12,14},{1,3,5,7,9,11,13,15},{16,18,20,22,24,26,28,30},{17..., dimensions={0} | all-to-all | bytes 196608 | tf_op jit(solution)/shard_map/all_to_all | solution.py:467
  94.2 10.0 %all_to_all.11.got = f32[8,40,128]{2,1,0:T(8,128)S(1)} all-to-all(f32[8,40,128]{2,1,0:T(8,128)S(1)} %shard_map.104), channel_id=1, replica_groups={{0,2,4,6,8,10,12,14},{1,3,5,7,9,11,13,15},{16,18,20,22,24,26,28,30},{17..., dimensions={0} | all-to-all | bytes 327680 | tf_op jit(solution)/shard_map/all_to_all | solution.py:467
  (58 shorter events, 14.1 us)
Async XLA Ops:
  0.6 19.5 %collective-permute-start.1 = (bf16[512,2048]{1,0:T(8,128)(2,1)}, bf16[512,2048]{1,0:T(8,128)(2,1)S(1)}, u32[]{:S(2)}, u32[]{:S(2)}) collective-permute-start(bf16[512,2048]{1,0:T(8,128)(2,1)} %context.7), channel_id=1, source_target_pairs={{0,1},{1,0},{2,3},{3,2},{4,5},{5,4},{6,7},{7,6},{8,9},{9,8},{10,11... | collective-permute-start | bytes 6291464 | tf_op jit(solution)/shard_map/ppermute | solution.py:371
  2.4 13.8 %collective-permute-start.2 = (bf16[1024,256]{1,0:T(8,128)(2,1)S(1)}, bf16[1024,256]{1,0:T(8,128)(2,1)S(1)}, u32[]{:S(2)}, u32[]{:S(2)}) collective-permute-start(bf16[1024,256]{1,0:T(8,128)(2,1)S(1)} %shard_map.94), channel_id=1, source_target_pairs={{0,2},{1,5},{4,0},{5,9},{8,4},{9,13},{12,8},{13,15},{14,12},{15,11... | collective-permute-start | bytes 1572872 | tf_op jit(solution)/shard_map/ppermute | solution.py:362
  5.0 16.1 %collective-permute-start.3 = (bf16[112,4096]{1,0:T(8,128)(2,1)}, bf16[112,4096]{1,0:T(8,128)(2,1)S(1)}, u32[]{:S(2)}, u32[]{:S(2)}) collective-permute-start(bf16[112,4096]{1,0:T(8,128)(2,1)} %queries.1), channel_id=1, source_target_pairs={{0,1},{1,0},{2,3},{3,2},{4,5},{5,4},{6,7},{7,6},{8,9},{9,8},{10,11... | collective-permute-start | bytes 2752520 | tf_op jit(solution)/shard_map/ppermute | solution.py:371
  5.3 15.8 %collective-permute-start = (bf16[1024,256]{1,0:T(8,128)(2,1)S(1)}, bf16[1024,256]{1,0:T(8,128)(2,1)S(1)}, u32[]{:S(2)}, u32[]{:S(2)}) collective-permute-start(bf16[1024,256]{1,0:T(8,128)(2,1)S(1)} %shard_map.94), channel_id=1, source_target_pairs={{0,4},{1,3},{4,8},{5,1},{8,12},{9,5},{12,14},{13,9},{14,10},{15,13... | collective-permute-start | bytes 1572872 | tf_op jit(solution)/shard_map/ppermute | solution.py:365
  16.3 11.9 %collective-permute-start.6 = (bf16[1024,256]{1,0:T(8,128)(2,1)S(1)}, bf16[1024,256]{1,0:T(8,128)(2,1)S(1)}, u32[]{:S(2)}, u32[]{:S(2)}) collective-permute-start(bf16[1024,256]{1,0:T(8,128)(2,1)S(1)} %collective-permute-done.2.refs_3_), channel_id=1, source_target_pairs={{0,2},{1,5},{4,0},{5,9},{8,4},{9,13},{12,8},{13,15},{14,12},{15,11... | collective-permute-start | bytes 1572872 | tf_op jit(solution)/shard_map/ppermute | solution.py:362
  18.7 14.9 %collective-permute-start.5 = (bf16[1024,256]{1,0:T(8,128)(2,1)S(1)}, bf16[1024,256]{1,0:T(8,128)(2,1)S(1)}, u32[]{:S(2)}, u32[]{:S(2)}) collective-permute-start(bf16[1024,256]{1,0:T(8,128)(2,1)S(1)} %collective-permute-done.2.refs_3_), channel_id=1, source_target_pairs={{0,16},{16,0},{1,17},{17,1},{2,18},{18,2},{3,19},{19,3},{4,20},{20... | collective-permute-start | bytes 1572872 | tf_op jit(solution)/shard_map/ppermute | solution.py:368
  21.1 12.5 %collective-permute-start.7 = (f32[512,256]{1,0:T(8,128)S(1)}, f32[512,256]{1,0:T(8,128)S(1)}, u32[]{:S(2)}, u32[]{:S(2)}) collective-permute-start(f32[512,256]{1,0:T(8,128)S(1)} %shard_map.96), channel_id=1, source_target_pairs={{0,1},{1,0},{2,3},{3,2},{4,5},{5,4},{6,7},{7,6},{8,9},{9,8},{10,11... | collective-permute-start | bytes 1572872 | tf_op jit(solution)/shard_map/ppermute | solution.py:371
  21.1 14.2 %collective-permute-start.4 = (bf16[1024,256]{1,0:T(8,128)(2,1)S(1)}, bf16[1024,256]{1,0:T(8,128)(2,1)S(1)}, u32[]{:S(2)}, u32[]{:S(2)}) collective-permute-start(bf16[1024,256]{1,0:T(8,128)(2,1)S(1)} %collective-permute-done.refs_5_), channel_id=1, source_target_pairs={{0,4},{1,3},{4,8},{5,1},{8,12},{9,5},{12,14},{13,9},{14,10},{15,13... | collective-permute-start | bytes 1572872 | tf_op jit(solution)/shard_map/ppermute | solution.py:365
  28.1 13.8 %collective-permute-start.10 = (bf16[1024,256]{1,0:T(8,128)(2,1)S(1)}, bf16[1024,256]{1,0:T(8,128)(2,1)S(1)}, u32[]{:S(2)}, u32[]{:S(2)}) collective-permute-start(bf16[1024,256]{1,0:T(8,128)(2,1)S(1)} %collective-permute-done.6.refs_3_), channel_id=1, source_target_pairs={{0,16},{16,0},{1,17},{17,1},{2,18},{18,2},{3,19},{19,3},{4,20},{20... | collective-permute-start | bytes 1572872 | tf_op jit(solution)/shard_map/ppermute | solution.py:368
  30.9 12.7 %collective-permute-start.9 = (bf16[1024,256]{1,0:T(8,128)(2,1)S(1)}, bf16[1024,256]{1,0:T(8,128)(2,1)S(1)}, u32[]{:S(2)}, u32[]{:S(2)}) collective-permute-start(bf16[1024,256]{1,0:T(8,128)(2,1)S(1)} %collective-permute-done.6.refs_3_), channel_id=1, source_target_pairs={{0,2},{1,5},{4,0},{5,9},{8,4},{9,13},{12,8},{13,15},{14,12},{15,11... | collective-permute-start | bytes 1572872 | tf_op jit(solution)/shard_map/ppermute | solution.py:362
  35.3 8.6 %collective-permute-start.11 = (f32[512,256]{1,0:T(8,128)S(1)}, f32[512,256]{1,0:T(8,128)S(1)}, u32[]{:S(2)}, u32[]{:S(2)}) collective-permute-start(f32[512,256]{1,0:T(8,128)S(1)} %get-tuple-element.87), channel_id=1, source_target_pairs={{0,1},{1,0},{2,3},{3,2},{4,5},{5,4},{6,7},{7,6},{8,9},{9,8},{10,11... | collective-permute-start | bytes 1572872 | tf_op jit(solution)/shard_map/ppermute | solution.py:371
  35.4 12.0 %collective-permute-start.8 = (bf16[1024,256]{1,0:T(8,128)(2,1)S(1)}, bf16[1024,256]{1,0:T(8,128)(2,1)S(1)}, u32[]{:S(2)}, u32[]{:S(2)}) collective-permute-start(bf16[1024,256]{1,0:T(8,128)(2,1)S(1)} %collective-permute-done.4.refs_3_), channel_id=1, source_target_pairs={{0,4},{1,3},{4,8},{5,1},{8,12},{9,5},{12,14},{13,9},{14,10},{15,13... | collective-permute-start | bytes 1572872 | tf_op jit(solution)/shard_map/ppermute | solution.py:365
  41.9 11.4 %collective-permute-start.14 = (bf16[1024,256]{1,0:T(8,128)(2,1)S(1)}, bf16[1024,256]{1,0:T(8,128)(2,1)S(1)}, u32[]{:S(2)}, u32[]{:S(2)}) collective-permute-start(bf16[1024,256]{1,0:T(8,128)(2,1)S(1)} %collective-permute-done.10.refs_4_), channel_id=1, source_target_pairs={{0,2},{1,5},{4,0},{5,9},{8,4},{9,13},{12,8},{13,15},{14,12},{15,11... | collective-permute-start | bytes 1572872 | tf_op jit(solution)/shard_map/ppermute | solution.py:362
  43.7 10.2 %collective-permute-start.13 = (bf16[1024,256]{1,0:T(8,128)(2,1)S(1)}, bf16[1024,256]{1,0:T(8,128)(2,1)S(1)}, u32[]{:S(2)}, u32[]{:S(2)}) collective-permute-start(bf16[1024,256]{1,0:T(8,128)(2,1)S(1)} %collective-permute-done.4.refs_3_), channel_id=1, source_target_pairs={{0,16},{16,0},{1,17},{17,1},{2,18},{18,2},{3,19},{19,3},{4,20},{20... | collective-permute-start | bytes 1572872 | tf_op jit(solution)/shard_map/ppermute | solution.py:368
  47.4 7.5 %collective-permute-start.15 = (f32[512,256]{1,0:T(8,128)S(1)}, f32[512,256]{1,0:T(8,128)S(1)}, u32[]{:S(2)}, u32[]{:S(2)}) collective-permute-start(f32[512,256]{1,0:T(8,128)S(1)} %get-tuple-element.99), channel_id=1, source_target_pairs={{0,1},{1,0},{2,3},{3,2},{4,5},{5,4},{6,7},{7,6},{8,9},{9,8},{10,11... | collective-permute-start | bytes 1572872 | tf_op jit(solution)/shard_map/ppermute | solution.py:371
  48.0 14.7 %collective-permute-start.12 = (bf16[1024,256]{1,0:T(8,128)(2,1)S(1)}, bf16[1024,256]{1,0:T(8,128)(2,1)S(1)}, u32[]{:S(2)}, u32[]{:S(2)}) collective-permute-start(bf16[1024,256]{1,0:T(8,128)(2,1)S(1)} %collective-permute-done.8.refs_7_), channel_id=1, source_target_pairs={{0,4},{1,3},{4,8},{5,1},{8,12},{9,5},{12,14},{13,9},{14,10},{15,13... | collective-permute-start | bytes 1572872 | tf_op jit(solution)/shard_map/ppermute | solution.py:365
  50.5 12.2 %collective-permute-start.16 = (f32[512,256]{1,0:T(8,128)S(1)}, f32[512,256]{1,0:T(8,128)S(1)}, u32[]{:S(2)}, u32[]{:S(2)}) collective-permute-start(f32[512,256]{1,0:T(8,128)S(1)} %get-tuple-element.104), channel_id=1, source_target_pairs={{0,1},{1,0},{2,3},{3,2},{4,5},{5,4},{6,7},{7,6},{8,9},{9,8},{10,11... | collective-permute-start | bytes 1572872 | tf_op jit(solution)/shard_map/ppermute | solution.py:371
  53.3 12.1 %collective-permute-start.19 = (bf16[1024,256]{1,0:T(8,128)(2,1)S(1)}, bf16[1024,256]{1,0:T(8,128)(2,1)S(1)}, u32[]{:S(2)}, u32[]{:S(2)}) collective-permute-start(bf16[1024,256]{1,0:T(8,128)(2,1)S(1)} %collective-permute-done.14.refs_6_), channel_id=1, source_target_pairs={{0,2},{1,5},{4,0},{5,9},{8,4},{9,13},{12,8},{13,15},{14,12},{15,11... | collective-permute-start | bytes 1572872 | tf_op jit(solution)/shard_map/ppermute | solution.py:362
  53.9 12.9 %collective-permute-start.18 = (bf16[1024,256]{1,0:T(8,128)(2,1)S(1)}, bf16[1024,256]{1,0:T(8,128)(2,1)S(1)}, u32[]{:S(2)}, u32[]{:S(2)}) collective-permute-start(bf16[1024,256]{1,0:T(8,128)(2,1)S(1)} %collective-permute-done.refs_5_), channel_id=1, source_target_pairs={{0,16},{16,0},{1,17},{17,1},{2,18},{18,2},{3,19},{19,3},{4,20},{20... | collective-permute-start | bytes 1572872 | tf_op jit(solution)/shard_map/ppermute | solution.py:368
  62.7 9.2 %collective-permute-start.17 = (bf16[1024,256]{1,0:T(8,128)(2,1)S(1)}, bf16[1024,256]{1,0:T(8,128)(2,1)S(1)}, u32[]{:S(2)}, u32[]{:S(2)}) collective-permute-start(bf16[1024,256]{1,0:T(8,128)(2,1)S(1)} %collective-permute-done.13.refs_4_), channel_id=1, source_target_pairs={{0,4},{1,3},{4,8},{5,1},{8,12},{9,5},{12,14},{13,9},{14,10},{15,13... | collective-permute-start | bytes 1572872 | tf_op jit(solution)/shard_map/ppermute | solution.py:365
  65.2 8.0 %collective-permute-start.22 = (f32[2,512,256]{2,1,0:T(8,128)S(1)}, f32[2,512,256]{2,1,0:T(8,128)S(1)}, u32[]{:S(2)}, u32[]{:S(2)}) collective-permute-start(f32[2,512,256]{2,1,0:T(8,128)S(1)} %get-tuple-element.119), channel_id=1, source_target_pairs={{0,1},{1,0},{2,3},{3,2},{4,5},{5,4},{6,7},{7,6},{8,9},{9,8},{10,11... | collective-permute-start | bytes 3145736 | tf_op jit(solution)/shard_map/ppermute | solution.py:371
  65.4 6.5 %collective-permute-start.21 = (bf16[1024,256]{1,0:T(8,128)(2,1)S(1)}, bf16[1024,256]{1,0:T(8,128)(2,1)S(1)}, u32[]{:S(2)}, u32[]{:S(2)}) collective-permute-start(bf16[1024,256]{1,0:T(8,128)(2,1)S(1)} %collective-permute-done.19.refs_1_), channel_id=1, source_target_pairs={{0,1},{1,0},{2,3},{3,2},{4,5},{5,4},{6,7},{7,6},{8,9},{9,8},{10,11... | collective-permute-start | bytes 1572872 | tf_op jit(solution)/shard_map/ppermute | solution.py:371
  65.7 7.5 %collective-permute-start.20 = (bf16[1024,256]{1,0:T(8,128)(2,1)S(1)}, bf16[1024,256]{1,0:T(8,128)(2,1)S(1)}, u32[]{:S(2)}, u32[]{:S(2)}) collective-permute-start(bf16[1024,256]{1,0:T(8,128)(2,1)S(1)} %collective-permute-done.12.refs_0_), channel_id=1, source_target_pairs={{0,1},{1,0},{2,3},{3,2},{4,5},{5,4},{6,7},{7,6},{8,9},{9,8},{10,11... | collective-permute-start | bytes 1572872 | tf_op jit(solution)/shard_map/ppermute | solution.py:371
  66.8 8.2 %collective-permute-start.23 = (bf16[1024,256]{1,0:T(8,128)(2,1)S(1)}, bf16[1024,256]{1,0:T(8,128)(2,1)S(1)}, u32[]{:S(2)}, u32[]{:S(2)}) collective-permute-start(bf16[1024,256]{1,0:T(8,128)(2,1)S(1)} %collective-permute-done.18.refs_0_), channel_id=1, source_target_pairs={{0,1},{1,0},{2,3},{3,2},{4,5},{5,4},{6,7},{7,6},{8,9},{9,8},{10,11... | collective-permute-start | bytes 1572872 | tf_op jit(solution)/shard_map/ppermute | solution.py:371
  (9 other events, 84.1 us)

commit v15 on v13

--- a/solution.py
+++ b/solution.py
@@ -396,11 +396,13 @@
     h1, t1, f0, sq1 = wave(
         (1,), (), ((0, True), (0, False)), context, context2, residual, [n1, xn1], [p0, r0], None
     )
-    l2, n2, t1, sq1 = wait((b, n2, t1, sq1))
+    l2, n2, t1, sq1, own_pattern, lengths = wait((b, n2, t1, sq1, pattern, lengths))
     b = from_last(l2)
     r1 = other_core(t1)
-
-    xn2, l2 = wait((x, l2))
+    flags = jnp.pad(own_pattern.astype(jnp.float32), ((0, 0), (0, LANES - 1 - pattern.shape[1])))
+    flags = jnp.concatenate([flags, lengths.astype(jnp.float32)[:, None]], axis=1)
+
+    xn2, l2, flags = wait((x, l2, flags))
     x = over_x(l2)
     a2 = from_next(xn2)
     n3, xn2 = wait((a, xn2))
@@ -413,11 +415,11 @@
     a = from_next(n3x)
     xl2, l1, n3x = wait((x, l1, n3x))
     x = over_x(l1)
+    l4, xl2, n3x, r2p = wait((b, xl2, n3x, r2p))
+    b = from_last(xl2)
     h3, t3a, t3p, f2, sq3 = wave(
         (-2, 3), (-3,), ((2, False),), context, context2, residual, [l2, xl2, n3, n3x, l3], [r2], sq2, stacked=True
     )
-    l4, xl2, t3a, t3p, sq3, r2p = wait((b, xl2, t3a, t3p, sq3, r2p))
-    b = from_last(xl2)
     r3a, r3p = other_core(t3a), other_core(t3p)
     l4s = other_core(l4)
 
@@ -456,8 +458,6 @@
         (7, 2, 3, False),
         (7, 3, 4, False),
     )
-    flags = jnp.pad(pattern.astype(jnp.float32), ((0, 0), (0, LANES - 1 - pattern.shape[1])))
-    flags = jnp.concatenate([flags, lengths.astype(jnp.float32)[:, None]], axis=1)
     embedded, payload = finish(
         items, sources, context, residual, sq6, norm_gain.reshape(1, -1), flags, [xl1s, l3xs], hidden, size
     )

time: 99.3 us -> 99.9 us (level)
  waiting for transfers between devices: 29.3 us -> 27.1 us
  blocking collectives: 23.5 us -> 25 us
  starting transfers between devices: 23.7 us -> 24.9 us
    ppermute x4, waiting for transfers between devices: 15 us -> 8.92 us  [over_x(): return lax.ppermute(piece, 'groups', [(0, 1), (1, 0)])]
    ppermute x5, waiting for transfers between devices: 11.8 us -> 14.9 us  [from_next(): return lax.ppermute(piece, 'dp', ring(-1))]
    all_to_all x2, blocking collectives: 23.5 us -> 25 us  [spread(): lax.all_to_all(blocks, 'dp', 0, 0, axis_index_groups=same_core, tiled=True)]
where the time goes in v15:
time: 99.9 us; the launch traced here: 99.6 us
  waiting for transfers between devices  27.1 us (27%)
  blocking collectives  25 us (25%)
  starting transfers between devices  24.9 us (25%)
  Pallas kernels  18.2 us (18%)
  local copies, waits for them, and re-layouts  2.84 us (3%)
  between operations  1.49 us (1%)
    all_to_all x2, blocking collectives, spread(): lax.all_to_all(blocks, 'dp', 0, 0, axis_index_groups=same_core, tiled=True)  25 us
    ppermute x5, waiting for transfers between devices, from_next(): return lax.ppermute(piece, 'dp', ring(-1))  14.9 us
    pallas_call x5, Pallas kernels, wave(): pl.pallas_call(functools.partial(wave_kernel, full, part, arrived, whole,...  9.96 us
    ppermute x4, waiting for transfers between devices, over_x(): return lax.ppermute(piece, 'groups', [(0, 1), (1, 0)])  8.92 us
    ppermute x5, starting transfers between devices, from_last(): return lax.ppermute(piece, 'dp', ring(1))  8.5 us
    ppermute x5, starting transfers between devices, from_next(): return lax.ppermute(piece, 'dp', ring(-1))  7.38 us
    ppermute x4, starting transfers between devices, over_x(): return lax.ppermute(piece, 'groups', [(0, 1), (1, 0)])  6.37 us
    pallas_call x3, Pallas kernels, late(): pl.pallas_call(functools.partial(late_kernel, items, len(pieces)), out_sh...  3.38 us
  transfers between devices with their start and end apart: 26, of which 10 were waited for; matrix products, arithmetic and copies ran while one was open for 0% of the time, Pallas kernels for 13%

profile of v15, /device:TPU:0, one launch (start us, length us, event | category | flops | bytes accessed | tf_op | source)
XLA Modules:
  0.0 99.6 jit_solution(3928220113737189133)
XLA Ops:
  2.4 2.6 %collective-permute-start.2 = (bf16[1024,256]{1,0:T(8,128)(2,1)S(1)}, bf16[1024,256]{1,0:T(8,128)(2,1)S(1)}, u32[]{:S(2)}, u32[]{:S(2)}) collective-permute-start(bf16[1024,256]{1,0:T(8,128)(2,1)S(1)} %shard_map.94), channel_id=1, source_target_pairs={{0,2},{1,5},{4,0},{5,9},{8,4},{9,13},{12,8},{13,15},{14,12},{15,11... | collective-permute-start | bytes 1572872 | tf_op jit(solution)/shard_map/ppermute | solution.py:362
  5.3 1.6 %copy-done.1 = bf16[512,2048]{1,0:T(8,128)(2,1)S(1)} copy-done((bf16[512,2048]{1,0:T(8,128)(2,1)S(1)}, bf16[512,2048]{1,0:T(8,128)(2,1)}, u32[]{:S(2)}) %copy-start.1) | copy-done | bytes 2097176
  7.8 1.6 %collective-permute-start = (bf16[1024,256]{1,0:T(8,128)(2,1)S(1)}, bf16[1024,256]{1,0:T(8,128)(2,1)S(1)}, u32[]{:S(2)}, u32[]{:S(2)}) collective-permute-start(bf16[1024,256]{1,0:T(8,128)(2,1)S(1)} %shard_map.94), channel_id=1, source_target_pairs={{0,4},{1,3},{4,8},{5,1},{8,12},{9,5},{12,14},{13,9},{14,10},{15,13... | collective-permute-start | bytes 1572872 | tf_op jit(solution)/shard_map/ppermute | solution.py:365
  9.4 4.3 %collective-permute-done.2.refs_3_ = bf16[1024,256]{1,0:T(8,128)(2,1)S(1)} collective-permute-done((bf16[1024,256]{1,0:T(8,128)(2,1)S(1)}, bf16[1024,256]{1,0:T(8,128)(2,1)S(1)}, u32[]{:S(2)}, u32[]{:S(2)}) %collective-permute-start.2) | collective-permute-done | bytes 524320 | tf_op jit(solution)/shard_map/ppermute | solution.py:362
  13.7 2.3 %collective-permute-start.6 = (bf16[1024,256]{1,0:T(8,128)(2,1)S(1)}, bf16[1024,256]{1,0:T(8,128)(2,1)S(1)}, u32[]{:S(2)}, u32[]{:S(2)}) collective-permute-start(bf16[1024,256]{1,0:T(8,128)(2,1)S(1)} %collective-permute-done.2.refs_3_), channel_id=1, source_target_pairs={{0,2},{1,5},{4,0},{5,9},{8,4},{9,13},{12,8},{13,15},{14,12},{15,11... | collective-permute-start | bytes 1572872 | tf_op jit(solution)/shard_map/ppermute | solution.py:362
  19.5 2.0 %collective-permute-start.4 = (bf16[1024,256]{1,0:T(8,128)(2,1)S(1)}, bf16[1024,256]{1,0:T(8,128)(2,1)S(1)}, u32[]{:S(2)}, u32[]{:S(2)}) collective-permute-start(bf16[1024,256]{1,0:T(8,128)(2,1)S(1)} %collective-permute-done.refs_5_), channel_id=1, source_target_pairs={{0,4},{1,3},{4,8},{5,1},{8,12},{9,5},{12,14},{13,9},{14,10},{15,13... | collective-permute-start | bytes 1572872 | tf_op jit(solution)/shard_map/ppermute | solution.py:365
  21.5 2.8 %collective-permute-done.6.refs_3_ = bf16[1024,256]{1,0:T(8,128)(2,1)S(1)} collective-permute-done((bf16[1024,256]{1,0:T(8,128)(2,1)S(1)}, bf16[1024,256]{1,0:T(8,128)(2,1)S(1)}, u32[]{:S(2)}, u32[]{:S(2)}) %collective-permute-start.6) | collective-permute-done | bytes 524320 | tf_op jit(solution)/shard_map/ppermute | solution.py:362
  24.2 2.0 %collective-permute-start.10 = (bf16[1024,256]{1,0:T(8,128)(2,1)S(1)}, bf16[1024,256]{1,0:T(8,128)(2,1)S(1)}, u32[]{:S(2)}, u32[]{:S(2)}) collective-permute-start(bf16[1024,256]{1,0:T(8,128)(2,1)S(1)} %collective-permute-done.6.refs_3_), channel_id=1, source_target_pairs={{0,16},{16,0},{1,17},{17,1},{2,18},{18,2},{3,19},{19,3},{4,20},{20... | collective-permute-start | bytes 1572872 | tf_op jit(solution)/shard_map/ppermute | solution.py:368
  26.9 1.8 %collective-permute-start.9 = (bf16[1024,256]{1,0:T(8,128)(2,1)S(1)}, bf16[1024,256]{1,0:T(8,128)(2,1)S(1)}, u32[]{:S(2)}, u32[]{:S(2)}) collective-permute-start(bf16[1024,256]{1,0:T(8,128)(2,1)S(1)} %collective-permute-done.6.refs_3_), channel_id=1, source_target_pairs={{0,2},{1,5},{4,0},{5,9},{8,4},{9,13},{12,8},{13,15},{14,12},{15,11... | collective-permute-start | bytes 1572872 | tf_op jit(solution)/shard_map/ppermute | solution.py:362
  28.6 1.6 %collective-permute-done.5.refs_4_ = bf16[1024,256]{1,0:T(8,128)(2,1)S(1)} collective-permute-done((bf16[1024,256]{1,0:T(8,128)(2,1)S(1)}, bf16[1024,256]{1,0:T(8,128)(2,1)S(1)}, u32[]{:S(2)}, u32[]{:S(2)}) %collective-permute-start.5) | collective-permute-done | bytes 524320 | tf_op jit(solution)/shard_map/ppermute | solution.py:368
  30.3 1.8 %shard_map.97 = (f32[1,512,256]{2,1,0:T(8,128)S(1)}, f32[512,256]{1,0:T(8,128)S(1)}, f32[2,512,256]{2,1,0:T(8,128)S(1)}, f32[512,128]{1,0:T(8,128)S(1)}) custom-call(bf16[512,2048]{1,0:T(8,128)(2,1)S(1)} %copy-done.2, bf16[512,2048]{1,0:T(8,128)(2,1)S(1)} %collective-permute-done.1.refs_0_.refs_1_, bf16[512,4096]{1,0:T(8,128)(2,1)S(1)} %copy-done, ...), custom_call_target="tpu_custom_call" | custom-call | flops 1000 | bytes 1000 | tf_op jit(solution)/shard_map/pallas_call | solution.py:155
  33.3 6.1 %collective-permute-done.10.refs_4_ = bf16[1024,256]{1,0:T(8,128)(2,1)S(1)} collective-permute-done((bf16[1024,256]{1,0:T(8,128)(2,1)S(1)}, bf16[1024,256]{1,0:T(8,128)(2,1)S(1)}, u32[]{:S(2)}, u32[]{:S(2)}) %collective-permute-start.10) | collective-permute-done | bytes 524320 | tf_op jit(solution)/shard_map/ppermute | solution.py:368
  39.8 1.5 %collective-permute-start.13 = (bf16[1024,256]{1,0:T(8,128)(2,1)S(1)}, bf16[1024,256]{1,0:T(8,128)(2,1)S(1)}, u32[]{:S(2)}, u32[]{:S(2)}) collective-permute-start(bf16[1024,256]{1,0:T(8,128)(2,1)S(1)} %collective-permute-done.4.refs_3_), channel_id=1, source_target_pairs={{0,16},{16,0},{1,17},{17,1},{2,18},{18,2},{3,19},{19,3},{4,20},{20... | collective-permute-start | bytes 1572872 | tf_op jit(solution)/shard_map/ppermute | solution.py:368
  41.3 2.5 %shard_map.98 = (f32[2,512,256]{2,1,0:T(8,128)S(1)}, f32[512,256]{1,0:T(8,128)S(1)}, f32[512,256]{1,0:T(8,128)S(1)}, f32[1,512,256]{2,1,0:T(8,128)S(1)}, f32[512,128]{1,0:T(8,128)S(1)}) custom-call(bf16[512,2048]{1,0:T(8,128)(2,1)S(1)} %copy-done.2, bf16[512,2048]{1,0:T(8,128)(2,1)S(1)} %collective-permute-done.1.refs_0_.refs_1_, ...), custom_call_target="tpu_custom_call" | custom-call | flops 1000 | bytes 1000 | tf_op jit(solution)/shard_map/pallas_call | solution.py:155
  43.8 1.6 %collective-permute-start.12 = (bf16[1024,256]{1,0:T(8,128)(2,1)S(1)}, bf16[1024,256]{1,0:T(8,128)(2,1)S(1)}, u32[]{:S(2)}, u32[]{:S(2)}) collective-permute-start(bf16[1024,256]{1,0:T(8,128)(2,1)S(1)} %collective-permute-done.8.refs_7_), channel_id=1, source_target_pairs={{0,4},{1,3},{4,8},{5,1},{8,12},{9,5},{12,14},{13,9},{14,10},{15,13... | collective-permute-start | bytes 1572872 | tf_op jit(solution)/shard_map/ppermute | solution.py:365
  46.0 5.7 %collective-permute-done.14.refs_6_ = bf16[1024,256]{1,0:T(8,128)(2,1)S(1)} collective-permute-done((bf16[1024,256]{1,0:T(8,128)(2,1)S(1)}, bf16[1024,256]{1,0:T(8,128)(2,1)S(1)}, u32[]{:S(2)}, u32[]{:S(2)}) %collective-permute-start.14) | collective-permute-done | bytes 524320 | tf_op jit(solution)/shard_map/ppermute | solution.py:362
  54.5 1.8 %collective-permute-done.12.refs_0_ = bf16[1024,256]{1,0:T(8,128)(2,1)S(1)} collective-permute-done((bf16[1024,256]{1,0:T(8,128)(2,1)S(1)}, bf16[1024,256]{1,0:T(8,128)(2,1)S(1)}, u32[]{:S(2)}, u32[]{:S(2)}) %collective-permute-start.12) | collective-permute-done | bytes 524320 | tf_op jit(solution)/shard_map/ppermute | solution.py:365
  56.4 2.2 %collective-permute-start.16 = (bf16[1024,256]{1,0:T(8,128)(2,1)S(1)}, bf16[1024,256]{1,0:T(8,128)(2,1)S(1)}, u32[]{:S(2)}, u32[]{:S(2)}) collective-permute-start(bf16[1024,256]{1,0:T(8,128)(2,1)S(1)} %collective-permute-done.13.refs_4_), channel_id=1, source_target_pairs={{0,4},{1,3},{4,8},{5,1},{8,12},{9,5},{12,14},{13,9},{14,10},{15,13... | collective-permute-start | bytes 1572872 | tf_op jit(solution)/shard_map/ppermute | solution.py:365
  58.5 3.9 %shard_map.99 = (f32[3,512,256]{2,1,0:T(8,128)S(1)}, f32[2,512,256]{2,1,0:T(8,128)S(1)}, f32[1,512,256]{2,1,0:T(8,128)S(1)}, f32[1,512,256]{2,1,0:T(8,128)S(1)}, f32[512,128]{1,0:T(8,128)S(1)}) custom-call(bf16[512,2048]{1,0:T(8,128)(2,1)S(1)} %copy-done.2, bf16[512,2048]{1,0:T(8,128)(2,1)S(1)} %collective-permute-done.1.refs_0_.refs_1_, ...), custom_call_target="tpu_custom_call" | custom-call | flops 1000 | bytes 1000 | tf_op jit(solution)/shard_map/pallas_call | solution.py:155
  62.6 2.1 %collective-permute-done.18.refs_1_ = bf16[1024,256]{1,0:T(8,128)(2,1)S(1)} collective-permute-done((bf16[1024,256]{1,0:T(8,128)(2,1)S(1)}, bf16[1024,256]{1,0:T(8,128)(2,1)S(1)}, u32[]{:S(2)}, u32[]{:S(2)}) %collective-permute-start.18) | collective-permute-done | bytes 524320 | tf_op jit(solution)/shard_map/ppermute | solution.py:362
  67.6 1.8 %shard_map.102 = (f32[4,512,256]{2,1,0:T(8,128)S(1)}, f32[512,128]{1,0:T(8,128)S(1)}) custom-call(bf16[512,2048]{1,0:T(8,128)(2,1)S(1)} %copy-done.2, bf16[512,4096]{1,0:T(8,128)(2,1)S(1)} %copy-done, f32[512,128]{1,0:T(8,128)S(1)} %get-tuple-element.121.before, bf16[1024,256]{1,0:T(8,128)(2,1)S(1)} %collective-permute-done.16.refs_0_, ...), custom_call_target="tpu_custom_call" | custom-call | flops 1000 | bytes 1000 | tf_op jit(solution)/shard_map/pallas_call | solution.py:191
  69.8 2.9 %shard_map.103 = (f32[1,4096]{1,0:T(1,128)}, bf16[8,48,128]{2,1,0:T(8,128)(2,1)S(1)}) custom-call(bf16[512,2048]{1,0:T(8,128)(2,1)S(1)} %copy-done.2, bf16[512,4096]{1,0:T(8,128)(2,1)S(1)} %copy-done, f32[512,128]{1,0:T(8,128)S(1)} %get-tuple-element.125.before, f32[1,4096]{1,0:T(1,128)S(1)} %bitcast.3, f32[1,128]{1,0:T(1,128)S(1)} %fusion.flags, ...), custom_call_target="tpu_custom_call" | custom-call | flops 1000 | bytes 1000 | tf_op jit(solution)/shard_map/pallas_call | solution.py:245
  72.7 15.1 %all_to_all.10.got = bf16[8,48,128]{2,1,0:T(8,128)(2,1)S(1)} all-to-all(bf16[8,48,128]{2,1,0:T(8,128)(2,1)S(1)} %get-tuple-element.137), channel_id=1, replica_groups={{0,2,4,6,8,10,12,14},{1,3,5,7,9,11,13,15},{16,18,20,22,24,26,28,30},{17..., dimensions={0} | all-to-all | bytes 196608 | tf_op jit(solution)/shard_map/all_to_all | solution.py:468
  88.9 10.0 %all_to_all.11.got = f32[8,40,128]{2,1,0:T(8,128)S(1)} all-to-all(f32[8,40,128]{2,1,0:T(8,128)S(1)} %shard_map.104), channel_id=1, replica_groups={{0,2,4,6,8,10,12,14},{1,3,5,7,9,11,13,15},{16,18,20,22,24,26,28,30},{17..., dimensions={0} | all-to-all | bytes 327680 | tf_op jit(solution)/shard_map/all_to_all | solution.py:468
  (58 shorter events, 16.4 us)
Async XLA Ops:
  0.6 16.9 %collective-permute-start.1 = (bf16[512,2048]{1,0:T(8,128)(2,1)}, bf16[512,2048]{1,0:T(8,128)(2,1)S(1)}, u32[]{:S(2)}, u32[]{:S(2)}) collective-permute-start(bf16[512,2048]{1,0:T(8,128)(2,1)} %context.7), channel_id=1, source_target_pairs={{0,1},{1,0},{2,3},{3,2},{4,5},{5,4},{6,7},{7,6},{8,9},{9,8},{10,11... | collective-permute-start | bytes 6291464 | tf_op jit(solution)/shard_map/ppermute | solution.py:371
  2.4 11.3 %collective-permute-start.2 = (bf16[1024,256]{1,0:T(8,128)(2,1)S(1)}, bf16[1024,256]{1,0:T(8,128)(2,1)S(1)}, u32[]{:S(2)}, u32[]{:S(2)}) collective-permute-start(bf16[1024,256]{1,0:T(8,128)(2,1)S(1)} %shard_map.94), channel_id=1, source_target_pairs={{0,2},{1,5},{4,0},{5,9},{8,4},{9,13},{12,8},{13,15},{14,12},{15,11... | collective-permute-start | bytes 1572872 | tf_op jit(solution)/shard_map/ppermute | solution.py:362
  5.0 14.5 %collective-permute-start.3 = (bf16[112,4096]{1,0:T(8,128)(2,1)}, bf16[112,4096]{1,0:T(8,128)(2,1)S(1)}, u32[]{:S(2)}, u32[]{:S(2)}) collective-permute-start(bf16[112,4096]{1,0:T(8,128)(2,1)} %queries.1), channel_id=1, source_target_pairs={{0,1},{1,0},{2,3},{3,2},{4,5},{5,4},{6,7},{7,6},{8,9},{9,8},{10,11... | collective-permute-start | bytes 2752520 | tf_op jit(solution)/shard_map/ppermute | solution.py:371
  7.8 11.7 %collective-permute-start = (bf16[1024,256]{1,0:T(8,128)(2,1)S(1)}, bf16[1024,256]{1,0:T(8,128)(2,1)S(1)}, u32[]{:S(2)}, u32[]{:S(2)}) collective-permute-start(bf16[1024,256]{1,0:T(8,128)(2,1)S(1)} %shard_map.94), channel_id=1, source_target_pairs={{0,4},{1,3},{4,8},{5,1},{8,12},{9,5},{12,14},{13,9},{14,10},{15,13... | collective-permute-start | bytes 1572872 | tf_op jit(solution)/shard_map/ppermute | solution.py:365
  13.7 10.5 %collective-permute-start.6 = (bf16[1024,256]{1,0:T(8,128)(2,1)S(1)}, bf16[1024,256]{1,0:T(8,128)(2,1)S(1)}, u32[]{:S(2)}, u32[]{:S(2)}) collective-permute-start(bf16[1024,256]{1,0:T(8,128)(2,1)S(1)} %collective-permute-done.2.refs_3_), channel_id=1, source_target_pairs={{0,2},{1,5},{4,0},{5,9},{8,4},{9,13},{12,8},{13,15},{14,12},{15,11... | collective-permute-start | bytes 1572872 | tf_op jit(solution)/shard_map/ppermute | solution.py:362
  16.1 14.2 %collective-permute-start.5 = (bf16[1024,256]{1,0:T(8,128)(2,1)S(1)}, bf16[1024,256]{1,0:T(8,128)(2,1)S(1)}, u32[]{:S(2)}, u32[]{:S(2)}) collective-permute-start(bf16[1024,256]{1,0:T(8,128)(2,1)S(1)} %collective-permute-done.2.refs_3_), channel_id=1, source_target_pairs={{0,16},{16,0},{1,17},{17,1},{2,18},{18,2},{3,19},{19,3},{4,20},{20... | collective-permute-start | bytes 1572872 | tf_op jit(solution)/shard_map/ppermute | solution.py:368
  19.5 10.8 %collective-permute-start.7 = (f32[512,256]{1,0:T(8,128)S(1)}, f32[512,256]{1,0:T(8,128)S(1)}, u32[]{:S(2)}, u32[]{:S(2)}) collective-permute-start(f32[512,256]{1,0:T(8,128)S(1)} %shard_map.96), channel_id=1, source_target_pairs={{0,1},{1,0},{2,3},{3,2},{4,5},{5,4},{6,7},{7,6},{8,9},{9,8},{10,11... | collective-permute-start | bytes 1572872 | tf_op jit(solution)/shard_map/ppermute | solution.py:371
  19.5 12.6 %collective-permute-start.4 = (bf16[1024,256]{1,0:T(8,128)(2,1)S(1)}, bf16[1024,256]{1,0:T(8,128)(2,1)S(1)}, u32[]{:S(2)}, u32[]{:S(2)}) collective-permute-start(bf16[1024,256]{1,0:T(8,128)(2,1)S(1)} %collective-permute-done.refs_5_), channel_id=1, source_target_pairs={{0,4},{1,3},{4,8},{5,1},{8,12},{9,5},{12,14},{13,9},{14,10},{15,13... | collective-permute-start | bytes 1572872 | tf_op jit(solution)/shard_map/ppermute | solution.py:365
  24.2 15.2 %collective-permute-start.10 = (bf16[1024,256]{1,0:T(8,128)(2,1)S(1)}, bf16[1024,256]{1,0:T(8,128)(2,1)S(1)}, u32[]{:S(2)}, u32[]{:S(2)}) collective-permute-start(bf16[1024,256]{1,0:T(8,128)(2,1)S(1)} %collective-permute-done.6.refs_3_), channel_id=1, source_target_pairs={{0,16},{16,0},{1,17},{17,1},{2,18},{18,2},{3,19},{19,3},{4,20},{20... | collective-permute-start | bytes 1572872 | tf_op jit(solution)/shard_map/ppermute | solution.py:368
  26.9 13.0 %collective-permute-start.9 = (bf16[1024,256]{1,0:T(8,128)(2,1)S(1)}, bf16[1024,256]{1,0:T(8,128)(2,1)S(1)}, u32[]{:S(2)}, u32[]{:S(2)}) collective-permute-start(bf16[1024,256]{1,0:T(8,128)(2,1)S(1)} %collective-permute-done.6.refs_3_), channel_id=1, source_target_pairs={{0,2},{1,5},{4,0},{5,9},{8,4},{9,13},{12,8},{13,15},{14,12},{15,11... | collective-permute-start | bytes 1572872 | tf_op jit(solution)/shard_map/ppermute | solution.py:362
  32.1 9.2 %collective-permute-start.11 = (f32[512,256]{1,0:T(8,128)S(1)}, f32[512,256]{1,0:T(8,128)S(1)}, u32[]{:S(2)}, u32[]{:S(2)}) collective-permute-start(f32[512,256]{1,0:T(8,128)S(1)} %get-tuple-element.94), channel_id=1, source_target_pairs={{0,1},{1,0},{2,3},{3,2},{4,5},{5,4},{6,7},{7,6},{8,9},{9,8},{10,11... | collective-permute-start | bytes 1572872 | tf_op jit(solution)/shard_map/ppermute | solution.py:371
  32.2 11.7 %collective-permute-start.8 = (bf16[1024,256]{1,0:T(8,128)(2,1)S(1)}, bf16[1024,256]{1,0:T(8,128)(2,1)S(1)}, u32[]{:S(2)}, u32[]{:S(2)}) collective-permute-start(bf16[1024,256]{1,0:T(8,128)(2,1)S(1)} %collective-permute-done.4.refs_3_), channel_id=1, source_target_pairs={{0,4},{1,3},{4,8},{5,1},{8,12},{9,5},{12,14},{13,9},{14,10},{15,13... | collective-permute-start | bytes 1572872 | tf_op jit(solution)/shard_map/ppermute | solution.py:365
  39.4 12.3 %collective-permute-start.14 = (bf16[1024,256]{1,0:T(8,128)(2,1)S(1)}, bf16[1024,256]{1,0:T(8,128)(2,1)S(1)}, u32[]{:S(2)}, u32[]{:S(2)}) collective-permute-start(bf16[1024,256]{1,0:T(8,128)(2,1)S(1)} %collective-permute-done.10.refs_4_), channel_id=1, source_target_pairs={{0,2},{1,5},{4,0},{5,9},{8,4},{9,13},{12,8},{13,15},{14,12},{15,11... | collective-permute-start | bytes 1572872 | tf_op jit(solution)/shard_map/ppermute | solution.py:362
  39.8 13.3 %collective-permute-start.13 = (bf16[1024,256]{1,0:T(8,128)(2,1)S(1)}, bf16[1024,256]{1,0:T(8,128)(2,1)S(1)}, u32[]{:S(2)}, u32[]{:S(2)}) collective-permute-start(bf16[1024,256]{1,0:T(8,128)(2,1)S(1)} %collective-permute-done.4.refs_3_), channel_id=1, source_target_pairs={{0,16},{16,0},{1,17},{17,1},{2,18},{18,2},{3,19},{19,3},{4,20},{20... | collective-permute-start | bytes 1572872 | tf_op jit(solution)/shard_map/ppermute | solution.py:368
  43.8 12.5 %collective-permute-start.12 = (bf16[1024,256]{1,0:T(8,128)(2,1)S(1)}, bf16[1024,256]{1,0:T(8,128)(2,1)S(1)}, u32[]{:S(2)}, u32[]{:S(2)}) collective-permute-start(bf16[1024,256]{1,0:T(8,128)(2,1)S(1)} %collective-permute-done.8.refs_7_), channel_id=1, source_target_pairs={{0,4},{1,3},{4,8},{5,1},{8,12},{9,5},{12,14},{13,9},{14,10},{15,13... | collective-permute-start | bytes 1572872 | tf_op jit(solution)/shard_map/ppermute | solution.py:365
  45.5 10.9 %collective-permute-start.15 = (f32[512,256]{1,0:T(8,128)S(1)}, f32[512,256]{1,0:T(8,128)S(1)}, u32[]{:S(2)}, u32[]{:S(2)}) collective-permute-start(f32[512,256]{1,0:T(8,128)S(1)} %get-tuple-element.104), channel_id=1, source_target_pairs={{0,1},{1,0},{2,3},{3,2},{4,5},{5,4},{6,7},{7,6},{8,9},{9,8},{10,11... | collective-permute-start | bytes 1572872 | tf_op jit(solution)/shard_map/ppermute | solution.py:371
  45.5 13.1 %collective-permute-start.19 = (f32[512,256]{1,0:T(8,128)S(1)}, f32[512,256]{1,0:T(8,128)S(1)}, u32[]{:S(2)}, u32[]{:S(2)}) collective-permute-start(f32[512,256]{1,0:T(8,128)S(1)} %get-tuple-element.112), channel_id=1, source_target_pairs={{0,1},{1,0},{2,3},{3,2},{4,5},{5,4},{6,7},{7,6},{8,9},{9,8},{10,11... | collective-permute-start | bytes 1572872 | tf_op jit(solution)/shard_map/ppermute | solution.py:371
  51.7 13.1 %collective-permute-start.18 = (bf16[1024,256]{1,0:T(8,128)(2,1)S(1)}, bf16[1024,256]{1,0:T(8,128)(2,1)S(1)}, u32[]{:S(2)}, u32[]{:S(2)}) collective-permute-start(bf16[1024,256]{1,0:T(8,128)(2,1)S(1)} %collective-permute-done.14.refs_6_), channel_id=1, source_target_pairs={{0,2},{1,5},{4,0},{5,9},{8,4},{9,13},{12,8},{13,15},{14,12},{15,11... | collective-permute-start | bytes 1572872 | tf_op jit(solution)/shard_map/ppermute | solution.py:362
  53.1 13.1 %collective-permute-start.17 = (bf16[1024,256]{1,0:T(8,128)(2,1)S(1)}, bf16[1024,256]{1,0:T(8,128)(2,1)S(1)}, u32[]{:S(2)}, u32[]{:S(2)}) collective-permute-start(bf16[1024,256]{1,0:T(8,128)(2,1)S(1)} %collective-permute-done.refs_5_), channel_id=1, source_target_pairs={{0,16},{16,0},{1,17},{17,1},{2,18},{18,2},{3,19},{19,3},{4,20},{20... | collective-permute-start | bytes 1572872 | tf_op jit(solution)/shard_map/ppermute | solution.py:368
  56.4 10.5 %collective-permute-start.16 = (bf16[1024,256]{1,0:T(8,128)(2,1)S(1)}, bf16[1024,256]{1,0:T(8,128)(2,1)S(1)}, u32[]{:S(2)}, u32[]{:S(2)}) collective-permute-start(bf16[1024,256]{1,0:T(8,128)(2,1)S(1)} %collective-permute-done.13.refs_4_), channel_id=1, source_target_pairs={{0,4},{1,3},{4,8},{5,1},{8,12},{9,5},{12,14},{13,9},{14,10},{15,13... | collective-permute-start | bytes 1572872 | tf_op jit(solution)/shard_map/ppermute | solution.py:365
  62.5 5.1 %collective-permute-start.22 = (f32[2,512,256]{2,1,0:T(8,128)S(1)}, f32[2,512,256]{2,1,0:T(8,128)S(1)}, u32[]{:S(2)}, u32[]{:S(2)}) collective-permute-start(f32[2,512,256]{2,1,0:T(8,128)S(1)} %get-tuple-element.124), channel_id=1, source_target_pairs={{0,1},{1,0},{2,3},{3,2},{4,5},{5,4},{6,7},{7,6},{8,9},{9,8},{10,11... | collective-permute-start | bytes 3145736 | tf_op jit(solution)/shard_map/ppermute | solution.py:371
  64.7 2.7 %collective-permute-start.21 = (bf16[1024,256]{1,0:T(8,128)(2,1)S(1)}, bf16[1024,256]{1,0:T(8,128)(2,1)S(1)}, u32[]{:S(2)}, u32[]{:S(2)}) collective-permute-start(bf16[1024,256]{1,0:T(8,128)(2,1)S(1)} %collective-permute-done.18.refs_1_), channel_id=1, source_target_pairs={{0,1},{1,0},{2,3},{3,2},{4,5},{5,4},{6,7},{7,6},{8,9},{9,8},{10,11... | collective-permute-start | bytes 1572872 | tf_op jit(solution)/shard_map/ppermute | solution.py:371
  64.7 2.8 %collective-permute-start.20 = (bf16[1024,256]{1,0:T(8,128)(2,1)S(1)}, bf16[1024,256]{1,0:T(8,128)(2,1)S(1)}, u32[]{:S(2)}, u32[]{:S(2)}) collective-permute-start(bf16[1024,256]{1,0:T(8,128)(2,1)S(1)} %collective-permute-done.12.refs_0_), channel_id=1, source_target_pairs={{0,1},{1,0},{2,3},{3,2},{4,5},{5,4},{6,7},{7,6},{8,9},{9,8},{10,11... | collective-permute-start | bytes 1572872 | tf_op jit(solution)/shard_map/ppermute | solution.py:371
  66.2 3.2 %collective-permute-start.23 = (bf16[1024,256]{1,0:T(8,128)(2,1)S(1)}, bf16[1024,256]{1,0:T(8,128)(2,1)S(1)}, u32[]{:S(2)}, u32[]{:S(2)}) collective-permute-start(bf16[1024,256]{1,0:T(8,128)(2,1)S(1)} %collective-permute-done.17.refs_0_), channel_id=1, source_target_pairs={{0,1},{1,0},{2,3},{3,2},{4,5},{5,4},{6,7},{7,6},{8,9},{9,8},{10,11... | collective-permute-start | bytes 1572872 | tf_op jit(solution)/shard_map/ppermute | solution.py:371
  (9 other events, 79.0 us)

commit v16 on v15

--- a/solution.py
+++ b/solution.py
@@ -97,10 +97,9 @@
     mine = refs.pop(0) if "mine" in tokens else None
     theirs = None
     if "theirs" in tokens:
-        stacks = [refs.pop(0) for _ in range(2 if stacked else count)]
-        theirs = stacks
+        theirs = [refs.pop(0) for _ in range(1 if stacked else count)]
         if stacked:
-            theirs = [stacks[0].at[j] for j in range(len(full))] + [stacks[1].at[j] for j in range(len(part))]
+            theirs = [theirs[0].at[j] for j in range(count)]
     finished = refs.pop(0) if arrived else None
     squares = refs.pop(0) if "mine" in tokens else None
     rows, width = mine.shape[1:] if "mine" in tokens else theirs[0].shape
@@ -136,7 +135,7 @@
     tokens = (("mine",) if context is not None else ()) + (("theirs",) if other_context is not None else ())
     count = len(full) + len(part)
     rows = (context if other_context is None else other_context).shape[0]
-    whole = len(pieces) == 1
+    whole = len(pieces) == 1 and bool(full)
     block = jax.ShapeDtypeStruct((rows, pieces[0].shape[1]), jnp.float32)
 
     def stack(n):
@@ -144,12 +143,14 @@
 
     outs = [stack(count)] if "mine" in tokens else []
     if "theirs" in tokens:
-        outs += [stack(len(full)), stack(len(part))] if stacked else [block] * count
+        outs += [stack(count)] if stacked else [block] * count
     operands = [x for x in (context, other_context) if x is not None]
     operands += ([residual] if "mine" in tokens else []) + list(pieces)
     if arrived:
-        operands += [*received] + ([] if squares is None else [squares])
+        operands += [*received]
         outs.append(jax.ShapeDtypeStruct((len(arrived),) + block.shape, jnp.float32))
+    if squares is not None:
+        operands.append(squares)
     if "mine" in tokens:
         outs.append(jax.ShapeDtypeStruct((rows, LANES), jnp.float32))
     return pl.pallas_call(
@@ -415,11 +416,12 @@
     a = from_next(n3x)
     xl2, l1, n3x = wait((x, l1, n3x))
     x = over_x(l1)
-    l4, xl2, n3x, r2p = wait((b, xl2, n3x, r2p))
+    h3, t3a, sq3 = wave(
+        (-2, 3), (), (), context, context2, residual, [l2, xl2, n3, n3x], (), sq2, stacked=True
+    )
+    l4, xl2, t3a, sq3, l3, r2p = wait((b, xl2, t3a, sq3, l3, r2p))
     b = from_last(xl2)
-    h3, t3a, t3p, f2, sq3 = wave(
-        (-2, 3), (-3,), ((2, False),), context, context2, residual, [l2, xl2, n3, n3x, l3], [r2], sq2, stacked=True
-    )
+    h3p, t3p, f2, sq3 = wave((), (-3,), ((2, False),), context, context2, residual, [l3], [r2], sq3)
     r3a, r3p = other_core(t3a), other_core(t3p)
     l4s = other_core(l4)
 
@@ -434,13 +436,13 @@
     l3x, xl1, sq5 = wait((b, xl1, sq5))
     l3xs = other_core(l3x)
     items = (
-        ((0, 2), ((0, True),), False, -3, True),
+        ((0, 0), ((0, True),), False, -3, True),
         ((1, 0), (), True, -2, False),
         ((1, 1), (), True, 3, False),
         (None, ((1, False), (2, True)), True, 4, False),
     )
-    h6, sq6 = late(items, context, residual, sq5, [l3x, l4s, n4xs], [h3, r3a])
-    items = (((0, None), ((0, True),), True, -1, False), ((1, 0), ((1, True),), True, -3, False))
+    h6, sq6 = late(items, context, residual, sq5, [l3x, l4s, n4xs], [h3p, r3a])
+    items = (((0, None), ((0, True),), True, -1, False), ((1, None), ((1, True),), True, -3, False))
     hidden = [r2p, r3p, h1, h2, h3, h4, h5, h6, f0, f1, f2]
     sources = (
         (2, 0, 1, True),

time: 99.9 us -> 99.8 us (level)
  waiting for transfers between devices: 27.1 us -> 29.5 us
  blocking collectives: 25 us -> 23.8 us
  starting transfers between devices: 24.9 us -> 23.7 us
    ppermute x4, waiting for transfers between devices: 8.92 us -> 12.5 us  [over_x(): return lax.ppermute(piece, 'groups', [(0, 1), (1, 0)])]
    ppermute x5, waiting for transfers between devices: 2.88 us -> 1.03 us  [from_last(): return lax.ppermute(piece, 'dp', ring(1))]
    all_to_all x2, blocking collectives: 25 us -> 23.8 us  [spread(): lax.all_to_all(blocks, 'dp', 0, 0, axis_index_groups=same_core, tiled=True)]
    pallas_call x5 -> x6, Pallas kernels: 9.96 us -> 9.97 us  [wave(): pl.pallas_call(functools.partial(wave_kernel, full, part, arrived, whole,...]
where the time goes in v16:
time: 99.8 us; the launch traced here: 99.5 us
  waiting for transfers between devices  29.5 us (30%)
  blocking collectives  23.8 us (24%)
  starting transfers between devices  23.7 us (24%)
  Pallas kernels  18.1 us (18%)
  local copies, waits for them, and re-layouts  2.84 us (3%)
  between operations  1.49 us (1%)
    all_to_all x2, blocking collectives, spread(): lax.all_to_all(blocks, 'dp', 0, 0, axis_index_groups=same_core, tiled=True)  23.8 us
    ppermute x5, waiting for transfers between devices, from_next(): return lax.ppermute(piece, 'dp', ring(-1))  15.6 us
    ppermute x4, waiting for transfers between devices, over_x(): return lax.ppermute(piece, 'groups', [(0, 1), (1, 0)])  12.5 us
    pallas_call x6, Pallas kernels, wave(): pl.pallas_call(functools.partial(wave_kernel, full, part, arrived, whole,...  9.97 us
    ppermute x5, starting transfers between devices, from_last(): return lax.ppermute(piece, 'dp', ring(1))  7.89 us
    ppermute x5, starting transfers between devices, from_next(): return lax.ppermute(piece, 'dp', ring(-1))  7.38 us
    ppermute x4, starting transfers between devices, over_x(): return lax.ppermute(piece, 'groups', [(0, 1), (1, 0)])  6.37 us
    pallas_call x3, Pallas kernels, late(): pl.pallas_call(functools.partial(late_kernel, items, len(pieces)), out_sh...  3.4 us
  transfers between devices with their start and end apart: 26, of which 10 were waited for; matrix products, arithmetic and copies ran while one was open for 0% of the time, Pallas kernels for 13%

profile of v16, /device:TPU:0, one launch (start us, length us, event | category | flops | bytes accessed | tf_op | source)
XLA Modules:
  0.0 99.5 jit_solution(9315981456796030610)
XLA Ops:
  2.4 2.6 %collective-permute-start.2 = (bf16[1024,256]{1,0:T(8,128)(2,1)S(1)}, bf16[1024,256]{1,0:T(8,128)(2,1)S(1)}, u32[]{:S(2)}, u32[]{:S(2)}) collective-permute-start(bf16[1024,256]{1,0:T(8,128)(2,1)S(1)} %shard_map.94), channel_id=1, source_target_pairs={{0,2},{1,5},{4,0},{5,9},{8,4},{9,13},{12,8},{13,15},{14,12},{15,11... | collective-permute-start | bytes 1572872 | tf_op jit(solution)/shard_map/ppermute | solution.py:363
  5.3 1.6 %copy-done.1 = bf16[512,2048]{1,0:T(8,128)(2,1)S(1)} copy-done((bf16[512,2048]{1,0:T(8,128)(2,1)S(1)}, bf16[512,2048]{1,0:T(8,128)(2,1)}, u32[]{:S(2)}) %copy-start.1) | copy-done | bytes 2097176
  7.8 1.6 %collective-permute-start = (bf16[1024,256]{1,0:T(8,128)(2,1)S(1)}, bf16[1024,256]{1,0:T(8,128)(2,1)S(1)}, u32[]{:S(2)}, u32[]{:S(2)}) collective-permute-start(bf16[1024,256]{1,0:T(8,128)(2,1)S(1)} %shard_map.94), channel_id=1, source_target_pairs={{0,4},{1,3},{4,8},{5,1},{8,12},{9,5},{12,14},{13,9},{14,10},{15,13... | collective-permute-start | bytes 1572872 | tf_op jit(solution)/shard_map/ppermute | solution.py:366
  9.4 4.3 %collective-permute-done.2.refs_3_ = bf16[1024,256]{1,0:T(8,128)(2,1)S(1)} collective-permute-done((bf16[1024,256]{1,0:T(8,128)(2,1)S(1)}, bf16[1024,256]{1,0:T(8,128)(2,1)S(1)}, u32[]{:S(2)}, u32[]{:S(2)}) %collective-permute-start.2) | collective-permute-done | bytes 524320 | tf_op jit(solution)/shard_map/ppermute | solution.py:363
  13.7 2.3 %collective-permute-start.6 = (bf16[1024,256]{1,0:T(8,128)(2,1)S(1)}, bf16[1024,256]{1,0:T(8,128)(2,1)S(1)}, u32[]{:S(2)}, u32[]{:S(2)}) collective-permute-start(bf16[1024,256]{1,0:T(8,128)(2,1)S(1)} %collective-permute-done.2.refs_3_), channel_id=1, source_target_pairs={{0,2},{1,5},{4,0},{5,9},{8,4},{9,13},{12,8},{13,15},{14,12},{15,11... | collective-permute-start | bytes 1572872 | tf_op jit(solution)/shard_map/ppermute | solution.py:363
  19.5 2.0 %collective-permute-start.4 = (bf16[1024,256]{1,0:T(8,128)(2,1)S(1)}, bf16[1024,256]{1,0:T(8,128)(2,1)S(1)}, u32[]{:S(2)}, u32[]{:S(2)}) collective-permute-start(bf16[1024,256]{1,0:T(8,128)(2,1)S(1)} %collective-permute-done.refs_5_), channel_id=1, source_target_pairs={{0,4},{1,3},{4,8},{5,1},{8,12},{9,5},{12,14},{13,9},{14,10},{15,13... | collective-permute-start | bytes 1572872 | tf_op jit(solution)/shard_map/ppermute | solution.py:366
  21.5 2.8 %collective-permute-done.6.refs_3_ = bf16[1024,256]{1,0:T(8,128)(2,1)S(1)} collective-permute-done((bf16[1024,256]{1,0:T(8,128)(2,1)S(1)}, bf16[1024,256]{1,0:T(8,128)(2,1)S(1)}, u32[]{:S(2)}, u32[]{:S(2)}) %collective-permute-start.6) | collective-permute-done | bytes 524320 | tf_op jit(solution)/shard_map/ppermute | solution.py:363
  24.2 2.0 %collective-permute-start.10 = (bf16[1024,256]{1,0:T(8,128)(2,1)S(1)}, bf16[1024,256]{1,0:T(8,128)(2,1)S(1)}, u32[]{:S(2)}, u32[]{:S(2)}) collective-permute-start(bf16[1024,256]{1,0:T(8,128)(2,1)S(1)} %collective-permute-done.6.refs_3_), channel_id=1, source_target_pairs={{0,16},{16,0},{1,17},{17,1},{2,18},{18,2},{3,19},{19,3},{4,20},{20... | collective-permute-start | bytes 1572872 | tf_op jit(solution)/shard_map/ppermute | solution.py:369
  26.9 1.8 %collective-permute-start.9 = (bf16[1024,256]{1,0:T(8,128)(2,1)S(1)}, bf16[1024,256]{1,0:T(8,128)(2,1)S(1)}, u32[]{:S(2)}, u32[]{:S(2)}) collective-permute-start(bf16[1024,256]{1,0:T(8,128)(2,1)S(1)} %collective-permute-done.6.refs_3_), channel_id=1, source_target_pairs={{0,2},{1,5},{4,0},{5,9},{8,4},{9,13},{12,8},{13,15},{14,12},{15,11... | collective-permute-start | bytes 1572872 | tf_op jit(solution)/shard_map/ppermute | solution.py:363
  28.6 1.6 %collective-permute-done.5.refs_4_ = bf16[1024,256]{1,0:T(8,128)(2,1)S(1)} collective-permute-done((bf16[1024,256]{1,0:T(8,128)(2,1)S(1)}, bf16[1024,256]{1,0:T(8,128)(2,1)S(1)}, u32[]{:S(2)}, u32[]{:S(2)}) %collective-permute-start.5) | collective-permute-done | bytes 524320 | tf_op jit(solution)/shard_map/ppermute | solution.py:369
  30.3 1.8 %shard_map.97 = (f32[1,512,256]{2,1,0:T(8,128)S(1)}, f32[512,256]{1,0:T(8,128)S(1)}, f32[2,512,256]{2,1,0:T(8,128)S(1)}, f32[512,128]{1,0:T(8,128)S(1)}) custom-call(bf16[512,2048]{1,0:T(8,128)(2,1)S(1)} %copy-done.2, bf16[512,2048]{1,0:T(8,128)(2,1)S(1)} %collective-permute-done.1.refs_0_.refs_1_, bf16[512,4096]{1,0:T(8,128)(2,1)S(1)} %copy-done, ...), custom_call_target="tpu_custom_call" | custom-call | flops 1000 | bytes 1000 | tf_op jit(solution)/shard_map/pallas_call | solution.py:156
  33.3 6.1 %collective-permute-done.10.refs_4_ = bf16[1024,256]{1,0:T(8,128)(2,1)S(1)} collective-permute-done((bf16[1024,256]{1,0:T(8,128)(2,1)S(1)}, bf16[1024,256]{1,0:T(8,128)(2,1)S(1)}, u32[]{:S(2)}, u32[]{:S(2)}) %collective-permute-start.10) | collective-permute-done | bytes 524320 | tf_op jit(solution)/shard_map/ppermute | solution.py:369
  39.8 1.5 %collective-permute-start.13 = (bf16[1024,256]{1,0:T(8,128)(2,1)S(1)}, bf16[1024,256]{1,0:T(8,128)(2,1)S(1)}, u32[]{:S(2)}, u32[]{:S(2)}) collective-permute-start(bf16[1024,256]{1,0:T(8,128)(2,1)S(1)} %collective-permute-done.4.refs_3_), channel_id=1, source_target_pairs={{0,16},{16,0},{1,17},{17,1},{2,18},{18,2},{3,19},{19,3},{4,20},{20... | collective-permute-start | bytes 1572872 | tf_op jit(solution)/shard_map/ppermute | solution.py:369
  41.3 2.5 %shard_map.98 = (f32[2,512,256]{2,1,0:T(8,128)S(1)}, f32[512,256]{1,0:T(8,128)S(1)}, f32[512,256]{1,0:T(8,128)S(1)}, f32[1,512,256]{2,1,0:T(8,128)S(1)}, f32[512,128]{1,0:T(8,128)S(1)}) custom-call(bf16[512,2048]{1,0:T(8,128)(2,1)S(1)} %copy-done.2, bf16[512,2048]{1,0:T(8,128)(2,1)S(1)} %collective-permute-done.1.refs_0_.refs_1_, ...), custom_call_target="tpu_custom_call" | custom-call | flops 1000 | bytes 1000 | tf_op jit(solution)/shard_map/pallas_call | solution.py:156
  43.8 1.6 %collective-permute-start.12 = (bf16[1024,256]{1,0:T(8,128)(2,1)S(1)}, bf16[1024,256]{1,0:T(8,128)(2,1)S(1)}, u32[]{:S(2)}, u32[]{:S(2)}) collective-permute-start(bf16[1024,256]{1,0:T(8,128)(2,1)S(1)} %collective-permute-done.8.refs_3_), channel_id=1, source_target_pairs={{0,4},{1,3},{4,8},{5,1},{8,12},{9,5},{12,14},{13,9},{14,10},{15,13... | collective-permute-start | bytes 1572872 | tf_op jit(solution)/shard_map/ppermute | solution.py:366
  45.5 6.2 %collective-permute-done.14.refs_6_ = bf16[1024,256]{1,0:T(8,128)(2,1)S(1)} collective-permute-done((bf16[1024,256]{1,0:T(8,128)(2,1)S(1)}, bf16[1024,256]{1,0:T(8,128)(2,1)S(1)}, u32[]{:S(2)}, u32[]{:S(2)}) %collective-permute-start.14) | collective-permute-done | bytes 524320 | tf_op jit(solution)/shard_map/ppermute | solution.py:363
  54.5 2.9 %shard_map.99 = (f32[2,512,256]{2,1,0:T(8,128)S(1)}, f32[2,512,256]{2,1,0:T(8,128)S(1)}, f32[512,128]{1,0:T(8,128)S(1)}) custom-call(bf16[512,2048]{1,0:T(8,128)(2,1)S(1)} %copy-done.2, bf16[512,2048]{1,0:T(8,128)(2,1)S(1)} %collective-permute-done.1.refs_0_.refs_1_, bf16[512,4096]{1,0:T(8,128)(2,1)S(1)} %copy-done, ...), custom_call_target="tpu_custom_call" | custom-call | flops 1000 | bytes 1000 | tf_op jit(solution)/shard_map/pallas_call | solution.py:156
  57.5 1.6 %collective-permute-start.16 = (bf16[1024,256]{1,0:T(8,128)(2,1)S(1)}, bf16[1024,256]{1,0:T(8,128)(2,1)S(1)}, u32[]{:S(2)}, u32[]{:S(2)}) collective-permute-start(bf16[1024,256]{1,0:T(8,128)(2,1)S(1)} %collective-permute-done.13.refs_4_), channel_id=1, source_target_pairs={{0,4},{1,3},{4,8},{5,1},{8,12},{9,5},{12,14},{13,9},{14,10},{15,13... | collective-permute-start | bytes 1572872 | tf_op jit(solution)/shard_map/ppermute | solution.py:366
  59.0 2.3 %collective-permute-done.18.refs_1_ = bf16[1024,256]{1,0:T(8,128)(2,1)S(1)} collective-permute-done((bf16[1024,256]{1,0:T(8,128)(2,1)S(1)}, bf16[1024,256]{1,0:T(8,128)(2,1)S(1)}, u32[]{:S(2)}, u32[]{:S(2)}) %collective-permute-start.18) | collective-permute-done | bytes 524320 | tf_op jit(solution)/shard_map/ppermute | solution.py:363
  63.8 3.6 %collective-permute-done.17.refs_0_ = bf16[1024,256]{1,0:T(8,128)(2,1)S(1)} collective-permute-done((bf16[1024,256]{1,0:T(8,128)(2,1)S(1)}, bf16[1024,256]{1,0:T(8,128)(2,1)S(1)}, u32[]{:S(2)}, u32[]{:S(2)}) %collective-permute-start.17) | collective-permute-done | bytes 524320 | tf_op jit(solution)/shard_map/ppermute | solution.py:369
  68.8 1.8 %shard_map.103 = (f32[4,512,256]{2,1,0:T(8,128)S(1)}, f32[512,128]{1,0:T(8,128)S(1)}) custom-call(bf16[512,2048]{1,0:T(8,128)(2,1)S(1)} %copy-done.2, bf16[512,4096]{1,0:T(8,128)(2,1)S(1)} %copy-done, f32[512,128]{1,0:T(8,128)S(1)} %get-tuple-element.128.before, bf16[1024,256]{1,0:T(8,128)(2,1)S(1)} %collective-permute-done.16.refs_0_, ...), custom_call_target="tpu_custom_call" | custom-call | flops 1000 | bytes 1000 | tf_op jit(solution)/shard_map/pallas_call | solution.py:192
  71.0 2.9 %shard_map.104 = (f32[1,4096]{1,0:T(1,128)}, bf16[8,48,128]{2,1,0:T(8,128)(2,1)S(1)}) custom-call(bf16[512,2048]{1,0:T(8,128)(2,1)S(1)} %copy-done.2, bf16[512,4096]{1,0:T(8,128)(2,1)S(1)} %copy-done, f32[512,128]{1,0:T(8,128)S(1)} %get-tuple-element.132.before, f32[1,4096]{1,0:T(1,128)S(1)} %bitcast.3, f32[1,128]{1,0:T(1,128)S(1)} %fusion.flags, ...), custom_call_target="tpu_custom_call" | custom-call | flops 1000 | bytes 1000 | tf_op jit(solution)/shard_map/pallas_call | solution.py:246
  73.8 13.9 %all_to_all.10.got = bf16[8,48,128]{2,1,0:T(8,128)(2,1)S(1)} all-to-all(bf16[8,48,128]{2,1,0:T(8,128)(2,1)S(1)} %get-tuple-element.145), channel_id=1, replica_groups={{0,2,4,6,8,10,12,14},{1,3,5,7,9,11,13,15},{16,18,20,22,24,26,28,30},{17..., dimensions={0} | all-to-all | bytes 196608 | tf_op jit(solution)/shard_map/all_to_all | solution.py:470
  88.8 10.0 %all_to_all.11.got = f32[8,40,128]{2,1,0:T(8,128)S(1)} all-to-all(f32[8,40,128]{2,1,0:T(8,128)S(1)} %shard_map.105), channel_id=1, replica_groups={{0,2,4,6,8,10,12,14},{1,3,5,7,9,11,13,15},{16,18,20,22,24,26,28,30},{17..., dimensions={0} | all-to-all | bytes 327680 | tf_op jit(solution)/shard_map/all_to_all | solution.py:470
  (59 shorter events, 16.8 us)
Async XLA Ops:
  0.6 16.9 %collective-permute-start.1 = (bf16[512,2048]{1,0:T(8,128)(2,1)}, bf16[512,2048]{1,0:T(8,128)(2,1)S(1)}, u32[]{:S(2)}, u32[]{:S(2)}) collective-permute-start(bf16[512,2048]{1,0:T(8,128)(2,1)} %context.7), channel_id=1, source_target_pairs={{0,1},{1,0},{2,3},{3,2},{4,5},{5,4},{6,7},{7,6},{8,9},{9,8},{10,11... | collective-permute-start | bytes 6291464 | tf_op jit(solution)/shard_map/ppermute | solution.py:372
  2.4 11.3 %collective-permute-start.2 = (bf16[1024,256]{1,0:T(8,128)(2,1)S(1)}, bf16[1024,256]{1,0:T(8,128)(2,1)S(1)}, u32[]{:S(2)}, u32[]{:S(2)}) collective-permute-start(bf16[1024,256]{1,0:T(8,128)(2,1)S(1)} %shard_map.94), channel_id=1, source_target_pairs={{0,2},{1,5},{4,0},{5,9},{8,4},{9,13},{12,8},{13,15},{14,12},{15,11... | collective-permute-start | bytes 1572872 | tf_op jit(solution)/shard_map/ppermute | solution.py:363
  5.0 14.5 %collective-permute-start.3 = (bf16[112,4096]{1,0:T(8,128)(2,1)}, bf16[112,4096]{1,0:T(8,128)(2,1)S(1)}, u32[]{:S(2)}, u32[]{:S(2)}) collective-permute-start(bf16[112,4096]{1,0:T(8,128)(2,1)} %queries.1), channel_id=1, source_target_pairs={{0,1},{1,0},{2,3},{3,2},{4,5},{5,4},{6,7},{7,6},{8,9},{9,8},{10,11... | collective-permute-start | bytes 2752520 | tf_op jit(solution)/shard_map/ppermute | solution.py:372
  7.8 11.7 %collective-permute-start = (bf16[1024,256]{1,0:T(8,128)(2,1)S(1)}, bf16[1024,256]{1,0:T(8,128)(2,1)S(1)}, u32[]{:S(2)}, u32[]{:S(2)}) collective-permute-start(bf16[1024,256]{1,0:T(8,128)(2,1)S(1)} %shard_map.94), channel_id=1, source_target_pairs={{0,4},{1,3},{4,8},{5,1},{8,12},{9,5},{12,14},{13,9},{14,10},{15,13... | collective-permute-start | bytes 1572872 | tf_op jit(solution)/shard_map/ppermute | solution.py:366
  13.7 10.5 %collective-permute-start.6 = (bf16[1024,256]{1,0:T(8,128)(2,1)S(1)}, bf16[1024,256]{1,0:T(8,128)(2,1)S(1)}, u32[]{:S(2)}, u32[]{:S(2)}) collective-permute-start(bf16[1024,256]{1,0:T(8,128)(2,1)S(1)} %collective-permute-done.2.refs_3_), channel_id=1, source_target_pairs={{0,2},{1,5},{4,0},{5,9},{8,4},{9,13},{12,8},{13,15},{14,12},{15,11... | collective-permute-start | bytes 1572872 | tf_op jit(solution)/shard_map/ppermute | solution.py:363
  16.1 14.2 %collective-permute-start.5 = (bf16[1024,256]{1,0:T(8,128)(2,1)S(1)}, bf16[1024,256]{1,0:T(8,128)(2,1)S(1)}, u32[]{:S(2)}, u32[]{:S(2)}) collective-permute-start(bf16[1024,256]{1,0:T(8,128)(2,1)S(1)} %collective-permute-done.2.refs_3_), channel_id=1, source_target_pairs={{0,16},{16,0},{1,17},{17,1},{2,18},{18,2},{3,19},{19,3},{4,20},{20... | collective-permute-start | bytes 1572872 | tf_op jit(solution)/shard_map/ppermute | solution.py:369
  19.5 10.8 %collective-permute-start.7 = (f32[512,256]{1,0:T(8,128)S(1)}, f32[512,256]{1,0:T(8,128)S(1)}, u32[]{:S(2)}, u32[]{:S(2)}) collective-permute-start(f32[512,256]{1,0:T(8,128)S(1)} %shard_map.96), channel_id=1, source_target_pairs={{0,1},{1,0},{2,3},{3,2},{4,5},{5,4},{6,7},{7,6},{8,9},{9,8},{10,11... | collective-permute-start | bytes 1572872 | tf_op jit(solution)/shard_map/ppermute | solution.py:372
  19.5 12.6 %collective-permute-start.4 = (bf16[1024,256]{1,0:T(8,128)(2,1)S(1)}, bf16[1024,256]{1,0:T(8,128)(2,1)S(1)}, u32[]{:S(2)}, u32[]{:S(2)}) collective-permute-start(bf16[1024,256]{1,0:T(8,128)(2,1)S(1)} %collective-permute-done.refs_5_), channel_id=1, source_target_pairs={{0,4},{1,3},{4,8},{5,1},{8,12},{9,5},{12,14},{13,9},{14,10},{15,13... | collective-permute-start | bytes 1572872 | tf_op jit(solution)/shard_map/ppermute | solution.py:366
  24.2 15.2 %collective-permute-start.10 = (bf16[1024,256]{1,0:T(8,128)(2,1)S(1)}, bf16[1024,256]{1,0:T(8,128)(2,1)S(1)}, u32[]{:S(2)}, u32[]{:S(2)}) collective-permute-start(bf16[1024,256]{1,0:T(8,128)(2,1)S(1)} %collective-permute-done.6.refs_3_), channel_id=1, source_target_pairs={{0,16},{16,0},{1,17},{17,1},{2,18},{18,2},{3,19},{19,3},{4,20},{20... | collective-permute-start | bytes 1572872 | tf_op jit(solution)/shard_map/ppermute | solution.py:369
  26.9 13.0 %collective-permute-start.9 = (bf16[1024,256]{1,0:T(8,128)(2,1)S(1)}, bf16[1024,256]{1,0:T(8,128)(2,1)S(1)}, u32[]{:S(2)}, u32[]{:S(2)}) collective-permute-start(bf16[1024,256]{1,0:T(8,128)(2,1)S(1)} %collective-permute-done.6.refs_3_), channel_id=1, source_target_pairs={{0,2},{1,5},{4,0},{5,9},{8,4},{9,13},{12,8},{13,15},{14,12},{15,11... | collective-permute-start | bytes 1572872 | tf_op jit(solution)/shard_map/ppermute | solution.py:363
  32.1 9.2 %collective-permute-start.11 = (f32[512,256]{1,0:T(8,128)S(1)}, f32[512,256]{1,0:T(8,128)S(1)}, u32[]{:S(2)}, u32[]{:S(2)}) collective-permute-start(f32[512,256]{1,0:T(8,128)S(1)} %get-tuple-element.98), channel_id=1, source_target_pairs={{0,1},{1,0},{2,3},{3,2},{4,5},{5,4},{6,7},{7,6},{8,9},{9,8},{10,11... | collective-permute-start | bytes 1572872 | tf_op jit(solution)/shard_map/ppermute | solution.py:372
  32.2 11.7 %collective-permute-start.8 = (bf16[1024,256]{1,0:T(8,128)(2,1)S(1)}, bf16[1024,256]{1,0:T(8,128)(2,1)S(1)}, u32[]{:S(2)}, u32[]{:S(2)}) collective-permute-start(bf16[1024,256]{1,0:T(8,128)(2,1)S(1)} %collective-permute-done.4.refs_3_), channel_id=1, source_target_pairs={{0,4},{1,3},{4,8},{5,1},{8,12},{9,5},{12,14},{13,9},{14,10},{15,13... | collective-permute-start | bytes 1572872 | tf_op jit(solution)/shard_map/ppermute | solution.py:366
  39.4 12.3 %collective-permute-start.14 = (bf16[1024,256]{1,0:T(8,128)(2,1)S(1)}, bf16[1024,256]{1,0:T(8,128)(2,1)S(1)}, u32[]{:S(2)}, u32[]{:S(2)}) collective-permute-start(bf16[1024,256]{1,0:T(8,128)(2,1)S(1)} %collective-permute-done.10.refs_4_), channel_id=1, source_target_pairs={{0,2},{1,5},{4,0},{5,9},{8,4},{9,13},{12,8},{13,15},{14,12},{15,11... | collective-permute-start | bytes 1572872 | tf_op jit(solution)/shard_map/ppermute | solution.py:363
  39.8 13.3 %collective-permute-start.13 = (bf16[1024,256]{1,0:T(8,128)(2,1)S(1)}, bf16[1024,256]{1,0:T(8,128)(2,1)S(1)}, u32[]{:S(2)}, u32[]{:S(2)}) collective-permute-start(bf16[1024,256]{1,0:T(8,128)(2,1)S(1)} %collective-permute-done.4.refs_3_), channel_id=1, source_target_pairs={{0,16},{16,0},{1,17},{17,1},{2,18},{18,2},{3,19},{19,3},{4,20},{20... | collective-permute-start | bytes 1572872 | tf_op jit(solution)/shard_map/ppermute | solution.py:369
  43.8 13.6 %collective-permute-start.12 = (bf16[1024,256]{1,0:T(8,128)(2,1)S(1)}, bf16[1024,256]{1,0:T(8,128)(2,1)S(1)}, u32[]{:S(2)}, u32[]{:S(2)}) collective-permute-start(bf16[1024,256]{1,0:T(8,128)(2,1)S(1)} %collective-permute-done.8.refs_3_), channel_id=1, source_target_pairs={{0,4},{1,3},{4,8},{5,1},{8,12},{9,5},{12,14},{13,9},{14,10},{15,13... | collective-permute-start | bytes 1572872 | tf_op jit(solution)/shard_map/ppermute | solution.py:366
  45.5 12.0 %collective-permute-start.15 = (f32[512,256]{1,0:T(8,128)S(1)}, f32[512,256]{1,0:T(8,128)S(1)}, u32[]{:S(2)}, u32[]{:S(2)}) collective-permute-start(f32[512,256]{1,0:T(8,128)S(1)} %get-tuple-element.113), channel_id=1, source_target_pairs={{0,1},{1,0},{2,3},{3,2},{4,5},{5,4},{6,7},{7,6},{8,9},{9,8},{10,11... | collective-permute-start | bytes 1572872 | tf_op jit(solution)/shard_map/ppermute | solution.py:372
  51.7 9.6 %collective-permute-start.18 = (bf16[1024,256]{1,0:T(8,128)(2,1)S(1)}, bf16[1024,256]{1,0:T(8,128)(2,1)S(1)}, u32[]{:S(2)}, u32[]{:S(2)}) collective-permute-start(bf16[1024,256]{1,0:T(8,128)(2,1)S(1)} %collective-permute-done.14.refs_6_), channel_id=1, source_target_pairs={{0,2},{1,5},{4,0},{5,9},{8,4},{9,13},{12,8},{13,15},{14,12},{15,11... | collective-permute-start | bytes 1572872 | tf_op jit(solution)/shard_map/ppermute | solution.py:363
  53.1 8.2 %collective-permute-start.19 = (f32[512,256]{1,0:T(8,128)S(1)}, f32[512,256]{1,0:T(8,128)S(1)}, u32[]{:S(2)}, u32[]{:S(2)}) collective-permute-start(f32[512,256]{1,0:T(8,128)S(1)} %get-tuple-element.119), channel_id=1, source_target_pairs={{0,1},{1,0},{2,3},{3,2},{4,5},{5,4},{6,7},{7,6},{8,9},{9,8},{10,11... | collective-permute-start | bytes 1572872 | tf_op jit(solution)/shard_map/ppermute | solution.py:372
  53.1 14.3 %collective-permute-start.17 = (bf16[1024,256]{1,0:T(8,128)(2,1)S(1)}, bf16[1024,256]{1,0:T(8,128)(2,1)S(1)}, u32[]{:S(2)}, u32[]{:S(2)}) collective-permute-start(bf16[1024,256]{1,0:T(8,128)(2,1)S(1)} %collective-permute-done.refs_5_), channel_id=1, source_target_pairs={{0,16},{16,0},{1,17},{17,1},{2,18},{18,2},{3,19},{19,3},{4,20},{20... | collective-permute-start | bytes 1572872 | tf_op jit(solution)/shard_map/ppermute | solution.py:369
  57.5 10.6 %collective-permute-start.16 = (bf16[1024,256]{1,0:T(8,128)(2,1)S(1)}, bf16[1024,256]{1,0:T(8,128)(2,1)S(1)}, u32[]{:S(2)}, u32[]{:S(2)}) collective-permute-start(bf16[1024,256]{1,0:T(8,128)(2,1)S(1)} %collective-permute-done.13.refs_4_), channel_id=1, source_target_pairs={{0,4},{1,3},{4,8},{5,1},{8,12},{9,5},{12,14},{13,9},{14,10},{15,13... | collective-permute-start | bytes 1572872 | tf_op jit(solution)/shard_map/ppermute | solution.py:366
  59.0 9.7 %collective-permute-start.22 = (f32[2,512,256]{2,1,0:T(8,128)S(1)}, f32[2,512,256]{2,1,0:T(8,128)S(1)}, u32[]{:S(2)}, u32[]{:S(2)}) collective-permute-start(f32[2,512,256]{2,1,0:T(8,128)S(1)} %get-tuple-element.131), channel_id=1, source_target_pairs={{0,1},{1,0},{2,3},{3,2},{4,5},{5,4},{6,7},{7,6},{8,9},{9,8},{10,11... | collective-permute-start | bytes 3145736 | tf_op jit(solution)/shard_map/ppermute | solution.py:372
  61.3 7.3 %collective-permute-start.21 = (bf16[1024,256]{1,0:T(8,128)(2,1)S(1)}, bf16[1024,256]{1,0:T(8,128)(2,1)S(1)}, u32[]{:S(2)}, u32[]{:S(2)}) collective-permute-start(bf16[1024,256]{1,0:T(8,128)(2,1)S(1)} %collective-permute-done.18.refs_1_), channel_id=1, source_target_pairs={{0,1},{1,0},{2,3},{3,2},{4,5},{5,4},{6,7},{7,6},{8,9},{9,8},{10,11... | collective-permute-start | bytes 1572872 | tf_op jit(solution)/shard_map/ppermute | solution.py:372
  61.3 7.4 %collective-permute-start.20 = (bf16[1024,256]{1,0:T(8,128)(2,1)S(1)}, bf16[1024,256]{1,0:T(8,128)(2,1)S(1)}, u32[]{:S(2)}, u32[]{:S(2)}) collective-permute-start(bf16[1024,256]{1,0:T(8,128)(2,1)S(1)} %collective-permute-done.12.refs_0_), channel_id=1, source_target_pairs={{0,1},{1,0},{2,3},{3,2},{4,5},{5,4},{6,7},{7,6},{8,9},{9,8},{10,11... | collective-permute-start | bytes 1572872 | tf_op jit(solution)/shard_map/ppermute | solution.py:372
  67.4 3.2 %collective-permute-start.23 = (bf16[1024,256]{1,0:T(8,128)(2,1)S(1)}, bf16[1024,256]{1,0:T(8,128)(2,1)S(1)}, u32[]{:S(2)}, u32[]{:S(2)}) collective-permute-start(bf16[1024,256]{1,0:T(8,128)(2,1)S(1)} %collective-permute-done.17.refs_0_), channel_id=1, source_target_pairs={{0,1},{1,0},{2,3},{3,2},{4,5},{5,4},{6,7},{7,6},{8,9},{9,8},{10,11... | collective-permute-start | bytes 1572872 | tf_op jit(solution)/shard_map/ppermute | solution.py:372
  (9 other events, 77.8 us)

commit v17 on v13

--- a/solution.py
+++ b/solution.py
@@ -10,6 +10,7 @@
 
 QB = 256
 LANES = 128
+SUBLANES = 8
 CORES = 2
 STEP = 256
 VMEM_BYTES = 12 << 20
@@ -216,11 +217,18 @@
     inverse = 1.0 / length
     done = [(blocks.at[i], distance, same) for i, (_, _, _, distance, same) in enumerate(items)]
     done += [(hidden[array].at[entry], distance, same) for array, entry, distance, same in sources]
-    for block, distance, same in done:
-        parts = [
-            jnp.sum(block[:, lane : lane + LANES] * scale_rows[...], axis=0, keepdims=True)
-            for lane in range(0, width, LANES)
-        ]
+    lanes = range(0, width, LANES)
+
+    def add_rows(k, sums):
+        at = pl.ds(pl.multiple_of(k * SUBLANES, SUBLANES), SUBLANES)
+        weight = scale_rows[at, :]
+        terms = [block[at, lane : lane + LANES] * weight for block, _, _ in done for lane in lanes]
+        return tuple(total + term for total, term in zip(sums, terms))
+
+    zero = jnp.zeros((SUBLANES, LANES), jnp.float32)
+    sums = lax.fori_loop(0, scale_rows.shape[0] // SUBLANES, add_rows, (zero,) * (len(done) * len(lanes)))
+    for i, (_, distance, same) in enumerate(done):
+        parts = [jnp.sum(part, axis=0, keepdims=True) for part in sums[i * len(lanes) : (i + 1) * len(lanes)]]
         where = columns(distance, same, width)
         embedded[:, where] = jnp.concatenate(parts, axis=1) * gain[:, where] * inverse
     pooled = embedded[...]
@@ -421,11 +429,13 @@
     r3a, r3p = other_core(t3a), other_core(t3p)
     l4s = other_core(l4)
 
-    n4x, l4 = wait((a, l4))
+    n4x, l4, own_pattern, lengths = wait((a, l4, pattern, lengths))
+    flags = jnp.pad(own_pattern.astype(jnp.float32), ((0, 0), (0, LANES - 1 - pattern.shape[1])))
+    flags = jnp.concatenate([flags, lengths.astype(jnp.float32)[:, None]], axis=1)
     n4xs = other_core(n4x)
     items = ((None, ((0, False), (1, True)), True, 4, True),)
     h4, sq4 = late(items, context, residual, sq3, [l4, n4x], [])
-    xl1, n4x, sq4 = wait((x, n4x, sq4))
+    xl1, n4x, sq4, flags = wait((x, n4x, sq4, flags))
     xl1s = other_core(xl1)
     items = (((0, 1), ((0, True),), False, -1, True),)
     h5, sq5 = late(items, context, residual, sq4, [xl1], [h2])
@@ -456,8 +466,6 @@
         (7, 2, 3, False),
         (7, 3, 4, False),
     )
-    flags = jnp.pad(pattern.astype(jnp.float32), ((0, 0), (0, LANES - 1 - pattern.shape[1])))
-    flags = jnp.concatenate([flags, lengths.astype(jnp.float32)[:, None]], axis=1)
     embedded, payload = finish(
         items, sources, context, residual, sq6, norm_gain.reshape(1, -1), flags, [xl1s, l3xs], hidden, size
     )

time: 99.3 us -> 99.6 us (level)
  transfers between devices with their start and end apart: 26 -> 26, of which waited for: 10 -> 11; matrix products, arithmetic and copies ran while one was open for 0% -> 0% of each run, Pallas kernels for 13% -> 13%
where the time goes in v17:
time: 99.6 us; the launch traced here: 99.3 us
  waiting for transfers between devices  28.8 us (29%)
  starting transfers between devices  23.7 us (24%)
  blocking collectives  23.5 us (24%)
  Pallas kernels  18.9 us (19%)
  local copies, waits for them, and re-layouts  2.84 us (3%)
  between operations  1.48 us (1%)
    all_to_all x2, blocking collectives, spread(): lax.all_to_all(blocks, 'dp', 0, 0, axis_index_groups=same_core, tiled=True)  23.5 us
    ppermute x4, waiting for transfers between devices, over_x(): return lax.ppermute(piece, 'groups', [(0, 1), (1, 0)])  14.2 us
    ppermute x5, waiting for transfers between devices, from_next(): return lax.ppermute(piece, 'dp', ring(-1))  11.8 us
    pallas_call x5, Pallas kernels, wave(): pl.pallas_call(functools.partial(wave_kernel, full, part, arrived, whole,...  9.95 us
    ppermute x5, starting transfers between devices, from_last(): return lax.ppermute(piece, 'dp', ring(1))  8.04 us
    ppermute x5, starting transfers between devices, from_next(): return lax.ppermute(piece, 'dp', ring(-1))  7.1 us
    ppermute x4, starting transfers between devices, over_x(): return lax.ppermute(piece, 'groups', [(0, 1), (1, 0)])  6.24 us
    pallas_call x1, Pallas kernels, finish(): pl.pallas_call(functools.partial(final_kernel, items, sources, len(pieces...  3.68 us
  transfers between devices with their start and end apart: 26, of which 11 were waited for; matrix products, arithmetic and copies ran while one was open for 0% of the time, Pallas kernels for 13%

profile of v17, /device:TPU:0, one launch (start us, length us, event | category | flops | bytes accessed | tf_op | source)
XLA Modules:
  0.0 99.3 jit_solution(10399370653819452116)
XLA Ops:
  2.4 2.6 %collective-permute-start.2 = (bf16[1024,256]{1,0:T(8,128)(2,1)S(1)}, bf16[1024,256]{1,0:T(8,128)(2,1)S(1)}, u32[]{:S(2)}, u32[]{:S(2)}) collective-permute-start(bf16[1024,256]{1,0:T(8,128)(2,1)S(1)} %shard_map.94), channel_id=1, source_target_pairs={{0,2},{1,5},{4,0},{5,9},{8,4},{9,13},{12,8},{13,15},{14,12},{15,11... | collective-permute-start | bytes 1572872 | tf_op jit(solution)/shard_map/ppermute | solution.py:370
  5.3 1.6 %copy-done.1 = bf16[512,2048]{1,0:T(8,128)(2,1)S(1)} copy-done((bf16[512,2048]{1,0:T(8,128)(2,1)S(1)}, bf16[512,2048]{1,0:T(8,128)(2,1)}, u32[]{:S(2)}) %copy-start.1) | copy-done | bytes 2097176
  7.8 1.6 %collective-permute-start = (bf16[1024,256]{1,0:T(8,128)(2,1)S(1)}, bf16[1024,256]{1,0:T(8,128)(2,1)S(1)}, u32[]{:S(2)}, u32[]{:S(2)}) collective-permute-start(bf16[1024,256]{1,0:T(8,128)(2,1)S(1)} %shard_map.94), channel_id=1, source_target_pairs={{0,4},{1,3},{4,8},{5,1},{8,12},{9,5},{12,14},{13,9},{14,10},{15,13... | collective-permute-start | bytes 1572872 | tf_op jit(solution)/shard_map/ppermute | solution.py:373
  9.4 4.3 %collective-permute-done.2.refs_3_ = bf16[1024,256]{1,0:T(8,128)(2,1)S(1)} collective-permute-done((bf16[1024,256]{1,0:T(8,128)(2,1)S(1)}, bf16[1024,256]{1,0:T(8,128)(2,1)S(1)}, u32[]{:S(2)}, u32[]{:S(2)}) %collective-permute-start.2) | collective-permute-done | bytes 524320 | tf_op jit(solution)/shard_map/ppermute | solution.py:370
  13.7 2.3 %collective-permute-start.6 = (bf16[1024,256]{1,0:T(8,128)(2,1)S(1)}, bf16[1024,256]{1,0:T(8,128)(2,1)S(1)}, u32[]{:S(2)}, u32[]{:S(2)}) collective-permute-start(bf16[1024,256]{1,0:T(8,128)(2,1)S(1)} %collective-permute-done.2.refs_3_), channel_id=1, source_target_pairs={{0,2},{1,5},{4,0},{5,9},{8,4},{9,13},{12,8},{13,15},{14,12},{15,11... | collective-permute-start | bytes 1572872 | tf_op jit(solution)/shard_map/ppermute | solution.py:370
  19.5 2.0 %collective-permute-start.4 = (bf16[1024,256]{1,0:T(8,128)(2,1)S(1)}, bf16[1024,256]{1,0:T(8,128)(2,1)S(1)}, u32[]{:S(2)}, u32[]{:S(2)}) collective-permute-start(bf16[1024,256]{1,0:T(8,128)(2,1)S(1)} %collective-permute-done.refs_5_), channel_id=1, source_target_pairs={{0,4},{1,3},{4,8},{5,1},{8,12},{9,5},{12,14},{13,9},{14,10},{15,13... | collective-permute-start | bytes 1572872 | tf_op jit(solution)/shard_map/ppermute | solution.py:373
  21.5 2.8 %collective-permute-done.6.refs_3_ = bf16[1024,256]{1,0:T(8,128)(2,1)S(1)} collective-permute-done((bf16[1024,256]{1,0:T(8,128)(2,1)S(1)}, bf16[1024,256]{1,0:T(8,128)(2,1)S(1)}, u32[]{:S(2)}, u32[]{:S(2)}) %collective-permute-start.6) | collective-permute-done | bytes 524320 | tf_op jit(solution)/shard_map/ppermute | solution.py:370
  24.2 2.0 %collective-permute-start.10 = (bf16[1024,256]{1,0:T(8,128)(2,1)S(1)}, bf16[1024,256]{1,0:T(8,128)(2,1)S(1)}, u32[]{:S(2)}, u32[]{:S(2)}) collective-permute-start(bf16[1024,256]{1,0:T(8,128)(2,1)S(1)} %collective-permute-done.6.refs_3_), channel_id=1, source_target_pairs={{0,16},{16,0},{1,17},{17,1},{2,18},{18,2},{3,19},{19,3},{4,20},{20... | collective-permute-start | bytes 1572872 | tf_op jit(solution)/shard_map/ppermute | solution.py:376
  26.2 1.7 %collective-permute-start.9 = (bf16[1024,256]{1,0:T(8,128)(2,1)S(1)}, bf16[1024,256]{1,0:T(8,128)(2,1)S(1)}, u32[]{:S(2)}, u32[]{:S(2)}) collective-permute-start(bf16[1024,256]{1,0:T(8,128)(2,1)S(1)} %collective-permute-done.6.refs_3_), channel_id=1, source_target_pairs={{0,2},{1,5},{4,0},{5,9},{8,4},{9,13},{12,8},{13,15},{14,12},{15,11... | collective-permute-start | bytes 1572872 | tf_op jit(solution)/shard_map/ppermute | solution.py:370
  27.9 2.3 %collective-permute-done.5.refs_4_ = bf16[1024,256]{1,0:T(8,128)(2,1)S(1)} collective-permute-done((bf16[1024,256]{1,0:T(8,128)(2,1)S(1)}, bf16[1024,256]{1,0:T(8,128)(2,1)S(1)}, u32[]{:S(2)}, u32[]{:S(2)}) %collective-permute-start.5) | collective-permute-done | bytes 524320 | tf_op jit(solution)/shard_map/ppermute | solution.py:376
  30.3 1.8 %shard_map.97 = (f32[1,512,256]{2,1,0:T(8,128)S(1)}, f32[512,256]{1,0:T(8,128)S(1)}, f32[2,512,256]{2,1,0:T(8,128)S(1)}, f32[512,128]{1,0:T(8,128)S(1)}) custom-call(bf16[512,2048]{1,0:T(8,128)(2,1)S(1)} %copy-done.2, bf16[512,2048]{1,0:T(8,128)(2,1)S(1)} %collective-permute-done.1.refs_0_.refs_1_, bf16[512,4096]{1,0:T(8,128)(2,1)S(1)} %copy-done, ...), custom_call_target="tpu_custom_call" | custom-call | flops 1000 | bytes 1000 | tf_op jit(solution)/shard_map/pallas_call | solution.py:156
  33.2 6.2 %collective-permute-done.10.refs_4_ = bf16[1024,256]{1,0:T(8,128)(2,1)S(1)} collective-permute-done((bf16[1024,256]{1,0:T(8,128)(2,1)S(1)}, bf16[1024,256]{1,0:T(8,128)(2,1)S(1)}, u32[]{:S(2)}, u32[]{:S(2)}) %collective-permute-start.10) | collective-permute-done | bytes 524320 | tf_op jit(solution)/shard_map/ppermute | solution.py:376
  39.8 1.5 %collective-permute-start.13 = (bf16[1024,256]{1,0:T(8,128)(2,1)S(1)}, bf16[1024,256]{1,0:T(8,128)(2,1)S(1)}, u32[]{:S(2)}, u32[]{:S(2)}) collective-permute-start(bf16[1024,256]{1,0:T(8,128)(2,1)S(1)} %collective-permute-done.4.refs_3_), channel_id=1, source_target_pairs={{0,16},{16,0},{1,17},{17,1},{2,18},{18,2},{3,19},{19,3},{4,20},{20... | collective-permute-start | bytes 1572872 | tf_op jit(solution)/shard_map/ppermute | solution.py:376
  41.3 2.5 %shard_map.98 = (f32[2,512,256]{2,1,0:T(8,128)S(1)}, f32[512,256]{1,0:T(8,128)S(1)}, f32[512,256]{1,0:T(8,128)S(1)}, f32[1,512,256]{2,1,0:T(8,128)S(1)}, f32[512,128]{1,0:T(8,128)S(1)}) custom-call(bf16[512,2048]{1,0:T(8,128)(2,1)S(1)} %copy-done.2, bf16[512,2048]{1,0:T(8,128)(2,1)S(1)} %collective-permute-done.1.refs_0_.refs_1_, ...), custom_call_target="tpu_custom_call" | custom-call | flops 1000 | bytes 1000 | tf_op jit(solution)/shard_map/pallas_call | solution.py:156
  43.9 1.6 %collective-permute-start.12 = (bf16[1024,256]{1,0:T(8,128)(2,1)S(1)}, bf16[1024,256]{1,0:T(8,128)(2,1)S(1)}, u32[]{:S(2)}, u32[]{:S(2)}) collective-permute-start(bf16[1024,256]{1,0:T(8,128)(2,1)S(1)} %collective-permute-done.8.refs_7_), channel_id=1, source_target_pairs={{0,4},{1,3},{4,8},{5,1},{8,12},{9,5},{12,14},{13,9},{14,10},{15,13... | collective-permute-start | bytes 1572872 | tf_op jit(solution)/shard_map/ppermute | solution.py:373
  45.9 4.2 %collective-permute-done.14.refs_6_ = bf16[1024,256]{1,0:T(8,128)(2,1)S(1)} collective-permute-done((bf16[1024,256]{1,0:T(8,128)(2,1)S(1)}, bf16[1024,256]{1,0:T(8,128)(2,1)S(1)}, u32[]{:S(2)}, u32[]{:S(2)}) %collective-permute-start.14) | collective-permute-done | bytes 524320 | tf_op jit(solution)/shard_map/ppermute | solution.py:370
  50.1 3.0 %collective-permute-done.13.refs_4_ = bf16[1024,256]{1,0:T(8,128)(2,1)S(1)} collective-permute-done((bf16[1024,256]{1,0:T(8,128)(2,1)S(1)}, bf16[1024,256]{1,0:T(8,128)(2,1)S(1)}, u32[]{:S(2)}, u32[]{:S(2)}) %collective-permute-start.13) | collective-permute-done | bytes 524320 | tf_op jit(solution)/shard_map/ppermute | solution.py:376
  54.4 3.9 %shard_map.99 = (f32[3,512,256]{2,1,0:T(8,128)S(1)}, f32[2,512,256]{2,1,0:T(8,128)S(1)}, f32[1,512,256]{2,1,0:T(8,128)S(1)}, f32[1,512,256]{2,1,0:T(8,128)S(1)}, f32[512,128]{1,0:T(8,128)S(1)}) custom-call(bf16[512,2048]{1,0:T(8,128)(2,1)S(1)} %copy-done.2, bf16[512,2048]{1,0:T(8,128)(2,1)S(1)} %collective-permute-done.1.refs_0_.refs_1_, ...), custom_call_target="tpu_custom_call" | custom-call | flops 1000 | bytes 1000 | tf_op jit(solution)/shard_map/pallas_call | solution.py:156
  58.3 1.7 %collective-permute-start.17 = (bf16[1024,256]{1,0:T(8,128)(2,1)S(1)}, bf16[1024,256]{1,0:T(8,128)(2,1)S(1)}, u32[]{:S(2)}, u32[]{:S(2)}) collective-permute-start(bf16[1024,256]{1,0:T(8,128)(2,1)S(1)} %collective-permute-done.13.refs_4_), channel_id=1, source_target_pairs={{0,4},{1,3},{4,8},{5,1},{8,12},{9,5},{12,14},{13,9},{14,10},{15,13... | collective-permute-start | bytes 1572872 | tf_op jit(solution)/shard_map/ppermute | solution.py:373
  62.8 2.6 %collective-permute-done.18.refs_0_ = bf16[1024,256]{1,0:T(8,128)(2,1)S(1)} collective-permute-done((bf16[1024,256]{1,0:T(8,128)(2,1)S(1)}, bf16[1024,256]{1,0:T(8,128)(2,1)S(1)}, u32[]{:S(2)}, u32[]{:S(2)}) %collective-permute-start.18) | collective-permute-done | bytes 524320 | tf_op jit(solution)/shard_map/ppermute | solution.py:376
  68.1 1.8 %shard_map.102 = (f32[4,512,256]{2,1,0:T(8,128)S(1)}, f32[512,128]{1,0:T(8,128)S(1)}) custom-call(bf16[512,2048]{1,0:T(8,128)(2,1)S(1)} %copy-done.2, bf16[512,4096]{1,0:T(8,128)(2,1)S(1)} %copy-done, f32[512,128]{1,0:T(8,128)S(1)} %get-tuple-element.125.before, bf16[1024,256]{1,0:T(8,128)(2,1)S(1)} %collective-permute-done.17.refs_0_, ...), custom_call_target="tpu_custom_call" | custom-call | flops 1000 | bytes 1000 | tf_op jit(solution)/shard_map/pallas_call | solution.py:192
  70.2 3.7 %shard_map.103 = (f32[1,4096]{1,0:T(1,128)}, bf16[8,48,128]{2,1,0:T(8,128)(2,1)S(1)}) custom-call(bf16[512,2048]{1,0:T(8,128)(2,1)S(1)} %copy-done.2, bf16[512,4096]{1,0:T(8,128)(2,1)S(1)} %copy-done, f32[512,128]{1,0:T(8,128)S(1)} %get-tuple-element.129.before, f32[1,4096]{1,0:T(1,128)S(1)} %bitcast.3, f32[1,128]{1,0:T(1,128)S(1)} %fusion.flags, ...), custom_call_target="tpu_custom_call" | custom-call | flops 1000 | bytes 1000 | tf_op jit(solution)/shard_map/pallas_call | solution.py:253
  73.9 13.5 %all_to_all.10.got = bf16[8,48,128]{2,1,0:T(8,128)(2,1)S(1)} all-to-all(bf16[8,48,128]{2,1,0:T(8,128)(2,1)S(1)} %get-tuple-element.141), channel_id=1, replica_groups={{0,2,4,6,8,10,12,14},{1,3,5,7,9,11,13,15},{16,18,20,22,24,26,28,30},{17..., dimensions={0} | all-to-all | bytes 196608 | tf_op jit(solution)/shard_map/all_to_all | solution.py:476
  88.6 10.0 %all_to_all.11.got = f32[8,40,128]{2,1,0:T(8,128)S(1)} all-to-all(f32[8,40,128]{2,1,0:T(8,128)S(1)} %shard_map.104), channel_id=1, replica_groups={{0,2,4,6,8,10,12,14},{1,3,5,7,9,11,13,15},{16,18,20,22,24,26,28,30},{17..., dimensions={0} | all-to-all | bytes 327680 | tf_op jit(solution)/shard_map/all_to_all | solution.py:476
  (58 shorter events, 16.5 us)
Async XLA Ops:
  0.6 16.9 %collective-permute-start.1 = (bf16[512,2048]{1,0:T(8,128)(2,1)}, bf16[512,2048]{1,0:T(8,128)(2,1)S(1)}, u32[]{:S(2)}, u32[]{:S(2)}) collective-permute-start(bf16[512,2048]{1,0:T(8,128)(2,1)} %context.7), channel_id=1, source_target_pairs={{0,1},{1,0},{2,3},{3,2},{4,5},{5,4},{6,7},{7,6},{8,9},{9,8},{10,11... | collective-permute-start | bytes 6291464 | tf_op jit(solution)/shard_map/ppermute | solution.py:379
  2.4 11.3 %collective-permute-start.2 = (bf16[1024,256]{1,0:T(8,128)(2,1)S(1)}, bf16[1024,256]{1,0:T(8,128)(2,1)S(1)}, u32[]{:S(2)}, u32[]{:S(2)}) collective-permute-start(bf16[1024,256]{1,0:T(8,128)(2,1)S(1)} %shard_map.94), channel_id=1, source_target_pairs={{0,2},{1,5},{4,0},{5,9},{8,4},{9,13},{12,8},{13,15},{14,12},{15,11... | collective-permute-start | bytes 1572872 | tf_op jit(solution)/shard_map/ppermute | solution.py:370
  5.0 14.5 %collective-permute-start.3 = (bf16[112,4096]{1,0:T(8,128)(2,1)}, bf16[112,4096]{1,0:T(8,128)(2,1)S(1)}, u32[]{:S(2)}, u32[]{:S(2)}) collective-permute-start(bf16[112,4096]{1,0:T(8,128)(2,1)} %queries.1), channel_id=1, source_target_pairs={{0,1},{1,0},{2,3},{3,2},{4,5},{5,4},{6,7},{7,6},{8,9},{9,8},{10,11... | collective-permute-start | bytes 2752520 | tf_op jit(solution)/shard_map/ppermute | solution.py:379
  7.8 11.7 %collective-permute-start = (bf16[1024,256]{1,0:T(8,128)(2,1)S(1)}, bf16[1024,256]{1,0:T(8,128)(2,1)S(1)}, u32[]{:S(2)}, u32[]{:S(2)}) collective-permute-start(bf16[1024,256]{1,0:T(8,128)(2,1)S(1)} %shard_map.94), channel_id=1, source_target_pairs={{0,4},{1,3},{4,8},{5,1},{8,12},{9,5},{12,14},{13,9},{14,10},{15,13... | collective-permute-start | bytes 1572872 | tf_op jit(solution)/shard_map/ppermute | solution.py:373
  13.7 10.5 %collective-permute-start.6 = (bf16[1024,256]{1,0:T(8,128)(2,1)S(1)}, bf16[1024,256]{1,0:T(8,128)(2,1)S(1)}, u32[]{:S(2)}, u32[]{:S(2)}) collective-permute-start(bf16[1024,256]{1,0:T(8,128)(2,1)S(1)} %collective-permute-done.2.refs_3_), channel_id=1, source_target_pairs={{0,2},{1,5},{4,0},{5,9},{8,4},{9,13},{12,8},{13,15},{14,12},{15,11... | collective-permute-start | bytes 1572872 | tf_op jit(solution)/shard_map/ppermute | solution.py:370
  16.1 14.2 %collective-permute-start.5 = (bf16[1024,256]{1,0:T(8,128)(2,1)S(1)}, bf16[1024,256]{1,0:T(8,128)(2,1)S(1)}, u32[]{:S(2)}, u32[]{:S(2)}) collective-permute-start(bf16[1024,256]{1,0:T(8,128)(2,1)S(1)} %collective-permute-done.2.refs_3_), channel_id=1, source_target_pairs={{0,16},{16,0},{1,17},{17,1},{2,18},{18,2},{3,19},{19,3},{4,20},{20... | collective-permute-start | bytes 1572872 | tf_op jit(solution)/shard_map/ppermute | solution.py:376
  19.5 10.8 %collective-permute-start.7 = (f32[512,256]{1,0:T(8,128)S(1)}, f32[512,256]{1,0:T(8,128)S(1)}, u32[]{:S(2)}, u32[]{:S(2)}) collective-permute-start(f32[512,256]{1,0:T(8,128)S(1)} %shard_map.96), channel_id=1, source_target_pairs={{0,1},{1,0},{2,3},{3,2},{4,5},{5,4},{6,7},{7,6},{8,9},{9,8},{10,11... | collective-permute-start | bytes 1572872 | tf_op jit(solution)/shard_map/ppermute | solution.py:379
  19.5 12.6 %collective-permute-start.4 = (bf16[1024,256]{1,0:T(8,128)(2,1)S(1)}, bf16[1024,256]{1,0:T(8,128)(2,1)S(1)}, u32[]{:S(2)}, u32[]{:S(2)}) collective-permute-start(bf16[1024,256]{1,0:T(8,128)(2,1)S(1)} %collective-permute-done.refs_5_), channel_id=1, source_target_pairs={{0,4},{1,3},{4,8},{5,1},{8,12},{9,5},{12,14},{13,9},{14,10},{15,13... | collective-permute-start | bytes 1572872 | tf_op jit(solution)/shard_map/ppermute | solution.py:373
  24.2 15.2 %collective-permute-start.10 = (bf16[1024,256]{1,0:T(8,128)(2,1)S(1)}, bf16[1024,256]{1,0:T(8,128)(2,1)S(1)}, u32[]{:S(2)}, u32[]{:S(2)}) collective-permute-start(bf16[1024,256]{1,0:T(8,128)(2,1)S(1)} %collective-permute-done.6.refs_3_), channel_id=1, source_target_pairs={{0,16},{16,0},{1,17},{17,1},{2,18},{18,2},{3,19},{19,3},{4,20},{20... | collective-permute-start | bytes 1572872 | tf_op jit(solution)/shard_map/ppermute | solution.py:376
  26.2 13.6 %collective-permute-start.9 = (bf16[1024,256]{1,0:T(8,128)(2,1)S(1)}, bf16[1024,256]{1,0:T(8,128)(2,1)S(1)}, u32[]{:S(2)}, u32[]{:S(2)}) collective-permute-start(bf16[1024,256]{1,0:T(8,128)(2,1)S(1)} %collective-permute-done.6.refs_3_), channel_id=1, source_target_pairs={{0,2},{1,5},{4,0},{5,9},{8,4},{9,13},{12,8},{13,15},{14,12},{15,11... | collective-permute-start | bytes 1572872 | tf_op jit(solution)/shard_map/ppermute | solution.py:370
  32.1 9.3 %collective-permute-start.11 = (f32[512,256]{1,0:T(8,128)S(1)}, f32[512,256]{1,0:T(8,128)S(1)}, u32[]{:S(2)}, u32[]{:S(2)}) collective-permute-start(f32[512,256]{1,0:T(8,128)S(1)} %get-tuple-element.94), channel_id=1, source_target_pairs={{0,1},{1,0},{2,3},{3,2},{4,5},{5,4},{6,7},{7,6},{8,9},{9,8},{10,11... | collective-permute-start | bytes 1572872 | tf_op jit(solution)/shard_map/ppermute | solution.py:379
  32.2 11.7 %collective-permute-start.8 = (bf16[1024,256]{1,0:T(8,128)(2,1)S(1)}, bf16[1024,256]{1,0:T(8,128)(2,1)S(1)}, u32[]{:S(2)}, u32[]{:S(2)}) collective-permute-start(bf16[1024,256]{1,0:T(8,128)(2,1)S(1)} %collective-permute-done.4.refs_3_), channel_id=1, source_target_pairs={{0,4},{1,3},{4,8},{5,1},{8,12},{9,5},{12,14},{13,9},{14,10},{15,13... | collective-permute-start | bytes 1572872 | tf_op jit(solution)/shard_map/ppermute | solution.py:373
  39.4 10.7 %collective-permute-start.14 = (bf16[1024,256]{1,0:T(8,128)(2,1)S(1)}, bf16[1024,256]{1,0:T(8,128)(2,1)S(1)}, u32[]{:S(2)}, u32[]{:S(2)}) collective-permute-start(bf16[1024,256]{1,0:T(8,128)(2,1)S(1)} %collective-permute-done.10.refs_4_), channel_id=1, source_target_pairs={{0,2},{1,5},{4,0},{5,9},{8,4},{9,13},{12,8},{13,15},{14,12},{15,11... | collective-permute-start | bytes 1572872 | tf_op jit(solution)/shard_map/ppermute | solution.py:370
  39.8 13.3 %collective-permute-start.13 = (bf16[1024,256]{1,0:T(8,128)(2,1)S(1)}, bf16[1024,256]{1,0:T(8,128)(2,1)S(1)}, u32[]{:S(2)}, u32[]{:S(2)}) collective-permute-start(bf16[1024,256]{1,0:T(8,128)(2,1)S(1)} %collective-permute-done.4.refs_3_), channel_id=1, source_target_pairs={{0,16},{16,0},{1,17},{17,1},{2,18},{18,2},{3,19},{19,3},{4,20},{20... | collective-permute-start | bytes 1572872 | tf_op jit(solution)/shard_map/ppermute | solution.py:376
  43.8 10.5 %collective-permute-start.15 = (f32[512,256]{1,0:T(8,128)S(1)}, f32[512,256]{1,0:T(8,128)S(1)}, u32[]{:S(2)}, u32[]{:S(2)}) collective-permute-start(f32[512,256]{1,0:T(8,128)S(1)} %get-tuple-element.106), channel_id=1, source_target_pairs={{0,1},{1,0},{2,3},{3,2},{4,5},{5,4},{6,7},{7,6},{8,9},{9,8},{10,11... | collective-permute-start | bytes 1572872 | tf_op jit(solution)/shard_map/ppermute | solution.py:379
  43.9 14.4 %collective-permute-start.12 = (bf16[1024,256]{1,0:T(8,128)(2,1)S(1)}, bf16[1024,256]{1,0:T(8,128)(2,1)S(1)}, u32[]{:S(2)}, u32[]{:S(2)}) collective-permute-start(bf16[1024,256]{1,0:T(8,128)(2,1)S(1)} %collective-permute-done.8.refs_7_), channel_id=1, source_target_pairs={{0,4},{1,3},{4,8},{5,1},{8,12},{9,5},{12,14},{13,9},{14,10},{15,13... | collective-permute-start | bytes 1572872 | tf_op jit(solution)/shard_map/ppermute | solution.py:373
  45.6 12.8 %collective-permute-start.16 = (f32[512,256]{1,0:T(8,128)S(1)}, f32[512,256]{1,0:T(8,128)S(1)}, u32[]{:S(2)}, u32[]{:S(2)}) collective-permute-start(f32[512,256]{1,0:T(8,128)S(1)} %get-tuple-element.111), channel_id=1, source_target_pairs={{0,1},{1,0},{2,3},{3,2},{4,5},{5,4},{6,7},{7,6},{8,9},{9,8},{10,11... | collective-permute-start | bytes 1572872 | tf_op jit(solution)/shard_map/ppermute | solution.py:379
  50.1 10.5 %collective-permute-start.19 = (bf16[1024,256]{1,0:T(8,128)(2,1)S(1)}, bf16[1024,256]{1,0:T(8,128)(2,1)S(1)}, u32[]{:S(2)}, u32[]{:S(2)}) collective-permute-start(bf16[1024,256]{1,0:T(8,128)(2,1)S(1)} %collective-permute-done.14.refs_6_), channel_id=1, source_target_pairs={{0,2},{1,5},{4,0},{5,9},{8,4},{9,13},{12,8},{13,15},{14,12},{15,11... | collective-permute-start | bytes 1572872 | tf_op jit(solution)/shard_map/ppermute | solution.py:370
  53.1 12.3 %collective-permute-start.18 = (bf16[1024,256]{1,0:T(8,128)(2,1)S(1)}, bf16[1024,256]{1,0:T(8,128)(2,1)S(1)}, u32[]{:S(2)}, u32[]{:S(2)}) collective-permute-start(bf16[1024,256]{1,0:T(8,128)(2,1)S(1)} %collective-permute-done.refs_5_), channel_id=1, source_target_pairs={{0,16},{16,0},{1,17},{17,1},{2,18},{18,2},{3,19},{19,3},{4,20},{20... | collective-permute-start | bytes 1572872 | tf_op jit(solution)/shard_map/ppermute | solution.py:376
  58.3 9.2 %collective-permute-start.17 = (bf16[1024,256]{1,0:T(8,128)(2,1)S(1)}, bf16[1024,256]{1,0:T(8,128)(2,1)S(1)}, u32[]{:S(2)}, u32[]{:S(2)}) collective-permute-start(bf16[1024,256]{1,0:T(8,128)(2,1)S(1)} %collective-permute-done.13.refs_4_), channel_id=1, source_target_pairs={{0,4},{1,3},{4,8},{5,1},{8,12},{9,5},{12,14},{13,9},{14,10},{15,13... | collective-permute-start | bytes 1572872 | tf_op jit(solution)/shard_map/ppermute | solution.py:373
  60.1 8.0 %collective-permute-start.22 = (f32[2,512,256]{2,1,0:T(8,128)S(1)}, f32[2,512,256]{2,1,0:T(8,128)S(1)}, u32[]{:S(2)}, u32[]{:S(2)}) collective-permute-start(f32[2,512,256]{2,1,0:T(8,128)S(1)} %get-tuple-element.128), channel_id=1, source_target_pairs={{0,1},{1,0},{2,3},{3,2},{4,5},{5,4},{6,7},{7,6},{8,9},{9,8},{10,11... | collective-permute-start | bytes 3145736 | tf_op jit(solution)/shard_map/ppermute | solution.py:379
  60.6 7.0 %collective-permute-start.21 = (bf16[1024,256]{1,0:T(8,128)(2,1)S(1)}, bf16[1024,256]{1,0:T(8,128)(2,1)S(1)}, u32[]{:S(2)}, u32[]{:S(2)}) collective-permute-start(bf16[1024,256]{1,0:T(8,128)(2,1)S(1)} %collective-permute-done.19.refs_1_), channel_id=1, source_target_pairs={{0,1},{1,0},{2,3},{3,2},{4,5},{5,4},{6,7},{7,6},{8,9},{9,8},{10,11... | collective-permute-start | bytes 1572872 | tf_op jit(solution)/shard_map/ppermute | solution.py:379
  61.2 6.8 %collective-permute-start.20 = (bf16[1024,256]{1,0:T(8,128)(2,1)S(1)}, bf16[1024,256]{1,0:T(8,128)(2,1)S(1)}, u32[]{:S(2)}, u32[]{:S(2)}) collective-permute-start(bf16[1024,256]{1,0:T(8,128)(2,1)S(1)} %collective-permute-done.12.refs_0_), channel_id=1, source_target_pairs={{0,1},{1,0},{2,3},{3,2},{4,5},{5,4},{6,7},{7,6},{8,9},{9,8},{10,11... | collective-permute-start | bytes 1572872 | tf_op jit(solution)/shard_map/ppermute | solution.py:379
  65.4 4.5 %collective-permute-start.23 = (bf16[1024,256]{1,0:T(8,128)(2,1)S(1)}, bf16[1024,256]{1,0:T(8,128)(2,1)S(1)}, u32[]{:S(2)}, u32[]{:S(2)}) collective-permute-start(bf16[1024,256]{1,0:T(8,128)(2,1)S(1)} %collective-permute-done.18.refs_0_), channel_id=1, source_target_pairs={{0,1},{1,0},{2,3},{3,2},{4,5},{5,4},{6,7},{7,6},{8,9},{9,8},{10,11... | collective-permute-start | bytes 1572872 | tf_op jit(solution)/shard_map/ppermute | solution.py:379
  (9 other events, 74.7 us)

commit v18 on v13

--- a/solution.py
+++ b/solution.py
@@ -421,11 +421,13 @@
     r3a, r3p = other_core(t3a), other_core(t3p)
     l4s = other_core(l4)
 
-    n4x, l4 = wait((a, l4))
+    n4x, l4, own_pattern, lengths = wait((a, l4, pattern, lengths))
+    flags = jnp.pad(own_pattern.astype(jnp.float32), ((0, 0), (0, LANES - 1 - pattern.shape[1])))
+    flags = jnp.concatenate([flags, lengths.astype(jnp.float32)[:, None]], axis=1)
     n4xs = other_core(n4x)
     items = ((None, ((0, False), (1, True)), True, 4, True),)
     h4, sq4 = late(items, context, residual, sq3, [l4, n4x], [])
-    xl1, n4x, sq4 = wait((x, n4x, sq4))
+    xl1, n4x, sq4, flags = wait((x, n4x, sq4, flags))
     xl1s = other_core(xl1)
     items = (((0, 1), ((0, True),), False, -1, True),)
     h5, sq5 = late(items, context, residual, sq4, [xl1], [h2])
@@ -456,8 +458,6 @@
         (7, 2, 3, False),
         (7, 3, 4, False),
     )
-    flags = jnp.pad(pattern.astype(jnp.float32), ((0, 0), (0, LANES - 1 - pattern.shape[1])))
-    flags = jnp.concatenate([flags, lengths.astype(jnp.float32)[:, None]], axis=1)
     embedded, payload = finish(
         items, sources, context, residual, sq6, norm_gain.reshape(1, -1), flags, [xl1s, l3xs], hidden, size
     )

time: 99.3 us -> 98.8 us (level)
  transfers between devices with their start and end apart: 26 -> 26, of which waited for: 10 -> 11; matrix products, arithmetic and copies ran while one was open for 0% -> 0% of each run, Pallas kernels for 13% -> 14%
where the time goes in v18:
time: 98.8 us; the launch traced here: 98.6 us
  waiting for transfers between devices  28.8 us (29%)
  starting transfers between devices  23.7 us (24%)
  blocking collectives  23.5 us (24%)
  Pallas kernels  18.2 us (18%)
  local copies, waits for them, and re-layouts  2.84 us (3%)
  between operations  1.48 us (1%)
    all_to_all x2, blocking collectives, spread(): lax.all_to_all(blocks, 'dp', 0, 0, axis_index_groups=same_core, tiled=True)  23.5 us
    ppermute x4, waiting for transfers between devices, over_x(): return lax.ppermute(piece, 'groups', [(0, 1), (1, 0)])  14.2 us
    ppermute x5, waiting for transfers between devices, from_next(): return lax.ppermute(piece, 'dp', ring(-1))  11.8 us
    pallas_call x5, Pallas kernels, wave(): pl.pallas_call(functools.partial(wave_kernel, full, part, arrived, whole,...  9.95 us
    ppermute x5, starting transfers between devices, from_last(): return lax.ppermute(piece, 'dp', ring(1))  8.04 us
    ppermute x5, starting transfers between devices, from_next(): return lax.ppermute(piece, 'dp', ring(-1))  7.1 us
    ppermute x4, starting transfers between devices, over_x(): return lax.ppermute(piece, 'groups', [(0, 1), (1, 0)])  6.24 us
    pallas_call x3, Pallas kernels, late(): pl.pallas_call(functools.partial(late_kernel, items, len(pieces)), out_sh...  3.37 us
  transfers between devices with their start and end apart: 26, of which 11 were waited for; matrix products, arithmetic and copies ran while one was open for 0% of the time, Pallas kernels for 14%

profile of v18, /device:TPU:0, one launch (start us, length us, event | category | flops | bytes accessed | tf_op | source)
XLA Modules:
  0.0 98.6 jit_solution(12349537185980396603)
XLA Ops:
  2.4 2.6 %collective-permute-start.2 = (bf16[1024,256]{1,0:T(8,128)(2,1)S(1)}, bf16[1024,256]{1,0:T(8,128)(2,1)S(1)}, u32[]{:S(2)}, u32[]{:S(2)}) collective-permute-start(bf16[1024,256]{1,0:T(8,128)(2,1)S(1)} %shard_map.94), channel_id=1, source_target_pairs={{0,2},{1,5},{4,0},{5,9},{8,4},{9,13},{12,8},{13,15},{14,12},{15,11... | collective-permute-start | bytes 1572872 | tf_op jit(solution)/shard_map/ppermute | solution.py:362
  5.3 1.6 %copy-done.1 = bf16[512,2048]{1,0:T(8,128)(2,1)S(1)} copy-done((bf16[512,2048]{1,0:T(8,128)(2,1)S(1)}, bf16[512,2048]{1,0:T(8,128)(2,1)}, u32[]{:S(2)}) %copy-start.1) | copy-done | bytes 2097176
  7.8 1.6 %collective-permute-start = (bf16[1024,256]{1,0:T(8,128)(2,1)S(1)}, bf16[1024,256]{1,0:T(8,128)(2,1)S(1)}, u32[]{:S(2)}, u32[]{:S(2)}) collective-permute-start(bf16[1024,256]{1,0:T(8,128)(2,1)S(1)} %shard_map.94), channel_id=1, source_target_pairs={{0,4},{1,3},{4,8},{5,1},{8,12},{9,5},{12,14},{13,9},{14,10},{15,13... | collective-permute-start | bytes 1572872 | tf_op jit(solution)/shard_map/ppermute | solution.py:365
  9.4 4.3 %collective-permute-done.2.refs_3_ = bf16[1024,256]{1,0:T(8,128)(2,1)S(1)} collective-permute-done((bf16[1024,256]{1,0:T(8,128)(2,1)S(1)}, bf16[1024,256]{1,0:T(8,128)(2,1)S(1)}, u32[]{:S(2)}, u32[]{:S(2)}) %collective-permute-start.2) | collective-permute-done | bytes 524320 | tf_op jit(solution)/shard_map/ppermute | solution.py:362
  13.7 2.3 %collective-permute-start.6 = (bf16[1024,256]{1,0:T(8,128)(2,1)S(1)}, bf16[1024,256]{1,0:T(8,128)(2,1)S(1)}, u32[]{:S(2)}, u32[]{:S(2)}) collective-permute-start(bf16[1024,256]{1,0:T(8,128)(2,1)S(1)} %collective-permute-done.2.refs_3_), channel_id=1, source_target_pairs={{0,2},{1,5},{4,0},{5,9},{8,4},{9,13},{12,8},{13,15},{14,12},{15,11... | collective-permute-start | bytes 1572872 | tf_op jit(solution)/shard_map/ppermute | solution.py:362
  19.5 2.0 %collective-permute-start.4 = (bf16[1024,256]{1,0:T(8,128)(2,1)S(1)}, bf16[1024,256]{1,0:T(8,128)(2,1)S(1)}, u32[]{:S(2)}, u32[]{:S(2)}) collective-permute-start(bf16[1024,256]{1,0:T(8,128)(2,1)S(1)} %collective-permute-done.refs_5_), channel_id=1, source_target_pairs={{0,4},{1,3},{4,8},{5,1},{8,12},{9,5},{12,14},{13,9},{14,10},{15,13... | collective-permute-start | bytes 1572872 | tf_op jit(solution)/shard_map/ppermute | solution.py:365
  21.5 2.8 %collective-permute-done.6.refs_3_ = bf16[1024,256]{1,0:T(8,128)(2,1)S(1)} collective-permute-done((bf16[1024,256]{1,0:T(8,128)(2,1)S(1)}, bf16[1024,256]{1,0:T(8,128)(2,1)S(1)}, u32[]{:S(2)}, u32[]{:S(2)}) %collective-permute-start.6) | collective-permute-done | bytes 524320 | tf_op jit(solution)/shard_map/ppermute | solution.py:362
  24.2 2.0 %collective-permute-start.10 = (bf16[1024,256]{1,0:T(8,128)(2,1)S(1)}, bf16[1024,256]{1,0:T(8,128)(2,1)S(1)}, u32[]{:S(2)}, u32[]{:S(2)}) collective-permute-start(bf16[1024,256]{1,0:T(8,128)(2,1)S(1)} %collective-permute-done.6.refs_3_), channel_id=1, source_target_pairs={{0,16},{16,0},{1,17},{17,1},{2,18},{18,2},{3,19},{19,3},{4,20},{20... | collective-permute-start | bytes 1572872 | tf_op jit(solution)/shard_map/ppermute | solution.py:368
  26.2 1.7 %collective-permute-start.9 = (bf16[1024,256]{1,0:T(8,128)(2,1)S(1)}, bf16[1024,256]{1,0:T(8,128)(2,1)S(1)}, u32[]{:S(2)}, u32[]{:S(2)}) collective-permute-start(bf16[1024,256]{1,0:T(8,128)(2,1)S(1)} %collective-permute-done.6.refs_3_), channel_id=1, source_target_pairs={{0,2},{1,5},{4,0},{5,9},{8,4},{9,13},{12,8},{13,15},{14,12},{15,11... | collective-permute-start | bytes 1572872 | tf_op jit(solution)/shard_map/ppermute | solution.py:362
  27.9 2.3 %collective-permute-done.5.refs_4_ = bf16[1024,256]{1,0:T(8,128)(2,1)S(1)} collective-permute-done((bf16[1024,256]{1,0:T(8,128)(2,1)S(1)}, bf16[1024,256]{1,0:T(8,128)(2,1)S(1)}, u32[]{:S(2)}, u32[]{:S(2)}) %collective-permute-start.5) | collective-permute-done | bytes 524320 | tf_op jit(solution)/shard_map/ppermute | solution.py:368
  30.3 1.8 %shard_map.97 = (f32[1,512,256]{2,1,0:T(8,128)S(1)}, f32[512,256]{1,0:T(8,128)S(1)}, f32[2,512,256]{2,1,0:T(8,128)S(1)}, f32[512,128]{1,0:T(8,128)S(1)}) custom-call(bf16[512,2048]{1,0:T(8,128)(2,1)S(1)} %copy-done.2, bf16[512,2048]{1,0:T(8,128)(2,1)S(1)} %collective-permute-done.1.refs_0_.refs_1_, bf16[512,4096]{1,0:T(8,128)(2,1)S(1)} %copy-done, ...), custom_call_target="tpu_custom_call" | custom-call | flops 1000 | bytes 1000 | tf_op jit(solution)/shard_map/pallas_call | solution.py:155
  33.2 6.2 %collective-permute-done.10.refs_4_ = bf16[1024,256]{1,0:T(8,128)(2,1)S(1)} collective-permute-done((bf16[1024,256]{1,0:T(8,128)(2,1)S(1)}, bf16[1024,256]{1,0:T(8,128)(2,1)S(1)}, u32[]{:S(2)}, u32[]{:S(2)}) %collective-permute-start.10) | collective-permute-done | bytes 524320 | tf_op jit(solution)/shard_map/ppermute | solution.py:368
  39.8 1.5 %collective-permute-start.13 = (bf16[1024,256]{1,0:T(8,128)(2,1)S(1)}, bf16[1024,256]{1,0:T(8,128)(2,1)S(1)}, u32[]{:S(2)}, u32[]{:S(2)}) collective-permute-start(bf16[1024,256]{1,0:T(8,128)(2,1)S(1)} %collective-permute-done.4.refs_3_), channel_id=1, source_target_pairs={{0,16},{16,0},{1,17},{17,1},{2,18},{18,2},{3,19},{19,3},{4,20},{20... | collective-permute-start | bytes 1572872 | tf_op jit(solution)/shard_map/ppermute | solution.py:368
  41.3 2.5 %shard_map.98 = (f32[2,512,256]{2,1,0:T(8,128)S(1)}, f32[512,256]{1,0:T(8,128)S(1)}, f32[512,256]{1,0:T(8,128)S(1)}, f32[1,512,256]{2,1,0:T(8,128)S(1)}, f32[512,128]{1,0:T(8,128)S(1)}) custom-call(bf16[512,2048]{1,0:T(8,128)(2,1)S(1)} %copy-done.2, bf16[512,2048]{1,0:T(8,128)(2,1)S(1)} %collective-permute-done.1.refs_0_.refs_1_, ...), custom_call_target="tpu_custom_call" | custom-call | flops 1000 | bytes 1000 | tf_op jit(solution)/shard_map/pallas_call | solution.py:155
  43.9 1.6 %collective-permute-start.12 = (bf16[1024,256]{1,0:T(8,128)(2,1)S(1)}, bf16[1024,256]{1,0:T(8,128)(2,1)S(1)}, u32[]{:S(2)}, u32[]{:S(2)}) collective-permute-start(bf16[1024,256]{1,0:T(8,128)(2,1)S(1)} %collective-permute-done.8.refs_7_), channel_id=1, source_target_pairs={{0,4},{1,3},{4,8},{5,1},{8,12},{9,5},{12,14},{13,9},{14,10},{15,13... | collective-permute-start | bytes 1572872 | tf_op jit(solution)/shard_map/ppermute | solution.py:365
  45.9 4.2 %collective-permute-done.14.refs_6_ = bf16[1024,256]{1,0:T(8,128)(2,1)S(1)} collective-permute-done((bf16[1024,256]{1,0:T(8,128)(2,1)S(1)}, bf16[1024,256]{1,0:T(8,128)(2,1)S(1)}, u32[]{:S(2)}, u32[]{:S(2)}) %collective-permute-start.14) | collective-permute-done | bytes 524320 | tf_op jit(solution)/shard_map/ppermute | solution.py:362
  50.1 3.0 %collective-permute-done.13.refs_4_ = bf16[1024,256]{1,0:T(8,128)(2,1)S(1)} collective-permute-done((bf16[1024,256]{1,0:T(8,128)(2,1)S(1)}, bf16[1024,256]{1,0:T(8,128)(2,1)S(1)}, u32[]{:S(2)}, u32[]{:S(2)}) %collective-permute-start.13) | collective-permute-done | bytes 524320 | tf_op jit(solution)/shard_map/ppermute | solution.py:368
  54.4 3.9 %shard_map.99 = (f32[3,512,256]{2,1,0:T(8,128)S(1)}, f32[2,512,256]{2,1,0:T(8,128)S(1)}, f32[1,512,256]{2,1,0:T(8,128)S(1)}, f32[1,512,256]{2,1,0:T(8,128)S(1)}, f32[512,128]{1,0:T(8,128)S(1)}) custom-call(bf16[512,2048]{1,0:T(8,128)(2,1)S(1)} %copy-done.2, bf16[512,2048]{1,0:T(8,128)(2,1)S(1)} %collective-permute-done.1.refs_0_.refs_1_, ...), custom_call_target="tpu_custom_call" | custom-call | flops 1000 | bytes 1000 | tf_op jit(solution)/shard_map/pallas_call | solution.py:155
  58.3 1.7 %collective-permute-start.17 = (bf16[1024,256]{1,0:T(8,128)(2,1)S(1)}, bf16[1024,256]{1,0:T(8,128)(2,1)S(1)}, u32[]{:S(2)}, u32[]{:S(2)}) collective-permute-start(bf16[1024,256]{1,0:T(8,128)(2,1)S(1)} %collective-permute-done.13.refs_4_), channel_id=1, source_target_pairs={{0,4},{1,3},{4,8},{5,1},{8,12},{9,5},{12,14},{13,9},{14,10},{15,13... | collective-permute-start | bytes 1572872 | tf_op jit(solution)/shard_map/ppermute | solution.py:365
  62.8 2.6 %collective-permute-done.18.refs_0_ = bf16[1024,256]{1,0:T(8,128)(2,1)S(1)} collective-permute-done((bf16[1024,256]{1,0:T(8,128)(2,1)S(1)}, bf16[1024,256]{1,0:T(8,128)(2,1)S(1)}, u32[]{:S(2)}, u32[]{:S(2)}) %collective-permute-start.18) | collective-permute-done | bytes 524320 | tf_op jit(solution)/shard_map/ppermute | solution.py:368
  68.1 1.8 %shard_map.102 = (f32[4,512,256]{2,1,0:T(8,128)S(1)}, f32[512,128]{1,0:T(8,128)S(1)}) custom-call(bf16[512,2048]{1,0:T(8,128)(2,1)S(1)} %copy-done.2, bf16[512,4096]{1,0:T(8,128)(2,1)S(1)} %copy-done, f32[512,128]{1,0:T(8,128)S(1)} %get-tuple-element.125.before, bf16[1024,256]{1,0:T(8,128)(2,1)S(1)} %collective-permute-done.17.refs_0_, ...), custom_call_target="tpu_custom_call" | custom-call | flops 1000 | bytes 1000 | tf_op jit(solution)/shard_map/pallas_call | solution.py:191
  70.2 2.9 %shard_map.103 = (f32[1,4096]{1,0:T(1,128)}, bf16[8,48,128]{2,1,0:T(8,128)(2,1)S(1)}) custom-call(bf16[512,2048]{1,0:T(8,128)(2,1)S(1)} %copy-done.2, bf16[512,4096]{1,0:T(8,128)(2,1)S(1)} %copy-done, f32[512,128]{1,0:T(8,128)S(1)} %get-tuple-element.129.before, f32[1,4096]{1,0:T(1,128)S(1)} %bitcast.3, f32[1,128]{1,0:T(1,128)S(1)} %fusion.flags, ...), custom_call_target="tpu_custom_call" | custom-call | flops 1000 | bytes 1000 | tf_op jit(solution)/shard_map/pallas_call | solution.py:245
  73.2 13.5 %all_to_all.10.got = bf16[8,48,128]{2,1,0:T(8,128)(2,1)S(1)} all-to-all(bf16[8,48,128]{2,1,0:T(8,128)(2,1)S(1)} %get-tuple-element.141), channel_id=1, replica_groups={{0,2,4,6,8,10,12,14},{1,3,5,7,9,11,13,15},{16,18,20,22,24,26,28,30},{17..., dimensions={0} | all-to-all | bytes 196608 | tf_op jit(solution)/shard_map/all_to_all | solution.py:468
  87.8 10.0 %all_to_all.11.got = f32[8,40,128]{2,1,0:T(8,128)S(1)} all-to-all(f32[8,40,128]{2,1,0:T(8,128)S(1)} %shard_map.104), channel_id=1, replica_groups={{0,2,4,6,8,10,12,14},{1,3,5,7,9,11,13,15},{16,18,20,22,24,26,28,30},{17..., dimensions={0} | all-to-all | bytes 327680 | tf_op jit(solution)/shard_map/all_to_all | solution.py:468
  (58 shorter events, 16.5 us)
Async XLA Ops:
  0.6 16.9 %collective-permute-start.1 = (bf16[512,2048]{1,0:T(8,128)(2,1)}, bf16[512,2048]{1,0:T(8,128)(2,1)S(1)}, u32[]{:S(2)}, u32[]{:S(2)}) collective-permute-start(bf16[512,2048]{1,0:T(8,128)(2,1)} %context.7), channel_id=1, source_target_pairs={{0,1},{1,0},{2,3},{3,2},{4,5},{5,4},{6,7},{7,6},{8,9},{9,8},{10,11... | collective-permute-start | bytes 6291464 | tf_op jit(solution)/shard_map/ppermute | solution.py:371
  2.4 11.3 %collective-permute-start.2 = (bf16[1024,256]{1,0:T(8,128)(2,1)S(1)}, bf16[1024,256]{1,0:T(8,128)(2,1)S(1)}, u32[]{:S(2)}, u32[]{:S(2)}) collective-permute-start(bf16[1024,256]{1,0:T(8,128)(2,1)S(1)} %shard_map.94), channel_id=1, source_target_pairs={{0,2},{1,5},{4,0},{5,9},{8,4},{9,13},{12,8},{13,15},{14,12},{15,11... | collective-permute-start | bytes 1572872 | tf_op jit(solution)/shard_map/ppermute | solution.py:362
  5.0 14.5 %collective-permute-start.3 = (bf16[112,4096]{1,0:T(8,128)(2,1)}, bf16[112,4096]{1,0:T(8,128)(2,1)S(1)}, u32[]{:S(2)}, u32[]{:S(2)}) collective-permute-start(bf16[112,4096]{1,0:T(8,128)(2,1)} %queries.1), channel_id=1, source_target_pairs={{0,1},{1,0},{2,3},{3,2},{4,5},{5,4},{6,7},{7,6},{8,9},{9,8},{10,11... | collective-permute-start | bytes 2752520 | tf_op jit(solution)/shard_map/ppermute | solution.py:371
  7.8 11.7 %collective-permute-start = (bf16[1024,256]{1,0:T(8,128)(2,1)S(1)}, bf16[1024,256]{1,0:T(8,128)(2,1)S(1)}, u32[]{:S(2)}, u32[]{:S(2)}) collective-permute-start(bf16[1024,256]{1,0:T(8,128)(2,1)S(1)} %shard_map.94), channel_id=1, source_target_pairs={{0,4},{1,3},{4,8},{5,1},{8,12},{9,5},{12,14},{13,9},{14,10},{15,13... | collective-permute-start | bytes 1572872 | tf_op jit(solution)/shard_map/ppermute | solution.py:365
  13.7 10.5 %collective-permute-start.6 = (bf16[1024,256]{1,0:T(8,128)(2,1)S(1)}, bf16[1024,256]{1,0:T(8,128)(2,1)S(1)}, u32[]{:S(2)}, u32[]{:S(2)}) collective-permute-start(bf16[1024,256]{1,0:T(8,128)(2,1)S(1)} %collective-permute-done.2.refs_3_), channel_id=1, source_target_pairs={{0,2},{1,5},{4,0},{5,9},{8,4},{9,13},{12,8},{13,15},{14,12},{15,11... | collective-permute-start | bytes 1572872 | tf_op jit(solution)/shard_map/ppermute | solution.py:362
  16.1 14.2 %collective-permute-start.5 = (bf16[1024,256]{1,0:T(8,128)(2,1)S(1)}, bf16[1024,256]{1,0:T(8,128)(2,1)S(1)}, u32[]{:S(2)}, u32[]{:S(2)}) collective-permute-start(bf16[1024,256]{1,0:T(8,128)(2,1)S(1)} %collective-permute-done.2.refs_3_), channel_id=1, source_target_pairs={{0,16},{16,0},{1,17},{17,1},{2,18},{18,2},{3,19},{19,3},{4,20},{20... | collective-permute-start | bytes 1572872 | tf_op jit(solution)/shard_map/ppermute | solution.py:368
  19.5 10.8 %collective-permute-start.7 = (f32[512,256]{1,0:T(8,128)S(1)}, f32[512,256]{1,0:T(8,128)S(1)}, u32[]{:S(2)}, u32[]{:S(2)}) collective-permute-start(f32[512,256]{1,0:T(8,128)S(1)} %shard_map.96), channel_id=1, source_target_pairs={{0,1},{1,0},{2,3},{3,2},{4,5},{5,4},{6,7},{7,6},{8,9},{9,8},{10,11... | collective-permute-start | bytes 1572872 | tf_op jit(solution)/shard_map/ppermute | solution.py:371
  19.5 12.6 %collective-permute-start.4 = (bf16[1024,256]{1,0:T(8,128)(2,1)S(1)}, bf16[1024,256]{1,0:T(8,128)(2,1)S(1)}, u32[]{:S(2)}, u32[]{:S(2)}) collective-permute-start(bf16[1024,256]{1,0:T(8,128)(2,1)S(1)} %collective-permute-done.refs_5_), channel_id=1, source_target_pairs={{0,4},{1,3},{4,8},{5,1},{8,12},{9,5},{12,14},{13,9},{14,10},{15,13... | collective-permute-start | bytes 1572872 | tf_op jit(solution)/shard_map/ppermute | solution.py:365
  24.2 15.2 %collective-permute-start.10 = (bf16[1024,256]{1,0:T(8,128)(2,1)S(1)}, bf16[1024,256]{1,0:T(8,128)(2,1)S(1)}, u32[]{:S(2)}, u32[]{:S(2)}) collective-permute-start(bf16[1024,256]{1,0:T(8,128)(2,1)S(1)} %collective-permute-done.6.refs_3_), channel_id=1, source_target_pairs={{0,16},{16,0},{1,17},{17,1},{2,18},{18,2},{3,19},{19,3},{4,20},{20... | collective-permute-start | bytes 1572872 | tf_op jit(solution)/shard_map/ppermute | solution.py:368
  26.2 13.6 %collective-permute-start.9 = (bf16[1024,256]{1,0:T(8,128)(2,1)S(1)}, bf16[1024,256]{1,0:T(8,128)(2,1)S(1)}, u32[]{:S(2)}, u32[]{:S(2)}) collective-permute-start(bf16[1024,256]{1,0:T(8,128)(2,1)S(1)} %collective-permute-done.6.refs_3_), channel_id=1, source_target_pairs={{0,2},{1,5},{4,0},{5,9},{8,4},{9,13},{12,8},{13,15},{14,12},{15,11... | collective-permute-start | bytes 1572872 | tf_op jit(solution)/shard_map/ppermute | solution.py:362
  32.1 9.3 %collective-permute-start.11 = (f32[512,256]{1,0:T(8,128)S(1)}, f32[512,256]{1,0:T(8,128)S(1)}, u32[]{:S(2)}, u32[]{:S(2)}) collective-permute-start(f32[512,256]{1,0:T(8,128)S(1)} %get-tuple-element.94), channel_id=1, source_target_pairs={{0,1},{1,0},{2,3},{3,2},{4,5},{5,4},{6,7},{7,6},{8,9},{9,8},{10,11... | collective-permute-start | bytes 1572872 | tf_op jit(solution)/shard_map/ppermute | solution.py:371
  32.2 11.7 %collective-permute-start.8 = (bf16[1024,256]{1,0:T(8,128)(2,1)S(1)}, bf16[1024,256]{1,0:T(8,128)(2,1)S(1)}, u32[]{:S(2)}, u32[]{:S(2)}) collective-permute-start(bf16[1024,256]{1,0:T(8,128)(2,1)S(1)} %collective-permute-done.4.refs_3_), channel_id=1, source_target_pairs={{0,4},{1,3},{4,8},{5,1},{8,12},{9,5},{12,14},{13,9},{14,10},{15,13... | collective-permute-start | bytes 1572872 | tf_op jit(solution)/shard_map/ppermute | solution.py:365
  39.4 10.7 %collective-permute-start.14 = (bf16[1024,256]{1,0:T(8,128)(2,1)S(1)}, bf16[1024,256]{1,0:T(8,128)(2,1)S(1)}, u32[]{:S(2)}, u32[]{:S(2)}) collective-permute-start(bf16[1024,256]{1,0:T(8,128)(2,1)S(1)} %collective-permute-done.10.refs_4_), channel_id=1, source_target_pairs={{0,2},{1,5},{4,0},{5,9},{8,4},{9,13},{12,8},{13,15},{14,12},{15,11... | collective-permute-start | bytes 1572872 | tf_op jit(solution)/shard_map/ppermute | solution.py:362
  39.8 13.3 %collective-permute-start.13 = (bf16[1024,256]{1,0:T(8,128)(2,1)S(1)}, bf16[1024,256]{1,0:T(8,128)(2,1)S(1)}, u32[]{:S(2)}, u32[]{:S(2)}) collective-permute-start(bf16[1024,256]{1,0:T(8,128)(2,1)S(1)} %collective-permute-done.4.refs_3_), channel_id=1, source_target_pairs={{0,16},{16,0},{1,17},{17,1},{2,18},{18,2},{3,19},{19,3},{4,20},{20... | collective-permute-start | bytes 1572872 | tf_op jit(solution)/shard_map/ppermute | solution.py:368
  43.8 10.5 %collective-permute-start.15 = (f32[512,256]{1,0:T(8,128)S(1)}, f32[512,256]{1,0:T(8,128)S(1)}, u32[]{:S(2)}, u32[]{:S(2)}) collective-permute-start(f32[512,256]{1,0:T(8,128)S(1)} %get-tuple-element.106), channel_id=1, source_target_pairs={{0,1},{1,0},{2,3},{3,2},{4,5},{5,4},{6,7},{7,6},{8,9},{9,8},{10,11... | collective-permute-start | bytes 1572872 | tf_op jit(solution)/shard_map/ppermute | solution.py:371
  43.9 14.4 %collective-permute-start.12 = (bf16[1024,256]{1,0:T(8,128)(2,1)S(1)}, bf16[1024,256]{1,0:T(8,128)(2,1)S(1)}, u32[]{:S(2)}, u32[]{:S(2)}) collective-permute-start(bf16[1024,256]{1,0:T(8,128)(2,1)S(1)} %collective-permute-done.8.refs_7_), channel_id=1, source_target_pairs={{0,4},{1,3},{4,8},{5,1},{8,12},{9,5},{12,14},{13,9},{14,10},{15,13... | collective-permute-start | bytes 1572872 | tf_op jit(solution)/shard_map/ppermute | solution.py:365
  45.6 12.8 %collective-permute-start.16 = (f32[512,256]{1,0:T(8,128)S(1)}, f32[512,256]{1,0:T(8,128)S(1)}, u32[]{:S(2)}, u32[]{:S(2)}) collective-permute-start(f32[512,256]{1,0:T(8,128)S(1)} %get-tuple-element.111), channel_id=1, source_target_pairs={{0,1},{1,0},{2,3},{3,2},{4,5},{5,4},{6,7},{7,6},{8,9},{9,8},{10,11... | collective-permute-start | bytes 1572872 | tf_op jit(solution)/shard_map/ppermute | solution.py:371
  50.1 10.5 %collective-permute-start.19 = (bf16[1024,256]{1,0:T(8,128)(2,1)S(1)}, bf16[1024,256]{1,0:T(8,128)(2,1)S(1)}, u32[]{:S(2)}, u32[]{:S(2)}) collective-permute-start(bf16[1024,256]{1,0:T(8,128)(2,1)S(1)} %collective-permute-done.14.refs_6_), channel_id=1, source_target_pairs={{0,2},{1,5},{4,0},{5,9},{8,4},{9,13},{12,8},{13,15},{14,12},{15,11... | collective-permute-start | bytes 1572872 | tf_op jit(solution)/shard_map/ppermute | solution.py:362
  53.1 12.3 %collective-permute-start.18 = (bf16[1024,256]{1,0:T(8,128)(2,1)S(1)}, bf16[1024,256]{1,0:T(8,128)(2,1)S(1)}, u32[]{:S(2)}, u32[]{:S(2)}) collective-permute-start(bf16[1024,256]{1,0:T(8,128)(2,1)S(1)} %collective-permute-done.refs_5_), channel_id=1, source_target_pairs={{0,16},{16,0},{1,17},{17,1},{2,18},{18,2},{3,19},{19,3},{4,20},{20... | collective-permute-start | bytes 1572872 | tf_op jit(solution)/shard_map/ppermute | solution.py:368
  58.3 9.2 %collective-permute-start.17 = (bf16[1024,256]{1,0:T(8,128)(2,1)S(1)}, bf16[1024,256]{1,0:T(8,128)(2,1)S(1)}, u32[]{:S(2)}, u32[]{:S(2)}) collective-permute-start(bf16[1024,256]{1,0:T(8,128)(2,1)S(1)} %collective-permute-done.13.refs_4_), channel_id=1, source_target_pairs={{0,4},{1,3},{4,8},{5,1},{8,12},{9,5},{12,14},{13,9},{14,10},{15,13... | collective-permute-start | bytes 1572872 | tf_op jit(solution)/shard_map/ppermute | solution.py:365
  60.1 8.0 %collective-permute-start.22 = (f32[2,512,256]{2,1,0:T(8,128)S(1)}, f32[2,512,256]{2,1,0:T(8,128)S(1)}, u32[]{:S(2)}, u32[]{:S(2)}) collective-permute-start(f32[2,512,256]{2,1,0:T(8,128)S(1)} %get-tuple-element.128), channel_id=1, source_target_pairs={{0,1},{1,0},{2,3},{3,2},{4,5},{5,4},{6,7},{7,6},{8,9},{9,8},{10,11... | collective-permute-start | bytes 3145736 | tf_op jit(solution)/shard_map/ppermute | solution.py:371
  60.6 7.0 %collective-permute-start.21 = (bf16[1024,256]{1,0:T(8,128)(2,1)S(1)}, bf16[1024,256]{1,0:T(8,128)(2,1)S(1)}, u32[]{:S(2)}, u32[]{:S(2)}) collective-permute-start(bf16[1024,256]{1,0:T(8,128)(2,1)S(1)} %collective-permute-done.19.refs_1_), channel_id=1, source_target_pairs={{0,1},{1,0},{2,3},{3,2},{4,5},{5,4},{6,7},{7,6},{8,9},{9,8},{10,11... | collective-permute-start | bytes 1572872 | tf_op jit(solution)/shard_map/ppermute | solution.py:371
  61.2 6.8 %collective-permute-start.20 = (bf16[1024,256]{1,0:T(8,128)(2,1)S(1)}, bf16[1024,256]{1,0:T(8,128)(2,1)S(1)}, u32[]{:S(2)}, u32[]{:S(2)}) collective-permute-start(bf16[1024,256]{1,0:T(8,128)(2,1)S(1)} %collective-permute-done.12.refs_0_), channel_id=1, source_target_pairs={{0,1},{1,0},{2,3},{3,2},{4,5},{5,4},{6,7},{7,6},{8,9},{9,8},{10,11... | collective-permute-start | bytes 1572872 | tf_op jit(solution)/shard_map/ppermute | solution.py:371
  65.4 4.5 %collective-permute-start.23 = (bf16[1024,256]{1,0:T(8,128)(2,1)S(1)}, bf16[1024,256]{1,0:T(8,128)(2,1)S(1)}, u32[]{:S(2)}, u32[]{:S(2)}) collective-permute-start(bf16[1024,256]{1,0:T(8,128)(2,1)S(1)} %collective-permute-done.18.refs_0_), channel_id=1, source_target_pairs={{0,1},{1,0},{2,3},{3,2},{4,5},{5,4},{6,7},{7,6},{8,9},{9,8},{10,11... | collective-permute-start | bytes 1572872 | tf_op jit(solution)/shard_map/ppermute | solution.py:371
  (9 other events, 73.9 us)

commit v19 on v13

--- a/solution.py
+++ b/solution.py
@@ -405,11 +405,13 @@
     a2 = from_next(xn2)
     n3, xn2 = wait((a, xn2))
     h2, t2, t2p, f1, sq2 = wave((2,), (-1,), ((1, False),), context, context2, residual, [n2, xn2, l1], [r1], sq1)
-    l3, n3, t2, t2p, sq2 = wait((b, n3, t2, t2p, sq2))
+    l3, n3, t2, t2p, sq2, own_pattern, lengths = wait((b, n3, t2, t2p, sq2, pattern, lengths))
     b = from_last(l3)
     r2, r2p = other_core(t2), other_core(t2p)
 
-    n3x, l3 = wait((a2, l3))
+    flags = jnp.pad(own_pattern.astype(jnp.float32), ((0, 0), (0, LANES - 1 - pattern.shape[1])))
+    flags = jnp.concatenate([flags, lengths.astype(jnp.float32)[:, None]], axis=1)
+    n3x, l3, flags = wait((a2, l3, flags))
     a = from_next(n3x)
     xl2, l1, n3x = wait((x, l1, n3x))
     x = over_x(l1)
@@ -456,8 +458,6 @@
         (7, 2, 3, False),
         (7, 3, 4, False),
     )
-    flags = jnp.pad(pattern.astype(jnp.float32), ((0, 0), (0, LANES - 1 - pattern.shape[1])))
-    flags = jnp.concatenate([flags, lengths.astype(jnp.float32)[:, None]], axis=1)
     embedded, payload = finish(
         items, sources, context, residual, sq6, norm_gain.reshape(1, -1), flags, [xl1s, l3xs], hidden, size
     )

time: 99.3 us -> 100 us (level)
    ppermute x5, waiting for transfers between devices: 11.8 us -> 9.65 us  [from_next(): return lax.ppermute(piece, 'dp', ring(-1))]
    ppermute x4, waiting for transfers between devices: 15 us -> 17 us  [over_x(): return lax.ppermute(piece, 'groups', [(0, 1), (1, 0)])]
where the time goes in v19:
time: 100 us
  waiting for transfers between devices  29.5 us (30%)
  blocking collectives  24.2 us (24%)
  starting transfers between devices  23.7 us (24%)
  Pallas kernels  18.2 us (18%)
  local copies, waits for them, and re-layouts  2.84 us (3%)
  between operations  1.49 us (1%)
    all_to_all x2, blocking collectives, spread(): lax.all_to_all(blocks, 'dp', 0, 0, axis_index_groups=same_core, tiled=True)  24.2 us
    ppermute x4, waiting for transfers between devices, over_x(): return lax.ppermute(piece, 'groups', [(0, 1), (1, 0)])  17 us
    pallas_call x5, Pallas kernels, wave(): pl.pallas_call(functools.partial(wave_kernel, full, part, arrived, whole,...  9.98 us
    ppermute x5, waiting for transfers between devices, from_next(): return lax.ppermute(piece, 'dp', ring(-1))  9.65 us
    ppermute x5, starting transfers between devices, from_last(): return lax.ppermute(piece, 'dp', ring(1))  8.01 us
    ppermute x5, starting transfers between devices, from_next(): return lax.ppermute(piece, 'dp', ring(-1))  7.1 us
    ppermute x4, starting transfers between devices, over_x(): return lax.ppermute(piece, 'groups', [(0, 1), (1, 0)])  6.31 us
    pallas_call x3, Pallas kernels, late(): pl.pallas_call(functools.partial(late_kernel, items, len(pieces)), out_sh...  3.38 us
  transfers between devices with their start and end apart: 26, of which 10 were waited for; matrix products, arithmetic and copies ran while one was open for 0% of the time, Pallas kernels for 13%

profile of v19, /device:TPU:0, one launch (start us, length us, event | category | flops | bytes accessed | tf_op | source)
XLA Modules:
  0.0 100.0 jit_solution(18015570253028814680)
XLA Ops:
  2.4 2.6 %collective-permute-start.2 = (bf16[1024,256]{1,0:T(8,128)(2,1)S(1)}, bf16[1024,256]{1,0:T(8,128)(2,1)S(1)}, u32[]{:S(2)}, u32[]{:S(2)}) collective-permute-start(bf16[1024,256]{1,0:T(8,128)(2,1)S(1)} %shard_map.94), channel_id=1, source_target_pairs={{0,2},{1,5},{4,0},{5,9},{8,4},{9,13},{12,8},{13,15},{14,12},{15,11... | collective-permute-start | bytes 1572872 | tf_op jit(solution)/shard_map/ppermute | solution.py:362
  5.3 1.6 %copy-done.1 = bf16[512,2048]{1,0:T(8,128)(2,1)S(1)} copy-done((bf16[512,2048]{1,0:T(8,128)(2,1)S(1)}, bf16[512,2048]{1,0:T(8,128)(2,1)}, u32[]{:S(2)}) %copy-start.1) | copy-done | bytes 2097176
  7.8 1.6 %collective-permute-start = (bf16[1024,256]{1,0:T(8,128)(2,1)S(1)}, bf16[1024,256]{1,0:T(8,128)(2,1)S(1)}, u32[]{:S(2)}, u32[]{:S(2)}) collective-permute-start(bf16[1024,256]{1,0:T(8,128)(2,1)S(1)} %shard_map.94), channel_id=1, source_target_pairs={{0,4},{1,3},{4,8},{5,1},{8,12},{9,5},{12,14},{13,9},{14,10},{15,13... | collective-permute-start | bytes 1572872 | tf_op jit(solution)/shard_map/ppermute | solution.py:365
  9.4 4.3 %collective-permute-done.2.refs_3_ = bf16[1024,256]{1,0:T(8,128)(2,1)S(1)} collective-permute-done((bf16[1024,256]{1,0:T(8,128)(2,1)S(1)}, bf16[1024,256]{1,0:T(8,128)(2,1)S(1)}, u32[]{:S(2)}, u32[]{:S(2)}) %collective-permute-start.2) | collective-permute-done | bytes 524320 | tf_op jit(solution)/shard_map/ppermute | solution.py:362
  13.7 2.3 %collective-permute-start.6 = (bf16[1024,256]{1,0:T(8,128)(2,1)S(1)}, bf16[1024,256]{1,0:T(8,128)(2,1)S(1)}, u32[]{:S(2)}, u32[]{:S(2)}) collective-permute-start(bf16[1024,256]{1,0:T(8,128)(2,1)S(1)} %collective-permute-done.2.refs_3_), channel_id=1, source_target_pairs={{0,2},{1,5},{4,0},{5,9},{8,4},{9,13},{12,8},{13,15},{14,12},{15,11... | collective-permute-start | bytes 1572872 | tf_op jit(solution)/shard_map/ppermute | solution.py:362
  19.5 2.0 %collective-permute-start.4 = (bf16[1024,256]{1,0:T(8,128)(2,1)S(1)}, bf16[1024,256]{1,0:T(8,128)(2,1)S(1)}, u32[]{:S(2)}, u32[]{:S(2)}) collective-permute-start(bf16[1024,256]{1,0:T(8,128)(2,1)S(1)} %collective-permute-done.refs_5_), channel_id=1, source_target_pairs={{0,4},{1,3},{4,8},{5,1},{8,12},{9,5},{12,14},{13,9},{14,10},{15,13... | collective-permute-start | bytes 1572872 | tf_op jit(solution)/shard_map/ppermute | solution.py:365
  21.5 2.8 %collective-permute-done.6.refs_3_ = bf16[1024,256]{1,0:T(8,128)(2,1)S(1)} collective-permute-done((bf16[1024,256]{1,0:T(8,128)(2,1)S(1)}, bf16[1024,256]{1,0:T(8,128)(2,1)S(1)}, u32[]{:S(2)}, u32[]{:S(2)}) %collective-permute-start.6) | collective-permute-done | bytes 524320 | tf_op jit(solution)/shard_map/ppermute | solution.py:362
  24.2 2.0 %collective-permute-start.10 = (bf16[1024,256]{1,0:T(8,128)(2,1)S(1)}, bf16[1024,256]{1,0:T(8,128)(2,1)S(1)}, u32[]{:S(2)}, u32[]{:S(2)}) collective-permute-start(bf16[1024,256]{1,0:T(8,128)(2,1)S(1)} %collective-permute-done.6.refs_3_), channel_id=1, source_target_pairs={{0,16},{16,0},{1,17},{17,1},{2,18},{18,2},{3,19},{19,3},{4,20},{20... | collective-permute-start | bytes 1572872 | tf_op jit(solution)/shard_map/ppermute | solution.py:368
  26.2 1.7 %collective-permute-start.9 = (bf16[1024,256]{1,0:T(8,128)(2,1)S(1)}, bf16[1024,256]{1,0:T(8,128)(2,1)S(1)}, u32[]{:S(2)}, u32[]{:S(2)}) collective-permute-start(bf16[1024,256]{1,0:T(8,128)(2,1)S(1)} %collective-permute-done.6.refs_3_), channel_id=1, source_target_pairs={{0,2},{1,5},{4,0},{5,9},{8,4},{9,13},{12,8},{13,15},{14,12},{15,11... | collective-permute-start | bytes 1572872 | tf_op jit(solution)/shard_map/ppermute | solution.py:362
  27.9 2.3 %collective-permute-done.5.refs_4_ = bf16[1024,256]{1,0:T(8,128)(2,1)S(1)} collective-permute-done((bf16[1024,256]{1,0:T(8,128)(2,1)S(1)}, bf16[1024,256]{1,0:T(8,128)(2,1)S(1)}, u32[]{:S(2)}, u32[]{:S(2)}) %collective-permute-start.5) | collective-permute-done | bytes 524320 | tf_op jit(solution)/shard_map/ppermute | solution.py:368
  30.3 1.8 %shard_map.97 = (f32[1,512,256]{2,1,0:T(8,128)S(1)}, f32[512,256]{1,0:T(8,128)S(1)}, f32[2,512,256]{2,1,0:T(8,128)S(1)}, f32[512,128]{1,0:T(8,128)S(1)}) custom-call(bf16[512,2048]{1,0:T(8,128)(2,1)S(1)} %copy-done.2, bf16[512,2048]{1,0:T(8,128)(2,1)S(1)} %collective-permute-done.1.refs_0_.refs_1_, bf16[512,4096]{1,0:T(8,128)(2,1)S(1)} %copy-done, ...), custom_call_target="tpu_custom_call" | custom-call | flops 1000 | bytes 1000 | tf_op jit(solution)/shard_map/pallas_call | solution.py:155
  33.2 6.2 %collective-permute-done.10.refs_4_ = bf16[1024,256]{1,0:T(8,128)(2,1)S(1)} collective-permute-done((bf16[1024,256]{1,0:T(8,128)(2,1)S(1)}, bf16[1024,256]{1,0:T(8,128)(2,1)S(1)}, u32[]{:S(2)}, u32[]{:S(2)}) %collective-permute-start.10) | collective-permute-done | bytes 524320 | tf_op jit(solution)/shard_map/ppermute | solution.py:368
  40.5 1.6 %collective-permute-start.13 = (bf16[1024,256]{1,0:T(8,128)(2,1)S(1)}, bf16[1024,256]{1,0:T(8,128)(2,1)S(1)}, u32[]{:S(2)}, u32[]{:S(2)}) collective-permute-start(bf16[1024,256]{1,0:T(8,128)(2,1)S(1)} %collective-permute-done.4.refs_3_), channel_id=1, source_target_pairs={{0,16},{16,0},{1,17},{17,1},{2,18},{18,2},{3,19},{19,3},{4,20},{20... | collective-permute-start | bytes 1572872 | tf_op jit(solution)/shard_map/ppermute | solution.py:368
  42.1 2.5 %shard_map.98 = (f32[2,512,256]{2,1,0:T(8,128)S(1)}, f32[512,256]{1,0:T(8,128)S(1)}, f32[512,256]{1,0:T(8,128)S(1)}, f32[1,512,256]{2,1,0:T(8,128)S(1)}, f32[512,128]{1,0:T(8,128)S(1)}) custom-call(bf16[512,2048]{1,0:T(8,128)(2,1)S(1)} %copy-done.2, bf16[512,2048]{1,0:T(8,128)(2,1)S(1)} %collective-permute-done.1.refs_0_.refs_1_, ...), custom_call_target="tpu_custom_call" | custom-call | flops 1000 | bytes 1000 | tf_op jit(solution)/shard_map/pallas_call | solution.py:155
  44.7 1.6 %collective-permute-start.12 = (bf16[1024,256]{1,0:T(8,128)(2,1)S(1)}, bf16[1024,256]{1,0:T(8,128)(2,1)S(1)}, u32[]{:S(2)}, u32[]{:S(2)}) collective-permute-start(bf16[1024,256]{1,0:T(8,128)(2,1)S(1)} %collective-permute-done.8.refs_7_), channel_id=1, source_target_pairs={{0,4},{1,3},{4,8},{5,1},{8,12},{9,5},{12,14},{13,9},{14,10},{15,13... | collective-permute-start | bytes 1572872 | tf_op jit(solution)/shard_map/ppermute | solution.py:365
  46.7 2.6 %collective-permute-done.14.refs_6_ = bf16[1024,256]{1,0:T(8,128)(2,1)S(1)} collective-permute-done((bf16[1024,256]{1,0:T(8,128)(2,1)S(1)}, bf16[1024,256]{1,0:T(8,128)(2,1)S(1)}, u32[]{:S(2)}, u32[]{:S(2)}) %collective-permute-start.14) | collective-permute-done | bytes 524320 | tf_op jit(solution)/shard_map/ppermute | solution.py:362
  49.3 4.5 %collective-permute-done.13.refs_4_ = bf16[1024,256]{1,0:T(8,128)(2,1)S(1)} collective-permute-done((bf16[1024,256]{1,0:T(8,128)(2,1)S(1)}, bf16[1024,256]{1,0:T(8,128)(2,1)S(1)}, u32[]{:S(2)}, u32[]{:S(2)}) %collective-permute-start.13) | collective-permute-done | bytes 524320 | tf_op jit(solution)/shard_map/ppermute | solution.py:368
  55.1 3.9 %shard_map.99 = (f32[3,512,256]{2,1,0:T(8,128)S(1)}, f32[2,512,256]{2,1,0:T(8,128)S(1)}, f32[1,512,256]{2,1,0:T(8,128)S(1)}, f32[1,512,256]{2,1,0:T(8,128)S(1)}, f32[512,128]{1,0:T(8,128)S(1)}) custom-call(bf16[512,2048]{1,0:T(8,128)(2,1)S(1)} %copy-done.2, bf16[512,2048]{1,0:T(8,128)(2,1)S(1)} %collective-permute-done.1.refs_0_.refs_1_, ...), custom_call_target="tpu_custom_call" | custom-call | flops 1000 | bytes 1000 | tf_op jit(solution)/shard_map/pallas_call | solution.py:155
  59.1 1.7 %collective-permute-start.17 = (bf16[1024,256]{1,0:T(8,128)(2,1)S(1)}, bf16[1024,256]{1,0:T(8,128)(2,1)S(1)}, u32[]{:S(2)}, u32[]{:S(2)}) collective-permute-start(bf16[1024,256]{1,0:T(8,128)(2,1)S(1)} %collective-permute-done.13.refs_4_), channel_id=1, source_target_pairs={{0,4},{1,3},{4,8},{5,1},{8,12},{9,5},{12,14},{13,9},{14,10},{15,13... | collective-permute-start | bytes 1572872 | tf_op jit(solution)/shard_map/ppermute | solution.py:365
  62.2 3.9 %collective-permute-done.18.refs_0_ = bf16[1024,256]{1,0:T(8,128)(2,1)S(1)} collective-permute-done((bf16[1024,256]{1,0:T(8,128)(2,1)S(1)}, bf16[1024,256]{1,0:T(8,128)(2,1)S(1)}, u32[]{:S(2)}, u32[]{:S(2)}) %collective-permute-start.18) | collective-permute-done | bytes 524320 | tf_op jit(solution)/shard_map/ppermute | solution.py:368
  68.8 1.8 %shard_map.102 = (f32[4,512,256]{2,1,0:T(8,128)S(1)}, f32[512,128]{1,0:T(8,128)S(1)}) custom-call(bf16[512,2048]{1,0:T(8,128)(2,1)S(1)} %copy-done.2, bf16[512,4096]{1,0:T(8,128)(2,1)S(1)} %copy-done, f32[512,128]{1,0:T(8,128)S(1)} %get-tuple-element.125.before, bf16[1024,256]{1,0:T(8,128)(2,1)S(1)} %collective-permute-done.17.refs_0_, ...), custom_call_target="tpu_custom_call" | custom-call | flops 1000 | bytes 1000 | tf_op jit(solution)/shard_map/pallas_call | solution.py:191
  71.0 2.9 %shard_map.103 = (f32[1,4096]{1,0:T(1,128)}, bf16[8,48,128]{2,1,0:T(8,128)(2,1)S(1)}) custom-call(bf16[512,2048]{1,0:T(8,128)(2,1)S(1)} %copy-done.2, bf16[512,4096]{1,0:T(8,128)(2,1)S(1)} %copy-done, f32[512,128]{1,0:T(8,128)S(1)} %get-tuple-element.129.before, f32[1,4096]{1,0:T(1,128)S(1)} %bitcast.3, f32[1,128]{1,0:T(1,128)S(1)} %fusion.flags, ...), custom_call_target="tpu_custom_call" | custom-call | flops 1000 | bytes 1000 | tf_op jit(solution)/shard_map/pallas_call | solution.py:245
  73.9 14.2 %all_to_all.10.got = bf16[8,48,128]{2,1,0:T(8,128)(2,1)S(1)} all-to-all(bf16[8,48,128]{2,1,0:T(8,128)(2,1)S(1)} %get-tuple-element.141), channel_id=1, replica_groups={{0,2,4,6,8,10,12,14},{1,3,5,7,9,11,13,15},{16,18,20,22,24,26,28,30},{17..., dimensions={0} | all-to-all | bytes 196608 | tf_op jit(solution)/shard_map/all_to_all | solution.py:468
  89.3 10.0 %all_to_all.11.got = f32[8,40,128]{2,1,0:T(8,128)S(1)} all-to-all(f32[8,40,128]{2,1,0:T(8,128)S(1)} %shard_map.104), channel_id=1, replica_groups={{0,2,4,6,8,10,12,14},{1,3,5,7,9,11,13,15},{16,18,20,22,24,26,28,30},{17..., dimensions={0} | all-to-all | bytes 327680 | tf_op jit(solution)/shard_map/all_to_all | solution.py:468
  (58 shorter events, 15.9 us)
Async XLA Ops:
  0.6 16.9 %collective-permute-start.1 = (bf16[512,2048]{1,0:T(8,128)(2,1)}, bf16[512,2048]{1,0:T(8,128)(2,1)S(1)}, u32[]{:S(2)}, u32[]{:S(2)}) collective-permute-start(bf16[512,2048]{1,0:T(8,128)(2,1)} %context.7), channel_id=1, source_target_pairs={{0,1},{1,0},{2,3},{3,2},{4,5},{5,4},{6,7},{7,6},{8,9},{9,8},{10,11... | collective-permute-start | bytes 6291464 | tf_op jit(solution)/shard_map/ppermute | solution.py:371
  2.4 11.3 %collective-permute-start.2 = (bf16[1024,256]{1,0:T(8,128)(2,1)S(1)}, bf16[1024,256]{1,0:T(8,128)(2,1)S(1)}, u32[]{:S(2)}, u32[]{:S(2)}) collective-permute-start(bf16[1024,256]{1,0:T(8,128)(2,1)S(1)} %shard_map.94), channel_id=1, source_target_pairs={{0,2},{1,5},{4,0},{5,9},{8,4},{9,13},{12,8},{13,15},{14,12},{15,11... | collective-permute-start | bytes 1572872 | tf_op jit(solution)/shard_map/ppermute | solution.py:362
  5.0 14.5 %collective-permute-start.3 = (bf16[112,4096]{1,0:T(8,128)(2,1)}, bf16[112,4096]{1,0:T(8,128)(2,1)S(1)}, u32[]{:S(2)}, u32[]{:S(2)}) collective-permute-start(bf16[112,4096]{1,0:T(8,128)(2,1)} %queries.1), channel_id=1, source_target_pairs={{0,1},{1,0},{2,3},{3,2},{4,5},{5,4},{6,7},{7,6},{8,9},{9,8},{10,11... | collective-permute-start | bytes 2752520 | tf_op jit(solution)/shard_map/ppermute | solution.py:371
  7.8 11.7 %collective-permute-start = (bf16[1024,256]{1,0:T(8,128)(2,1)S(1)}, bf16[1024,256]{1,0:T(8,128)(2,1)S(1)}, u32[]{:S(2)}, u32[]{:S(2)}) collective-permute-start(bf16[1024,256]{1,0:T(8,128)(2,1)S(1)} %shard_map.94), channel_id=1, source_target_pairs={{0,4},{1,3},{4,8},{5,1},{8,12},{9,5},{12,14},{13,9},{14,10},{15,13... | collective-permute-start | bytes 1572872 | tf_op jit(solution)/shard_map/ppermute | solution.py:365
  13.7 10.5 %collective-permute-start.6 = (bf16[1024,256]{1,0:T(8,128)(2,1)S(1)}, bf16[1024,256]{1,0:T(8,128)(2,1)S(1)}, u32[]{:S(2)}, u32[]{:S(2)}) collective-permute-start(bf16[1024,256]{1,0:T(8,128)(2,1)S(1)} %collective-permute-done.2.refs_3_), channel_id=1, source_target_pairs={{0,2},{1,5},{4,0},{5,9},{8,4},{9,13},{12,8},{13,15},{14,12},{15,11... | collective-permute-start | bytes 1572872 | tf_op jit(solution)/shard_map/ppermute | solution.py:362
  16.1 14.2 %collective-permute-start.5 = (bf16[1024,256]{1,0:T(8,128)(2,1)S(1)}, bf16[1024,256]{1,0:T(8,128)(2,1)S(1)}, u32[]{:S(2)}, u32[]{:S(2)}) collective-permute-start(bf16[1024,256]{1,0:T(8,128)(2,1)S(1)} %collective-permute-done.2.refs_3_), channel_id=1, source_target_pairs={{0,16},{16,0},{1,17},{17,1},{2,18},{18,2},{3,19},{19,3},{4,20},{20... | collective-permute-start | bytes 1572872 | tf_op jit(solution)/shard_map/ppermute | solution.py:368
  19.5 10.8 %collective-permute-start.7 = (f32[512,256]{1,0:T(8,128)S(1)}, f32[512,256]{1,0:T(8,128)S(1)}, u32[]{:S(2)}, u32[]{:S(2)}) collective-permute-start(f32[512,256]{1,0:T(8,128)S(1)} %shard_map.96), channel_id=1, source_target_pairs={{0,1},{1,0},{2,3},{3,2},{4,5},{5,4},{6,7},{7,6},{8,9},{9,8},{10,11... | collective-permute-start | bytes 1572872 | tf_op jit(solution)/shard_map/ppermute | solution.py:371
  19.5 12.6 %collective-permute-start.4 = (bf16[1024,256]{1,0:T(8,128)(2,1)S(1)}, bf16[1024,256]{1,0:T(8,128)(2,1)S(1)}, u32[]{:S(2)}, u32[]{:S(2)}) collective-permute-start(bf16[1024,256]{1,0:T(8,128)(2,1)S(1)} %collective-permute-done.refs_5_), channel_id=1, source_target_pairs={{0,4},{1,3},{4,8},{5,1},{8,12},{9,5},{12,14},{13,9},{14,10},{15,13... | collective-permute-start | bytes 1572872 | tf_op jit(solution)/shard_map/ppermute | solution.py:365
  24.2 15.2 %collective-permute-start.10 = (bf16[1024,256]{1,0:T(8,128)(2,1)S(1)}, bf16[1024,256]{1,0:T(8,128)(2,1)S(1)}, u32[]{:S(2)}, u32[]{:S(2)}) collective-permute-start(bf16[1024,256]{1,0:T(8,128)(2,1)S(1)} %collective-permute-done.6.refs_3_), channel_id=1, source_target_pairs={{0,16},{16,0},{1,17},{17,1},{2,18},{18,2},{3,19},{19,3},{4,20},{20... | collective-permute-start | bytes 1572872 | tf_op jit(solution)/shard_map/ppermute | solution.py:368
  26.2 14.3 %collective-permute-start.9 = (bf16[1024,256]{1,0:T(8,128)(2,1)S(1)}, bf16[1024,256]{1,0:T(8,128)(2,1)S(1)}, u32[]{:S(2)}, u32[]{:S(2)}) collective-permute-start(bf16[1024,256]{1,0:T(8,128)(2,1)S(1)} %collective-permute-done.6.refs_3_), channel_id=1, source_target_pairs={{0,2},{1,5},{4,0},{5,9},{8,4},{9,13},{12,8},{13,15},{14,12},{15,11... | collective-permute-start | bytes 1572872 | tf_op jit(solution)/shard_map/ppermute | solution.py:362
  32.1 10.0 %collective-permute-start.11 = (f32[512,256]{1,0:T(8,128)S(1)}, f32[512,256]{1,0:T(8,128)S(1)}, u32[]{:S(2)}, u32[]{:S(2)}) collective-permute-start(f32[512,256]{1,0:T(8,128)S(1)} %get-tuple-element.94), channel_id=1, source_target_pairs={{0,1},{1,0},{2,3},{3,2},{4,5},{5,4},{6,7},{7,6},{8,9},{9,8},{10,11... | collective-permute-start | bytes 1572872 | tf_op jit(solution)/shard_map/ppermute | solution.py:371
  32.2 12.4 %collective-permute-start.8 = (bf16[1024,256]{1,0:T(8,128)(2,1)S(1)}, bf16[1024,256]{1,0:T(8,128)(2,1)S(1)}, u32[]{:S(2)}, u32[]{:S(2)}) collective-permute-start(bf16[1024,256]{1,0:T(8,128)(2,1)S(1)} %collective-permute-done.4.refs_3_), channel_id=1, source_target_pairs={{0,4},{1,3},{4,8},{5,1},{8,12},{9,5},{12,14},{13,9},{14,10},{15,13... | collective-permute-start | bytes 1572872 | tf_op jit(solution)/shard_map/ppermute | solution.py:365
  39.4 9.9 %collective-permute-start.14 = (bf16[1024,256]{1,0:T(8,128)(2,1)S(1)}, bf16[1024,256]{1,0:T(8,128)(2,1)S(1)}, u32[]{:S(2)}, u32[]{:S(2)}) collective-permute-start(bf16[1024,256]{1,0:T(8,128)(2,1)S(1)} %collective-permute-done.10.refs_4_), channel_id=1, source_target_pairs={{0,2},{1,5},{4,0},{5,9},{8,4},{9,13},{12,8},{13,15},{14,12},{15,11... | collective-permute-start | bytes 1572872 | tf_op jit(solution)/shard_map/ppermute | solution.py:362
  40.5 13.3 %collective-permute-start.13 = (bf16[1024,256]{1,0:T(8,128)(2,1)S(1)}, bf16[1024,256]{1,0:T(8,128)(2,1)S(1)}, u32[]{:S(2)}, u32[]{:S(2)}) collective-permute-start(bf16[1024,256]{1,0:T(8,128)(2,1)S(1)} %collective-permute-done.4.refs_3_), channel_id=1, source_target_pairs={{0,16},{16,0},{1,17},{17,1},{2,18},{18,2},{3,19},{19,3},{4,20},{20... | collective-permute-start | bytes 1572872 | tf_op jit(solution)/shard_map/ppermute | solution.py:368
  44.6 10.5 %collective-permute-start.15 = (f32[512,256]{1,0:T(8,128)S(1)}, f32[512,256]{1,0:T(8,128)S(1)}, u32[]{:S(2)}, u32[]{:S(2)}) collective-permute-start(f32[512,256]{1,0:T(8,128)S(1)} %get-tuple-element.108), channel_id=1, source_target_pairs={{0,1},{1,0},{2,3},{3,2},{4,5},{5,4},{6,7},{7,6},{8,9},{9,8},{10,11... | collective-permute-start | bytes 1572872 | tf_op jit(solution)/shard_map/ppermute | solution.py:371
  44.7 14.4 %collective-permute-start.12 = (bf16[1024,256]{1,0:T(8,128)(2,1)S(1)}, bf16[1024,256]{1,0:T(8,128)(2,1)S(1)}, u32[]{:S(2)}, u32[]{:S(2)}) collective-permute-start(bf16[1024,256]{1,0:T(8,128)(2,1)S(1)} %collective-permute-done.8.refs_7_), channel_id=1, source_target_pairs={{0,4},{1,3},{4,8},{5,1},{8,12},{9,5},{12,14},{13,9},{14,10},{15,13... | collective-permute-start | bytes 1572872 | tf_op jit(solution)/shard_map/ppermute | solution.py:365
  46.3 12.7 %collective-permute-start.16 = (f32[512,256]{1,0:T(8,128)S(1)}, f32[512,256]{1,0:T(8,128)S(1)}, u32[]{:S(2)}, u32[]{:S(2)}) collective-permute-start(f32[512,256]{1,0:T(8,128)S(1)} %get-tuple-element.113), channel_id=1, source_target_pairs={{0,1},{1,0},{2,3},{3,2},{4,5},{5,4},{6,7},{7,6},{8,9},{9,8},{10,11... | collective-permute-start | bytes 1572872 | tf_op jit(solution)/shard_map/ppermute | solution.py:371
  49.3 11.5 %collective-permute-start.19 = (bf16[1024,256]{1,0:T(8,128)(2,1)S(1)}, bf16[1024,256]{1,0:T(8,128)(2,1)S(1)}, u32[]{:S(2)}, u32[]{:S(2)}) collective-permute-start(bf16[1024,256]{1,0:T(8,128)(2,1)S(1)} %collective-permute-done.14.refs_6_), channel_id=1, source_target_pairs={{0,2},{1,5},{4,0},{5,9},{8,4},{9,13},{12,8},{13,15},{14,12},{15,11... | collective-permute-start | bytes 1572872 | tf_op jit(solution)/shard_map/ppermute | solution.py:362
  53.8 12.3 %collective-permute-start.18 = (bf16[1024,256]{1,0:T(8,128)(2,1)S(1)}, bf16[1024,256]{1,0:T(8,128)(2,1)S(1)}, u32[]{:S(2)}, u32[]{:S(2)}) collective-permute-start(bf16[1024,256]{1,0:T(8,128)(2,1)S(1)} %collective-permute-done.refs_5_), channel_id=1, source_target_pairs={{0,16},{16,0},{1,17},{17,1},{2,18},{18,2},{3,19},{19,3},{4,20},{20... | collective-permute-start | bytes 1572872 | tf_op jit(solution)/shard_map/ppermute | solution.py:368
  59.1 9.2 %collective-permute-start.17 = (bf16[1024,256]{1,0:T(8,128)(2,1)S(1)}, bf16[1024,256]{1,0:T(8,128)(2,1)S(1)}, u32[]{:S(2)}, u32[]{:S(2)}) collective-permute-start(bf16[1024,256]{1,0:T(8,128)(2,1)S(1)} %collective-permute-done.13.refs_4_), channel_id=1, source_target_pairs={{0,4},{1,3},{4,8},{5,1},{8,12},{9,5},{12,14},{13,9},{14,10},{15,13... | collective-permute-start | bytes 1572872 | tf_op jit(solution)/shard_map/ppermute | solution.py:365
  60.8 8.0 %collective-permute-start.22 = (f32[2,512,256]{2,1,0:T(8,128)S(1)}, f32[2,512,256]{2,1,0:T(8,128)S(1)}, u32[]{:S(2)}, u32[]{:S(2)}) collective-permute-start(f32[2,512,256]{2,1,0:T(8,128)S(1)} %get-tuple-element.128), channel_id=1, source_target_pairs={{0,1},{1,0},{2,3},{3,2},{4,5},{5,4},{6,7},{7,6},{8,9},{9,8},{10,11... | collective-permute-start | bytes 3145736 | tf_op jit(solution)/shard_map/ppermute | solution.py:371
  60.8 7.5 %collective-permute-start.21 = (bf16[1024,256]{1,0:T(8,128)(2,1)S(1)}, bf16[1024,256]{1,0:T(8,128)(2,1)S(1)}, u32[]{:S(2)}, u32[]{:S(2)}) collective-permute-start(bf16[1024,256]{1,0:T(8,128)(2,1)S(1)} %collective-permute-done.19.refs_1_), channel_id=1, source_target_pairs={{0,1},{1,0},{2,3},{3,2},{4,5},{5,4},{6,7},{7,6},{8,9},{9,8},{10,11... | collective-permute-start | bytes 1572872 | tf_op jit(solution)/shard_map/ppermute | solution.py:371
  61.3 7.5 %collective-permute-start.20 = (bf16[1024,256]{1,0:T(8,128)(2,1)S(1)}, bf16[1024,256]{1,0:T(8,128)(2,1)S(1)}, u32[]{:S(2)}, u32[]{:S(2)}) collective-permute-start(bf16[1024,256]{1,0:T(8,128)(2,1)S(1)} %collective-permute-done.12.refs_0_), channel_id=1, source_target_pairs={{0,1},{1,0},{2,3},{3,2},{4,5},{5,4},{6,7},{7,6},{8,9},{9,8},{10,11... | collective-permute-start | bytes 1572872 | tf_op jit(solution)/shard_map/ppermute | solution.py:371
  66.2 4.5 %collective-permute-start.23 = (bf16[1024,256]{1,0:T(8,128)(2,1)S(1)}, bf16[1024,256]{1,0:T(8,128)(2,1)S(1)}, u32[]{:S(2)}, u32[]{:S(2)}) collective-permute-start(bf16[1024,256]{1,0:T(8,128)(2,1)S(1)} %collective-permute-done.18.refs_0_), channel_id=1, source_target_pairs={{0,1},{1,0},{2,3},{3,2},{4,5},{5,4},{6,7},{7,6},{8,9},{9,8},{10,11... | collective-permute-start | bytes 1572872 | tf_op jit(solution)/shard_map/ppermute | solution.py:371
  (9 other events, 77.2 us)
